TPU v7x, 32 devices: a whole 2x2x4 slice. The times are simulated.
32 devices in a mesh: rep: 8 (over z, y), grp: 4 (over x, core).
Axes of the slice: x: 2, y: 2, z: 4, core: 2. Of those that a mesh axis runs over, the one named last changes fastest.
Arguments:
- params: float32 [14115072], P(('rep', 'grp'))
- first_moment: float32 [14115072], P(('rep', 'grp')), may hold values from -1.9073486e-05 to 1.9073486e-05
- second_moment: float32 [14115072], P(('rep', 'grp')), may hold values from 1.5420462e-13 to 6.168185e-13
- teacher: float32 [14115072], P(('rep', 'grp'))
- protos: float32 [256, 8192], P('rep', 'grp'), may hold values from -6 to 6
- proto_first: float32 [256, 8192], P('rep', 'grp'), may hold values from -1.9073486e-05 to 1.9073486e-05
- proto_second: float32 [256, 8192], P('rep', 'grp'), may hold values from 1.5420462e-13 to 6.168185e-13
- teacher_protos: float32 [256, 8192], P('rep', 'grp'), may hold values from -6 to 6
- center: float32 [8192], P('grp'), may hold values from -0.3125 to 0.3125
- patches: bfloat16 [128, 196, 768], P(('rep', 'grp')), may hold values from -6 to 6
- partner: int32 [128], P(('rep', 'grp')), may hold values from 0 to 3, as said below
Outputs:
- new_params: float32 [14115072], P(('rep', 'grp'))
- new_first: float32 [14115072], P(('rep', 'grp'))
- new_second: float32 [14115072], P(('rep', 'grp'))
- new_teacher: float32 [14115072], P(('rep', 'grp'))
- new_protos: float32 [256, 8192], P('rep', 'grp')
- new_proto_first: float32 [256, 8192], P('rep', 'grp')
- new_proto_second: float32 [256, 8192], P('rep', 'grp')
- new_teacher_protos: float32 [256, 8192], P('rep', 'grp')
- new_center: float32 [8192], P('grp')
- loss: float32 [], replicated
- grad_norm: float32 [], replicated
Inputs may be any that keep to these rules, and one draw needn't show every extreme that they name: In each aligned block of 4 views (the views of one device) partner pairs the views: partner[i] is the place in the block of another view of the block, whose partner is view i.
All inputs are finite; a program needn't handle non-finite values.
Results may differ from a plain program's by a relative error of at most 0.0071.
The roundings to bfloat16 on the way count: a program that leaves them out, or rounds other values in their place, can miss the bound.
Values may be sent and summed in bfloat16 or wider, within the bound.
No kernel may reach another device: no remote copies, remote signals or barrier semaphores. Data moves between devices by JAX's collectives and lax.ppermute only.
A program may use at most 320 MiB of HBM per device.

v0:
```python
import jax
import jax.numpy as jnp
from jax import lax
from jax.sharding import PartitionSpec as P

D = 768
HEADS = 12
HDIM = 64
F = 3072
PD = 768
NTOK = 197
H = 2048
B = 256
LAYERS = 1
STEP = 10


PRECISE = lax.Precision.HIGHEST
STUDENT_TEMP = 0.1
TEACHER_TEMP = 0.04
CENTER_MOMENTUM = 0.9
TEACHER_MOMENTUM = 0.8
CLIP_NORM = 0.05
LEARNING_RATE = 0.03
PROTO_RATE = 0.6
BETA_FIRST = 0.9
BETA_SECOND = 0.999
ADAM_EPSILON = 1e-08
WEIGHT_DECAY = 0.04


def shape_list():
    shapes = [(PD, D), (NTOK, D)]
    shapes = shapes + [(4, D), (D, 3 * D), (D, D), (D, F), (F, D)]
    return shapes + [(2, D), (D, H), (H, H), (H, B)]


def unpack(flat_params):
    pieces = []
    offset = 0
    for dims_pair in shape_list():
        entries = dims_pair[0] * dims_pair[1]
        pieces.append(flat_params[offset : offset + entries].reshape(dims_pair))
        offset = offset + entries
    return pieces


def layer_norm(stream, gain_row, shift_row):
    middle_mean = jnp.mean(stream, -1, keepdims=True)
    centred = stream - middle_mean
    spread = jnp.mean(centred * centred, -1, keepdims=True)
    return centred * lax.rsqrt(spread + 1e-06) * gain_row + shift_row


def activate(values):
    return jax.nn.gelu(values, approximate=False)


def unit_rows(values):
    return values * lax.rsqrt(jnp.sum(values * values, -1, keepdims=True) + 1e-06)


def unit_columns(table):
    return table * lax.rsqrt(jnp.sum(table * table, 0, keepdims=True) + 1e-06)


def product(left, right):
    return jnp.dot(left, right, preferred_element_type=jnp.float32)


def back_product(left, right):
    return lax.dot_general(
        left, right, (((left.ndim - 1,), (1,)), ((), ())), preferred_element_type=jnp.float32
    )


def weight_grad(left, right):
    return lax.dot_general(
        left.reshape(-1, left.shape[-1]),
        right.reshape(-1, right.shape[-1]),
        (((0,), (0,)), ((), ())),
        preferred_element_type=jnp.float32,
    )


def gelu_back(values, grad):
    return jax.vjp(activate, values)[1](grad)[0]


def block_forward(stream, weights):
    norms, qkv_w, out_w, up_w, down_w = weights
    norms = norms.astype(jnp.float32)
    view_count = stream.shape[0]
    normed = layer_norm(stream, norms[0], norms[1]).astype(jnp.bfloat16)
    qkv = product(normed, qkv_w).astype(jnp.bfloat16)
    heads_view = qkv.reshape(view_count, NTOK, 3, HEADS, HDIM)
    scores = jnp.einsum(
        "vqhd,vkhd->vhqk",
        heads_view[:, :, 0],
        heads_view[:, :, 1],
        preferred_element_type=jnp.float32,
    ) * HDIM ** (-0.5)
    row_top = jax.nn.logsumexp(scores, -1)
    probs = jnp.exp(scores - row_top[..., None]).astype(jnp.bfloat16)
    attended = jnp.einsum(
        "vhqk,vkhd->vqhd", probs, heads_view[:, :, 2], preferred_element_type=jnp.float32
    )
    attended = attended.reshape(view_count, NTOK, D).astype(jnp.bfloat16)
    middle = stream + product(attended, out_w)
    normed_two = layer_norm(middle, norms[2], norms[3]).astype(jnp.bfloat16)
    hidden = product(normed_two, up_w)
    act = activate(hidden).astype(jnp.bfloat16)
    return (
        middle + product(act, down_w),
        (stream, qkv, row_top, attended, middle, normed_two, hidden, act),
    )


def block_backward(grad_stream, stored, weights):
    norms, qkv_w, out_w, up_w, down_w = weights
    stream, qkv, row_top, attended, middle, normed_two, hidden, act = stored
    norms = norms.astype(jnp.float32)
    view_count = stream.shape[0]
    grad_branch = grad_stream.astype(jnp.bfloat16)
    grad_down = weight_grad(act, grad_branch)
    grad_hidden = gelu_back(hidden, back_product(grad_branch, down_w)).astype(jnp.bfloat16)
    grad_up = weight_grad(normed_two, grad_hidden)
    norm_back = jax.vjp(layer_norm, middle, norms[2], norms[3])[1]
    grad_middle, gain_two, shift_two = norm_back(back_product(grad_hidden, up_w))
    grad_middle = grad_middle + grad_stream
    grad_mixed = grad_middle.astype(jnp.bfloat16)
    grad_out = weight_grad(attended, grad_mixed)
    grad_att = (
        back_product(grad_mixed, out_w).astype(jnp.bfloat16).reshape(view_count, NTOK, HEADS, HDIM)
    )
    heads_view = qkv.reshape(view_count, NTOK, 3, HEADS, HDIM)
    queries, keys_part, values_part = (
        heads_view[:, :, 0],
        heads_view[:, :, 1],
        heads_view[:, :, 2],
    )
    scale_factor = HDIM ** (-0.5)
    scores = (
        jnp.einsum("vqhd,vkhd->vhqk", queries, keys_part, preferred_element_type=jnp.float32)
        * scale_factor
    )
    probs = jnp.exp(scores - row_top[..., None])
    grad_probs = jnp.einsum(
        "vqhd,vkhd->vhqk", grad_att, values_part, preferred_element_type=jnp.float32
    )
    delta = jnp.sum(probs * grad_probs, -1, keepdims=True)
    grad_scores = (probs * (grad_probs - delta)).astype(jnp.bfloat16)
    grad_q = (
        jnp.einsum("vhqk,vkhd->vqhd", grad_scores, keys_part, preferred_element_type=jnp.float32)
        * scale_factor
    )
    grad_k = (
        jnp.einsum("vhqk,vqhd->vkhd", grad_scores, queries, preferred_element_type=jnp.float32)
        * scale_factor
    )
    grad_v = jnp.einsum(
        "vhqk,vqhd->vkhd", probs.astype(jnp.bfloat16), grad_att, preferred_element_type=jnp.float32
    )
    grad_qkv = (
        jnp.stack([grad_q, grad_k, grad_v], 2).reshape(view_count, NTOK, 3 * D).astype(jnp.bfloat16)
    )
    normed, first_back = jax.vjp(layer_norm, stream, norms[0], norms[1])
    grad_qkv_w = weight_grad(normed.astype(jnp.bfloat16), grad_qkv)
    grad_input, gain_one, shift_one = first_back(back_product(grad_qkv, qkv_w))
    grad_norms = jnp.stack([gain_one, shift_one, gain_two, shift_two])
    return (grad_input + grad_middle, [grad_norms, grad_qkv_w, grad_out, grad_up, grad_down])


def trunk_forward(patches, pieces):
    view_count = patches.shape[0]
    embedded = product(patches, pieces[0])
    stream = jnp.concatenate([jnp.zeros((view_count, 1, D), jnp.float32), embedded], 1) + pieces[
        1
    ].astype(jnp.float32)
    stream, saved = block_forward(stream, pieces[2:7])
    stored = [saved]
    final = pieces[2 + 5 * LAYERS].astype(jnp.float32)
    cls, final_back = jax.vjp(layer_norm, stream[:, 0], final[0], final[1])
    cls = cls.astype(jnp.bfloat16)
    pre_one = product(cls, pieces[3 + 5 * LAYERS])
    first = activate(pre_one).astype(jnp.bfloat16)
    pre_two = product(first, pieces[4 + 5 * LAYERS])
    second = activate(pre_two).astype(jnp.bfloat16)
    unit, unit_back = jax.vjp(unit_rows, product(second, pieces[5 + 5 * LAYERS]))
    return (
        unit.astype(jnp.bfloat16),
        stored,
        (final_back, cls, pre_one, first, pre_two, second, unit_back),
    )


def head_backward(grad_unit, head_stored, pieces):
    final_back, cls, pre_one, first, pre_two, second, unit_back = head_stored
    grad_bottle = unit_back(grad_unit)[0].astype(jnp.bfloat16)
    grad_three = weight_grad(second, grad_bottle)
    grad_pre_two = gelu_back(pre_two, back_product(grad_bottle, pieces[5 + 5 * LAYERS])).astype(
        jnp.bfloat16
    )
    grad_two = weight_grad(first, grad_pre_two)
    grad_pre_one = gelu_back(pre_one, back_product(grad_pre_two, pieces[4 + 5 * LAYERS])).astype(
        jnp.bfloat16
    )
    grad_one = weight_grad(cls, grad_pre_one)
    grad_cls, grad_gain, grad_shift = final_back(back_product(grad_pre_one, pieces[3 + 5 * LAYERS]))
    return (grad_cls, [jnp.stack([grad_gain, grad_shift]), grad_one, grad_two, grad_three])


def adam_update(weight, grad, first, second, rate):
    first = BETA_FIRST * first + (1.0 - BETA_FIRST) * grad
    second = BETA_SECOND * second + (1.0 - BETA_SECOND) * grad * grad
    stepped = (
        first
        / (1.0 - BETA_FIRST**STEP)
        / (jnp.sqrt(second / (1.0 - BETA_SECOND**STEP)) + ADAM_EPSILON)
    )
    return (weight - rate * (stepped + WEIGHT_DECAY * weight), first, second)


def per_device(
    params,
    first_moment,
    second_moment,
    teacher,
    protos,
    proto_first,
    proto_second,
    teacher_protos,
    center,
    patches,
    partner,
):
    view_count = patches.shape[0]
    pieces = unpack(lax.all_gather(params.astype(jnp.bfloat16), ("rep", "grp"), axis=0, tiled=True))
    teacher_pieces = unpack(
        lax.all_gather(teacher.astype(jnp.bfloat16), ("rep", "grp"), axis=0, tiled=True)
    )
    table, teacher_table = (
        lax.all_gather(protos.astype(jnp.bfloat16), "rep", axis=0, tiled=True),
        lax.all_gather(teacher_protos.astype(jnp.bfloat16), "rep", axis=0, tiled=True),
    )
    columns, column_back = jax.vjp(unit_columns, table.astype(jnp.float32))
    columns = columns.astype(jnp.bfloat16)
    teacher_columns = unit_columns(teacher_table.astype(jnp.float32)).astype(jnp.bfloat16)
    teacher_rows = trunk_forward(patches, teacher_pieces)[0]
    selector = (partner[:, None] == jnp.arange(view_count, dtype=jnp.int32)[None, :]).astype(
        jnp.bfloat16
    )
    teacher_rows = product(selector, teacher_rows).astype(jnp.bfloat16)
    student_rows, stored, head_stored = trunk_forward(patches, pieces)
    all_rows, all_targets = (
        lax.all_gather(student_rows, "grp", axis=0, tiled=True),
        lax.all_gather(teacher_rows, "grp", axis=0, tiled=True),
    )
    teacher_logits = product(all_targets, teacher_columns)
    column_total = lax.psum(jnp.sum(teacher_logits, 0), "rep")
    total_views = view_count * lax.axis_size("rep") * lax.axis_size("grp")
    new_center = CENTER_MOMENTUM * center + (1.0 - CENTER_MOMENTUM) * column_total / total_views
    shifted = (teacher_logits - center) / TEACHER_TEMP
    scaled = product(all_rows, columns) / STUDENT_TEMP
    top_teacher, top_student = lax.pmax((jnp.max(shifted, 1), jnp.max(scaled, 1)), "grp")
    exp_teacher = jnp.exp(shifted - top_teacher[:, None])
    exp_student = jnp.exp(scaled - top_student[:, None])
    sum_teacher, sum_student = lax.psum((jnp.sum(exp_teacher, 1), jnp.sum(exp_student, 1)), "grp")
    targets = exp_teacher / sum_teacher[:, None]
    log_probs = scaled - top_student[:, None] - jnp.log(sum_student)[:, None]
    partial_loss = -jnp.sum(targets * log_probs)
    loss_value = lax.psum(partial_loss, ("rep", "grp"))
    grad_logits = (jnp.exp(log_probs) - targets) / STUDENT_TEMP
    grad_rows = jnp.dot(grad_logits, columns.astype(jnp.float32).T, precision=PRECISE)
    grad_columns = jnp.dot(all_rows.astype(jnp.float32).T, grad_logits, precision=PRECISE)
    grad_protos = lax.psum_scatter(
        column_back(grad_columns)[0], "rep", scatter_dimension=0, tiled=True
    )
    own_rows = lax.psum_scatter(grad_rows, "grp", scatter_dimension=0, tiled=True)
    own_rows = lax.optimization_barrier(own_rows.astype(jnp.bfloat16)).astype(jnp.float32)
    grad_cls, head_grads = head_backward(own_rows, head_stored, pieces)
    grad_stream = jnp.concatenate(
        [grad_cls[:, None], jnp.zeros((view_count, NTOK - 1, D), jnp.float32)], 1
    )
    layer_grads = []
    for level_index in reversed(range(LAYERS)):
        grad_stream, grads = block_backward(
            grad_stream, stored[level_index], pieces[2 + 5 * level_index : 7 + 5 * level_index]
        )
        layer_grads = grads + layer_grads
    grad_position = jnp.sum(grad_stream, 0)
    grad_patch = weight_grad(patches, grad_stream[:, 1:].astype(jnp.bfloat16))
    every_grad = [grad_patch, grad_position] + layer_grads + head_grads
    local_flat = jnp.concatenate([piece.reshape(-1) for piece in every_grad])
    wide_count = lax.axis_size("rep")
    group_count = lax.axis_size("grp")
    blocked = local_flat.reshape(wide_count, group_count, -1)
    wide_part = lax.psum_scatter(blocked, "rep", scatter_dimension=0, tiled=True)
    grad_flat = lax.psum_scatter(wide_part, "grp", scatter_dimension=1, tiled=True).reshape(-1)
    squares = jnp.sum(grad_flat * grad_flat) + jnp.sum(grad_protos * grad_protos)
    grand_total = lax.psum(squares, ("rep", "grp"))
    grad_norm = jnp.sqrt(grand_total)
    factor = jnp.minimum(1.0, CLIP_NORM / (grad_norm + 1e-06))
    new_params, new_first, new_second = adam_update(
        params, grad_flat * factor, first_moment, second_moment, LEARNING_RATE
    )
    new_protos, new_proto_first, new_proto_second = adam_update(
        protos, grad_protos * factor, proto_first, proto_second, PROTO_RATE
    )
    new_teacher = TEACHER_MOMENTUM * teacher + (1.0 - TEACHER_MOMENTUM) * new_params
    new_teacher_protos = TEACHER_MOMENTUM * teacher_protos + (1.0 - TEACHER_MOMENTUM) * new_protos
    return (
        new_params,
        new_first,
        new_second,
        new_teacher,
        new_protos,
        new_proto_first,
        new_proto_second,
        new_teacher_protos,
        new_center,
        loss_value,
        grad_norm,
    )


def solution(mesh):
    placed = (
        P(("rep", "grp")),
        P(("rep", "grp")),
        P(("rep", "grp")),
        P(("rep", "grp")),
        P("rep", "grp"),
        P("rep", "grp"),
        P("rep", "grp"),
        P("rep", "grp"),
        P("grp"),
        P(("rep", "grp"), None, None),
        P(("rep", "grp")),
    )
    return jax.shard_map(
        per_device,
        mesh=mesh,
        in_specs=placed,
        out_specs=(
            P(("rep", "grp")),
            P(("rep", "grp")),
            P(("rep", "grp")),
            P(("rep", "grp")),
            P("rep", "grp"),
            P("rep", "grp"),
            P("rep", "grp"),
            P("rep", "grp"),
            P("grp"),
            P(),
            P(),
        ),
        check_vma=False,
    )
```

profile of v0, /device:TPU:0, one launch (start us, length us, event | category | flops | bytes accessed | tf_op | source)
XLA Modules:
  0.0 3876.4 jit_solution(5352574899940449527)
XLA Ops:
  15.1 9.5 broadcast.554.clone
  24.6 14.0 dynamic-update-slice
  38.6 9.3 broadcast.554.clone.1
  48.0 14.1 dynamic-update-slice.1
  65.4 48.1 %all-gather.7.cloned.1.call-done = bf16[256,2048]{1,0:T(8,128)(2,1)} async-done(((bf16[32,2048]{1,0:T(8,128)(2,1)}), bf16[256,2048]{1,0:T(8,128)(2,1)}) %all-gather.7.cloned.1.call-update) | async-done | bytes 1048592 | tf_op jit(solution)/shard_map/all_gather | solution.py:244
  116.2 758.2 %all-reduce.20.cloned.1.call-done = (bf16[14115072]{0:T(1024)(128)(2,1)}, bf16[14115072]{0:T(1024)(128)(2,1)}) async-done(((bf16[14115072]{0:T(1024)(128)(2,1)}, bf16[14115072]{0:T(1024)(128)(2,1)}), (bf16[14115072]{0:T(1024)(128)(2,1)}, bf16[14115072]{0:T(1024)(128)(2,1)})) %all-reduce.20.cloned.1.call-update) | async-done | bytes 56460304
  874.3 9.5 fusion.305
  914.6 7.8 slice.369
  925.8 9.2 reshape.582
  935.1 8.2 reshape.581
  943.3 7.6 reshape.579
  986.7 8.3 reshape.576
  1002.0 7.8 reshape.574
  1058.1 9.3 reshape.577
  1072.6 9.4 fusion.23
  1082.0 23.5 multiply_convert_fusion.1
  1109.7 10.1 fusion.24
  1119.9 28.6 fusion.19
  1155.6 13.4 reshape.542
  1185.7 13.3 reshape.547
  1222.7 7.3 all-reduce.10
  1242.1 10.7 all-reduce.5
  1262.6 11.7 add_convert_fusion
  1282.3 9.4 fusion.296
  1305.4 8.8 multiply_reduce_fusion
  1314.2 11.9 multiply_convert_fusion
  1349.9 8.2 convolution_bitcast_fusion.3
  1358.1 7.6 convolution_bitcast_fusion.1
  1369.4 8.2 convolution_bitcast_fusion
  1383.2 9.3 fusion.295
  1412.5 7.9 reshape.552
  1423.6 9.5 copy.225
  1433.1 10.7 reshape.555
  1450.7 14.4 copy.227
  1469.5 60.9 %dynamic-update-slice.5 = f32[14115072]{0:T(1024)} dynamic-update-slice(f32[14115072]{0:T(1024)} %constant_dynamic-update-slice_fusion.1, f32[1769472]{0:T(1024)} %reshape.552, s32[]{} %constant.223) | dynamic-update-slice | bytes 14155780
  1530.3 21.3 dynamic-update-slice.6
  1551.6 80.5 %dynamic-update-slice.7 = f32[14115072]{0:T(1024)} dynamic-update-slice(f32[14115072]{0:T(1024)} %dynamic-update-slice.6, f32[2359296]{0:T(1024)} %bitcast.183, s32[]{} %constant.225) | dynamic-update-slice | bytes 18874372
  1632.1 80.5 %dynamic-update-slice.8 = f32[14115072]{0:T(1024)} dynamic-update-slice(f32[14115072]{0:T(1024)} %dynamic-update-slice.7, f32[2359296]{0:T(1024)} %reshape.555, s32[]{} %constant.226) | dynamic-update-slice | bytes 18874372
  1714.0 54.2 %dynamic-update-slice.10 = f32[14115072]{0:T(1024)} dynamic-update-slice(f32[14115072]{0:T(1024)} %constant_dynamic-update-slice_fusion, f32[1572864]{0:T(1024)} %bitcast.184, s32[]{} %constant.228) | dynamic-update-slice | bytes 12582916
  1768.1 142.2 %dynamic-update-slice.11 = f32[14115072]{0:T(1024)} dynamic-update-slice(f32[14115072]{0:T(1024)} %dynamic-update-slice.10, f32[4194304]{0:T(1024)} %bitcast.177, s32[]{} %constant.229) | dynamic-update-slice | bytes 33554436
  1910.3 18.3 dynamic-update-slice.12
  1928.6 85.6 %reshape.562 = f32[8,4,441096]{2,1,0:T(4,128)} reshape(f32[14115072]{0:T(1024)} %dynamic-update-slice.12) | data formatting | bytes 112920576 | tf_op jit(solution)/shard_map/reshape | solution.py:297
  2018.6 1636.0 %all-reduce.16.cloned.1.call-done = f32[8,4,441096]{2,1,0:T(4,128)} async-done(((f32[8,4,441096]{2,1,0:T(4,128)}), f32[8,4,441096]{2,1,0:T(4,128)}) %all-reduce.16.cloned.1.call-update) | async-done | bytes 56460304
  3663.0 19.6 psum.38
  3682.6 42.7 %reduce-scatter.3.cloned.1.call-done = f32[32,2048]{1,0:T(8,128)} async-done(((f32[256,2048]{1,0:T(8,128)}), f32[32,2048]{1,0:T(8,128)}) %reduce-scatter.3.cloned.1.call-update) | async-done | bytes 262160 | tf_op jit(solution)/shard_map/reduce_scatter | solution.py:276
  3726.9 65.9 %all-reduce.18.cloned.1.call-done = f32[1,4,441096]{2,1,0:T(4,128)} async-done(((f32[1,4,441096]{2,1,0:T(4,128)}), f32[1,4,441096]{2,1,0:T(4,128)}) %all-reduce.18.cloned.1.call-update) | async-done | bytes 7057552
  3801.8 39.6 %all-reduce.8 = (f32[]{:T(128)}, f32[]{:T(128)}) all-reduce(f32[]{:T(128)S(6)} %add.303, f32[]{:T(128)S(6)} %neg.57), channel_id=1, replica_groups=mesh['rep'=8,'grp'=4] {'rep','grp'}, use_global_device_ids=true, to_apply=%region_50.0 | all-reduce | flops 2 | bytes 16 | tf_op jit(solution)/shard_map/psum | solution.py:301
  3842.2 18.9 multiply_reduce_fusion.11
  (426 shorter events, 334.0 us)
Async XLA Ops:
  8.0 944.8 %copy-start = (bf16[4,196,768]{2,0,1:T(4,128)(2,1)S(1)}, bf16[4,196,768]{2,0,1:T(4,128)(2,1)}, u32[]{:S(2)}) copy-start(bf16[4,196,768]{2,0,1:T(4,128)(2,1)} %param.20) | copy-start | bytes 3612676
  8.0 55.9 %all-gather.5.cloned.1.call-start = ((), (), s32[]{:S(2)}) async-start(), calls=%async_computation.1 | async-start | bytes 1179648 | tf_op jit(solution)/shard_map/all_gather | solution.py:243
  9.9 103.6 %all-gather.7.cloned.1.call-start = ((), (), s32[]{:S(2)}) async-start(), calls=%async_computation.2 | async-start | bytes 1179648 | tf_op jit(solution)/shard_map/all_gather | solution.py:244
  11.6 862.8 %all-reduce.20.cloned.1.call-start = ((), (), s32[]{:S(2)}) async-start(), calls=%async_computation.6 | async-start | bytes 112926720
  62.0 3592.6 %all-reduce.16.cloned.1.call-start = ((), (), s32[]{:S(2)}) async-start(), calls=%async_computation.4 | async-start | bytes 112951296
  65.4 818.4 %copy-start.67 = (f32[2048]{0:T(1024)}, f32[2048]{0:T(1024)S(1)}, u32[]{:S(2)}) copy-start(f32[2048]{0:T(1024)S(1)} %fusion.27) | copy-start | bytes 24580
  874.3 19.4 copy-start.6
  995.0 21.6 copy-start.69
  995.0 72.4 %copy-start.71 = (f32[768]{0:T(1024)}, f32[768]{0:T(1024)S(1)}, u32[]{:S(2)}) copy-start(f32[768]{0:T(1024)S(1)} %get-tuple-element.74) | copy-start | bytes 9220
  1013.3 15.7 copy-start.33
  1016.4 12.7 copy-start.73
  1016.6 12.5 copy-start.44
  1054.9 12.5 copy-start.35
  1067.4 38.1 slice-start.4
  1072.5 33.0 slice-start.5
  1072.5 37.1 slice-start.8
  1082.0 23.5 copy-start.14
  1082.0 27.7 slice-start.9
  1105.6 14.3 slice-start.6
  1119.9 29.9 copy-start.79
  1149.5 19.8 copy-start.80
  1149.7 19.2 copy-start.97
  1149.7 19.6 copy-start.82
  1155.6 13.4 copy-start.28
  1172.5 12.0 copy-start.27
  1184.5 34.4 copy-start.65
  1207.5 11.4 copy-start.10
  1207.5 11.4 copy-start.63
  1207.5 12.3 copy-start.61
  1207.5 12.3 copy-start.77
  1219.8 41.0 %copy-start.38 = (f32[16,2048]{1,0:T(8,128)}, f32[16,2048]{1,0:T(8,128)S(1)}, u32[]{:S(2)}) copy-start(f32[16,2048]{1,0:T(8,128)S(1)} %get-tuple-element.90) | copy-start | bytes 393220
  1230.0 12.1 copy-start.86
  1230.0 30.9 copy-start.84
  1238.4 15.2 copy-start.90
  1255.0 19.3 slice-start.2
  1262.6 11.7 copy-start.48
  1262.6 11.7 slice-start.3
  1282.3 12.4 copy-start.25
  1334.6 15.3 slice-start.10
  1336.6 13.3 slice-start.11
  1340.6 38.8 %copy-start.15 = (f32[4,197,768]{2,1,0:T(8,128)}, f32[4,197,768]{2,1,0:T(8,128)S(1)}, u32[]{:S(2)}) copy-start(f32[4,197,768]{2,1,0:T(8,128)S(1)} %get-tuple-element.106) | copy-start | bytes 7262212
  1450.7 14.4 copy-start.17
  1450.7 15.5 copy-start.37
  2014.4 1710.9 %reduce-scatter.3.cloned.1.call-start = ((), (), s32[]{:S(2)}) async-start(), calls=%async_computation.3 | async-start | bytes 2359296 | tf_op jit(solution)/shard_map/reduce_scatter | solution.py:276
  2018.6 1774.3 %all-reduce.18.cloned.1.call-start = ((), (), s32[]{:S(2)}) async-start(), calls=%async_computation.5 | async-start | bytes 14118912
  3661.6 199.5 %copy-start.19 = (f32[441096]{0:T(1024)S(1)}, f32[441096]{0:T(1024)}, u32[]{:S(2)}) copy-start(f32[441096]{0:T(1024)} %param.14) | copy-start | bytes 5293156
  3842.2 18.9 copy-start.20
  3842.2 18.9 copy-start.41
  (73 other events, 356.1 us)
Sparse Core Ops, SparseCore 0:
  11.8 42.8 all-gather.4
  57.6 55.8 all-gather.6
  2014.5 1640.0 all-reduce.15
  3658.0 67.2 reduce-scatter.2
Sparse Core Ops, SparseCore 1:
  62.1 812.2 all-reduce.19
  3661.7 131.1 all-reduce.17
where the time goes:
time: 3920 us; the launch traced here: 3880 us
  waiting for transfers between devices  2550 us (65%)
  local copies, waits for them, and re-layouts  846 us (22%)
  matrix products  211 us (5%)
  other arithmetic  152 us (4%)
  blocking collectives  94.2 us (2%)
    unnamed x9, waiting for transfers between devices  2460 us
    unnamed x253, local copies, waits for them, and re-layouts  546 us
    dot_general x18, matrix products, product(): return jnp.dot(left, right, preferred_element_type=jnp.float32)  99.4 us
    reshape x1, local copies, waits for them, and re-layouts, per_device(): blocked = local_flat.reshape(wide_count, group_count, -1)  85.6 us
    slice x20, local copies, waits for them, and re-layouts, unpack(): pieces.append(flat_params[offset:offset + entries].reshape(dims_pair))  78.5 us
  transfers between devices with their start and end apart: 6, of which 5 were waited for; matrix products, arithmetic and copies ran while one was open for 2% of the time, Pallas kernels for 0%

commit v1 on v0

v1 whole, which is shorter than its diff:
```python
import functools
import math

import jax
import jax.numpy as jnp
import numpy as np
from jax import lax
from jax.experimental import pallas as pl
from jax.experimental.pallas import tpu as pltpu
from jax.sharding import PartitionSpec as P

D = 768
HEADS = 12
HDIM = 64
F = 3072
PD = 768
NTOK = 197
H = 2048
B = 256
STEP = 10
NPATCH = NTOK - 1

PRECISE = lax.Precision.HIGHEST
STUDENT_TEMP = 0.1
TEACHER_TEMP = 0.04
CENTER_MOMENTUM = 0.9
TEACHER_MOMENTUM = 0.8
CLIP_NORM = 0.05
LEARNING_RATE = 0.03
PROTO_RATE = 0.6
BETA_FIRST = 0.9
BETA_SECOND = 0.999
ADAM_EPSILON = 1e-08
WEIGHT_DECAY = 0.04
BOTH = ("rep", "grp")
LANES = 128
F32 = jnp.float32
BF16 = jnp.bfloat16

SEGMENTS = []
_offset = 0
for _rows, _cols in ((PD + NTOK + 4, D), (D, 3 * D), (D, D), (D, F), (F + 2, D), (D + H, H), (H, B)):
    SEGMENTS.append((_offset, _rows, _cols))
    _offset += _rows * _cols
PFLAT = _offset
WIDTHS = sorted({cols // LANES for _, _, cols in SEGMENTS})

PIECES = []
_offset = 0
for _rows, _cols in (
    (PD + NTOK + 4, D),
    (D, 3 * D),
    (D, D),
    (D, F),
    (F, D),
    (2, D),
    (D, H),
    (H, H),
    (H, B),
):
    PIECES.append((_offset, _rows, _cols))
    _offset += _rows * _cols

FRONT = 24
GRAD_FRONT = 8 * FRONT
CHUNK = 64


def round_up(value, step):
    return -(-value // step) * step


def shard_parts(start, stop, table):
    parts = []
    line0 = start // LANES
    for index, (offset, rows, cols) in enumerate(table):
        low, high = max(start, offset), min(stop, offset + rows * cols)
        if low >= high:
            continue
        row0 = (low - offset) // cols
        row1 = -(-(high - offset) // cols)
        parts.append((index, row0, row1 - row0, (offset + row0 * cols) // LANES - line0))
    return parts


FINAL_ROW = round_up(PD + NTOK + 4, 8)


class Plan:
    def __init__(self, count):
        self.count = count
        self.size = PFLAT // count
        self.lines = round_up(-(-self.size // LANES) + 1, CHUNK)
        self.scratch = FRONT + self.lines + 8 * max(WIDTHS) + 16
        table = []
        self.blocks = [[] for _ in SEGMENTS]
        longest = 0
        for device in range(count):
            start = device * self.size
            entry = [start % LANES]
            target = 0
            parts = shard_parts(start, start + self.size, SEGMENTS)
            for index, row0, rows, line in parts:
                width = SEGMENTS[index][2] // LANES
                tiles = round_up(rows, 8) // 8
                self.blocks[index].append((device, target, row0, tiles * 8))
                entry += [WIDTHS.index(width), FRONT + line, tiles, target]
                target += tiles * 8 * width
            longest = max(longest, target)
            entry += [-1, 0, 0, 0] * (2 - len(parts))
            table.append(entry)
        self.buffer = round_up(longest, 16)
        self.lay_table = np.array(table, np.int32)
        table = []
        self.most = max(
            len(shard_parts(d * self.size, (d + 1) * self.size, PIECES)) for d in range(count)
        )
        for device in range(count):
            start = device * self.size
            entry = [start % LANES]
            parts = shard_parts(start, start + self.size, PIECES)
            for index, row0, rows, line in parts:
                skew = row0 % 8
                line -= skew * (PIECES[index][2] // LANES)
                entry += [index, GRAD_FRONT + line, -(-(rows + skew) // CHUNK), row0 - skew]
            entry += [-1, 0, 0, 0] * (self.most - len(parts))
            table.append(entry)
        self.grad_table = np.array(table, np.int32)
        self.grad_scratch = GRAD_FRONT + self.lines + CHUNK * max(WIDTHS) + 16


def lay_kernel(plan, tab_ref, x_ref, out_ref, line_ref):
    shift = tab_ref[0]
    lane = lax.broadcasted_iota(jnp.int32, (CHUNK + 8, LANES), 1)
    line_ref[pl.ds(0, FRONT), :] = jnp.zeros((FRONT, LANES), F32)
    tail = plan.scratch - FRONT - plan.lines
    line_ref[pl.ds(FRONT + plan.lines, tail), :] = jnp.zeros((tail, LANES), F32)

    def align(step, carry):
        base = pl.multiple_of(step * CHUNK, 8)
        here = pltpu.roll(x_ref[pl.ds(base, CHUNK + 8), :], shift, 1)
        above = pltpu.roll(here, 1, 0)
        both = jnp.where(lane >= shift, here, above)
        line_ref[pl.ds(pl.multiple_of(FRONT + base, 8), CHUNK), :] = both[8:]
        return carry

    lax.fori_loop(0, plan.lines // CHUNK, align, 0)
    for part in range(2):
        kind, base, tiles, target = (tab_ref[1 + 4 * part + i] for i in range(4))
        for index, width in enumerate(WIDTHS):

            @pl.when(kind == index)
            def _():
                def move(tile, carry):
                    row = base + tile * (8 * width)
                    goal = target + tile * (8 * width)
                    for pair in range(0, width, 2):
                        two = jnp.concatenate(
                            [
                                line_ref[pl.ds(row + pair, 8, stride=width), :],
                                line_ref[pl.ds(row + pair + 1, 8, stride=width), :],
                            ],
                            0,
                        )
                        out_ref[pl.ds(pl.multiple_of(goal + 8 * pair, 16), 16), :] = two.astype(BF16)
                    return carry

                lax.fori_loop(0, tiles, move, 0)


def lay_out(plan, table, flat):
    padded = jnp.pad(flat, (8 * LANES, plan.lines * LANES - plan.size))
    lines = padded.reshape(8 + plan.lines, LANES)
    return pl.pallas_call(
        functools.partial(lay_kernel, plan),
        out_shape=jax.ShapeDtypeStruct((plan.buffer, LANES), BF16),
        in_specs=[
            pl.BlockSpec(memory_space=pltpu.SMEM),
            pl.BlockSpec(memory_space=pltpu.VMEM),
        ],
        out_specs=pl.BlockSpec(memory_space=pltpu.VMEM),
        scratch_shapes=[pltpu.VMEM((plan.scratch, LANES), F32)],
        compiler_params=pltpu.CompilerParams(vmem_limit_bytes=24 * 1024 * 1024),
    )(table, lines)


def blocks_of(plan, index, first, count):
    return [
        (device, target, row0 - first, rows)
        for device, target, row0, rows in plan.blocks[index]
        if row0 < first + count and row0 + rows > first
    ]


class Rows:
    def __init__(self, plan, gathered, index, first, count):
        width = SEGMENTS[index][2] // LANES
        half = plan.count // 2
        self.count = count
        self.blocks = [block[2:] for block in blocks_of(plan, index, first, count)]
        pieces = [
            gathered[device % half, device // half, target : target + rows * width]
            for device, target, _, rows in blocks_of(plan, index, first, count)
        ]
        tiles = jnp.concatenate(pieces, 0).reshape(-1, width, 8, LANES)
        self.matrix = tiles.transpose(0, 2, 1, 3).reshape(-1, width * LANES)

    def spread(self, values):
        before = max(0, -min(row0 for row0, _ in self.blocks))
        after = max(0, max(row0 + rows for row0, rows in self.blocks) - self.count)
        padded = jnp.pad(values, ((0, 0), (before, after)))
        return jnp.concatenate(
            [padded[:, before + row0 : before + row0 + rows] for row0, rows in self.blocks], 1
        )

    def times(self, values):
        return product(self.spread(values), self.matrix)

    def back(self, values):
        wide = product_t(values, self.matrix)
        total, place = 0.0, 0
        for row0, rows in self.blocks:
            low, high = max(0, row0), min(self.count, row0 + rows)
            piece = wide[:, place + low - row0 : place + high - row0]
            total = total + jnp.pad(piece, ((0, 0), (low, self.count - high)))
            place += rows
        return total

    def folded(self):
        total, place = 0.0, 0
        for row0, rows in self.blocks:
            low, high = max(0, row0), min(self.count, row0 + rows)
            piece = self.matrix[place + low - row0 : place + high - row0]
            total = total + jnp.pad(piece, ((low, self.count - high), (0, 0)))
            place += rows
        return total


def product(left, right):
    return jnp.dot(left, right, preferred_element_type=F32)


def product_t(left, right):
    return lax.dot_general(
        left, right, (((left.ndim - 1,), (1,)), ((), ())), preferred_element_type=F32
    )


def activate(values):
    return jax.nn.gelu(values, approximate=False)


def gelu_back(values, grad):
    return jax.vjp(activate, values)[1](grad)[0]


def normalised(values):
    centred = values - jnp.mean(values, -1, keepdims=True)
    scale = lax.rsqrt(jnp.mean(centred * centred, -1, keepdims=True) + 1e-06)
    return centred * scale, scale


def norm_back(grad, gain, unit, scale):
    inner = grad * gain
    return scale * (
        inner
        - jnp.mean(inner, -1, keepdims=True)
        - unit * jnp.mean(inner * unit, -1, keepdims=True)
    )


def head_mask():
    return jnp.arange(HEADS)[:, None] == jnp.arange(D)[None, :] // HDIM


def trunk_forward(patches, wide, qkv_w):
    views = patches.shape[0]
    position = wide[PD : PD + NTOK].astype(F32)
    norms = wide[PD + NTOK :].astype(F32)
    embedded = product(patches, wide[:PD])
    unit, scale = normalised(embedded + position[1:])
    normed = (unit * norms[0] + norms[1]).astype(BF16)
    class_unit, class_scale = normalised(position[:1])
    class_normed = (class_unit * norms[0] + norms[1]).astype(BF16)
    query = product(class_normed, qkv_w[:, :D]).astype(BF16)
    by_head = jnp.where(head_mask(), query, 0).astype(BF16)
    looked = product_t(by_head, qkv_w[:, D : 2 * D]).astype(BF16)
    temper = HDIM ** (-0.5)
    scores = jnp.einsum("hd,vkd->vhk", looked, normed, preferred_element_type=F32) * temper
    class_score = product_t(looked, class_normed)[None] * temper
    top = jnp.maximum(jnp.max(scores, -1, keepdims=True), class_score)
    total = jnp.sum(jnp.exp(scores - top), -1, keepdims=True) + jnp.exp(class_score - top)
    row_top = top + jnp.log(total)
    probs = jnp.exp(scores - row_top)
    class_probs = jnp.exp(class_score - row_top)
    mixed = jnp.einsum("vhk,vkd->vhd", probs.astype(BF16), normed, preferred_element_type=F32)
    mixed = mixed + class_probs.astype(BF16).astype(F32) * class_normed.astype(F32)
    mixed = mixed.astype(BF16)
    valued = product(mixed.reshape(-1, D), qkv_w[:, 2 * D :]).reshape(views, HEADS, D)
    attended = jnp.sum(jnp.where(head_mask(), valued, 0.0), 1).astype(BF16)
    kept = (unit, scale, normed, class_unit, class_scale, class_normed, query, looked)
    return position[0], attended, mixed, kept + (probs, class_probs)


def trunk_backward(patches, wide, qkv_w, grad_att, grad_class, kept):
    unit, scale, normed, class_unit, class_scale, class_normed, query, looked = kept[:8]
    probs, class_probs = kept[8:]
    views = patches.shape[0]
    norms = wide[PD + NTOK :].astype(F32)
    temper = HDIM ** (-0.5)
    spread = jnp.where(head_mask(), grad_att[:, None], 0).astype(BF16).reshape(-1, D)
    back = product_t(spread, qkv_w[:, 2 * D :]).astype(BF16).reshape(views, HEADS, D)
    grad_probs = jnp.einsum("vhd,vkd->vhk", back, normed, preferred_element_type=F32)
    class_grad = jnp.sum(
        back.astype(F32) * class_normed.astype(F32), -1, keepdims=True
    )
    delta = jnp.sum(probs * grad_probs, -1, keepdims=True) + class_probs * class_grad
    grad_scores = (probs * (grad_probs - delta)).astype(BF16)
    class_scores = (class_probs * (class_grad - delta)).astype(BF16)
    reach = jnp.einsum("vhk,vkd->vhd", grad_scores, normed, preferred_element_type=F32)
    reach = (reach + class_scores.astype(F32) * class_normed.astype(F32)) * temper
    keyed = product(reach.astype(BF16).reshape(-1, D), qkv_w[:, D : 2 * D])
    keyed = keyed.reshape(views, HEADS, D)
    grad_query = jnp.sum(jnp.where(head_mask(), keyed, 0.0), 1).astype(BF16)
    left = jnp.concatenate([grad_scores, probs.astype(BF16)], 1)
    right = jnp.concatenate(
        [jnp.broadcast_to((looked.astype(F32) * temper).astype(BF16), back.shape), back], 1
    )
    grad_normed = jnp.einsum("vhk,vhd->vkd", left, right, preferred_element_type=F32)
    class_left = jnp.concatenate([class_scores, class_probs.astype(BF16)], 1).astype(F32)
    class_row = jnp.sum(class_left * right.astype(F32), 1) + product_t(grad_query, qkv_w[:, :D])
    gain = jnp.sum(grad_normed * unit, (0, 1)) + jnp.sum(class_row * class_unit, 0)
    offset = jnp.sum(grad_normed, (0, 1)) + jnp.sum(class_row, 0)
    grad_stream = norm_back(grad_normed, norms[0], unit, scale)
    class_stream = norm_back(class_row, norms[0], class_unit, class_scale) + grad_class
    grad_patch = lax.dot_general(
        patches.reshape(-1, PD),
        grad_stream.astype(BF16).reshape(-1, D),
        (((0,), (0,)), ((), ())),
        preferred_element_type=F32,
    )
    return (
        grad_patch,
        jnp.sum(class_stream, 0, keepdims=True),
        jnp.sum(grad_stream, 0),
        gain[None],
        offset[None],
        jnp.sum(grad_query.astype(F32), 0, keepdims=True),
        jnp.sum(reach, 0),
    )


def grad_kernel(plan, spans, tab_ref, rows_ref, cols_ref, wide_ref, qkv_ref, out_ref, line_ref):
    for part in range(plan.most):
        kind, base, chunks, row0 = (tab_ref[1 + 4 * part + i] for i in range(4))
        for index, (_, _, cols) in enumerate(PIECES):
            width = cols // LANES

            @pl.when(kind == index)
            def _():
                def move(step, carry):
                    row = pl.multiple_of(row0 + step * CHUNK, 8)
                    goal = base + step * (CHUNK * width)
                    if spans[index] is None:
                        source = qkv_ref if index == 1 else wide_ref
                        first = row if index == 0 else row + FINAL_ROW
                        if index == 1:
                            first = step * CHUNK
                        block = source[pl.ds(pl.multiple_of(first, 8), CHUNK), :]
                    else:
                        first, column = spans[index]
                        left = rows_ref[pl.ds(pl.multiple_of(first + row, 8), CHUNK), :].astype(BF16)
                        block = product(left, cols_ref[:, column : column + cols])
                    for tile in range(width):
                        line_ref[pl.ds(goal + tile, CHUNK, stride=width), :] = block[
                            :, tile * LANES : (tile + 1) * LANES
                        ]
                    return carry

                lax.fori_loop(0, chunks, move, 0)

    shift = tab_ref[0]
    turn = lax.rem(LANES - shift, LANES)
    lane = lax.broadcasted_iota(jnp.int32, (CHUNK + 8, LANES), 1)

    def align(step, carry):
        start = pl.multiple_of(step * CHUNK, 8)
        here = pltpu.roll(line_ref[pl.ds(pl.multiple_of(GRAD_FRONT + start, 8), CHUNK + 8), :], turn, 1)
        below = pltpu.roll(here, CHUNK + 7, 0)
        both = jnp.where(lane < LANES - shift, here, below)
        out_ref[pl.ds(start, CHUNK), :] = both[:CHUNK]
        return carry

    lax.fori_loop(0, plan.lines // CHUNK, align, 0)


def adam_update(weight, grad, first, second, rate):
    first = BETA_FIRST * first + (1.0 - BETA_FIRST) * grad
    second = BETA_SECOND * second + (1.0 - BETA_SECOND) * grad * grad
    stepped = (
        first
        / (1.0 - BETA_FIRST**STEP)
        / (jnp.sqrt(second / (1.0 - BETA_SECOND**STEP)) + ADAM_EPSILON)
    )
    return (weight - rate * (stepped + WEIGHT_DECAY * weight), first, second)


def per_device(
    plan,
    params,
    first_moment,
    second_moment,
    teacher,
    protos,
    proto_first,
    proto_second,
    teacher_protos,
    center,
    patches,
    partner,
):
    reps, groups = lax.axis_size("rep"), lax.axis_size("grp")
    count, half = reps * groups, reps * groups // 2
    rep, grp = lax.axis_index("rep"), lax.axis_index("grp")
    device = rep * groups + grp
    low = rep < reps // 2
    halves = [list(range(half)), list(range(half, count))]
    swap = [(r, (r + reps // 2) % reps) for r in range(reps)]
    own_views = patches.shape[0]
    views = 2 * own_views

    def trade(values):
        return lax.ppermute(values, "rep", swap)

    def in_order(values):
        other = trade(values)
        return jnp.where(low, values, other), jnp.where(low, other, values)

    table = jnp.asarray(plan.lay_table)[device]
    kept = lay_out(plan, table, jnp.where(low, params, teacher))
    given = trade(lay_out(plan, table, jnp.where(low, teacher, params)))
    shards = jnp.stack([jnp.where(low, kept, given), jnp.where(low, given, kept)])
    gathered = lax.all_gather(shards, BOTH, axis=0, axis_index_groups=halves)
    pixels = jnp.concatenate(in_order(patches), 0)
    places = in_order(partner.astype(F32))
    tables = lax.all_gather(
        jnp.stack([protos, teacher_protos]).astype(BF16), "rep", axis=1, tiled=True
    ).astype(F32)

    def columns_of(values):
        scale = lax.rsqrt(jnp.sum(values * values, 0, keepdims=True) + 1e-06)
        return (values * scale).astype(BF16), scale

    columns, column_scale = columns_of(tables[0])
    teacher_columns = columns_of(tables[1])[0]

    wide = Rows(plan, gathered, 0, 0, PD + NTOK + 4).folded()
    qkv_w = Rows(plan, gathered, 1, 0, D).folded()
    out_w = Rows(plan, gathered, 2, 0, D)
    up_w = Rows(plan, gathered, 3, 0, D)
    down_w = Rows(plan, gathered, 4, 0, F)
    final = Rows(plan, gathered, 4, F, 2).folded().astype(F32)
    head_one = Rows(plan, gathered, 5, 0, D)
    head_two = Rows(plan, gathered, 5, D, H)
    head_three = Rows(plan, gathered, 6, 0, H)
    norms = wide[PD + NTOK :].astype(F32)

    class_row, attended, mixed, trunk_kept = trunk_forward(pixels, wide, qkv_w)
    middle = class_row + out_w.times(attended)
    unit_two, scale_two = normalised(middle)
    normed_two = (unit_two * norms[2] + norms[3]).astype(BF16)
    hidden = up_w.times(normed_two)
    act = activate(hidden).astype(BF16)
    stream = middle + down_w.times(act)
    unit_three, scale_three = normalised(stream)
    cls = (unit_three * final[0] + final[1]).astype(BF16)
    pre_one = head_one.times(cls)
    first = activate(pre_one).astype(BF16)
    pre_two = head_two.times(first)
    second = activate(pre_two).astype(BF16)
    bottle = head_three.times(second)
    bottle_scale = lax.rsqrt(jnp.sum(bottle * bottle, -1, keepdims=True) + 1e-06)
    rows = (bottle * bottle_scale).astype(BF16)

    here = jnp.arange(views)
    place = jnp.concatenate([places[0], places[1] + own_views]).astype(jnp.int32)
    place = jnp.where(low, here, place)
    rows = product((place[:, None] == here[None, :]).astype(BF16), rows).astype(BF16)
    all_rows = lax.all_to_all(
        jnp.broadcast_to(rows[None], (count, views, B)), BOTH, 0, 0
    )
    student_rows = all_rows[:half].reshape(-1, B)
    teacher_rows = all_rows[half:].reshape(-1, B)

    teacher_logits = product(teacher_rows, teacher_columns)
    new_center = CENTER_MOMENTUM * center + (1.0 - CENTER_MOMENTUM) * jnp.mean(teacher_logits, 0)
    exp_teacher = jnp.exp((teacher_logits - center) / TEACHER_TEMP)
    scaled = product(student_rows, columns) / STUDENT_TEMP
    exp_student = jnp.exp(scaled)
    sums = jnp.stack(
        [jnp.sum(exp_student, 1), jnp.sum(exp_teacher, 1), jnp.sum(exp_teacher * scaled, 1)]
    )
    band = groups * views
    start = lax.rem(rep, reps // 2) * band
    pulls = jnp.concatenate(
        [
            lax.dynamic_slice_in_dim(exp_student, start, band, 0),
            lax.dynamic_slice_in_dim(exp_teacher, start, band, 0),
        ],
        0,
    )
    pulls = lax.dot_general(
        pulls, columns.astype(F32), (((1,), (1,)), ((), ())), precision=PRECISE
    ).reshape(2, groups, views * B)
    note = jnp.concatenate(
        [
            pulls.transpose(1, 0, 2).reshape(groups, -1),
            jnp.broadcast_to(sums.reshape(1, -1), (groups, sums.size)),
        ],
        1,
    ).reshape(groups, -1, LANES)
    note = jnp.sum(lax.all_to_all(note, "grp", 0, 0), 0).reshape(-1)
    pulls = note[: 2 * views * B].reshape(2, views, B)
    sum_student, sum_teacher, crossed = note[2 * views * B :].reshape(3, -1)
    loss_value = jnp.sum(jnp.log(sum_student) - crossed / sum_teacher)
    own = lax.rem(device, half) * views
    own_student = lax.dynamic_slice_in_dim(sum_student, own, views)[:, None]
    own_teacher = lax.dynamic_slice_in_dim(sum_teacher, own, views)[:, None]
    grad_rows = (pulls[0] / own_student - pulls[1] / own_teacher) / STUDENT_TEMP
    grad_rows = jnp.where(low, grad_rows, 0.0).astype(BF16).astype(F32)

    grad_logits = (
        exp_student / sum_student[:, None] - exp_teacher / sum_teacher[:, None]
    ) / STUDENT_TEMP
    grad_columns = lax.dot_general(
        student_rows.astype(F32), grad_logits, (((0,), (0,)), ((), ())), precision=PRECISE
    )
    inner = jnp.sum(grad_columns * tables[0], 0, keepdims=True)
    depth = protos.shape[0]
    grad_protos = (
        lax.dynamic_slice_in_dim(grad_columns, rep * depth, depth, 0) * column_scale
        - protos.astype(BF16).astype(F32) * column_scale**3 * inner
    )

    grad_bottle = (
        grad_rows * bottle_scale
        - bottle * bottle_scale**3 * jnp.sum(grad_rows * bottle, -1, keepdims=True)
    ).astype(BF16)
    grad_two = gelu_back(pre_two, head_three.back(grad_bottle)).astype(BF16)
    grad_one = gelu_back(pre_one, head_two.back(grad_two)).astype(BF16)
    grad_cls = head_one.back(grad_one)
    head_pack = jnp.concatenate([cls, first, second, grad_bottle, grad_two, grad_one], 1)
    head_pack = lax.all_gather(head_pack, BOTH, axis=0)
    grad_stream = norm_back(grad_cls, final[0], unit_three, scale_three)
    grad_branch = grad_stream.astype(BF16)
    grad_hidden = gelu_back(hidden, down_w.back(grad_branch)).astype(BF16)
    grad_normed = up_w.back(grad_hidden)
    grad_middle = grad_stream + norm_back(grad_normed, norms[2], unit_two, scale_two)
    grad_mixed = grad_middle.astype(BF16)
    grad_att = out_w.back(grad_mixed).astype(BF16)
    body_pack = jnp.concatenate(
        [attended, normed_two, act, grad_mixed, grad_hidden, grad_branch, grad_att], 1
    )
    body_pack = lax.all_gather(body_pack, BOTH, axis=0)
    mixed_pack = lax.all_gather(mixed, BOTH, axis=0)

    pieces = trunk_backward(pixels, wide, qkv_w, grad_att, grad_middle, trunk_kept)
    partial = jnp.concatenate(
        pieces[:5]
        + (
            jnp.sum(grad_normed * unit_two, 0, keepdims=True),
            jnp.sum(grad_normed, 0, keepdims=True),
            jnp.zeros((FINAL_ROW - PD - NTOK - 4, D), F32),
            jnp.sum(grad_cls * unit_three, 0, keepdims=True),
            jnp.sum(grad_cls, 0, keepdims=True),
        )
        + pieces[5:],
        0,
    )
    depth = round_up(-(-partial.shape[0] // half), 8)
    partial = jnp.pad(partial, ((0, half * depth - partial.shape[0]), (0, 0)))
    partial = lax.all_to_all(
        partial.astype(BF16).reshape(half, depth, D), BOTH, 0, 0, axis_index_groups=halves
    )
    partial = jnp.sum(partial.astype(F32), 0)
    summed = lax.all_gather(partial, BOTH, axis=0)[:half].reshape(-1, D)

    head_rows = head_pack[:half].reshape(half * views, -1)
    body_rows = body_pack[:half].reshape(half * views, -1)
    mixed_rows = mixed_pack[:half].reshape(half * views, HEADS, D)
    rows_all = jnp.concatenate(
        [body_rows[:, : 2 * D + F], head_rows[:, : D + 2 * H]], 1
    ).astype(F32)
    rows_all = jnp.pad(rows_all.T, ((0, CHUNK), (0, 0)))
    cols_all = jnp.concatenate(
        [body_rows[:, 2 * D + F : 4 * D + 2 * F], head_rows[:, D + 2 * H :]], 1
    )
    spans = [
        None,
        None,
        (0, 0),
        (D, D),
        (2 * D, D + F),
        None,
        (2 * D + F, 2 * D + F + B + H),
        (3 * D + F, 2 * D + F + B),
        (3 * D + F + H, 2 * D + F),
    ]
    qkv_row = jnp.asarray(
        [
            max([0] + [p[1] // 8 * 8 for p in shard_parts(d * plan.size, (d + 1) * plan.size, PIECES) if p[0] == 1])
            for d in range(count)
        ],
        jnp.int32,
    )[device]
    qkv_rows = round_up(min(D, -(-plan.size // (3 * D)) + 9), CHUNK)
    base = FINAL_ROW
    sum_query, reach = summed[base + 2], summed[base + 3 : base + 3 + HEADS]

    def slab(values):
        return lax.dynamic_slice_in_dim(
            jnp.pad(values, ((0, 0),) * (values.ndim - 1) + ((0, qkv_rows),)),
            qkv_row,
            qkv_rows,
            values.ndim - 1,
        )

    class_normed, query = trunk_kept[5].astype(F32), trunk_kept[6].astype(F32)
    qkv_q = slab(class_normed).T * sum_query[None]
    qkv_k = lax.dot_general(
        slab(reach), jnp.where(head_mask(), query, 0.0), (((0,), (0,)), ((), ())), precision=PRECISE
    )
    grad_att_rows = body_rows[:, 4 * D + 2 * F :].reshape(-1, HEADS, HDIM)
    qkv_v = jnp.einsum(
        "vhd,vhc->dhc", slab(mixed_rows), grad_att_rows, preferred_element_type=F32
    ).reshape(qkv_rows, D)
    qkv_grad = jnp.concatenate([qkv_q, qkv_k, qkv_v], 1)
    wide_grad = jnp.pad(summed[: base + 2], ((0, 8 * CHUNK), (0, 0)))
    flat_lines = pl.pallas_call(
        functools.partial(grad_kernel, plan, spans),
        out_shape=jax.ShapeDtypeStruct((plan.lines, LANES), F32),
        in_specs=[pl.BlockSpec(memory_space=pltpu.SMEM)]
        + [pl.BlockSpec(memory_space=pltpu.VMEM)] * 4,
        out_specs=pl.BlockSpec(memory_space=pltpu.VMEM),
        scratch_shapes=[pltpu.VMEM((plan.grad_scratch, LANES), F32)],
        compiler_params=pltpu.CompilerParams(vmem_limit_bytes=48 * 1024 * 1024),
    )(jnp.asarray(plan.grad_table)[device], rows_all, cols_all, wide_grad, qkv_grad)
    grad_flat = flat_lines.reshape(-1)[: plan.size]

    squares = jnp.sum(grad_flat * grad_flat) + jnp.sum(grad_protos * grad_protos)
    squares = lax.all_to_all(
        jnp.broadcast_to(squares.reshape(1, 1, 1), (count, 1, LANES)), BOTH, 0, 0
    )
    grad_norm = jnp.sqrt(jnp.sum(squares[:, 0, 0]))
    factor = jnp.minimum(1.0, CLIP_NORM / (grad_norm + 1e-06))
    new_params, new_first, new_second = adam_update(
        params, grad_flat * factor, first_moment, second_moment, LEARNING_RATE
    )
    new_protos, new_proto_first, new_proto_second = adam_update(
        protos, grad_protos * factor, proto_first, proto_second, PROTO_RATE
    )
    new_teacher = TEACHER_MOMENTUM * teacher + (1.0 - TEACHER_MOMENTUM) * new_params
    new_teacher_protos = TEACHER_MOMENTUM * teacher_protos + (1.0 - TEACHER_MOMENTUM) * new_protos
    return (
        new_params,
        new_first,
        new_second,
        new_teacher,
        new_protos,
        new_proto_first,
        new_proto_second,
        new_teacher_protos,
        new_center,
        loss_value,
        grad_norm,
    )


def solution(mesh):
    placed = (
        P(BOTH),
        P(BOTH),
        P(BOTH),
        P(BOTH),
        P("rep", "grp"),
        P("rep", "grp"),
        P("rep", "grp"),
        P("rep", "grp"),
        P("grp"),
        P(BOTH, None, None),
        P(BOTH),
    )
    plan = Plan(math.prod(mesh.shape.values()))
    return jax.shard_map(
        functools.partial(per_device, plan),
        mesh=mesh,
        in_specs=placed,
        out_specs=placed[:9] + (P(), P()),
        check_vma=False,
    )
```

time: 3920 us -> 703 us (0.18)
  waiting for transfers between devices: 2550 us -> 370 us
  local copies, waits for them, and re-layouts: 846 us -> 91.6 us
  matrix products: 211 us -> 70.8 us
  other arithmetic: 152 us -> 64.7 us
  blocking collectives: 94.2 us -> 36.3 us
    unnamed x9 -> x6, waiting for transfers between devices: 2460 us -> 0.1 us
    unnamed x253 -> x164, local copies, waits for them, and re-layouts: 546 us -> 38.8 us
    all_gather x2 -> x6, waiting for transfers between devices: 48.1 us -> 242 us  [the longest x1 133 us: per_device(): gathered = lax.all_gather(shards, BOTH, axis=0, axis_index_groups=halves)]
    reshape x18 -> x6, local copies, waits for them, and re-layouts: 182 us -> 4.26 us  [the longest x1 2.38 us: per_device(): qkv_v = jnp.einsum('vhd,vhc->dhc', slab(mixed_rows), grad_att_rows, prefe...]
    dot_general x43 -> x33, matrix products: 211 us -> 70.8 us  [the longest x13 27.2 us: product(): return jnp.dot(left, right, preferred_element_type=F32)]
    ppermute x0 -> x3, waiting for transfers between devices: none -> 112 us  [trade(): return lax.ppermute(values, 'rep', swap)]
    psum x3 -> x0, blocking collectives: 65.8 us -> none  [the longest x1 39.6 us: per_device(): grand_total = lax.psum(squares, ('rep', 'grp'))]
    slice x25 -> x51, local copies, waits for them, and re-layouts: 78.9 us -> 18.9 us  [the longest x6 3.6 us: folded(): piece = self.matrix[place + low - row0:place + high - row0]]
  transfers between devices with their start and end apart: 6 -> 12, of which waited for: 5 -> 8; matrix products, arithmetic and copies ran while one was open for 2% -> 18% of each run, Pallas kernels for 0% -> 2%
where the time goes in v1:
time: 703 us; the launch traced here: 695 us
  waiting for transfers between devices  370 us (53%)
  local copies, waits for them, and re-layouts  91.6 us (13%)
  matrix products  70.8 us (10%)
  other arithmetic  64.7 us (9%)
  blocking collectives  36.3 us (5%)
  between operations  22.1 us (3%)
  Pallas kernels  20.3 us (3%)
  starting transfers between devices  19.8 us (3%)
    all_gather x1, waiting for transfers between devices, per_device(): gathered = lax.all_gather(shards, BOTH, axis=0, axis_index_groups=halves)  133 us
    ppermute x3, waiting for transfers between devices, trade(): return lax.ppermute(values, 'rep', swap)  112 us
    all_gather x1, waiting for transfers between devices, per_device(): body_pack = lax.all_gather(body_pack, BOTH, axis=0)  56.9 us
    all_gather x1, waiting for transfers between devices, per_device(): summed = lax.all_gather(partial, BOTH, axis=0)[:half].reshape(-1, D)  51.7 us
    unnamed x164, local copies, waits for them, and re-layouts  38.8 us
    all_to_all x1, blocking collectives, per_device(): lax.all_to_all(partial.astype(BF16).reshape(half, depth, D), BOTH, 0, 0,...  36.3 us
    dot_general x13, matrix products, product(): return jnp.dot(left, right, preferred_element_type=F32)  27.2 us
    dot_general x10, matrix products, product_t(): lax.dot_general(left, right, (((left.ndim - 1,), (1,)), ((), ())), prefer...  25.2 us
  transfers between devices with their start and end apart: 12, of which 8 were waited for; matrix products, arithmetic and copies ran while one was open for 18% of the time, Pallas kernels for 2%

profile of v1, /device:TPU:0, one launch (start us, length us, event | category | flops | bytes accessed | tf_op | source)
XLA Modules:
  0.0 695.3 jit_solution(434929008223263585)
XLA Ops:
  12.2 5.5 shard_map.222
  17.6 4.1 collective-permute-start.1
  21.9 5.5 shard_map.221
  27.4 43.6 %collective-permute-done.1 = bf16[3648,128]{1,0:T(8,128)(2,1)S(1)} collective-permute-done((bf16[3648,128]{1,0:T(8,128)(2,1)S(1)}, bf16[3648,128]{1,0:T(8,128)(2,1)S(1)}, u32[]{:S(2)}, u32[]{:S(2)}) %collective-permute-start.1) | collective-permute-done | bytes 933920 | tf_op jit(solution)/shard_map/ppermute | solution.py:433
  72.9 2.9 collective-permute-start.2
  75.9 68.4 %collective-permute-done.2 = f32[4]{0:T(128)S(1)} collective-permute-done((f32[4]{0:T(128)S(1)}, f32[4]{0:T(128)S(1)}, u32[]{:S(2)}, u32[]{:S(2)}) %collective-permute-start.2) | collective-permute-done | bytes 48 | tf_op jit(solution)/shard_map/ppermute | solution.py:433
  146.7 4.1 convert_element_type.341
  153.2 133.2 %all-gather.14.cloned.1.call-done = bf16[32,3648,128]{2,1,0:T(8,128)(2,1)} async-done(((bf16[2,3648,128]{2,1,0:T(8,128)(2,1)}), bf16[32,3648,128]{2,1,0:T(8,128)(2,1)}) %all-gather.14.cloned.1.call-update) | async-done | bytes 29884432 | tf_op jit(solution)/shard_map/all_gather | solution.py:443
  293.5 2.5 fusion.56
  297.3 3.1 fusion.55
  302.6 2.5 fusion.50
  305.1 3.7 fusion.54
  312.2 3.9 fusion.53
  322.1 3.1 slice_bitcast_fusion.11
  334.1 2.8 pad_add_fusion
  351.7 3.4 constant_dynamic-update-slice_fusion.4
  359.3 3.2 fusion.220
  364.3 2.8 fusion.49
  367.2 3.4 constant_dynamic-update-slice_fusion.11
  373.7 5.8 constant_dynamic-update-slice_fusion.10
  382.9 2.8 all-to-all-start
  388.0 5.8 all-to-all-done
  395.9 3.9 exponential_reduce_fusion.1
  400.8 2.7 fusion.29
  404.2 3.3 all-to-all-start.1
  407.6 4.1 all-to-all-done.1
  415.7 5.9 fusion.223
  422.7 3.2 fusion.224
  427.0 3.7 fusion.155
  431.0 3.9 fusion.225
  441.3 3.1 multiply_reduce_fusion.8
  455.2 2.3 multiply_reduce_fusion.3
  457.6 2.9 multiply_reduce_fusion
  460.7 3.9 bitcast_convert_fusion
  465.9 36.3 %all_to_all.20 = bf16[16,64,768]{2,1,0:T(8,128)(2,1)S(1)} all-to-all(bf16[16,64,768]{2,1,0:T(8,128)(2,1)S(1)} %bitcast.378), channel_id=1, replica_groups={{0,1,2,3,4,5,6,7,8,9,10,11,12,13,14,15},{16,17,18,19,20,21,22,23,24,25,..., dimensions={0} | all-to-all | bytes 3145728 | tf_op jit(solution)/shard_map/all_to_all | solution.py:582
  507.7 3.0 fusion.4
  513.6 2.4 slice.788
  516.0 56.9 %all-gather.16.cloned.1.call-done = bf16[256,9984]{1,0:T(8,128)(2,1)} async-done(((bf16[8,9984]{1,0:T(8,128)(2,1)}), bf16[256,9984]{1,0:T(8,128)(2,1)}) %all-gather.16.cloned.1.call-update) | async-done | bytes 5111824 | tf_op jit(solution)/shard_map/all_gather | solution.py:564
  576.3 2.3 fusion.70
  578.6 2.4 copy.70
  582.9 2.6 pad_convert_fusion
  585.5 5.7 copy.71.rows_ref
  592.9 51.7 %all-gather.20.cloned.1.call-done = f32[2048,768]{1,0:T(8,128)} async-done(((f32[64,768]{1,0:T(8,128)}), f32[2048,768]{1,0:T(8,128)}) %all-gather.20.cloned.1.call-update) | async-done | bytes 6291472 | tf_op jit(solution)/shard_map/all_gather | solution.py:586
  649.3 2.5 slice_select_fusion.wide_ref
  651.8 9.4 %shard_map.223 = f32[3456,128]{1,0:T(8,128)S(1)} custom-call(s32[13]{0:T(128)S(1)} %fusion.170.tab_ref, f32[9536,128]{1,0:T(8,128)} %copy.71.rows_ref, bf16[128,8960]{1,0:T(8,128)(2,1)S(1)} %copy-done, f32[1490,768]{1,0:T(8,128)} %slice_select_fusion.wide_ref, f32[256,2304]{1,0:T(8,128)} %pad_maximum_fusion.1.qkv_ref), custom_call_target="tpu_custom_call" | custom-call | tf_op jit(solution)/shard_map/pallas_call | solution.py:639
  664.1 6.4 all-to-all-start.3
  671.9 5.7 all-to-all-done.3
  679.1 6.9 multiply_add_fusion
  (376 shorter events, 119.9 us)
Async XLA Ops:
  7.2 139.5 %all-gather.12.cloned.1.call-start = ((), (), s32[]{:S(2)}) async-start(), calls=%async_computation.4 | async-start | bytes 2359296 | tf_op jit(solution)/shard_map/all_gather | solution.py:446
  9.0 277.4 %all-gather.14.cloned.1.call-start = ((), (), s32[]{:S(2)}) async-start(), calls=%async_computation.5 | async-start | bytes 31752192 | tf_op jit(solution)/shard_map/all_gather | solution.py:443
  17.6 53.3 %collective-permute-start.1 = (bf16[3648,128]{1,0:T(8,128)(2,1)S(1)}, bf16[3648,128]{1,0:T(8,128)(2,1)S(1)}, u32[]{:S(2)}, u32[]{:S(2)}) collective-permute-start(bf16[3648,128]{1,0:T(8,128)(2,1)S(1)} %shard_map.222), channel_id=1, source_target_pairs={{0,16},{4,20},{8,24},{12,28},{16,0},{20,4},{24,8},{28,12},{1,17},{... | collective-permute-start | bytes 2801672 | tf_op jit(solution)/shard_map/ppermute | solution.py:433
  72.7 439.4 %all-gather.22.cloned.1.call-start = ((), (), s32[]{:S(2)}) async-start(), calls=%async_computation.9 | async-start | bytes 4866048 | tf_op jit(solution)/shard_map/all_gather | solution.py:565
  72.9 72.0 %collective-permute-start = (bf16[4,196,768]{2,0,1:T(4,128)(2,1)S(1)}, bf16[4,196,768]{2,0,1:T(4,128)(2,1)S(1)}, u32[]{:S(2)}, u32[]{:S(2)}) collective-permute-start(bf16[4,196,768]{2,0,1:T(4,128)(2,1)S(1)} %copy-done.25), channel_id=1, source_target_pairs={{0,16},{4,20},{8,24},{12,28},{16,0},{20,4},{24,8},{28,12},{1,17},{... | collective-permute-start | bytes 3612680 | tf_op jit(solution)/shard_map/ppermute | solution.py:433
  72.9 71.4 %collective-permute-start.2 = (f32[4]{0:T(128)S(1)}, f32[4]{0:T(128)S(1)}, u32[]{:S(2)}, u32[]{:S(2)}) collective-permute-start(f32[4]{0:T(128)S(1)} %convert_element_type.336), channel_id=1, source_target_pairs={{0,16},{4,20},{8,24},{12,28},{16,0},{20,4},{24,8},{28,12},{1,17},{... | collective-permute-start | bytes 56 | tf_op jit(solution)/shard_map/ppermute | solution.py:433
  75.9 261.4 %copy-start.44 = (s32[768]{0:T(1024)}, s32[768]{0:T(1024)S(1)}, u32[]{:S(2)}) copy-start(s32[768]{0:T(1024)S(1)} %add_select_fusion) | copy-start | bytes 9220
  75.9 269.6 %copy-start.40 = (pred[12,768]{1,0:T(8,128)(4,1)}, pred[12,768]{1,0:T(8,128)(4,1)S(1)}, u32[]{:S(2)}) copy-start(pred[12,768]{1,0:T(8,128)(4,1)S(1)} %iota_compare_fusion) | copy-start | bytes 27652
  316.1 10.5 %copy-start.1 = (bf16[34432,128]{1,0:T(8,128)(2,1)}, bf16[34432,128]{1,0:T(8,128)(2,1)S(1)}, u32[]{:S(2)}) copy-start(bf16[34432,128]{1,0:T(8,128)(2,1)S(1)} %get-tuple-element.90) | copy-start | bytes 26443780
  327.5 14.4 %copy-start.3 = (f32[196,768]{1,0:T(8,128)}, f32[196,768]{1,0:T(8,128)S(1)}, u32[]{:S(2)}) copy-start(f32[196,768]{1,0:T(8,128)S(1)} %slice.670) | copy-start | bytes 1806340
  332.9 102.2 %copy-start.39 = (f32[768]{0:T(1024)}, f32[768]{0:T(1024)S(1)}, u32[]{:S(2)}) copy-start(f32[768]{0:T(1024)S(1)} %get-tuple-element.34) | copy-start | bytes 9220
  334.1 11.0 %copy-start.42 = (f32[768]{0:T(1024)}, f32[768]{0:T(1024)S(1)}, u32[]{:S(2)}) copy-start(f32[768]{0:T(1024)S(1)} %fusion.177) | copy-start | bytes 9220
  336.9 8.6 %copy-start.7 = (bf16[768,2304]{1,0:T(8,128)(2,1)}, bf16[768,2304]{1,0:T(8,128)(2,1)S(1)}, u32[]{:S(2)}) copy-start(bf16[768,2304]{1,0:T(8,128)(2,1)S(1)} %pad_add_fusion) | copy-start | bytes 10616836
  355.1 18.6 %copy-start.35 = (bf16[8,9984]{1,0:T(8,128)(2,1)}, bf16[8,9984]{1,0:T(8,128)(2,1)S(1)}, u32[]{:S(2)}) copy-start(bf16[8,9984]{1,0:T(8,128)(2,1)S(1)} %get-tuple-element.60) | copy-start | bytes 479236
  373.7 8.3 %copy-start.69 = (s32[8]{0:T(128)S(1)}, s32[8]{0:T(128)}, u32[]{:S(2)}) copy-start(s32[8]{0:T(128)} %broadcast_select_fusion.7) | copy-start | bytes 100
  379.5 14.4 %copy-start.50 = (f32[2048]{0:T(1024)S(1)}, f32[2048]{0:T(1024)}, u32[]{:S(2)}) copy-start(f32[2048]{0:T(1024)} %add_rsqrt_fusion) | copy-start | bytes 24580
  380.6 15.2 %copy-start.46 = (f32[2048]{0:T(1024)S(1)}, f32[2048]{0:T(1024)}, u32[]{:S(2)}) copy-start(f32[2048]{0:T(1024)} %param.22) | copy-start | bytes 24580
  382.9 11.0 %all-to-all-start = ((bf16[32,8,256]{2,1,0:T(8,128)(2,1)}), bf16[32,8,256]{2,1,0:T(8,128)(2,1)S(1)}, u32[]{:S(2)}, u32[]{:S(2)}) async-start(bf16[32,8,256]{2,1,0:T(8,128)(2,1)} %broadcast_in_dim.86), calls=%async_computation | async-start | bytes 262144 | tf_op jit(solution)/shard_map/all_to_all | solution.py:489
  399.8 15.2 %copy-start.62 = (pred[2048]{0:T(1024)(128)(4,1)S(1)}, pred[2048]{0:T(1024)(128)(4,1)}, u32[]{:S(2)}) copy-start(pred[2048]{0:T(1024)(128)(4,1)} %constant.124.clone.1) | copy-start | bytes 6148
  404.2 7.5 %all-to-all-start.1 = ((f32[4,35,128]{2,1,0:T(8,128)}), f32[4,35,128]{2,1,0:T(8,128)S(1)}, u32[]{:S(2)}, u32[]{:S(2)}) async-start(f32[4,35,128]{2,1,0:T(8,128)} %reshape.692), calls=%async_computation.1 | async-start | bytes 163840 | tf_op jit(solution)/shard_map/all_to_all | solution.py:522
  407.5 104.6 %all-gather.18.cloned.1.call-start = ((), (), s32[]{:S(2)}) async-start(), calls=%async_computation.7 | async-start | bytes 4866048 | tf_op jit(solution)/shard_map/all_gather | solution.py:553
  422.7 150.2 %all-gather.16.cloned.1.call-start = ((), (), s32[]{:S(2)}) async-start(), calls=%async_computation.6 | async-start | bytes 5271552 | tf_op jit(solution)/shard_map/all_gather | solution.py:564
  430.8 8.3 %copy-start.63 = (pred[768]{0:T(1024)(128)(4,1)S(1)}, pred[768]{0:T(1024)(128)(4,1)}, u32[]{:S(2)}) copy-start(pred[768]{0:T(1024)(128)(4,1)} %constant.250.clone.1) | copy-start | bytes 2308
  437.2 18.0 %slice-start = ((s8[4915200]{0:T(1024)(128)(4,1)}), s8[720896]{0:T(1024)(128)(4,1)S(1)}, s32[]{:S(2)}) async-start(s8[4915200]{0:T(1024)(128)(4,1)} %bitcast.346), calls=%async_computation.10 | async-start | bytes 1441792
  439.8 204.9 %all-gather.20.cloned.1.call-start = ((), (), s32[]{:S(2)}) async-start(), calls=%async_computation.8 | async-start | bytes 6488064 | tf_op jit(solution)/shard_map/all_gather | solution.py:586
  446.6 8.6 %slice-start.1 = ((s8[4915200]{0:T(1024)(128)(4,1)}), s8[4194304]{0:T(1024)(128)(4,1)S(1)}, s32[]{:S(2)}) async-start(s8[4915200]{0:T(1024)(128)(4,1)} %bitcast.346), calls=%async_computation.11 | async-start | bytes 8388608
  447.4 7.8 %copy-start.4 = (f32[196,768]{1,0:T(8,128)S(1)}, f32[196,768]{1,0:T(8,128)}, u32[]{:S(2)}) copy-start(f32[196,768]{1,0:T(8,128)} %copy-done.3) | copy-start | bytes 1806340
  447.4 7.8 %copy-start.30 = (bf16[8,12,196]{2,1,0:T(8,128)(2,1)S(1)}, bf16[8,12,196]{2,1,0:T(8,128)(2,1)}, u32[]{:S(2)}) copy-start(bf16[8,12,196]{2,1,0:T(8,128)(2,1)} %copy-done.29) | copy-start | bytes 112900
  447.4 7.8 %copy-start.37 = (f32[8,196]{1,0:T(8,128)S(1)}, f32[8,196]{1,0:T(8,128)}, u32[]{:S(2)}) copy-start(f32[8,196]{1,0:T(8,128)} %copy-done.36) | copy-start | bytes 18820
  465.7 37.4 %copy-start.70 = (s32[32]{0:T(128)S(1)}, s32[32]{0:T(128)}, u32[]{:S(2)}) copy-start(s32[32]{0:T(128)} %constant.267.clone) | copy-start | bytes 388
  465.7 40.7 %copy-start.53 = (bf16[768]{0:T(1024)(128)(2,1)S(1)}, bf16[768]{0:T(1024)(128)(2,1)}, u32[]{:S(2)}) copy-start(bf16[768]{0:T(1024)(128)(2,1)} %copy-done.52) | copy-start | bytes 4612
  465.7 40.7 %copy-start.51 = (f32[1,768]{1,0:T(1,128)S(1)}, f32[1,768]{1,0:T(1,128)}, u32[]{:S(2)}) copy-start(f32[1,768]{1,0:T(1,128)} %get-tuple-element.50) | copy-start | bytes 9220
  465.7 41.3 %copy-start.47 = (f32[2048]{0:T(1024)S(1)}, f32[2048]{0:T(1024)}, u32[]{:S(2)}) copy-start(f32[2048]{0:T(1024)} %param.22) | copy-start | bytes 24580
  465.7 41.3 %copy-start.49 = (f32[2048]{0:T(1024)S(1)}, f32[2048]{0:T(1024)}, u32[]{:S(2)}) copy-start(f32[2048]{0:T(1024)} %get-tuple-element.116) | copy-start | bytes 24580
  465.7 41.9 %copy-start.20 = (f32[128,2048]{1,0:T(8,128)S(1)}, f32[128,2048]{1,0:T(8,128)}, u32[]{:S(2)}) copy-start(f32[128,2048]{1,0:T(8,128)} %copy-done.19) | copy-start | bytes 3145732
  465.7 41.9 %copy-start.32 = (bf16[32,8,256]{2,1,0:T(8,128)(2,1)S(1)}, bf16[32,8,256]{2,1,0:T(8,128)(2,1)}, u32[]{:S(2)}) copy-start(bf16[32,8,256]{2,1,0:T(8,128)(2,1)} %copy-done.31) | copy-start | bytes 393220
  465.7 41.9 %copy-start.67 = (f32[128]{0:T(128)S(1)}, f32[128]{0:T(128)}, u32[]{:S(2)}) copy-start(f32[128]{0:T(128)} %get-tuple-element.149) | copy-start | bytes 1540
  465.8 41.9 %copy-start.68 = (f32[128]{0:T(128)S(1)}, f32[128]{0:T(128)}, u32[]{:S(2)}) copy-start(f32[128]{0:T(128)} %get-tuple-element.150) | copy-start | bytes 1540
  465.9 41.8 %copy-start.28 = (f32[128,2048]{1,0:T(8,128)S(1)}, f32[128,2048]{1,0:T(8,128)}, u32[]{:S(2)}) copy-start(f32[128,2048]{1,0:T(8,128)} %get-tuple-element.184) | copy-start | bytes 3145732
  512.1 64.1 %slice-start.2 = ((bf16[256,12,768]{2,0,1:T(8,128)(2,1)}), bf16[128,12,768]{2,0,1:T(8,128)(2,1)S(1)}, s32[]{:S(2)}) async-start(bf16[256,12,768]{2,0,1:T(8,128)(2,1)} %all-gather.22.cloned.1.call-done), calls=%async_computation.12 | async-start | bytes 4718592 | tf_op jit(solution)/shard_map/slice | solution.py:590
  591.3 54.3 %copy-start.59 = (f32[1,256]{1,0:T(1,128)S(1)}, f32[1,256]{1,0:T(1,128)}, u32[]{:S(2)}) copy-start(f32[1,256]{1,0:T(1,128)} %pad_dynamic-slice_fusion.4) | copy-start | bytes 3076
  591.3 55.5 %copy-start.45 = (s32[768]{0:T(1024)S(1)}, s32[768]{0:T(1024)}, u32[]{:S(2)}) copy-start(s32[768]{0:T(1024)} %copy-done.44) | copy-start | bytes 9220
  591.3 56.4 %copy-start.15 = (f32[256,768]{1,0:T(8,128)S(1)}, f32[256,768]{1,0:T(8,128)}, u32[]{:S(2)}) copy-start(f32[256,768]{1,0:T(8,128)} %copy.70) | copy-start | bytes 2359300
  592.9 56.4 %copy-start.61 = (pred[1490]{0:T(1024)(128)(4,1)S(1)}, pred[1490]{0:T(1024)(128)(4,1)}, u32[]{:S(2)}) copy-start(pred[1490]{0:T(1024)(128)(4,1)} %constant.370) | copy-start | bytes 4474
  651.8 27.2 %copy-start.9 = (f32[441096]{0:T(1024)S(1)}, f32[441096]{0:T(1024)}, u32[]{:S(2)}) copy-start(f32[441096]{0:T(1024)} %param.17) | copy-start | bytes 5293156
  664.1 13.5 %all-to-all-start.3 = ((f32[32,1,128]{2,1,0:T(1,128)}), f32[32,1,128]{2,1,0:T(1,128)S(1)}, u32[]{:S(2)}, u32[]{:S(2)}) async-start(f32[32,1,128]{2,1,0:T(1,128)} %broadcast_in_dim.172), calls=%async_computation.3 | async-start | bytes 32768 | tf_op jit(solution)/shard_map/all_to_all | solution.py:651
  679.0 6.9 copy-start.18
  679.0 6.9 copy-start.26
  (38 other events, 147.1 us)
Sparse Core Ops, SparseCore 0:
  10.8 118.0 all-gather.11
  130.4 155.9 all-gather.13
  371.7 64.1 all-gather.21
  439.2 67.1 all-gather.17
  509.7 63.1 all-gather.15
  576.2 68.3 all-gather.19

commit v2 on v1

--- a/solution.py
+++ b/solution.py
@@ -1,5 +1,4 @@
 import functools
-import math
 
 import jax
 import jax.numpy as jnp
@@ -60,7 +59,6 @@
 ):
     PIECES.append((_offset, _rows, _cols))
     _offset += _rows * _cols
-
 FRONT = 24
 GRAD_FRONT = 8 * FRONT
 CHUNK = 64
@@ -87,8 +85,9 @@
 
 
 class Plan:
-    def __init__(self, count):
-        self.count = count
+    def __init__(self, reps, groups):
+        count = reps * groups
+        self.count, self.groups = count, groups
         self.size = PFLAT // count
         self.lines = round_up(-(-self.size // LANES) + 1, CHUNK)
         self.scratch = FRONT + self.lines + 8 * max(WIDTHS) + 16
@@ -111,22 +110,36 @@
             table.append(entry)
         self.buffer = round_up(longest, 16)
         self.lay_table = np.array(table, np.int32)
+        self.grad_table = self.tabulate(lambda index: index > 1)
+        self.late_table = self.tabulate(lambda index: index < 2)
+        edge = SEGMENTS[0][1] * SEGMENTS[0][2]
+        self.odd_owner = any(
+            device * self.size < edge and self.place(device)[1] for device in range(count)
+        )
+        self.grad_scratch = GRAD_FRONT + self.lines + CHUNK * max(WIDTHS) + 16
+
+
+    def place(self, device):
+        rep, grp = divmod(device, self.groups)
+        return rep // 2 * self.groups + grp, rep % 2
+
+    def tabulate(self, chosen):
         table = []
-        self.most = max(
-            len(shard_parts(d * self.size, (d + 1) * self.size, PIECES)) for d in range(count)
-        )
-        for device in range(count):
+        for device in range(self.count):
             start = device * self.size
-            entry = [start % LANES]
-            parts = shard_parts(start, start + self.size, PIECES)
-            for index, row0, rows, line in parts:
+            entry = []
+            for index, row0, rows, line in shard_parts(start, start + self.size, PIECES):
+                if not chosen(index):
+                    continue
                 skew = row0 % 8
                 line -= skew * (PIECES[index][2] // LANES)
                 entry += [index, GRAD_FRONT + line, -(-(rows + skew) // CHUNK), row0 - skew]
-            entry += [-1, 0, 0, 0] * (self.most - len(parts))
             table.append(entry)
-        self.grad_table = np.array(table, np.int32)
-        self.grad_scratch = GRAD_FRONT + self.lines + CHUNK * max(WIDTHS) + 16
+        most = max(len(entry) for entry in table) // 4
+        for device, entry in enumerate(table):
+            entry += [-1, 0, 0, 0] * (most - len(entry) // 4)
+            entry.insert(0, device * self.size % LANES)
+        return np.array(table, np.int32)
 
 
 def lay_kernel(plan, tab_ref, x_ref, out_ref, line_ref):
@@ -192,15 +205,28 @@
     ]
 
 
+MATRICES = (
+    (0, 0, PD + NTOK + 4),
+    (1, 0, D),
+    (2, 0, D),
+    (3, 0, D),
+    (4, 0, F),
+    (4, F, 2),
+    (5, 0, D),
+    (5, D, H),
+    (6, 0, H),
+)
+
+
 class Rows:
-    def __init__(self, plan, gathered, index, first, count):
+    def __init__(self, plan, gathered, which):
+        index, first, self.count = MATRICES[which]
         width = SEGMENTS[index][2] // LANES
-        half = plan.count // 2
-        self.count = count
-        self.blocks = [block[2:] for block in blocks_of(plan, index, first, count)]
+        blocks = blocks_of(plan, index, first, self.count)
+        self.blocks = [block[2:] for block in blocks]
         pieces = [
-            gathered[device % half, device // half, target : target + rows * width]
-            for device, target, _, rows in blocks_of(plan, index, first, count)
+            gathered[plan.place(device)][target : target + rows * width]
+            for device, target, _, rows in blocks
         ]
         tiles = jnp.concatenate(pieces, 0).reshape(-1, width, 8, LANES)
         self.matrix = tiles.transpose(0, 2, 1, 3).reshape(-1, width * LANES)
@@ -350,27 +376,28 @@
     )
 
 
-def grad_kernel(plan, spans, tab_ref, rows_ref, cols_ref, wide_ref, qkv_ref, out_ref, line_ref):
-    for part in range(plan.most):
+def grad_kernel(plan, most, spans, tab_ref, *refs):
+    refs, out_ref, line_ref = refs[:-2], refs[-2], refs[-1]
+    line_ref[...] = jnp.zeros(line_ref.shape, F32)
+    for part in range(most):
         kind, base, chunks, row0 = (tab_ref[1 + 4 * part + i] for i in range(4))
-        for index, (_, _, cols) in enumerate(PIECES):
+        for index, span in spans.items():
+            cols = PIECES[index][2]
             width = cols // LANES
 
             @pl.when(kind == index)
             def _():
-                def move(step, carry):
+                def move(step, carry, span=span, cols=cols, width=width):
                     row = pl.multiple_of(row0 + step * CHUNK, 8)
                     goal = base + step * (CHUNK * width)
-                    if spans[index] is None:
-                        source = qkv_ref if index == 1 else wide_ref
-                        first = row if index == 0 else row + FINAL_ROW
-                        if index == 1:
-                            first = step * CHUNK
-                        block = source[pl.ds(pl.multiple_of(first, 8), CHUNK), :]
+                    if len(span) == 2:
+                        first = step * CHUNK if span[1] else row
+                        block = refs[span[0]][pl.ds(pl.multiple_of(first, 8), CHUNK), :]
                     else:
-                        first, column = spans[index]
-                        left = rows_ref[pl.ds(pl.multiple_of(first + row, 8), CHUNK), :].astype(BF16)
-                        block = product(left, cols_ref[:, column : column + cols])
+                        first, column = span[1:3]
+                        first = pl.multiple_of(first + row, 8)
+                        left = refs[0][pl.ds(first, CHUNK), :].astype(BF16)
+                        block = product(left, refs[1][:, column : column + cols])
                     for tile in range(width):
                         line_ref[pl.ds(goal + tile, CHUNK, stride=width), :] = block[
                             :, tile * LANES : (tile + 1) * LANES
@@ -392,6 +419,18 @@
         return carry
 
     lax.fori_loop(0, plan.lines // CHUNK, align, 0)
+
+
+def flat_gradient(plan, table, spans, refs, device):
+    return pl.pallas_call(
+        functools.partial(grad_kernel, plan, table.shape[1] // 4, spans),
+        out_shape=jax.ShapeDtypeStruct((plan.lines, LANES), F32),
+        in_specs=[pl.BlockSpec(memory_space=pltpu.SMEM)]
+        + [pl.BlockSpec(memory_space=pltpu.VMEM)] * len(refs),
+        out_specs=pl.BlockSpec(memory_space=pltpu.VMEM),
+        scratch_shapes=[pltpu.VMEM((plan.grad_scratch, LANES), F32)],
+        compiler_params=pltpu.CompilerParams(vmem_limit_bytes=48 * 1024 * 1024),
+    )(jnp.asarray(table)[device], *refs).reshape(-1)[: plan.size]
 
 
 def adam_update(weight, grad, first, second, rate):
@@ -423,14 +462,20 @@
     count, half = reps * groups, reps * groups // 2
     rep, grp = lax.axis_index("rep"), lax.axis_index("grp")
     device = rep * groups + grp
-    low = rep < reps // 2
-    halves = [list(range(half)), list(range(half, count))]
-    swap = [(r, (r + reps // 2) % reps) for r in range(reps)]
+    low = rep % 2 == 0
+    place = rep // 2 * groups + grp
+    halves = [
+        [r * groups + g for r in range(parity, reps, 2) for g in range(groups)] for parity in (0, 1)
+    ]
+    swap = [(r, r ^ 1) for r in range(reps)]
     own_views = patches.shape[0]
     views = 2 * own_views
 
     def trade(values):
         return lax.ppermute(values, "rep", swap)
+
+    def trade_low(values):
+        return jnp.where(low, values, trade(values))
 
     def in_order(values):
         other = trade(values)
@@ -439,13 +484,14 @@
     table = jnp.asarray(plan.lay_table)[device]
     kept = lay_out(plan, table, jnp.where(low, params, teacher))
     given = trade(lay_out(plan, table, jnp.where(low, teacher, params)))
+    patches, partner, given = lax.optimization_barrier((patches, partner, given))
     shards = jnp.stack([jnp.where(low, kept, given), jnp.where(low, given, kept)])
     gathered = lax.all_gather(shards, BOTH, axis=0, axis_index_groups=halves)
     pixels = jnp.concatenate(in_order(patches), 0)
     places = in_order(partner.astype(F32))
-    tables = lax.all_gather(
-        jnp.stack([protos, teacher_protos]).astype(BF16), "rep", axis=1, tiled=True
-    ).astype(F32)
+    tables = jnp.stack([protos, teacher_protos]).astype(BF16)
+    tables, gathered = lax.optimization_barrier((tables, gathered))
+    tables = lax.all_gather(tables, "rep", axis=1, tiled=True).astype(F32)
 
     def columns_of(values):
         scale = lax.rsqrt(jnp.sum(values * values, 0, keepdims=True) + 1e-06)
@@ -454,15 +500,11 @@
     columns, column_scale = columns_of(tables[0])
     teacher_columns = columns_of(tables[1])[0]
 
-    wide = Rows(plan, gathered, 0, 0, PD + NTOK + 4).folded()
-    qkv_w = Rows(plan, gathered, 1, 0, D).folded()
-    out_w = Rows(plan, gathered, 2, 0, D)
-    up_w = Rows(plan, gathered, 3, 0, D)
-    down_w = Rows(plan, gathered, 4, 0, F)
-    final = Rows(plan, gathered, 4, F, 2).folded().astype(F32)
-    head_one = Rows(plan, gathered, 5, 0, D)
-    head_two = Rows(plan, gathered, 5, D, H)
-    head_three = Rows(plan, gathered, 6, 0, H)
+    wide = Rows(plan, gathered, 0).folded()
+    qkv_w = Rows(plan, gathered, 1).folded()
+    out_w, up_w, down_w = (Rows(plan, gathered, which) for which in (2, 3, 4))
+    final = Rows(plan, gathered, 5).folded().astype(F32)
+    head_one, head_two, head_three = (Rows(plan, gathered, which) for which in (6, 7, 8))
     norms = wide[PD + NTOK :].astype(F32)
 
     class_row, attended, mixed, trunk_kept = trunk_forward(pixels, wide, qkv_w)
@@ -482,15 +524,25 @@
     bottle_scale = lax.rsqrt(jnp.sum(bottle * bottle, -1, keepdims=True) + 1e-06)
     rows = (bottle * bottle_scale).astype(BF16)
 
+    def gather_rows(values):
+        values = trade_low(values)
+        return lax.all_gather(values, BOTH, axis=0, axis_index_groups=halves).reshape(
+            half * views, -1
+        )
+
+    ahead = [attended, normed_two, act, cls, first, second, mixed.reshape(views, -1)]
+    ahead = gather_rows(jnp.concatenate(ahead, 1))
+
     here = jnp.arange(views)
-    place = jnp.concatenate([places[0], places[1] + own_views]).astype(jnp.int32)
-    place = jnp.where(low, here, place)
-    rows = product((place[:, None] == here[None, :]).astype(BF16), rows).astype(BF16)
+    source = jnp.concatenate([places[0], places[1] + own_views]).astype(jnp.int32)
+    source = jnp.where(low, here, source)
+    rows = product((source[:, None] == here[None, :]).astype(BF16), rows).astype(BF16)
     all_rows = lax.all_to_all(
         jnp.broadcast_to(rows[None], (count, views, B)), BOTH, 0, 0
     )
-    student_rows = all_rows[:half].reshape(-1, B)
-    teacher_rows = all_rows[half:].reshape(-1, B)
+    all_rows = all_rows.reshape(reps // 2, 2, groups * views, B)
+    student_rows = all_rows[:, 0].reshape(-1, B)
+    teacher_rows = all_rows[:, 1].reshape(-1, B)
 
     teacher_logits = product(teacher_rows, teacher_columns)
     new_center = CENTER_MOMENTUM * center + (1.0 - CENTER_MOMENTUM) * jnp.mean(teacher_logits, 0)
@@ -501,7 +553,7 @@
         [jnp.sum(exp_student, 1), jnp.sum(exp_teacher, 1), jnp.sum(exp_teacher * scaled, 1)]
     )
     band = groups * views
-    start = lax.rem(rep, reps // 2) * band
+    start = rep // 2 * band
     pulls = jnp.concatenate(
         [
             lax.dynamic_slice_in_dim(exp_student, start, band, 0),
@@ -523,7 +575,7 @@
     pulls = note[: 2 * views * B].reshape(2, views, B)
     sum_student, sum_teacher, crossed = note[2 * views * B :].reshape(3, -1)
     loss_value = jnp.sum(jnp.log(sum_student) - crossed / sum_teacher)
-    own = lax.rem(device, half) * views
+    own = place * views
     own_student = lax.dynamic_slice_in_dim(sum_student, own, views)[:, None]
     own_teacher = lax.dynamic_slice_in_dim(sum_teacher, own, views)[:, None]
     grad_rows = (pulls[0] / own_student - pulls[1] / own_teacher) / STUDENT_TEMP
@@ -549,8 +601,6 @@
     grad_two = gelu_back(pre_two, head_three.back(grad_bottle)).astype(BF16)
     grad_one = gelu_back(pre_one, head_two.back(grad_two)).astype(BF16)
     grad_cls = head_one.back(grad_one)
-    head_pack = jnp.concatenate([cls, first, second, grad_bottle, grad_two, grad_one], 1)
-    head_pack = lax.all_gather(head_pack, BOTH, axis=0)
     grad_stream = norm_back(grad_cls, final[0], unit_three, scale_three)
     grad_branch = grad_stream.astype(BF16)
     grad_hidden = gelu_back(hidden, down_w.back(grad_branch)).astype(BF16)
@@ -558,11 +608,9 @@
     grad_middle = grad_stream + norm_back(grad_normed, norms[2], unit_two, scale_two)
     grad_mixed = grad_middle.astype(BF16)
     grad_att = out_w.back(grad_mixed).astype(BF16)
-    body_pack = jnp.concatenate(
-        [attended, normed_two, act, grad_mixed, grad_hidden, grad_branch, grad_att], 1
-    )
-    body_pack = lax.all_gather(body_pack, BOTH, axis=0)
-    mixed_pack = lax.all_gather(mixed, BOTH, axis=0)
+    behind = [grad_mixed, grad_hidden, grad_branch, grad_bottle, grad_two, grad_one, grad_att]
+    behind += [(grad_cls * unit_three).astype(BF16), grad_cls.astype(BF16)]
+    cols_all = gather_rows(jnp.concatenate(behind, 1))
 
     pieces = trunk_backward(pixels, wide, qkv_w, grad_att, grad_middle, trunk_kept)
     partial = jnp.concatenate(
@@ -570,89 +618,87 @@
         + (
             jnp.sum(grad_normed * unit_two, 0, keepdims=True),
             jnp.sum(grad_normed, 0, keepdims=True),
-            jnp.zeros((FINAL_ROW - PD - NTOK - 4, D), F32),
-            jnp.sum(grad_cls * unit_three, 0, keepdims=True),
-            jnp.sum(grad_cls, 0, keepdims=True),
-        )
-        + pieces[5:],
+        ),
         0,
     )
-    depth = round_up(-(-partial.shape[0] // half), 8)
-    partial = jnp.pad(partial, ((0, half * depth - partial.shape[0]), (0, 0)))
-    partial = lax.all_to_all(
-        partial.astype(BF16).reshape(half, depth, D), BOTH, 0, 0, axis_index_groups=halves
-    )
+    base = PD + NTOK + 4
+    depth = -(-base // half)
+    partial = jnp.pad(partial, ((0, half * depth - base), (0, 0))).reshape(half, depth, D)
+    shared = jnp.concatenate(pieces[5:], 0)
+    slots = round_up(depth + shared.shape[0], 8)
+    partial = jnp.concatenate(
+        [
+            partial,
+            jnp.broadcast_to(shared[None], (half,) + shared.shape),
+            jnp.zeros((half, slots - depth - shared.shape[0], D), F32),
+        ],
+        1,
+    ).astype(BF16)
+    partial = lax.all_to_all(partial, BOTH, 0, 0, axis_index_groups=halves)
     partial = jnp.sum(partial.astype(F32), 0)
-    summed = lax.all_gather(partial, BOTH, axis=0)[:half].reshape(-1, D)
-
-    head_rows = head_pack[:half].reshape(half * views, -1)
-    body_rows = body_pack[:half].reshape(half * views, -1)
-    mixed_rows = mixed_pack[:half].reshape(half * views, HEADS, D)
-    rows_all = jnp.concatenate(
-        [body_rows[:, : 2 * D + F], head_rows[:, : D + 2 * H]], 1
-    ).astype(F32)
-    rows_all = jnp.pad(rows_all.T, ((0, CHUNK), (0, 0)))
-    cols_all = jnp.concatenate(
-        [body_rows[:, 2 * D + F : 4 * D + 2 * F], head_rows[:, D + 2 * H :]], 1
-    )
-    spans = [
-        None,
-        None,
-        (0, 0),
-        (D, D),
-        (2 * D, D + F),
-        None,
-        (2 * D + F, 2 * D + F + B + H),
-        (3 * D + F, 2 * D + F + B),
-        (3 * D + F + H, 2 * D + F),
-    ]
-    qkv_row = jnp.asarray(
-        [
-            max([0] + [p[1] // 8 * 8 for p in shard_parts(d * plan.size, (d + 1) * plan.size, PIECES) if p[0] == 1])
-            for d in range(count)
-        ],
-        jnp.int32,
-    )[device]
-    qkv_rows = round_up(min(D, -(-plan.size // (3 * D)) + 9), CHUNK)
-    base = FINAL_ROW
-    sum_query, reach = summed[base + 2], summed[base + 3 : base + 3 + HEADS]
-
-    def slab(values):
-        return lax.dynamic_slice_in_dim(
-            jnp.pad(values, ((0, 0),) * (values.ndim - 1) + ((0, qkv_rows),)),
-            qkv_row,
-            qkv_rows,
-            values.ndim - 1,
-        )
-
-    class_normed, query = trunk_kept[5].astype(F32), trunk_kept[6].astype(F32)
-    qkv_q = slab(class_normed).T * sum_query[None]
-    qkv_k = lax.dot_general(
-        slab(reach), jnp.where(head_mask(), query, 0.0), (((0,), (0,)), ((), ())), precision=PRECISE
-    )
-    grad_att_rows = body_rows[:, 4 * D + 2 * F :].reshape(-1, HEADS, HDIM)
+    shared = partial[depth : depth + shared.shape[0]]
+    shared = jnp.where(low, shared, trade(shared))
+    partial = partial[:depth]
+    slots = round_up(depth, 8)
+    summed = jnp.pad(partial, ((0, slots - depth), (0, 0))).astype(BF16)
+    summed = lax.all_to_all(
+        jnp.broadcast_to(summed[None], (half, slots, D)), BOTH, 0, 0, axis_index_groups=halves
+    )
+    summed = summed[:, :depth].reshape(-1, D)[:base]
+    if plan.odd_owner:
+        summed = trade_low(summed)
+    summed = summed.astype(F32)
+
+    split = 3 * D + F + 2 * H
+    rows_all = jnp.pad(ahead[:, :split].astype(F32).T, ((0, CHUNK), (0, 0)))
+    mixed_rows = ahead[:, split:].reshape(half * views, HEADS, D)
+    ends = jnp.sum(cols_all[:, -2 * D :].astype(F32), 0).reshape(2, D)
+    ends = jnp.pad(ends, ((0, CHUNK - 2), (0, 0)))
+    spans = {
+        2: (0, 0, 0),
+        3: (0, D, D),
+        4: (0, 2 * D, D + F),
+        5: (2, False),
+        6: (0, 2 * D + F, 2 * D + F + B + H),
+        7: (0, 3 * D + F, 2 * D + F + B),
+        8: (0, 3 * D + F + H, 2 * D + F),
+    }
+    early = flat_gradient(plan, plan.grad_table, spans, (rows_all, cols_all, ends), device)
+    values_att = cols_all[:, 2 * D + F + B + 2 * H : 3 * D + F + B + 2 * H]
+    values_att = values_att.reshape(-1, HEADS, HDIM)
     qkv_v = jnp.einsum(
-        "vhd,vhc->dhc", slab(mixed_rows), grad_att_rows, preferred_element_type=F32
-    ).reshape(qkv_rows, D)
-    qkv_grad = jnp.concatenate([qkv_q, qkv_k, qkv_v], 1)
-    wide_grad = jnp.pad(summed[: base + 2], ((0, 8 * CHUNK), (0, 0)))
-    flat_lines = pl.pallas_call(
-        functools.partial(grad_kernel, plan, spans),
-        out_shape=jax.ShapeDtypeStruct((plan.lines, LANES), F32),
-        in_specs=[pl.BlockSpec(memory_space=pltpu.SMEM)]
-        + [pl.BlockSpec(memory_space=pltpu.VMEM)] * 4,
-        out_specs=pl.BlockSpec(memory_space=pltpu.VMEM),
-        scratch_shapes=[pltpu.VMEM((plan.grad_scratch, LANES), F32)],
-        compiler_params=pltpu.CompilerParams(vmem_limit_bytes=48 * 1024 * 1024),
-    )(jnp.asarray(plan.grad_table)[device], rows_all, cols_all, wide_grad, qkv_grad)
-    grad_flat = flat_lines.reshape(-1)[: plan.size]
-
-    squares = jnp.sum(grad_flat * grad_flat) + jnp.sum(grad_protos * grad_protos)
+        "vhd,vhc->dhc", mixed_rows, values_att, preferred_element_type=F32
+    ).reshape(D, D)
+
+    class_normed, query = (trade_low(trunk_kept[which].astype(F32)) for which in (5, 6))
+    by_head = jnp.where(head_mask(), query, 0.0)
+    sum_query, reach = shared[0], shared[1:]
+    outer = jnp.sum(class_normed * class_normed) * jnp.sum(sum_query * sum_query) + jnp.sum(
+        jnp.sum(reach * reach, 1) * jnp.sum(by_head * by_head, 1)
+    )
+    squares = jnp.sum(partial * partial) + (jnp.sum(qkv_v * qkv_v) + outer) / half
+    squares = jnp.where(low, squares, 0.0)
+    squares = squares + jnp.sum(early * early) + jnp.sum(grad_protos * grad_protos)
     squares = lax.all_to_all(
         jnp.broadcast_to(squares.reshape(1, 1, 1), (count, 1, LANES)), BOTH, 0, 0
     )
     grad_norm = jnp.sqrt(jnp.sum(squares[:, 0, 0]))
     factor = jnp.minimum(1.0, CLIP_NORM / (grad_norm + 1e-06))
+
+    qkv_grad = jnp.concatenate(
+        [
+            class_normed.T * sum_query[None],
+            lax.dot_general(reach, by_head, (((0,), (0,)), ((), ())), precision=PRECISE),
+            qkv_v,
+        ],
+        1,
+    )
+    qkv_grad = jnp.pad(qkv_grad, ((0, CHUNK), (0, 0)))
+    wide_grad = jnp.pad(summed, ((0, CHUNK), (0, 0)))
+    late = flat_gradient(
+        plan, plan.late_table, {0: (0, False), 1: (1, False)}, (wide_grad, qkv_grad), device
+    )
+    grad_flat = early + late
     new_params, new_first, new_second = adam_update(
         params, grad_flat * factor, first_moment, second_moment, LEARNING_RATE
     )
@@ -690,7 +736,7 @@
         P(BOTH, None, None),
         P(BOTH),
     )
-    plan = Plan(math.prod(mesh.shape.values()))
+    plan = Plan(mesh.shape["rep"], mesh.shape["grp"])
     return jax.shard_map(
         functools.partial(per_device, plan),
         mesh=mesh,

time: 703 us -> 585 us (0.83)
  waiting for transfers between devices: 370 us -> 237 us
  blocking collectives: 36.3 us -> 0 us
  starting transfers between devices: 19.8 us -> 50.4 us
    all_gather x5 -> x3, waiting for transfers between devices: 109 us -> 8.42 us  [the longest x1 8.39 us: per_device(): tables = lax.all_gather(tables, 'rep', axis=1, tiled=True).astype(F32)]
    ppermute x3 -> x8, waiting for transfers between devices: 112 us -> 43.1 us  [trade(): return lax.ppermute(values, 'rep', swap)]
    all_to_all x0 -> x2, waiting for transfers between devices: none -> 45.6 us  [the longest x1 34.2 us: per_device(): partial = lax.all_to_all(partial, BOTH, 0, 0, axis_index_groups=halves)]
    all_to_all x1 -> x0, blocking collectives: 36.3 us -> none  [per_device(): lax.all_to_all(partial.astype(BF16).reshape(half, depth, D), BOTH, 0, 0,...]
    all_to_all x1, starting transfers between devices: 6.42 us -> 23.3 us  [per_device(): lax.all_to_all(jnp.broadcast_to(squares.reshape(1, 1, 1), (count, 1, LANE...]
    all_gather x1, waiting for transfers between devices: 133 us -> 122 us  [per_device(): gathered = lax.all_gather(shards, BOTH, axis=0, axis_index_groups=halves)]
    unnamed x164 -> x198, local copies, waits for them, and re-layouts: 38.8 us -> 47.9 us
    all_to_all x0 -> x2, starting transfers between devices: none -> 7.49 us  [the longest x1 3.79 us: per_device(): partial = lax.all_to_all(partial, BOTH, 0, 0, axis_index_groups=halves)]
  transfers between devices with their start and end apart: 12 -> 17, of which waited for: 8 -> 11; matrix products, arithmetic and copies ran while one was open for 18% -> 25% of each run, Pallas kernels for 2% -> 1%
where the time goes in v2:
time: 585 us; the launch traced here: 574 us
  waiting for transfers between devices  237 us (41%)
  local copies, waits for them, and re-layouts  96.1 us (16%)
  matrix products  71.1 us (12%)
  other arithmetic  69.9 us (12%)
  starting transfers between devices  50.4 us (9%)
  Pallas kernels  26.3 us (4%)
  between operations  23.7 us (4%)
    all_gather x1, waiting for transfers between devices, per_device(): gathered = lax.all_gather(shards, BOTH, axis=0, axis_index_groups=halves)  122 us
    unnamed x198, local copies, waits for them, and re-layouts  47.9 us
    ppermute x8, waiting for transfers between devices, trade(): return lax.ppermute(values, 'rep', swap)  43.1 us
    all_to_all x1, waiting for transfers between devices, per_device(): partial = lax.all_to_all(partial, BOTH, 0, 0, axis_index_groups=halves)  34.2 us
    dot_general x13, matrix products, product(): return jnp.dot(left, right, preferred_element_type=F32)  25.8 us
    dot_general x10, matrix products, product_t(): lax.dot_general(left, right, (((left.ndim - 1,), (1,)), ((), ())), prefer...  23.3 us
    all_to_all x1, starting transfers between devices, per_device(): lax.all_to_all(jnp.broadcast_to(squares.reshape(1, 1, 1), (count, 1, LANE...  23.3 us
    pallas_call x2, Pallas kernels, flat_gradient(): pl.pallas_call(functools.partial(grad_kernel, plan, table.shape[1] // 4,...  15.3 us
  transfers between devices with their start and end apart: 17, of which 11 were waited for; matrix products, arithmetic and copies ran while one was open for 25% of the time, Pallas kernels for 1%

profile of v2, /device:TPU:0, one launch (start us, length us, event | category | flops | bytes accessed | tf_op | source)
XLA Modules:
  0.0 574.2 jit_solution(3974265481464743646)
XLA Ops:
  10.3 5.5 shard_map.221
  15.8 2.8 collective-permute-start
  18.7 5.5 shard_map.222
  24.2 15.2 %collective-permute-done = bf16[3648,128]{1,0:T(8,128)(2,1)S(1)} collective-permute-done((bf16[3648,128]{1,0:T(8,128)(2,1)S(1)}, bf16[3648,128]{1,0:T(8,128)(2,1)S(1)}, u32[]{:S(2)}, u32[]{:S(2)}) %collective-permute-start) | collective-permute-done | bytes 933920 | tf_op jit(solution)/shard_map/ppermute | solution.py:475
  44.6 25.0 %collective-permute-done.3 = f32[4]{0:T(128)S(1)} collective-permute-done((f32[4]{0:T(128)S(1)}, f32[4]{0:T(128)S(1)}, u32[]{:S(2)}, u32[]{:S(2)}) %collective-permute-start.3) | collective-permute-done | bytes 48 | tf_op jit(solution)/shard_map/ppermute | solution.py:475
  72.0 122.4 %all-gather.10.cloned.1.call-done = bf16[32,3648,128]{2,1,0:T(8,128)(2,1)} async-done(((bf16[2,3648,128]{2,1,0:T(8,128)(2,1)}), bf16[32,3648,128]{2,1,0:T(8,128)(2,1)}) %all-gather.10.cloned.1.call-update) | async-done | bytes 29884432 | tf_op jit(solution)/shard_map/all_gather | solution.py:489
  200.8 2.5 bitcast_dynamic-update-slice_fusion.13
  204.6 3.1 bitcast_dynamic-update-slice_fusion.12
  211.5 3.5 bitcast_dynamic-update-slice_fusion.11
  218.5 3.8 bitcast_dynamic-update-slice_fusion.10
  228.7 3.1 slice_bitcast_fusion.4
  245.4 2.8 bitcast_dynamic-update-slice_fusion.4
  275.4 4.0 constant_dynamic-update-slice_fusion.4
  279.7 3.2 fusion.193
  284.1 3.4 constant_dynamic-update-slice_fusion.2
  287.8 5.8 %constant_dynamic-update-slice_fusion.1 = (bf16[8,18688]{1,0:T(8,128)(2,1)}, bf16[8,2048]{1,0:T(8,128)(2,1)S(1)}, f32[8,2048]{1,0:T(8,128)S(1)}, f32[8,2048]{1,0:T(8,128)}) fusion(bf16[8,18688]{1,0:T(8,128)(2,1)} %get-tuple-element.64, bf16[8,2152]{1,0:T(8,128)(2,1)S(1)} %concatenate.103, bf16[2152,2048]{1,0:T(8,128)(2,1)} %bitcast.287), kind=kOutput, calls=%fused_computation.180 | convolution fusion | flops 71581696 | bytes 9045632 | tf_op jit(solution)/shard_map/dot_general | solution.py:266
  295.5 3.9 all-to-all-start
  302.1 7.8 %all-to-all-done = bf16[32,8,256]{2,1,0:T(8,128)(2,1)S(1)} async-done(((bf16[32,8,256]{2,1,0:T(8,128)(2,1)}), bf16[32,8,256]{2,1,0:T(8,128)(2,1)S(1)}, u32[]{:S(2)}, u32[]{:S(2)}) %all-to-all-start) | async-done | bytes 131104 | tf_op jit(solution)/shard_map/all_to_all | solution.py:540
  309.9 8.4 %all-gather.8.cloned.1.call-done = bf16[2,256,2048]{2,1,0:T(8,128)(2,1)} async-done(((bf16[2,32,2048]{2,1,0:T(8,128)(2,1)}), bf16[2,256,2048]{2,1,0:T(8,128)(2,1)}) %all-gather.8.cloned.1.call-update) | async-done | bytes 2097168 | tf_op jit(solution)/shard_map/all_gather | solution.py:494
  327.3 3.3 all-to-all-start.1
  332.4 2.4 all-to-all-done.1
  337.6 6.2 %fusion.196 = f32[8,2152]{1,0:T(8,128)S(1)} fusion(bf16[8,2048]{1,0:T(8,128)(2,1)S(1)} %add_convert_fusion.3, bf16[2152,2048]{1,0:T(8,128)(2,1)} %bitcast.288), kind=kOutput, calls=%fused_computation.468 | convolution fusion | flops 70516736 | bytes 8916224 | tf_op jit(solution)/shard_map/dot_general | solution.py:270
  345.9 3.7 fusion.129
  350.0 3.9 fusion.198
  361.8 3.1 multiply_reduce_fusion.8
  375.8 2.3 multiply_reduce_fusion.3
  378.2 2.7 multiply_reduce_fusion
  381.0 3.9 bitcast_convert_fusion
  388.6 3.8 all-to-all-start.2
  398.0 3.4 fusion.5
  402.8 34.2 %all-to-all-done.2 = bf16[16,80,768]{2,1,0:T(8,128)(2,1)S(1)} async-done(((bf16[16,80,768]{2,1,0:T(8,128)(2,1)}), bf16[16,80,768]{2,1,0:T(8,128)(2,1)S(1)}, u32[]{:S(2)}, u32[]{:S(2)}) %all-to-all-start.2) | async-done | bytes 1966112 | tf_op jit(solution)/shard_map/all_to_all | solution.py:637
  445.3 3.4 slice.914
  448.7 4.3 copy.93
  453.0 3.2 slice.963
  456.2 4.3 copy.94
  460.5 3.6 pad_convert_fusion.refs_0_
  467.0 7.3 %shard_map.223 = f32[3456,128]{1,0:T(8,128)S(1)} custom-call(s32[13]{0:T(128)S(1)} %fusion.143.tab_ref, f32[9536,128]{1,0:T(8,128)} %pad_convert_fusion.refs_0_, bf16[128,11264]{1,0:T(8,128)(2,1)S(1)} %copy-done, f32[64,768]{1,0:T(8,128)S(1)} %pad.260.refs_2_), custom_call_target="tpu_custom_call" | custom-call | tf_op jit(solution)/shard_map/pallas_call | solution.py:425
  475.6 4.6 fusion.2
  483.4 23.3 %all-to-all-start.4 = ((f32[32,1,128]{2,1,0:T(1,128)}), f32[32,1,128]{2,1,0:T(1,128)S(1)}, u32[]{:S(2)}, u32[]{:S(2)}) async-start(f32[32,1,128]{2,1,0:T(1,128)} %broadcast_in_dim.178), calls=%async_computation.4 | async-start | bytes 32768 | tf_op jit(solution)/shard_map/all_to_all | solution.py:682
  506.8 7.0 %all-to-all-done.4 = f32[32,1,128]{2,1,0:T(1,128)S(1)} async-done(((f32[32,1,128]{2,1,0:T(1,128)}), f32[32,1,128]{2,1,0:T(1,128)S(1)}, u32[]{:S(2)}, u32[]{:S(2)}) %all-to-all-start.4) | async-done | bytes 16416 | tf_op jit(solution)/shard_map/all_to_all | solution.py:682
  515.1 3.7 all-to-all-start.3
  523.2 3.4 fusion.88
  526.6 3.1 copy.88
  529.7 5.9 %select_maximum_fusion.refs_1_ = f32[832,2304]{1,0:T(8,128)} fusion(f32[768,768]{1,0:T(8,128)} %copy.88, f32[768,768]{1,0:T(8,128)} %fusion.88, f32[768,768]{1,0:T(8,128)} %broadcast_multiply_fusion), kind=kLoop, calls=%fused_computation | loop fusion | flops 11501568 | bytes 14745600 | tf_op jit(solution)/shard_map/concatenate | solution.py:688
  537.0 2.4 multiply_add_fusion.2
  539.3 11.4 %all-to-all-done.3 = bf16[16,64,768]{2,1,0:T(8,128)(2,1)S(1)} async-done(((bf16[16,64,768]{2,1,0:T(8,128)(2,1)}), bf16[16,64,768]{2,1,0:T(8,128)(2,1)S(1)}, u32[]{:S(2)}, u32[]{:S(2)}) %all-to-all-start.3) | async-done | bytes 1572896 | tf_op jit(solution)/shard_map/all_to_all | solution.py:644
  553.7 8.0 %shard_map.224 = f32[3456,128]{1,0:T(8,128)S(1)} custom-call(s32[9]{0:T(128)S(1)} %fusion.147.tab_ref, f32[1033,768]{1,0:T(8,128)S(1)} %pad_convert_fusion.1.refs_0_, f32[832,2304]{1,0:T(8,128)} %select_maximum_fusion.refs_1_), custom_call_target="tpu_custom_call" | custom-call | tf_op jit(solution)/shard_map/pallas_call | solution.py:425
  561.8 4.3 multiply_add_fusion
  (434 shorter events, 143.0 us)
Async XLA Ops:
  7.2 187.2 %all-gather.10.cloned.1.call-start = ((), (), s32[]{:S(2)}) async-start(), calls=%async_computation.6 | async-start | bytes 31752192 | tf_op jit(solution)/shard_map/all_gather | solution.py:489
  15.8 23.6 %collective-permute-start = (bf16[3648,128]{1,0:T(8,128)(2,1)S(1)}, bf16[3648,128]{1,0:T(8,128)(2,1)S(1)}, u32[]{:S(2)}, u32[]{:S(2)}) collective-permute-start(bf16[3648,128]{1,0:T(8,128)(2,1)S(1)} %shard_map.221), channel_id=1, source_target_pairs={{0,4},{4,0},{8,12},{12,8},{16,20},{20,16},{24,28},{28,24},{1,5},{5... | collective-permute-start | bytes 2801672 | tf_op jit(solution)/shard_map/ppermute | solution.py:475
  41.0 277.3 %all-gather.8.cloned.1.call-start = ((), (), s32[]{:S(2)}) async-start(), calls=%async_computation.5 | async-start | bytes 2359296 | tf_op jit(solution)/shard_map/all_gather | solution.py:494
  41.7 213.4 %copy-start.42 = (s32[768]{0:T(1024)}, s32[768]{0:T(1024)S(1)}, u32[]{:S(2)}) copy-start(s32[768]{0:T(1024)S(1)} %add_select_fusion) | copy-start | bytes 9220
  41.7 28.5 %collective-permute-start.1 = (bf16[4,196,768]{2,0,1:T(4,128)(2,1)S(1)}, bf16[4,196,768]{2,0,1:T(4,128)(2,1)S(1)}, u32[]{:S(2)}, u32[]{:S(2)}) collective-permute-start(bf16[4,196,768]{2,0,1:T(4,128)(2,1)S(1)} %copy-done.28), channel_id=1, source_target_pairs={{0,4},{4,0},{8,12},{12,8},{16,20},{20,16},{24,28},{28,24},{1,5},{5... | collective-permute-start | bytes 3612680 | tf_op jit(solution)/shard_map/ppermute | solution.py:475
  43.5 227.8 %copy-start.46 = (pred[12,768]{1,0:T(8,128)(4,1)}, pred[12,768]{1,0:T(8,128)(4,1)S(1)}, u32[]{:S(2)}) copy-start(pred[12,768]{1,0:T(8,128)(4,1)S(1)} %iota_compare_fusion.1) | copy-start | bytes 27652
  44.3 25.3 %collective-permute-start.3 = (f32[4]{0:T(128)S(1)}, f32[4]{0:T(128)S(1)}, u32[]{:S(2)}, u32[]{:S(2)}) collective-permute-start(f32[4]{0:T(128)S(1)} %convert_element_type.352), channel_id=1, source_target_pairs={{0,4},{4,0},{8,12},{12,8},{16,20},{20,16},{24,28},{28,24},{1,5},{5... | collective-permute-start | bytes 56 | tf_op jit(solution)/shard_map/ppermute | solution.py:475
  222.3 10.8 %copy-start.1 = (bf16[34432,128]{1,0:T(8,128)(2,1)}, bf16[34432,128]{1,0:T(8,128)(2,1)S(1)}, u32[]{:S(2)}) copy-start(bf16[34432,128]{1,0:T(8,128)(2,1)S(1)} %get-tuple-element.95) | copy-start | bytes 26443780
  222.3 10.9 %copy-start.4 = (bf16[15104,128]{1,0:T(8,128)(2,1)}, bf16[15104,128]{1,0:T(8,128)(2,1)S(1)}, u32[]{:S(2)}) copy-start(bf16[15104,128]{1,0:T(8,128)(2,1)S(1)} %get-tuple-element.96) | copy-start | bytes 11599876
  234.1 25.9 %copy-start.6 = (f32[196,768]{1,0:T(8,128)}, f32[196,768]{1,0:T(8,128)S(1)}, u32[]{:S(2)}) copy-start(f32[196,768]{1,0:T(8,128)S(1)} %slice.872) | copy-start | bytes 1806340
  237.4 37.0 %copy-start.44 = (f32[768]{0:T(1024)}, f32[768]{0:T(1024)S(1)}, u32[]{:S(2)}) copy-start(f32[768]{0:T(1024)S(1)} %get-tuple-element.42) | copy-start | bytes 9220
  244.3 8.7 %copy-start.15 = (bf16[200,2304]{1,0:T(8,128)(2,1)S(1)}, bf16[200,2304]{1,0:T(8,128)(2,1)}, u32[]{:S(2)}) copy-start(bf16[200,2304]{1,0:T(8,128)(2,1)} %get-tuple-element.112) | copy-start | bytes 2764804
  244.3 8.7 %copy-start.16 = (bf16[192,2304]{1,0:T(8,128)(2,1)S(1)}, bf16[192,2304]{1,0:T(8,128)(2,1)}, u32[]{:S(2)}) copy-start(bf16[192,2304]{1,0:T(8,128)(2,1)} %slice_bitcast_fusion.2) | copy-start | bytes 2654212
  263.0 7.1 %collective-permute-start.5 = (f32[1,768]{1,0:T(1,128)}, f32[1,768]{1,0:T(1,128)S(1)}, u32[]{:S(2)}, u32[]{:S(2)}) collective-permute-start(f32[1,768]{1,0:T(1,128)} %get-tuple-element.88), channel_id=1, source_target_pairs={{0,4},{4,0},{8,12},{12,8},{16,20},{20,16},{24,28},{28,24},{1,5},{5... | collective-permute-start | bytes 9224 | tf_op jit(solution)/shard_map/ppermute | solution.py:475
  270.9 8.6 %copy-start.49 = (f32[768]{0:T(1024)}, f32[768]{0:T(1024)S(1)}, u32[]{:S(2)}) copy-start(f32[768]{0:T(1024)S(1)} %get-tuple-element.50) | copy-start | bytes 9220
  294.1 26.3 %copy-start.40 = (f32[8,256]{1,0:T(8,128)}, f32[8,256]{1,0:T(8,128)S(1)}, u32[]{:S(2)}) copy-start(f32[8,256]{1,0:T(8,128)S(1)} %get-tuple-element.188) | copy-start | bytes 24580
  294.7 23.6 %copy-start.80 = (f32[8]{0:T(128)}, f32[8]{0:T(128)S(1)}, u32[]{:S(2)}) copy-start(f32[8]{0:T(128)S(1)} %get-tuple-element.175) | copy-start | bytes 100
  295.5 14.3 %all-to-all-start = ((bf16[32,8,256]{2,1,0:T(8,128)(2,1)}), bf16[32,8,256]{2,1,0:T(8,128)(2,1)S(1)}, u32[]{:S(2)}, u32[]{:S(2)}) async-start(bf16[32,8,256]{2,1,0:T(8,128)(2,1)} %broadcast_in_dim.85), calls=%async_computation | async-start | bytes 262144 | tf_op jit(solution)/shard_map/all_to_all | solution.py:540
  300.2 30.4 %collective-permute-start.2 = (bf16[8,18688]{1,0:T(8,128)(2,1)}, bf16[8,18688]{1,0:T(8,128)(2,1)}, u32[]{:S(2)}, u32[]{:S(2)}) collective-permute-start(bf16[8,18688]{1,0:T(8,128)(2,1)} %constant_dynamic-update-slice_fusion), channel_id=1, source_target_pairs={{0,4},{4,0},{8,12},{12,8},{16,20},{20,16},{24,28},{28,24},{1,5},{5... | collective-permute-start | bytes 897032 | tf_op jit(solution)/shard_map/ppermute | solution.py:475
  309.9 12.3 %copy-start.33 = (bf16[4,1,32,256]{3,2,1,0:T(8,128)(2,1)}, bf16[4,1,32,256]{3,2,1,0:T(8,128)(2,1)S(1)}, u32[]{:S(2)}) copy-start(bf16[4,1,32,256]{3,2,1,0:T(8,128)(2,1)S(1)} %get-tuple-element.122) | copy-start | bytes 196612
  324.4 11.1 %copy-start.41 = (f32[8,256]{1,0:T(8,128)S(1)}, f32[8,256]{1,0:T(8,128)}, u32[]{:S(2)}) copy-start(f32[8,256]{1,0:T(8,128)} %copy-done.40) | copy-start | bytes 24580
  324.4 11.3 %copy-start.79 = (f32[8]{0:T(128)S(1)}, f32[8]{0:T(128)}, u32[]{:S(2)}) copy-start(f32[8]{0:T(128)} %get-tuple-element.174) | copy-start | bytes 100
  324.4 11.3 %copy-start.81 = (f32[8]{0:T(128)S(1)}, f32[8]{0:T(128)}, u32[]{:S(2)}) copy-start(f32[8]{0:T(128)} %copy-done.80) | copy-start | bytes 100
  324.4 13.1 %copy-start.35 = (f32[8,2048]{1,0:T(8,128)S(1)}, f32[8,2048]{1,0:T(8,128)}, u32[]{:S(2)}) copy-start(f32[8,2048]{1,0:T(8,128)} %get-tuple-element.186) | copy-start | bytes 196612
  324.4 13.1 %copy-start.72 = (pred[2048]{0:T(1024)(128)(4,1)S(1)}, pred[2048]{0:T(1024)(128)(4,1)}, u32[]{:S(2)}) copy-start(pred[2048]{0:T(1024)(128)(4,1)} %constant.259.clone.1) | copy-start | bytes 6148
  327.3 7.5 %all-to-all-start.1 = ((f32[4,35,128]{2,1,0:T(8,128)}), f32[4,35,128]{2,1,0:T(8,128)S(1)}, u32[]{:S(2)}, u32[]{:S(2)}) async-start(f32[4,35,128]{2,1,0:T(8,128)} %reshape.743), calls=%async_computation.1 | async-start | bytes 163840 | tf_op jit(solution)/shard_map/all_to_all | solution.py:574
  330.6 114.7 %all-gather.12.cloned.1.call-start = ((), (), s32[]{:S(2)}) async-start(), calls=%async_computation.7 | async-start | bytes 5083136 | tf_op jit(solution)/shard_map/all_gather | solution.py:529
  334.8 9.0 %copy-start.39 = (f32[35,128]{1,0:T(8,128)}, f32[35,128]{1,0:T(8,128)S(1)}, u32[]{:S(2)}) copy-start(f32[35,128]{1,0:T(8,128)S(1)} %reduce_sum.513) | copy-start | bytes 53764
  349.8 9.3 %copy-start.73 = (pred[768]{0:T(1024)(128)(4,1)S(1)}, pred[768]{0:T(1024)(128)(4,1)}, u32[]{:S(2)}) copy-start(pred[768]{0:T(1024)(128)(4,1)} %constant.268.clone.1) | copy-start | bytes 2308
  349.8 11.3 %copy-start.47 = (pred[12,768]{1,0:T(8,128)(4,1)S(1)}, pred[12,768]{1,0:T(8,128)(4,1)}, u32[]{:S(2)}) copy-start(pred[12,768]{1,0:T(8,128)(4,1)} %copy-done.46) | copy-start | bytes 27652
  355.5 20.3 %slice-start.1 = ((s8[4915200]{0:T(1024)(128)(4,1)}), s8[720896]{0:T(1024)(128)(4,1)S(1)}, s32[]{:S(2)}) async-start(s8[4915200]{0:T(1024)(128)(4,1)} %bitcast.289), calls=%async_computation.10 | async-start | bytes 1441792
  361.1 31.4 %collective-permute-start.4 = (bf16[8,11264]{1,0:T(8,128)(2,1)}, bf16[8,11264]{1,0:T(8,128)(2,1)}, u32[]{:S(2)}, u32[]{:S(2)}) collective-permute-start(bf16[8,11264]{1,0:T(8,128)(2,1)} %constant_dynamic-update-slice_fusion.7), channel_id=1, source_target_pairs={{0,4},{4,0},{8,12},{12,8},{16,20},{20,16},{24,28},{28,24},{1,5},{5... | collective-permute-start | bytes 540680 | tf_op jit(solution)/shard_map/ppermute | solution.py:475
  367.2 8.6 %slice-start.2 = ((s8[4915200]{0:T(1024)(128)(4,1)}), s8[4194304]{0:T(1024)(128)(4,1)S(1)}, s32[]{:S(2)}) async-start(s8[4915200]{0:T(1024)(128)(4,1)} %bitcast.289), calls=%async_computation.11 | async-start | bytes 8388608
  386.6 11.2 %copy-start.43 = (s32[768]{0:T(1024)S(1)}, s32[768]{0:T(1024)}, u32[]{:S(2)}) copy-start(s32[768]{0:T(1024)} %copy-done.42) | copy-start | bytes 9220
  386.6 11.4 %copy-start.23 = (f32[128,2048]{1,0:T(8,128)S(1)}, f32[128,2048]{1,0:T(8,128)}, u32[]{:S(2)}) copy-start(f32[128,2048]{1,0:T(8,128)} %copy-done.22) | copy-start | bytes 3145732
  386.6 11.3 %copy-start.34 = (bf16[4,1,32,256]{3,2,1,0:T(8,128)(2,1)S(1)}, bf16[4,1,32,256]{3,2,1,0:T(8,128)(2,1)}, u32[]{:S(2)}) copy-start(bf16[4,1,32,256]{3,2,1,0:T(8,128)(2,1)} %copy-done.33) | copy-start | bytes 196612
  386.6 11.3 %copy-start.82 = (f32[128]{0:T(128)S(1)}, f32[128]{0:T(128)}, u32[]{:S(2)}) copy-start(f32[128]{0:T(128)} %get-tuple-element.154) | copy-start | bytes 1540
  386.6 11.3 %copy-start.83 = (f32[128]{0:T(128)S(1)}, f32[128]{0:T(128)}, u32[]{:S(2)}) copy-start(f32[128]{0:T(128)} %get-tuple-element.155) | copy-start | bytes 1540
  388.6 48.4 %all-to-all-start.2 = ((bf16[16,80,768]{2,1,0:T(8,128)(2,1)}), bf16[16,80,768]{2,1,0:T(8,128)(2,1)S(1)}, u32[]{:S(2)}, u32[]{:S(2)}) async-start(bf16[16,80,768]{2,1,0:T(8,128)(2,1)} %maximum_maximum_fusion), calls=%async_computation.2 | async-start | bytes 3932160 | tf_op jit(solution)/shard_map/all_to_all | solution.py:637
  392.4 71.7 %all-gather.14.cloned.1.call-start = ((), (), s32[]{:S(2)}) async-start(), calls=%async_computation.8 | async-start | bytes 3063808 | tf_op jit(solution)/shard_map/all_gather | solution.py:529
  394.2 3.7 collective-permute-start.7
  437.3 4.6 collective-permute-start.6
  474.3 32.4 %copy-start.76 = (pred[64]{0:T(512)(128)(4,1)S(1)}, pred[64]{0:T(512)(128)(4,1)}, u32[]{:S(2)}) copy-start(pred[64]{0:T(512)(128)(4,1)} %constant.269.clone.1) | copy-start | bytes 196
  480.2 39.3 %copy-start.52 = (f32[2048]{0:T(1024)S(1)}, f32[2048]{0:T(1024)}, u32[]{:S(2)}) copy-start(f32[2048]{0:T(1024)} %param.22) | copy-start | bytes 24580
  480.2 39.3 %copy-start.53 = (f32[2048]{0:T(1024)S(1)}, f32[2048]{0:T(1024)}, u32[]{:S(2)}) copy-start(f32[2048]{0:T(1024)} %get-tuple-element.119) | copy-start | bytes 24580
  480.2 41.3 %copy-start.58 = (f32[768]{0:T(1024)S(1)}, f32[768]{0:T(1024)}, u32[]{:S(2)}) copy-start(f32[768]{0:T(1024)} %get-tuple-element.46) | copy-start | bytes 9220
  483.4 30.3 %all-to-all-start.4 = ((f32[32,1,128]{2,1,0:T(1,128)}), f32[32,1,128]{2,1,0:T(1,128)S(1)}, u32[]{:S(2)}, u32[]{:S(2)}) async-start(f32[32,1,128]{2,1,0:T(1,128)} %broadcast_in_dim.178), calls=%async_computation.4 | async-start | bytes 32768 | tf_op jit(solution)/shard_map/all_to_all | solution.py:682
  515.1 35.6 %all-to-all-start.3 = ((bf16[16,64,768]{2,1,0:T(8,128)(2,1)}), bf16[16,64,768]{2,1,0:T(8,128)(2,1)S(1)}, u32[]{:S(2)}, u32[]{:S(2)}) async-start(bf16[16,64,768]{2,1,0:T(8,128)(2,1)} %broadcast_in_dim.102), calls=%async_computation.3 | async-start | bytes 3145728 | tf_op jit(solution)/shard_map/all_to_all | solution.py:644
  (57 other events, 250.3 us)
Sparse Core Ops, SparseCore 0:
  41.1 153.2 all-gather.9
  266.7 51.5 all-gather.7
  333.6 53.3 all-gather.11
  395.8 61.8 all-gather.13

commit v3 on v2

--- a/solution.py
+++ b/solution.py
@@ -59,9 +59,12 @@
 ):
     PIECES.append((_offset, _rows, _cols))
     _offset += _rows * _cols
-FRONT = 24
-GRAD_FRONT = 8 * FRONT
+FRONT = 192
 CHUNK = 64
+TILE = 16
+TOKENS = 208
+HEADROWS = 16
+VMEM_LIMIT = 60 * 1024 * 1024
 
 
 def round_up(value, step):
@@ -98,15 +101,21 @@
             start = device * self.size
             entry = [start % LANES]
             target = 0
-            parts = shard_parts(start, start + self.size, SEGMENTS)
-            for index, row0, rows, line in parts:
+            for index, row0, rows, line in shard_parts(start, start + self.size, SEGMENTS):
                 width = SEGMENTS[index][2] // LANES
-                tiles = round_up(rows, 8) // 8
-                self.blocks[index].append((device, target, row0, tiles * 8))
-                entry += [WIDTHS.index(width), FRONT + line, tiles, target]
+                skew = row0 % 8
+                tiles = -(-(rows + skew) // 8)
+                self.blocks[index].append((device, target // TILE, row0 // 8, tiles))
+                entry += [
+                    WIDTHS.index(width),
+                    FRONT + line - skew * width,
+                    tiles // 2,
+                    tiles % 2,
+                    target // TILE,
+                ]
                 target += tiles * 8 * width
             longest = max(longest, target)
-            entry += [-1, 0, 0, 0] * (2 - len(parts))
+            entry += [-1, 0, 0, 0, 0] * (2 - len(entry) // 5)
             table.append(entry)
         self.buffer = round_up(longest, 16)
         self.lay_table = np.array(table, np.int32)
@@ -116,8 +125,12 @@
         self.odd_owner = any(
             device * self.size < edge and self.place(device)[1] for device in range(count)
         )
-        self.grad_scratch = GRAD_FRONT + self.lines + CHUNK * max(WIDTHS) + 16
-
+        self.grad_scratch = FRONT + self.lines + CHUNK * max(WIDTHS) + 16
+
+
+    def largest(self):
+        longest = max(8 * block[3] for blocks in self.blocks for block in blocks)
+        return max(len(blocks) for blocks in self.blocks), round_up(longest, LANES) + 2 * LANES
 
     def place(self, device):
         rep, grp = divmod(device, self.groups)
@@ -133,7 +146,7 @@
                     continue
                 skew = row0 % 8
                 line -= skew * (PIECES[index][2] // LANES)
-                entry += [index, GRAD_FRONT + line, -(-(rows + skew) // CHUNK), row0 - skew]
+                entry += [index, FRONT + line, -(-(rows + skew) // CHUNK), row0 - skew]
             table.append(entry)
         most = max(len(entry) for entry in table) // 4
         for device, entry in enumerate(table):
@@ -159,26 +172,34 @@
 
     lax.fori_loop(0, plan.lines // CHUNK, align, 0)
     for part in range(2):
-        kind, base, tiles, target = (tab_ref[1 + 4 * part + i] for i in range(4))
+        kind, base, pairs, odd, target = (tab_ref[1 + 5 * part + i] for i in range(5))
         for index, width in enumerate(WIDTHS):
 
             @pl.when(kind == index)
-            def _():
-                def move(tile, carry):
-                    row = base + tile * (8 * width)
-                    goal = target + tile * (8 * width)
-                    for pair in range(0, width, 2):
-                        two = jnp.concatenate(
-                            [
-                                line_ref[pl.ds(row + pair, 8, stride=width), :],
-                                line_ref[pl.ds(row + pair + 1, 8, stride=width), :],
-                            ],
-                            0,
-                        )
-                        out_ref[pl.ds(pl.multiple_of(goal + 8 * pair, 16), 16), :] = two.astype(BF16)
+            def _(width=width):
+                def move(step, carry):
+                    row = base + step * (TILE * width)
+                    goal = (target + step * width) * TILE
+                    for tile in range(width):
+                        both = line_ref[pl.ds(row + tile, TILE, stride=width), :]
+                        place = pl.multiple_of(goal + TILE * tile, TILE)
+                        out_ref[pl.ds(place, TILE), :] = both.astype(BF16)
                     return carry
 
-                lax.fori_loop(0, tiles, move, 0)
+                def last(step, carry):
+                    row = base + pairs * (TILE * width)
+                    goal = (target + pairs * width) * TILE
+                    for tile in range(0, width, 2):
+                        both = [
+                            line_ref[pl.ds(row + tile + side, 8, stride=width), :]
+                            for side in range(2)
+                        ]
+                        place = pl.multiple_of(goal + 8 * tile, TILE)
+                        out_ref[pl.ds(place, TILE), :] = jnp.concatenate(both, 0).astype(BF16)
+                    return carry
+
+                lax.fori_loop(0, pairs, move, 0)
+                lax.fori_loop(0, odd, last, 0)
 
 
 def lay_out(plan, table, flat):
@@ -197,69 +218,144 @@
     )(table, lines)
 
 
-def blocks_of(plan, index, first, count):
-    return [
-        (device, target, row0 - first, rows)
-        for device, target, row0, rows in plan.blocks[index]
-        if row0 < first + count and row0 + rows > first
-    ]
-
-
-MATRICES = (
-    (0, 0, PD + NTOK + 4),
-    (1, 0, D),
-    (2, 0, D),
-    (3, 0, D),
-    (4, 0, F),
-    (4, F, 2),
-    (5, 0, D),
-    (5, D, H),
-    (6, 0, H),
-)
-
-
-class Rows:
-    def __init__(self, plan, gathered, which):
-        index, first, self.count = MATRICES[which]
+class Shards:
+    def __init__(self, plan, gathered_ref, ref, sems, order):
+        self.plan, self.ref, self.sems, self.waited = plan, ref, sems, set()
+        self.copies = {}
+        for device in order:
+            place, side = plan.place(device)
+            copy = pltpu.make_async_copy(
+                gathered_ref.at[place, side], ref.at[device], sems.at[device]
+            )
+            copy.start()
+            self.copies[device] = copy
+
+    def wait(self, device):
+        if device in self.copies:
+            self.copies.pop(device).wait()
+
+    def finish(self):
+        for device in list(self.copies):
+            self.wait(device)
+
+    def blocks(self, index, first, count):
+        found = [
+            block
+            for block in self.plan.blocks[index]
+            if 8 * block[2] < first + count and 8 * (block[2] + block[3]) > first
+        ]
+        for block in found:
+            self.wait(block[0])
+        return found
+
+    def eight(self, index, tile, pair, side):
         width = SEGMENTS[index][2] // LANES
-        blocks = blocks_of(plan, index, first, self.count)
-        self.blocks = [block[2:] for block in blocks]
-        pieces = [
-            gathered[plan.place(device)][target : target + rows * width]
-            for device, target, _, rows in blocks
-        ]
-        tiles = jnp.concatenate(pieces, 0).reshape(-1, width, 8, LANES)
-        self.matrix = tiles.transpose(0, 2, 1, 3).reshape(-1, width * LANES)
-
-    def spread(self, values):
-        before = max(0, -min(row0 for row0, _ in self.blocks))
-        after = max(0, max(row0 + rows for row0, rows in self.blocks) - self.count)
-        padded = jnp.pad(values, ((0, 0), (before, after)))
-        return jnp.concatenate(
-            [padded[:, before + row0 : before + row0 + rows] for row0, rows in self.blocks], 1
+        total = None
+        for device, target, tile0, tiles in self.plan.blocks[index]:
+            own = tile - tile0
+            if not 0 <= own < tiles:
+                continue
+            if own < tiles // 2 * 2:
+                both = self.ref[device, target + own // 2 * width + 2 * pair + side]
+                half = own % 2
+            else:
+                both = self.ref[device, target + tiles // 2 * width + pair]
+                half = side
+            piece = both.astype(F32)[8 * half : 8 * half + 8]
+            total = piece if total is None else total + piece
+        return total
+
+    def assemble(self, index, out_ref):
+        width = SEGMENTS[index][2] // LANES
+        rows = out_ref.shape[0]
+        self.blocks(index, 0, rows)
+
+        def column(pair, carry):
+            for side in range(2):
+                lanes = pl.ds(pl.multiple_of(pair * 2 * LANES + side * LANES, LANES), LANES)
+                for group in range(rows // TILE):
+                    both = [
+                        self.eight(index, 2 * group + half, pair, side) for half in range(2)
+                    ]
+                    out_ref[TILE * group : TILE * (group + 1), lanes] = jnp.concatenate(
+                        both, 0
+                    ).astype(BF16)
+            return carry
+
+        lax.fori_loop(0, width // 2, column, 0)
+
+    def columns(self, index, block, pair):
+        width = SEGMENTS[index][2] // LANES
+        device, target, _, tiles = block
+        sides = []
+        for side in range(2):
+            pieces = [
+                self.ref[device, target + step * width + 2 * pair + side]
+                for step in range(tiles // 2)
+            ]
+            if tiles % 2:
+                both = self.ref[device, target + tiles // 2 * width + pair].astype(F32)
+                pieces.append(both[8 * side : 8 * side + 8].astype(BF16))
+            sides.append(jnp.concatenate(pieces, 0))
+        return jnp.concatenate(sides, 1)
+
+    def times(self, index, first, values, left_ref, out_ref):
+        views, count = values.shape
+        blocks = self.blocks(index, first, count)
+        top = max([first + count] + [8 * (tile0 + tiles) for _, _, tile0, tiles in blocks])
+        top = round_up(top, LANES) + LANES
+        parts = [values, jnp.zeros((views, top - first - count), F32)]
+        if first:
+            parts.insert(0, jnp.zeros((views, first), F32))
+        wide = jnp.concatenate(parts, 1)
+        for number, (_, _, tile0, tiles) in enumerate(blocks):
+            start = 8 * tile0 // LANES * LANES
+            turn = 8 * tile0 - start
+            piece = wide[:, start : start + round_up(turn + 8 * tiles, LANES)]
+            if turn:
+                piece = pltpu.roll(piece, piece.shape[1] - turn, 1)
+            left_ref[number, :, : 8 * tiles] = piece[:, : 8 * tiles]
+
+        def column(pair, carry):
+            total = jnp.zeros((views, 2 * LANES), F32)
+            for number, block in enumerate(blocks):
+                left = left_ref[number, :, : 8 * block[3]].astype(BF16)
+                total += product(left, self.columns(index, block, pair))
+            out_ref[:, pl.ds(pl.multiple_of(pair * 2 * LANES, LANES), 2 * LANES)] = total
+            return carry
+
+        lax.fori_loop(0, SEGMENTS[index][2] // LANES // 2, column, 0)
+
+
+    def back(self, index, first, count, values, grad_ref, left_ref, wide_ref):
+        views, cols = values.shape
+        grad_ref[:, :cols] = values
+        blocks = self.blocks(index, first, count)
+        top = max([first + count] + [8 * (tile0 + tiles) for _, _, tile0, tiles in blocks])
+        wide_ref[:, : round_up(top, LANES) + LANES] = jnp.zeros(
+            (views, round_up(top, LANES) + LANES), F32
         )
-
-    def times(self, values):
-        return product(self.spread(values), self.matrix)
-
-    def back(self, values):
-        wide = product_t(values, self.matrix)
-        total, place = 0.0, 0
-        for row0, rows in self.blocks:
-            low, high = max(0, row0), min(self.count, row0 + rows)
-            piece = wide[:, place + low - row0 : place + high - row0]
-            total = total + jnp.pad(piece, ((0, 0), (low, self.count - high)))
-            place += rows
-        return total
-
-    def folded(self):
-        total, place = 0.0, 0
-        for row0, rows in self.blocks:
-            low, high = max(0, row0), min(self.count, row0 + rows)
-            piece = self.matrix[place + low - row0 : place + high - row0]
-            total = total + jnp.pad(piece, ((low, self.count - high), (0, 0)))
-            place += rows
-        return total
+        for block in blocks:
+            _, _, tile0, tiles = block
+
+            def column(pair, total, block=block):
+                lanes = pl.ds(pl.multiple_of(pair * 2 * LANES, LANES), 2 * LANES)
+                left = grad_ref[:, lanes].astype(BF16)
+                return total + product_t(left, self.columns(index, block, pair))
+
+            total = lax.fori_loop(
+                0, cols // LANES // 2, column, jnp.zeros((views, 8 * tiles), F32)
+            )
+            start = 8 * tile0 // LANES * LANES
+            turn = 8 * tile0 - start
+            size = round_up(turn + 8 * tiles, LANES)
+            left_ref[0, :, :size] = jnp.zeros((views, size), F32)
+            left_ref[0, :, : 8 * tiles] = total
+            piece = left_ref[0, :, :size]
+            if turn:
+                piece = pltpu.roll(piece, turn, 1)
+            wide_ref[:, start : start + size] += piece
+        return wide_ref[:, first : first + count]
 
 
 def product(left, right):
@@ -272,12 +368,17 @@
     )
 
 
+def normal_share(values):
+    return 0.5 + 0.5 * lax.erf(values * 2**-0.5)
+
+
 def activate(values):
-    return jax.nn.gelu(values, approximate=False)
+    return values * normal_share(values)
 
 
 def gelu_back(values, grad):
-    return jax.vjp(activate, values)[1](grad)[0]
+    density = jnp.exp(-0.5 * values * values) * (2 * np.pi) ** -0.5
+    return grad * (normal_share(values) + values * density)
 
 
 def normalised(values):
@@ -296,84 +397,325 @@
 
 
 def head_mask():
-    return jnp.arange(HEADS)[:, None] == jnp.arange(D)[None, :] // HDIM
-
-
-def trunk_forward(patches, wide, qkv_w):
-    views = patches.shape[0]
-    position = wide[PD : PD + NTOK].astype(F32)
-    norms = wide[PD + NTOK :].astype(F32)
-    embedded = product(patches, wide[:PD])
-    unit, scale = normalised(embedded + position[1:])
-    normed = (unit * norms[0] + norms[1]).astype(BF16)
-    class_unit, class_scale = normalised(position[:1])
-    class_normed = (class_unit * norms[0] + norms[1]).astype(BF16)
-    query = product(class_normed, qkv_w[:, :D]).astype(BF16)
-    by_head = jnp.where(head_mask(), query, 0).astype(BF16)
-    looked = product_t(by_head, qkv_w[:, D : 2 * D]).astype(BF16)
+    shape = (HEADROWS, D)
+    return lax.broadcasted_iota(jnp.int32, shape, 0) == (
+        lax.broadcasted_iota(jnp.int32, shape, 1) // HDIM
+    )
+
+
+def token_norms(unit, norms, class_normed):
+    token = lax.broadcasted_iota(jnp.int32, (TOKENS, D), 0)
+    normed = unit * norms[0:1] + norms[1:2]
+    return jnp.where(
+        token < NPATCH, normed, jnp.where(token == NPATCH, class_normed, 0.0)
+    ).astype(BF16)
+
+
+def forward_kernel(
+    plan,
+    gathered_ref,
+    pixels_ref,
+    unit_ref,
+    scale_ref,
+    probs_ref,
+    mixed_ref,
+    looked_ref,
+    class_ref,
+    qkv_ref,
+    pack_ref,
+    hidden_ref,
+    one_ref,
+    two_ref,
+    bottle_ref,
+    middle_ref,
+    rows_ref,
+    shards_ref,
+    wide_ref,
+    place_ref,
+    left_ref,
+    sums_ref,
+    sems,
+):
+    shards = Shards(plan, gathered_ref, shards_ref, sems, range(plan.count))
+    views = pixels_ref.shape[0]
     temper = HDIM ** (-0.5)
-    scores = jnp.einsum("hd,vkd->vhk", looked, normed, preferred_element_type=F32) * temper
-    class_score = product_t(looked, class_normed)[None] * temper
-    top = jnp.maximum(jnp.max(scores, -1, keepdims=True), class_score)
-    total = jnp.sum(jnp.exp(scores - top), -1, keepdims=True) + jnp.exp(class_score - top)
-    row_top = top + jnp.log(total)
-    probs = jnp.exp(scores - row_top)
-    class_probs = jnp.exp(class_score - row_top)
-    mixed = jnp.einsum("vhk,vkd->vhd", probs.astype(BF16), normed, preferred_element_type=F32)
-    mixed = mixed + class_probs.astype(BF16).astype(F32) * class_normed.astype(F32)
-    mixed = mixed.astype(BF16)
-    valued = product(mixed.reshape(-1, D), qkv_w[:, 2 * D :]).reshape(views, HEADS, D)
-    attended = jnp.sum(jnp.where(head_mask(), valued, 0.0), 1).astype(BF16)
-    kept = (unit, scale, normed, class_unit, class_scale, class_normed, query, looked)
-    return position[0], attended, mixed, kept + (probs, class_probs)
-
-
-def trunk_backward(patches, wide, qkv_w, grad_att, grad_class, kept):
-    unit, scale, normed, class_unit, class_scale, class_normed, query, looked = kept[:8]
-    probs, class_probs = kept[8:]
-    views = patches.shape[0]
-    norms = wide[PD + NTOK :].astype(F32)
+    shards.assemble(0, wide_ref)
+    position = wide_ref[PD : PD + TOKENS].astype(F32)
+    place_ref[...] = pltpu.roll(position, TOKENS - 1, 0)
+    class_place = position[0:1]
+    norms = position[NTOK : NTOK + 4]
+    class_unit, class_scale = normalised(class_place)
+    class_normed = (class_unit * norms[0:1] + norms[1:2]).astype(BF16).astype(F32)
+    shards.assemble(1, qkv_ref)
+    mask = head_mask()
+    query = jnp.broadcast_to(class_normed, (HEADROWS, D)).astype(BF16)
+    query = product(query, qkv_ref[:, :D]).astype(BF16).astype(F32)
+    by_head = jnp.where(mask, query, 0.0).astype(BF16)
+    looked = product_t(by_head, qkv_ref[:, D : 2 * D]).astype(BF16)
+    looked_ref[...] = looked
+
+    def view(v, carry):
+        embedded = product(pixels_ref[v], wide_ref[:PD]) + place_ref[...]
+        unit, scale = normalised(embedded)
+        unit_ref[v] = unit
+        scale_ref[v] = jnp.broadcast_to(scale, (TOKENS, LANES))
+        normed = token_norms(unit, norms, class_normed)
+        scores = product_t(looked, normed) * temper
+        token = lax.broadcasted_iota(jnp.int32, scores.shape, 1)
+        scores = jnp.where(token < NTOK, scores, -1e30)
+        top = jnp.max(scores, -1, keepdims=True)
+        top = top + jnp.log(jnp.sum(jnp.exp(scores - top), -1, keepdims=True))
+        head = lax.broadcasted_iota(jnp.int32, scores.shape, 0)
+        probs = jnp.where(head < HEADS, jnp.exp(scores - top), 0.0)
+        probs_ref[v] = probs
+        mixed_ref[v] = product(probs.astype(BF16), normed).astype(BF16)
+        return carry
+
+    lax.fori_loop(0, views, view, 0)
+    mixed = mixed_ref[...].reshape(views * HEADROWS, D)
+    valued = product(mixed, qkv_ref[:, 2 * D :]).reshape(views, HEADROWS, D)
+    attended = jnp.sum(jnp.where(mask[None], valued, 0.0), 1).astype(BF16)
+    pack_ref[:, :D] = attended
+    shards.times(2, 0, attended.astype(F32), left_ref, sums_ref)
+    middle = class_place + sums_ref[...]
+    unit, scale = normalised(middle)
+    middle_ref[0], middle_ref[1] = unit, jnp.broadcast_to(scale, (views, D))
+    normed = (unit * norms[2:3] + norms[3:4]).astype(BF16)
+    pack_ref[:, D : 2 * D] = normed
+    shards.times(3, 0, normed.astype(F32), left_ref, hidden_ref)
+    act = activate(hidden_ref[...]).astype(BF16)
+    pack_ref[:, 2 * D : 2 * D + F] = act
+    shards.times(4, 0, act.astype(F32), left_ref, sums_ref)
+    unit, scale = normalised(middle + sums_ref[...])
+    middle_ref[2], middle_ref[3] = unit, jnp.broadcast_to(scale, (views, D))
+    final = jnp.concatenate(
+        [shards.eight(4, F // 8, tile // 2, tile % 2) for tile in range(D // LANES)], 1
+    )
+    cls = (unit * final[0:1] + final[1:2]).astype(BF16)
+    place = 2 * D + F
+    pack_ref[:, place : place + D] = cls
+    shards.times(5, 0, cls.astype(F32), left_ref, one_ref)
+    first = activate(one_ref[...]).astype(BF16)
+    pack_ref[:, place + D : place + D + H] = first
+    shards.times(5, D, first.astype(F32), left_ref, two_ref)
+    second = activate(two_ref[...]).astype(BF16)
+    pack_ref[:, place + D + H :] = second
+    shards.times(6, 0, second.astype(F32), left_ref, bottle_ref)
+    bottle = bottle_ref[...]
+    scale = lax.rsqrt(jnp.sum(bottle * bottle, -1, keepdims=True) + 1e-06)
+    rows_ref[...] = (bottle * scale).astype(BF16)
+    class_ref[...] = jnp.concatenate(
+        [
+            class_unit,
+            class_normed,
+            query[0:1],
+            jnp.broadcast_to(class_scale, (1, D)),
+            norms,
+            final,
+        ],
+        0,
+    )
+    shards.finish()
+
+
+def forward(plan, gathered, pixels):
+    views = pixels.shape[0]
+    shapes = [
+        ((views, TOKENS, D), F32),
+        ((views, TOKENS, LANES), F32),
+        ((views, HEADROWS, TOKENS), F32),
+        ((views, HEADROWS, D), BF16),
+        ((HEADROWS, D), BF16),
+        ((16, D), F32),
+        ((D, 3 * D), BF16),
+        ((views, 3 * D + F + 2 * H), BF16),
+        ((views, F), F32),
+        ((views, H), F32),
+        ((views, H), F32),
+        ((views, B), F32),
+        ((4, views, D), F32),
+        ((views, B), BF16),
+    ]
+    most, longest = plan.largest()
+    return pl.pallas_call(
+        functools.partial(forward_kernel, plan),
+        out_shape=[jax.ShapeDtypeStruct(shape, dtype) for shape, dtype in shapes],
+        in_specs=[
+            pl.BlockSpec(memory_space=pl.ANY),
+            pl.BlockSpec(memory_space=pltpu.VMEM),
+        ],
+        out_specs=[pl.BlockSpec(memory_space=pltpu.VMEM)] * len(shapes),
+        scratch_shapes=[
+            pltpu.VMEM((plan.count, plan.buffer // TILE, TILE, LANES), BF16),
+            pltpu.VMEM((round_up(PD + NTOK + 4, TILE), D), BF16),
+            pltpu.VMEM((TOKENS, D), F32),
+            pltpu.VMEM((most, views, longest), F32),
+            pltpu.VMEM((views, D), F32),
+            pltpu.SemaphoreType.DMA((plan.count,)),
+        ],
+        compiler_params=pltpu.CompilerParams(vmem_limit_bytes=VMEM_LIMIT),
+        cost_estimate=pl.CostEstimate(
+            flops=60 * 10**9, bytes_accessed=40 * 10**6, transcendentals=10**5
+        ),
+    )(gathered, pixels)
+
+
+def backward_kernel(
+    plan,
+    gathered_ref,
+    grad_ref,
+    unit_ref,
+    scale_ref,
+    probs_ref,
+    looked_ref,
+    class_ref,
+    qkv_ref,
+    hidden_ref,
+    one_ref,
+    two_ref,
+    bottle_ref,
+    middle_ref,
+    pack_ref,
+    token_ref,
+    place_ref,
+    extra_ref,
+    reach_ref,
+    shards_ref,
+    left_ref,
+    values_ref,
+    wide_ref,
+    back_ref,
+    mixed_ref,
+    rows_ref,
+    sems,
+):
+    shards = Shards(plan, gathered_ref, shards_ref, sems, reversed(range(plan.count)))
+    views = grad_ref.shape[0]
     temper = HDIM ** (-0.5)
-    spread = jnp.where(head_mask(), grad_att[:, None], 0).astype(BF16).reshape(-1, D)
-    back = product_t(spread, qkv_w[:, 2 * D :]).astype(BF16).reshape(views, HEADS, D)
-    grad_probs = jnp.einsum("vhd,vkd->vhk", back, normed, preferred_element_type=F32)
-    class_grad = jnp.sum(
-        back.astype(F32) * class_normed.astype(F32), -1, keepdims=True
-    )
-    delta = jnp.sum(probs * grad_probs, -1, keepdims=True) + class_probs * class_grad
-    grad_scores = (probs * (grad_probs - delta)).astype(BF16)
-    class_scores = (class_probs * (class_grad - delta)).astype(BF16)
-    reach = jnp.einsum("vhk,vkd->vhd", grad_scores, normed, preferred_element_type=F32)
-    reach = (reach + class_scores.astype(F32) * class_normed.astype(F32)) * temper
-    keyed = product(reach.astype(BF16).reshape(-1, D), qkv_w[:, D : 2 * D])
-    keyed = keyed.reshape(views, HEADS, D)
-    grad_query = jnp.sum(jnp.where(head_mask(), keyed, 0.0), 1).astype(BF16)
-    left = jnp.concatenate([grad_scores, probs.astype(BF16)], 1)
-    right = jnp.concatenate(
-        [jnp.broadcast_to((looked.astype(F32) * temper).astype(BF16), back.shape), back], 1
-    )
-    grad_normed = jnp.einsum("vhk,vhd->vkd", left, right, preferred_element_type=F32)
-    class_left = jnp.concatenate([class_scores, class_probs.astype(BF16)], 1).astype(F32)
-    class_row = jnp.sum(class_left * right.astype(F32), 1) + product_t(grad_query, qkv_w[:, :D])
-    gain = jnp.sum(grad_normed * unit, (0, 1)) + jnp.sum(class_row * class_unit, 0)
-    offset = jnp.sum(grad_normed, (0, 1)) + jnp.sum(class_row, 0)
-    grad_stream = norm_back(grad_normed, norms[0], unit, scale)
-    class_stream = norm_back(class_row, norms[0], class_unit, class_scale) + grad_class
-    grad_patch = lax.dot_general(
-        patches.reshape(-1, PD),
-        grad_stream.astype(BF16).reshape(-1, D),
-        (((0,), (0,)), ((), ())),
-        preferred_element_type=F32,
-    )
-    return (
-        grad_patch,
-        jnp.sum(class_stream, 0, keepdims=True),
-        jnp.sum(grad_stream, 0),
-        gain[None],
-        offset[None],
-        jnp.sum(grad_query.astype(F32), 0, keepdims=True),
-        jnp.sum(reach, 0),
-    )
+    work = (values_ref, left_ref, wide_ref)
+    mask = head_mask()
+    norms, final = class_ref[4:8], class_ref[8:10]
+    class_unit, class_normed, class_scale = (class_ref[row : row + 1] for row in (0, 1, 3))
+
+    grad_rows, bottle = grad_ref[...], bottle_ref[...]
+    scale = lax.rsqrt(jnp.sum(bottle * bottle, -1, keepdims=True) + 1e-06)
+    grad_bottle = (
+        grad_rows * scale - bottle * scale**3 * jnp.sum(grad_rows * bottle, -1, keepdims=True)
+    ).astype(BF16)
+    place = 2 * D + F
+    pack_ref[:, place : place + B] = grad_bottle
+    grad_two = shards.back(6, 0, H, grad_bottle.astype(F32), *work)
+    grad_two = gelu_back(two_ref[...], grad_two).astype(BF16)
+    pack_ref[:, place + B : place + B + H] = grad_two
+    grad_one = shards.back(5, D, H, grad_two.astype(F32), *work)
+    grad_one = gelu_back(one_ref[...], grad_one).astype(BF16)
+    pack_ref[:, place + B + H : place + B + 2 * H] = grad_one
+    grad_cls = shards.back(5, 0, D, grad_one.astype(F32), *work)
+    unit, scale = middle_ref[2], middle_ref[3]
+    pack_ref[:, place + B + 2 * H + D : place + B + 2 * H + 2 * D] = (grad_cls * unit).astype(BF16)
+    pack_ref[:, place + B + 2 * H + 2 * D :] = grad_cls.astype(BF16)
+    grad_stream = norm_back(grad_cls, final[0:1], unit, scale)
+    grad_branch = grad_stream.astype(BF16)
+    pack_ref[:, D + F : 2 * D + F] = grad_branch
+    grad_hidden = shards.back(4, 0, F, grad_branch.astype(F32), *work)
+    grad_hidden = gelu_back(hidden_ref[...], grad_hidden).astype(BF16)
+    pack_ref[:, D : D + F] = grad_hidden
+    grad_normed = shards.back(3, 0, D, grad_hidden.astype(F32), *work)
+    unit, scale = middle_ref[0], middle_ref[1]
+    gain_two = jnp.sum(grad_normed * unit, 0, keepdims=True)
+    shift_two = jnp.sum(grad_normed, 0, keepdims=True)
+    grad_middle = grad_stream + norm_back(grad_normed, norms[2:3], unit, scale)
+    grad_mixed = grad_middle.astype(BF16)
+    pack_ref[:, :D] = grad_mixed
+    grad_att = shards.back(2, 0, D, grad_mixed.astype(F32), *work).astype(BF16)
+    pack_ref[:, place + B + 2 * H : place + B + 2 * H + D] = grad_att
+    shards.finish()
+
+    spread = jnp.where(mask[None], grad_att.astype(F32)[:, None, :], 0.0).astype(BF16)
+    back = product_t(spread.reshape(views * HEADROWS, D), qkv_ref[:, 2 * D :])
+    back_ref[...] = back.astype(BF16).reshape(views, HEADROWS, D)
+    looked = (looked_ref[...].astype(F32) * temper).astype(BF16)
+    place_ref[...] = jnp.zeros((TOKENS, D), F32)
+    reach_ref[...] = jnp.zeros((HEADROWS, D), F32)
+    rows_ref[...] = jnp.zeros(rows_ref.shape, F32)
+
+    def view(v, carry):
+        unit = unit_ref[v]
+        scale = scale_ref[v][:, :1]
+        normed = token_norms(unit, norms, class_normed)
+        back = back_ref[v]
+        probs = probs_ref[v]
+        grad_probs = product_t(back, normed)
+        delta = jnp.sum(probs * grad_probs, -1, keepdims=True)
+        grad_scores = (probs * (grad_probs - delta)).astype(BF16)
+        reach = product(grad_scores, normed) * temper
+        mixed_ref[v] = reach.astype(BF16)
+        reach_ref[...] += reach
+        left = jnp.concatenate([grad_scores.astype(F32), probs.astype(BF16).astype(F32)], 0)
+        right = jnp.concatenate([looked, back], 0)
+        grad = product(left.T.astype(BF16), right)
+        row = lax.broadcasted_iota(jnp.int32, (8, D), 0)
+        rows_ref[0] += jnp.where(row == v, grad[NPATCH : NPATCH + 1], 0.0)
+        token = lax.broadcasted_iota(jnp.int32, (TOKENS, D), 0)
+        grad = jnp.where(token < NPATCH, grad, 0.0)
+        rows_ref[1, 0:1] += jnp.sum(grad * unit, 0, keepdims=True)
+        rows_ref[2, 0:1] += jnp.sum(grad, 0, keepdims=True)
+        stream = norm_back(grad, norms[0:1], unit, scale)
+        place_ref[...] += stream
+        token_ref[v] = stream.astype(BF16)
+        return carry
+
+    lax.fori_loop(0, views, view, 0)
+    keyed = product(mixed_ref[...].reshape(views * HEADROWS, D), qkv_ref[:, D : 2 * D])
+    keyed = jnp.where(mask[None], keyed.reshape(views, HEADROWS, D), 0.0)
+    grad_query = jnp.sum(keyed, 1).astype(BF16)
+    class_row = rows_ref[0][:views] + product_t(grad_query, qkv_ref[:, :D])
+    class_stream = norm_back(class_row, norms[0:1], class_unit, class_scale) + grad_middle
+    extra_ref[...] = jnp.concatenate(
+        [
+            jnp.sum(class_stream, 0, keepdims=True),
+            rows_ref[1, 0:1] + jnp.sum(class_row * class_unit, 0, keepdims=True),
+            rows_ref[2, 0:1] + jnp.sum(class_row, 0, keepdims=True),
+            gain_two,
+            shift_two,
+            jnp.sum(grad_query.astype(F32), 0, keepdims=True),
+            jnp.zeros((2, D), F32),
+        ],
+        0,
+    )
+
+
+def backward(plan, gathered, grad_rows, kept):
+    views = grad_rows.shape[0]
+    shapes = [
+        ((views, 5 * D + F + B + 2 * H), BF16),
+        ((views, TOKENS, D), BF16),
+        ((TOKENS, D), F32),
+        ((8, D), F32),
+        ((HEADROWS, D), F32),
+    ]
+    most, longest = plan.largest()
+    return pl.pallas_call(
+        functools.partial(backward_kernel, plan),
+        out_shape=[jax.ShapeDtypeStruct(shape, dtype) for shape, dtype in shapes],
+        in_specs=[pl.BlockSpec(memory_space=pl.ANY)]
+        + [pl.BlockSpec(memory_space=pltpu.VMEM)] * (1 + len(kept)),
+        out_specs=[pl.BlockSpec(memory_space=pltpu.VMEM)] * len(shapes),
+        scratch_shapes=[
+            pltpu.VMEM((plan.count, plan.buffer // TILE, TILE, LANES), BF16),
+            pltpu.VMEM((1, views, longest), F32),
+            pltpu.VMEM((views, F), F32),
+            pltpu.VMEM((views, F + 2 * LANES), F32),
+            pltpu.VMEM((views, HEADROWS, D), BF16),
+            pltpu.VMEM((views, HEADROWS, D), BF16),
+            pltpu.VMEM((3, 8, D), F32),
+            pltpu.SemaphoreType.DMA((plan.count,)),
+        ],
+        compiler_params=pltpu.CompilerParams(vmem_limit_bytes=VMEM_LIMIT),
+        cost_estimate=pl.CostEstimate(
+            flops=60 * 10**9, bytes_accessed=40 * 10**6, transcendentals=10**5
+        ),
+    )(gathered, grad_rows, *kept)
 
 
 def grad_kernel(plan, most, spans, tab_ref, *refs):
@@ -412,7 +754,7 @@
 
     def align(step, carry):
         start = pl.multiple_of(step * CHUNK, 8)
-        here = pltpu.roll(line_ref[pl.ds(pl.multiple_of(GRAD_FRONT + start, 8), CHUNK + 8), :], turn, 1)
+        here = pltpu.roll(line_ref[pl.ds(pl.multiple_of(FRONT + start, 8), CHUNK + 8), :], turn, 1)
         below = pltpu.roll(here, CHUNK + 7, 0)
         both = jnp.where(lane < LANES - shift, here, below)
         out_ref[pl.ds(start, CHUNK), :] = both[:CHUNK]
@@ -487,7 +829,9 @@
     patches, partner, given = lax.optimization_barrier((patches, partner, given))
     shards = jnp.stack([jnp.where(low, kept, given), jnp.where(low, given, kept)])
     gathered = lax.all_gather(shards, BOTH, axis=0, axis_index_groups=halves)
+    gathered = gathered.reshape(half, 2, -1, TILE, LANES)
     pixels = jnp.concatenate(in_order(patches), 0)
+    pixels = jnp.pad(pixels, ((0, 0), (0, TOKENS - NPATCH), (0, 0)))
     places = in_order(partner.astype(F32))
     tables = jnp.stack([protos, teacher_protos]).astype(BF16)
     tables, gathered = lax.optimization_barrier((tables, gathered))
@@ -500,29 +844,9 @@
     columns, column_scale = columns_of(tables[0])
     teacher_columns = columns_of(tables[1])[0]
 
-    wide = Rows(plan, gathered, 0).folded()
-    qkv_w = Rows(plan, gathered, 1).folded()
-    out_w, up_w, down_w = (Rows(plan, gathered, which) for which in (2, 3, 4))
-    final = Rows(plan, gathered, 5).folded().astype(F32)
-    head_one, head_two, head_three = (Rows(plan, gathered, which) for which in (6, 7, 8))
-    norms = wide[PD + NTOK :].astype(F32)
-
-    class_row, attended, mixed, trunk_kept = trunk_forward(pixels, wide, qkv_w)
-    middle = class_row + out_w.times(attended)
-    unit_two, scale_two = normalised(middle)
-    normed_two = (unit_two * norms[2] + norms[3]).astype(BF16)
-    hidden = up_w.times(normed_two)
-    act = activate(hidden).astype(BF16)
-    stream = middle + down_w.times(act)
-    unit_three, scale_three = normalised(stream)
-    cls = (unit_three * final[0] + final[1]).astype(BF16)
-    pre_one = head_one.times(cls)
-    first = activate(pre_one).astype(BF16)
-    pre_two = head_two.times(first)
-    second = activate(pre_two).astype(BF16)
-    bottle = head_three.times(second)
-    bottle_scale = lax.rsqrt(jnp.sum(bottle * bottle, -1, keepdims=True) + 1e-06)
-    rows = (bottle * bottle_scale).astype(BF16)
+    kept = forward(plan, gathered, pixels)
+    unit, scale, probs, mixed, looked, classes, qkv_w, ahead = kept[:8]
+    rows = kept[-1]
 
     def gather_rows(values):
         values = trade_low(values)
@@ -530,8 +854,9 @@
             half * views, -1
         )
 
-    ahead = [attended, normed_two, act, cls, first, second, mixed.reshape(views, -1)]
-    ahead = gather_rows(jnp.concatenate(ahead, 1))
+    ahead = gather_rows(
+        jnp.concatenate([ahead, mixed[:, :HEADS].reshape(views, -1)], 1)
+    )
 
     here = jnp.arange(views)
     source = jnp.concatenate([places[0], places[1] + own_views]).astype(jnp.int32)
@@ -594,37 +919,20 @@
         - protos.astype(BF16).astype(F32) * column_scale**3 * inner
     )
 
-    grad_bottle = (
-        grad_rows * bottle_scale
-        - bottle * bottle_scale**3 * jnp.sum(grad_rows * bottle, -1, keepdims=True)
-    ).astype(BF16)
-    grad_two = gelu_back(pre_two, head_three.back(grad_bottle)).astype(BF16)
-    grad_one = gelu_back(pre_one, head_two.back(grad_two)).astype(BF16)
-    grad_cls = head_one.back(grad_one)
-    grad_stream = norm_back(grad_cls, final[0], unit_three, scale_three)
-    grad_branch = grad_stream.astype(BF16)
-    grad_hidden = gelu_back(hidden, down_w.back(grad_branch)).astype(BF16)
-    grad_normed = up_w.back(grad_hidden)
-    grad_middle = grad_stream + norm_back(grad_normed, norms[2], unit_two, scale_two)
-    grad_mixed = grad_middle.astype(BF16)
-    grad_att = out_w.back(grad_mixed).astype(BF16)
-    behind = [grad_mixed, grad_hidden, grad_branch, grad_bottle, grad_two, grad_one, grad_att]
-    behind += [(grad_cls * unit_three).astype(BF16), grad_cls.astype(BF16)]
-    cols_all = gather_rows(jnp.concatenate(behind, 1))
-
-    pieces = trunk_backward(pixels, wide, qkv_w, grad_att, grad_middle, trunk_kept)
-    partial = jnp.concatenate(
-        pieces[:5]
-        + (
-            jnp.sum(grad_normed * unit_two, 0, keepdims=True),
-            jnp.sum(grad_normed, 0, keepdims=True),
-        ),
-        0,
-    )
+    saved = (unit, scale, probs, looked, classes, qkv_w) + tuple(kept[8:13])
+    behind, tokens, grad_place, extra, reach = backward(plan, gathered, grad_rows, saved)
+    cols_all = gather_rows(behind)
+    grad_patch = lax.dot_general(
+        pixels.reshape(-1, PD),
+        tokens.reshape(-1, D),
+        (((0,), (0,)), ((), ())),
+        preferred_element_type=F32,
+    )
+    partial = jnp.concatenate([grad_patch, extra[:1], grad_place[:NPATCH], extra[1:5]], 0)
+    shared = jnp.concatenate([extra[5:6], reach[:HEADS]], 0)
     base = PD + NTOK + 4
     depth = -(-base // half)
     partial = jnp.pad(partial, ((0, half * depth - base), (0, 0))).reshape(half, depth, D)
-    shared = jnp.concatenate(pieces[5:], 0)
     slots = round_up(depth + shared.shape[0], 8)
     partial = jnp.concatenate(
         [
@@ -670,8 +978,9 @@
         "vhd,vhc->dhc", mixed_rows, values_att, preferred_element_type=F32
     ).reshape(D, D)
 
-    class_normed, query = (trade_low(trunk_kept[which].astype(F32)) for which in (5, 6))
-    by_head = jnp.where(head_mask(), query, 0.0)
+    classes = trade_low(classes)
+    class_normed, query = classes[1:2], classes[2:3]
+    by_head = jnp.where(head_mask()[:HEADS], query, 0.0)
     sum_query, reach = shared[0], shared[1:]
     outer = jnp.sum(class_normed * class_normed) * jnp.sum(sum_query * sum_query) + jnp.sum(
         jnp.sum(reach * reach, 1) * jnp.sum(by_head * by_head, 1)

time: 585 us -> 517 us (0.88); the launches traced: 574 us -> 512 us
  Pallas kernels: 26.3 us -> 111 us
  local copies, waits for them, and re-layouts: 96.1 us -> 30 us
  matrix products: 71.1 us -> 18.4 us
  other arithmetic: 69.9 us -> 46.3 us
    pallas_call x0 -> x2, Pallas kernels: none -> 85.4 us  [the longest x1 56.7 us: backward(): pl.pallas_call(functools.partial(backward_kernel, plan), out_shape=[jax.S...]
    unnamed x198 -> x47, local copies, waits for them, and re-layouts: 47.9 us -> 10.7 us
    dot_general x16 -> x1, matrix products: 32.8 us -> 4.09 us  [per_device(): lax.dot_general(pixels.reshape(-1, PD), tokens.reshape(-1, D), (((0,), (0...]
    dot_general x13 -> x3, matrix products: 25.8 us -> 3.45 us  [product(): return jnp.dot(left, right, preferred_element_type=F32)]
    slice x47 -> x5, local copies, waits for them, and re-layouts: 16.2 us -> 2.67 us  [the longest x2 1.55 us: per_device(): shared = jnp.concatenate([extra[5:6], reach[:HEADS]], 0)]
    concatenate x10 -> x1, local copies, waits for them, and re-layouts: 9.27 us -> 0.67 us  [per_device(): jnp.concatenate([ahead, mixed[:, :HEADS].reshape(views, -1)], 1)]
    reduce_sum x13 -> x0, other arithmetic: 7.59 us -> none  [the longest x1 2.71 us: trunk_backward(): jnp.sum(grad_normed * unit, (0, 1)) + jnp.sum(class_row * class_unit, 0)]
    ppermute x8 -> x7, starting transfers between devices: 12.2 us -> 10.4 us  [trade(): return lax.ppermute(values, 'rep', swap)]
  transfers between devices with their start and end apart: 17 -> 16, of which waited for: 11 -> 12; matrix products, arithmetic and copies ran while one was open for 25% -> 13% of each run, Pallas kernels for 1% -> 18%
where the time goes in v3:
time: 517 us; the launch traced here: 512 us
  waiting for transfers between devices  236 us (46%)
  Pallas kernels  111 us (21%)
  starting transfers between devices  49.8 us (10%)
  other arithmetic  46.3 us (9%)
  local copies, waits for them, and re-layouts  30 us (6%)
  between operations  20.8 us (4%)
  matrix products  18.4 us (4%)
    all_gather x1, waiting for transfers between devices, per_device(): gathered = lax.all_gather(shards, BOTH, axis=0, axis_index_groups=halves)  121 us
    pallas_call x1, Pallas kernels, backward(): pl.pallas_call(functools.partial(backward_kernel, plan), out_shape=[jax.S...  56.7 us
    ppermute x7, waiting for transfers between devices, trade(): return lax.ppermute(values, 'rep', swap)  44.6 us
    all_to_all x1, waiting for transfers between devices, per_device(): partial = lax.all_to_all(partial, BOTH, 0, 0, axis_index_groups=halves)  32.5 us
    pallas_call x1, Pallas kernels, forward(): pl.pallas_call(functools.partial(forward_kernel, plan), out_shape=[jax.Sh...  28.7 us
    all_to_all x1, starting transfers between devices, per_device(): lax.all_to_all(jnp.broadcast_to(squares.reshape(1, 1, 1), (count, 1, LANE...  23.6 us
    pallas_call x2, Pallas kernels, flat_gradient(): pl.pallas_call(functools.partial(grad_kernel, plan, table.shape[1] // 4,...  15.2 us
    all_to_all x1, waiting for transfers between devices, per_device(): lax.all_to_all(jnp.broadcast_to(summed[None], (half, slots, D)), BOTH, 0,...  12.3 us
  transfers between devices with their start and end apart: 16, of which 12 were waited for; matrix products, arithmetic and copies ran while one was open for 13% of the time, Pallas kernels for 18%

profile of v3, /device:TPU:0, one launch (start us, length us, event | category | flops | bytes accessed | tf_op | source)
XLA Modules:
  0.0 512.4 jit_solution(12548815807552510835)
XLA Ops:
  7.2 2.2 broadcast_select_fusion.3
  10.3 5.4 %shard_map.222 = bf16[3648,128]{1,0:T(8,128)(2,1)S(1)} custom-call(s32[11]{0:T(128)S(1)} %fusion.58.tab_ref, f32[3464,128]{1,0:T(8,128)S(1)} %pad_bitcast_fusion.x_ref), custom_call_target="tpu_custom_call" | custom-call | tf_op jit(solution)/shard_map/pallas_call | solution.py:208
  15.7 2.9 collective-permute-start
  18.7 5.4 %shard_map.221 = bf16[3648,128]{1,0:T(8,128)(2,1)S(1)} custom-call(s32[11]{0:T(128)S(1)} %fusion.58.tab_ref, f32[3464,128]{1,0:T(8,128)S(1)} %pad_bitcast_fusion.1.x_ref), custom_call_target="tpu_custom_call" | custom-call | tf_op jit(solution)/shard_map/pallas_call | solution.py:208
  24.0 15.3 %collective-permute-done = bf16[3648,128]{1,0:T(8,128)(2,1)S(1)} collective-permute-done((bf16[3648,128]{1,0:T(8,128)(2,1)S(1)}, bf16[3648,128]{1,0:T(8,128)(2,1)S(1)}, u32[]{:S(2)}, u32[]{:S(2)}) %collective-permute-start) | collective-permute-done | bytes 933920 | tf_op jit(solution)/shard_map/ppermute | solution.py:817
  41.2 1.7 collective-permute-start.1
  44.1 24.9 %collective-permute-done.3 = f32[4]{0:T(128)S(1)} collective-permute-done((f32[4]{0:T(128)S(1)}, f32[4]{0:T(128)S(1)}, u32[]{:S(2)}, u32[]{:S(2)}) %collective-permute-start.3) | collective-permute-done | bytes 48 | tf_op jit(solution)/shard_map/ppermute | solution.py:817
  69.1 2.0 broadcast_select_fusion.1
  71.1 1.7 fusion.6.pixels_ref
  72.8 121.2 %all-gather.10.cloned.1.call-done = bf16[32,3648,128]{2,1,0:T(8,128)(2,1)} async-done(((bf16[2,3648,128]{2,1,0:T(8,128)(2,1)}), bf16[32,3648,128]{2,1,0:T(8,128)(2,1)}) %all-gather.10.cloned.1.call-update) | async-done | bytes 29884432 | tf_op jit(solution)/shard_map/all_gather | solution.py:831
  194.1 28.7 %shard_map.223 = (f32[8,208,768]{2,1,0:T(8,128)}, f32[8,208,128]{2,1,0:T(8,128)}, f32[8,16,208]{2,1,0:T(8,128)}, bf16[8,16,768]{2,1,0:T(8,128)(2,1)}, bf16[16,76...) custom-call(bf16[16,2,228,16,128]{4,3,2,1,0:T(8,128)(2,1)} %bitcast., ...), custom_call_target="tpu_custom_call" | custom-call | flops 60000002048 | bytes 40000000 | tf_op jit(solution)/shard_map/pallas_call | solution.py:540
  224.3 4.6 all-to-all-start
  232.1 1.8 collective-permute-start.2
  233.9 5.6 %all-to-all-done = bf16[32,8,256]{2,1,0:T(8,128)(2,1)S(1)} async-done(((bf16[32,8,256]{2,1,0:T(8,128)(2,1)}), bf16[32,8,256]{2,1,0:T(8,128)(2,1)S(1)}, u32[]{:S(2)}, u32[]{:S(2)}) %all-to-all-start) | async-done | bytes 131104 | tf_op jit(solution)/shard_map/all_to_all | solution.py:865
  239.5 10.1 %all-gather.8.cloned.1.call-done = bf16[2,256,2048]{2,1,0:T(8,128)(2,1)} async-done(((bf16[2,32,2048]{2,1,0:T(8,128)(2,1)}), bf16[2,256,2048]{2,1,0:T(8,128)(2,1)}) %all-gather.8.cloned.1.call-update) | async-done | bytes 2097168 | tf_op jit(solution)/shard_map/all_gather | solution.py:838
  249.6 2.1 convert_element_type.76
  253.0 2.2 exponential_reduce_fusion
  258.2 3.5 all-to-all-start.1
  261.7 1.7 broadcast_select_fusion.4
  263.5 2.4 all-to-all-done.1
  267.3 56.7 %shard_map.224 = (bf16[8,11264]{1,0:T(8,128)(2,1)}, bf16[8,208,768]{2,1,0:T(8,128)(2,1)}, f32[208,768]{1,0:T(8,128)}, f32[8,768]{1,0:T(8,128)}, f32[16,768]{1,0:T(8,128)}) custom-call(bf16[16,2,228,16,128]{4,3,2,1,0:T(8,128)(2,1)} %bitcast.111, f32[8,256]{1,0:T(8,128)} %fusion.54.grad_ref, f32[8,208,768]{2,1,0:T(8,128)} %get-tuple-element.43.unit_ref, ...), custom_call_target="tpu_custom_call" | custom-call | flops 60000002048 | bytes 40000000 | tf_op jit(solution)/shard_map/pallas_call | solution.py:698
  327.5 4.1 bitcast_convert_fusion
  332.3 1.9 maximum_maximum_fusion
  334.2 3.9 all-to-all-start.2
  342.6 2.0 collective-permute-done.5
  345.4 3.4 fusion.10
  350.1 32.5 %all-to-all-done.2 = bf16[16,80,768]{2,1,0:T(8,128)(2,1)S(1)} async-done(((bf16[16,80,768]{2,1,0:T(8,128)(2,1)}), bf16[16,80,768]{2,1,0:T(8,128)(2,1)S(1)}, u32[]{:S(2)}, u32[]{:S(2)}) %all-to-all-start.2) | async-done | bytes 1966112 | tf_op jit(solution)/shard_map/all_to_all | solution.py:945
  382.9 2.1 collective-permute-start.6
  385.7 1.9 collective-permute-done.6
  390.9 1.7 slice-done
  392.6 2.5 copy.86
  395.1 1.7 slice-done.1
  396.8 2.6 copy.85
  399.4 3.9 pad_convert_fusion.refs_0_
  404.5 3.0 fusion.7
  409.9 1.8 copy-done
  411.7 7.2 %shard_map.225 = f32[3456,128]{1,0:T(8,128)S(1)} custom-call(s32[13]{0:T(128)S(1)} %fusion.57.tab_ref, f32[9536,128]{1,0:T(8,128)} %pad_convert_fusion.refs_0_, bf16[128,11264]{1,0:T(8,128)(2,1)S(1)} %copy-done, f32[64,768]{1,0:T(8,128)S(1)} %pad.45.refs_2_), custom_call_target="tpu_custom_call" | custom-call | tf_op jit(solution)/shard_map/pallas_call | solution.py:767
  421.9 23.6 %all-to-all-start.4 = ((f32[32,1,128]{2,1,0:T(1,128)}), f32[32,1,128]{2,1,0:T(1,128)S(1)}, u32[]{:S(2)}, u32[]{:S(2)}) async-start(f32[32,1,128]{2,1,0:T(1,128)} %broadcast_in_dim.69), calls=%async_computation.4 | async-start | bytes 32768 | tf_op jit(solution)/shard_map/all_to_all | solution.py:991
  445.6 7.0 %all-to-all-done.4 = f32[32,1,128]{2,1,0:T(1,128)S(1)} async-done(((f32[32,1,128]{2,1,0:T(1,128)}), f32[32,1,128]{2,1,0:T(1,128)S(1)}, u32[]{:S(2)}, u32[]{:S(2)}) %all-to-all-start.4) | async-done | bytes 16416 | tf_op jit(solution)/shard_map/all_to_all | solution.py:991
  453.9 3.7 all-to-all-start.3
  459.5 1.6 broadcast_multiply_fusion
  461.1 3.5 fusion.40
  464.6 3.0 copy.80
  467.6 5.9 %select_maximum_fusion.refs_1_ = f32[832,2304]{1,0:T(8,128)} fusion(f32[768,768]{1,0:T(8,128)} %copy.80, f32[768,768]{1,0:T(8,128)} %fusion.40, f32[768,768]{1,0:T(8,128)} %broadcast_multiply_fusion), kind=kLoop, calls=%fused_computation | loop fusion | flops 11501568 | bytes 14745600 | tf_op jit(solution)/shard_map/concatenate | solution.py:997
  474.9 2.4 multiply_add_fusion.2
  477.2 12.3 %all-to-all-done.3 = bf16[16,64,768]{2,1,0:T(8,128)(2,1)S(1)} async-done(((bf16[16,64,768]{2,1,0:T(8,128)(2,1)}), bf16[16,64,768]{2,1,0:T(8,128)(2,1)S(1)}, u32[]{:S(2)}, u32[]{:S(2)}) %all-to-all-start.3) | async-done | bytes 1572896 | tf_op jit(solution)/shard_map/all_to_all | solution.py:952
  492.5 8.0 %shard_map.226 = f32[3456,128]{1,0:T(8,128)S(1)} custom-call(s32[9]{0:T(128)S(1)} %fusion.61.tab_ref, f32[1033,768]{1,0:T(8,128)S(1)} %pad_convert_fusion.1.refs_0_, f32[832,2304]{1,0:T(8,128)} %select_maximum_fusion.refs_1_), custom_call_target="tpu_custom_call" | custom-call | tf_op jit(solution)/shard_map/pallas_call | solution.py:767
  500.6 4.2 multiply_add_fusion
  (140 shorter events, 38.4 us)
Async XLA Ops:
  7.2 186.9 %all-gather.10.cloned.1.call-start = ((), (), s32[]{:S(2)}) async-start(), calls=%async_computation.6 | async-start | bytes 31752192 | tf_op jit(solution)/shard_map/all_gather | solution.py:831
  15.7 23.6 %collective-permute-start = (bf16[3648,128]{1,0:T(8,128)(2,1)S(1)}, bf16[3648,128]{1,0:T(8,128)(2,1)S(1)}, u32[]{:S(2)}, u32[]{:S(2)}) collective-permute-start(bf16[3648,128]{1,0:T(8,128)(2,1)S(1)} %shard_map.222), channel_id=1, source_target_pairs={{0,4},{4,0},{8,12},{12,8},{16,20},{20,16},{24,28},{28,24},{1,5},{5... | collective-permute-start | bytes 2801672 | tf_op jit(solution)/shard_map/ppermute | solution.py:817
  39.5 1.7 copy-start.10
  39.5 3.5 copy-start.5
  39.6 3.5 copy-start.11
  41.0 2.8 copy-start.18
  41.0 208.6 %all-gather.8.cloned.1.call-start = ((), (), s32[]{:S(2)}) async-start(), calls=%async_computation.5 | async-start | bytes 2359296 | tf_op jit(solution)/shard_map/all_gather | solution.py:838
  41.2 27.9 %collective-permute-start.1 = (bf16[4,196,768]{2,0,1:T(4,128)(2,1)S(1)}, bf16[4,196,768]{2,0,1:T(4,128)(2,1)}, u32[]{:S(2)}, u32[]{:S(2)}) collective-permute-start(bf16[4,196,768]{2,0,1:T(4,128)(2,1)S(1)} %copy-done.10), channel_id=1, source_target_pairs={{0,4},{4,0},{8,12},{12,8},{16,20},{20,16},{24,28},{28,24},{1,5},{5... | collective-permute-start | bytes 3612680 | tf_op jit(solution)/shard_map/ppermute | solution.py:817
  43.8 25.2 %collective-permute-start.3 = (f32[4]{0:T(128)S(1)}, f32[4]{0:T(128)S(1)}, u32[]{:S(2)}, u32[]{:S(2)}) collective-permute-start(f32[4]{0:T(128)S(1)} %convert_element_type.73), channel_id=1, source_target_pairs={{0,4},{4,0},{8,12},{12,8},{16,20},{20,16},{24,28},{28,24},{1,5},{5... | collective-permute-start | bytes 56 | tf_op jit(solution)/shard_map/ppermute | solution.py:817
  224.3 15.2 %all-to-all-start = ((bf16[32,8,256]{2,1,0:T(8,128)(2,1)}), bf16[32,8,256]{2,1,0:T(8,128)(2,1)S(1)}, u32[]{:S(2)}, u32[]{:S(2)}) async-start(bf16[32,8,256]{2,1,0:T(8,128)(2,1)} %broadcast_in_dim.28), calls=%async_computation | async-start | bytes 262144 | tf_op jit(solution)/shard_map/all_to_all | solution.py:865
  232.1 29.6 %collective-permute-start.2 = (bf16[8,18688]{1,0:T(8,128)(2,1)}, bf16[8,18688]{1,0:T(8,128)(2,1)}, u32[]{:S(2)}, u32[]{:S(2)}) collective-permute-start(bf16[8,18688]{1,0:T(8,128)(2,1)} %constant_dynamic-update-slice_fusion), channel_id=1, source_target_pairs={{0,4},{4,0},{8,12},{12,8},{16,20},{20,16},{24,28},{28,24},{1,5},{5... | collective-permute-start | bytes 897032 | tf_op jit(solution)/shard_map/ppermute | solution.py:817
  251.7 4.6 copy-start.1
  252.1 1.0 copy-start.13
  255.3 1.0 copy-start.8
  258.2 7.7 %all-to-all-start.1 = ((f32[4,35,128]{2,1,0:T(8,128)}), f32[4,35,128]{2,1,0:T(8,128)S(1)}, u32[]{:S(2)}, u32[]{:S(2)}) async-start(f32[4,35,128]{2,1,0:T(8,128)} %reshape.172), calls=%async_computation.1 | async-start | bytes 163840 | tf_op jit(solution)/shard_map/all_to_all | solution.py:899
  261.7 129.2 %all-gather.12.cloned.1.call-start = ((), (), s32[]{:S(2)}) async-start(), calls=%async_computation.7 | async-start | bytes 5083136 | tf_op jit(solution)/shard_map/all_gather | solution.py:853
  332.2 6.5 %collective-permute-start.4 = (bf16[8,11264]{1,0:T(8,128)(2,1)}, bf16[8,11264]{1,0:T(8,128)(2,1)}, u32[]{:S(2)}, u32[]{:S(2)}) collective-permute-start(bf16[8,11264]{1,0:T(8,128)(2,1)} %get-tuple-element.54), channel_id=1, source_target_pairs={{0,4},{4,0},{8,12},{12,8},{16,20},{20,16},{24,28},{28,24},{1,5},{5... | collective-permute-start | bytes 540680 | tf_op jit(solution)/shard_map/ppermute | solution.py:817
  334.2 6.2 %copy-start.12 = (f32[16,768]{1,0:T(8,128)S(1)}, f32[16,768]{1,0:T(8,128)}, u32[]{:S(2)}) copy-start(f32[16,768]{1,0:T(8,128)} %get-tuple-element.47.class_ref) | copy-start | bytes 147460
  334.2 11.1 %copy-start.9 = (f32[128,2048]{1,0:T(8,128)S(1)}, f32[128,2048]{1,0:T(8,128)}, u32[]{:S(2)}) copy-start(f32[128,2048]{1,0:T(8,128)} %copy-done.8) | copy-start | bytes 3145732
  334.2 11.1 %copy-start.19 = (f32[128]{0:T(128)S(1)}, f32[128]{0:T(128)}, u32[]{:S(2)}) copy-start(f32[128]{0:T(128)} %get-tuple-element.86) | copy-start | bytes 1540
  334.2 11.1 %copy-start.20 = (f32[128]{0:T(128)S(1)}, f32[128]{0:T(128)}, u32[]{:S(2)}) copy-start(f32[128]{0:T(128)} %get-tuple-element.87) | copy-start | bytes 1540
  334.2 48.4 %all-to-all-start.2 = ((bf16[16,80,768]{2,1,0:T(8,128)(2,1)}), bf16[16,80,768]{2,1,0:T(8,128)(2,1)S(1)}, u32[]{:S(2)}, u32[]{:S(2)}) async-start(bf16[16,80,768]{2,1,0:T(8,128)(2,1)} %maximum_maximum_fusion), calls=%async_computation.2 | async-start | bytes 3932160 | tf_op jit(solution)/shard_map/all_to_all | solution.py:945
  338.1 65.2 %all-gather.14.cloned.1.call-start = ((), (), s32[]{:S(2)}) async-start(), calls=%async_computation.8 | async-start | bytes 3063808 | tf_op jit(solution)/shard_map/all_gather | solution.py:853
  340.4 4.2 collective-permute-start.5
  345.3 3.4 copy-start.16
  382.9 4.6 collective-permute-start.6
  390.9 1.7 slice-start
  395.1 1.7 slice-start.1
  399.4 5.0 copy-start.2
  409.9 1.8 copy-start
  411.7 33.8 %copy-start.17 = (pred[64]{0:T(512)(128)(4,1)S(1)}, pred[64]{0:T(512)(128)(4,1)}, u32[]{:S(2)}) copy-start(pred[64]{0:T(512)(128)(4,1)} %constant.126.clone.1) | copy-start | bytes 196
  421.9 30.7 %all-to-all-start.4 = ((f32[32,1,128]{2,1,0:T(1,128)}), f32[32,1,128]{2,1,0:T(1,128)S(1)}, u32[]{:S(2)}, u32[]{:S(2)}) async-start(f32[32,1,128]{2,1,0:T(1,128)} %broadcast_in_dim.69), calls=%async_computation.4 | async-start | bytes 32768 | tf_op jit(solution)/shard_map/all_to_all | solution.py:991
  445.6 12.7 %copy-start.14 = (f32[2048]{0:T(1024)S(1)}, f32[2048]{0:T(1024)}, u32[]{:S(2)}) copy-start(f32[2048]{0:T(1024)} %param.22) | copy-start | bytes 24580
  445.6 12.7 %copy-start.15 = (f32[2048]{0:T(1024)S(1)}, f32[2048]{0:T(1024)}, u32[]{:S(2)}) copy-start(f32[2048]{0:T(1024)} %get-tuple-element.82) | copy-start | bytes 24580
  453.9 35.6 %all-to-all-start.3 = ((bf16[16,64,768]{2,1,0:T(8,128)(2,1)}), bf16[16,64,768]{2,1,0:T(8,128)(2,1)S(1)}, u32[]{:S(2)}, u32[]{:S(2)}) async-start(bf16[16,64,768]{2,1,0:T(8,128)(2,1)} %broadcast_in_dim.65), calls=%async_computation.3 | async-start | bytes 3145728 | tf_op jit(solution)/shard_map/all_to_all | solution.py:952
  492.5 8.1 %copy-start.3 = (f32[441096]{0:T(1024)S(1)}, f32[441096]{0:T(1024)}, u32[]{:S(2)}) copy-start(f32[441096]{0:T(1024)} %param.17) | copy-start | bytes 5293156
  492.5 8.1 %copy-start.4 = (f32[441096]{0:T(1024)S(1)}, f32[441096]{0:T(1024)}, u32[]{:S(2)}) copy-start(f32[441096]{0:T(1024)} %param.14) | copy-start | bytes 5293156
  492.5 8.1 %copy-start.6 = (f32[441096]{0:T(1024)S(1)}, f32[441096]{0:T(1024)}, u32[]{:S(2)}) copy-start(f32[441096]{0:T(1024)} %param.15) | copy-start | bytes 5293156
  492.5 8.1 %copy-start.7 = (f32[441096]{0:T(1024)S(1)}, f32[441096]{0:T(1024)}, u32[]{:S(2)}) copy-start(f32[441096]{0:T(1024)} %param.16) | copy-start | bytes 5293156
Sparse Core Ops, SparseCore 0:
  41.1 152.8 all-gather.9
  196.8 52.7 all-gather.7
  264.7 53.2 all-gather.11
  341.5 61.8 all-gather.13

commit v4 on v3

--- a/solution.py
+++ b/solution.py
@@ -60,7 +60,12 @@
     PIECES.append((_offset, _rows, _cols))
     _offset += _rows * _cols
 FRONT = 192
-CHUNK = 64
+CHUNK = 128
+SET = 288
+SHARED = 32
+STEPS = 64
+AHEAD = 3 * D + F + 2 * H
+BEHIND = 5 * D + F + B + 2 * H
 TILE = 16
 TOKENS = 208
 HEADROWS = 16
@@ -92,7 +97,7 @@
         count = reps * groups
         self.count, self.groups = count, groups
         self.size = PFLAT // count
-        self.lines = round_up(-(-self.size // LANES) + 1, CHUNK)
+        self.lines = round_up(-(-self.size // LANES) + 1, STEPS)
         self.scratch = FRONT + self.lines + 8 * max(WIDTHS) + 16
         table = []
         self.blocks = [[] for _ in SEGMENTS]
@@ -119,12 +124,12 @@
             table.append(entry)
         self.buffer = round_up(longest, 16)
         self.lay_table = np.array(table, np.int32)
-        self.grad_table = self.tabulate(lambda index: index > 1)
-        self.late_table = self.tabulate(lambda index: index < 2)
         edge = SEGMENTS[0][1] * SEGMENTS[0][2]
-        self.odd_owner = any(
-            device * self.size < edge and self.place(device)[1] for device in range(count)
-        )
+        owners = [device for device in range(count) if device * self.size < edge]
+        self.odd_owner = any(self.place(device)[1] for device in owners)
+        self.all_sets = len(owners) > 2
+        self.grad_table = self.tabulate(lambda index: index)
+        self.late_table = self.tabulate(lambda index: index < 2, self.wide_row)
         self.grad_scratch = FRONT + self.lines + CHUNK * max(WIDTHS) + 16
 
 
@@ -136,7 +141,7 @@
         rep, grp = divmod(device, self.groups)
         return rep // 2 * self.groups + grp, rep % 2
 
-    def tabulate(self, chosen):
+    def tabulate(self, chosen, rows_of=lambda device, index, row0: row0):
         table = []
         for device in range(self.count):
             start = device * self.size
@@ -146,7 +151,8 @@
                     continue
                 skew = row0 % 8
                 line -= skew * (PIECES[index][2] // LANES)
-                entry += [index, FRONT + line, -(-(rows + skew) // CHUNK), row0 - skew]
+                chunks = -(-(rows + skew) // CHUNK)
+                entry += [index, FRONT + line, chunks, rows_of(device, index, row0 - skew)]
             table.append(entry)
         most = max(len(entry) for entry in table) // 4
         for device, entry in enumerate(table):
@@ -154,23 +160,33 @@
             entry.insert(0, device * self.size % LANES)
         return np.array(table, np.int32)
 
+    def wide_row(self, device, index, row0):
+        if index:
+            return row0
+        late = row0 >= 2 * SET - 8
+        if not self.all_sets:
+            if late != device % 2:
+                raise ValueError("owner")
+            return row0 - (2 * SET - 8) * late
+        return row0 + 8 * late
+
 
 def lay_kernel(plan, tab_ref, x_ref, out_ref, line_ref):
     shift = tab_ref[0]
-    lane = lax.broadcasted_iota(jnp.int32, (CHUNK + 8, LANES), 1)
+    lane = lax.broadcasted_iota(jnp.int32, (STEPS + 8, LANES), 1)
     line_ref[pl.ds(0, FRONT), :] = jnp.zeros((FRONT, LANES), F32)
     tail = plan.scratch - FRONT - plan.lines
     line_ref[pl.ds(FRONT + plan.lines, tail), :] = jnp.zeros((tail, LANES), F32)
 
     def align(step, carry):
-        base = pl.multiple_of(step * CHUNK, 8)
-        here = pltpu.roll(x_ref[pl.ds(base, CHUNK + 8), :], shift, 1)
+        base = pl.multiple_of(step * STEPS, 8)
+        here = pltpu.roll(x_ref[pl.ds(base, STEPS + 8), :], shift, 1)
         above = pltpu.roll(here, 1, 0)
         both = jnp.where(lane >= shift, here, above)
-        line_ref[pl.ds(pl.multiple_of(FRONT + base, 8), CHUNK), :] = both[8:]
+        line_ref[pl.ds(pl.multiple_of(FRONT + base, 8), STEPS), :] = both[8:]
         return carry
 
-    lax.fori_loop(0, plan.lines // CHUNK, align, 0)
+    lax.fori_loop(0, plan.lines // STEPS, align, 0)
     for part in range(2):
         kind, base, pairs, odd, target = (tab_ref[1 + 5 * part + i] for i in range(5))
         for index, width in enumerate(WIDTHS):
@@ -335,23 +351,24 @@
         wide_ref[:, : round_up(top, LANES) + LANES] = jnp.zeros(
             (views, round_up(top, LANES) + LANES), F32
         )
-        for block in blocks:
-            _, _, tile0, tiles = block
-
-            def column(pair, total, block=block):
-                lanes = pl.ds(pl.multiple_of(pair * 2 * LANES, LANES), 2 * LANES)
-                left = grad_ref[:, lanes].astype(BF16)
-                return total + product_t(left, self.columns(index, block, pair))
-
-            total = lax.fori_loop(
-                0, cols // LANES // 2, column, jnp.zeros((views, 8 * tiles), F32)
-            )
+        for number, (_, _, _, tiles) in enumerate(blocks):
+            size = round_up(8 * tiles, LANES) + LANES
+            left_ref[number, :, :size] = jnp.zeros((views, size), F32)
+
+        def column(pair, carry):
+            lanes = pl.ds(pl.multiple_of(pair * 2 * LANES, LANES), 2 * LANES)
+            left = grad_ref[:, lanes].astype(BF16)
+            for number, block in enumerate(blocks):
+                size = 8 * block[3]
+                left_ref[number, :, :size] += product_t(left, self.columns(index, block, pair))
+            return carry
+
+        lax.fori_loop(0, cols // LANES // 2, column, 0)
+        for number, (_, _, tile0, tiles) in enumerate(blocks):
             start = 8 * tile0 // LANES * LANES
             turn = 8 * tile0 - start
             size = round_up(turn + 8 * tiles, LANES)
-            left_ref[0, :, :size] = jnp.zeros((views, size), F32)
-            left_ref[0, :, : 8 * tiles] = total
-            piece = left_ref[0, :, :size]
+            piece = left_ref[number, :, :size]
             if turn:
                 piece = pltpu.roll(piece, turn, 1)
             wide_ref[:, start : start + size] += piece
@@ -560,42 +577,28 @@
     )(gathered, pixels)
 
 
-def backward_kernel(
+def rows_back_kernel(
     plan,
     gathered_ref,
     grad_ref,
-    unit_ref,
-    scale_ref,
-    probs_ref,
-    looked_ref,
     class_ref,
-    qkv_ref,
     hidden_ref,
     one_ref,
     two_ref,
     bottle_ref,
     middle_ref,
     pack_ref,
-    token_ref,
-    place_ref,
+    stream_ref,
     extra_ref,
-    reach_ref,
     shards_ref,
     left_ref,
     values_ref,
     wide_ref,
-    back_ref,
-    mixed_ref,
-    rows_ref,
     sems,
 ):
     shards = Shards(plan, gathered_ref, shards_ref, sems, reversed(range(plan.count)))
-    views = grad_ref.shape[0]
-    temper = HDIM ** (-0.5)
     work = (values_ref, left_ref, wide_ref)
-    mask = head_mask()
     norms, final = class_ref[4:8], class_ref[8:10]
-    class_unit, class_normed, class_scale = (class_ref[row : row + 1] for row in (0, 1, 3))
 
     grad_rows, bottle = grad_ref[...], bottle_ref[...]
     scale = lax.rsqrt(jnp.sum(bottle * bottle, -1, keepdims=True) + 1e-06)
@@ -622,157 +625,360 @@
     pack_ref[:, D : D + F] = grad_hidden
     grad_normed = shards.back(3, 0, D, grad_hidden.astype(F32), *work)
     unit, scale = middle_ref[0], middle_ref[1]
-    gain_two = jnp.sum(grad_normed * unit, 0, keepdims=True)
-    shift_two = jnp.sum(grad_normed, 0, keepdims=True)
+    extra_ref[...] = jnp.concatenate(
+        [
+            jnp.sum(grad_normed * unit, 0, keepdims=True),
+            jnp.sum(grad_normed, 0, keepdims=True),
+            jnp.zeros((6, D), F32),
+        ],
+        0,
+    )
     grad_middle = grad_stream + norm_back(grad_normed, norms[2:3], unit, scale)
+    stream_ref[...] = grad_middle
     grad_mixed = grad_middle.astype(BF16)
     pack_ref[:, :D] = grad_mixed
     grad_att = shards.back(2, 0, D, grad_mixed.astype(F32), *work).astype(BF16)
     pack_ref[:, place + B + 2 * H : place + B + 2 * H + D] = grad_att
     shards.finish()
 
-    spread = jnp.where(mask[None], grad_att.astype(F32)[:, None, :], 0.0).astype(BF16)
-    back = product_t(spread.reshape(views * HEADROWS, D), qkv_ref[:, 2 * D :])
-    back_ref[...] = back.astype(BF16).reshape(views, HEADROWS, D)
-    looked = (looked_ref[...].astype(F32) * temper).astype(BF16)
-    place_ref[...] = jnp.zeros((TOKENS, D), F32)
-    reach_ref[...] = jnp.zeros((HEADROWS, D), F32)
-    rows_ref[...] = jnp.zeros(rows_ref.shape, F32)
-
-    def view(v, carry):
-        unit = unit_ref[v]
-        scale = scale_ref[v][:, :1]
-        normed = token_norms(unit, norms, class_normed)
-        back = back_ref[v]
-        probs = probs_ref[v]
-        grad_probs = product_t(back, normed)
-        delta = jnp.sum(probs * grad_probs, -1, keepdims=True)
-        grad_scores = (probs * (grad_probs - delta)).astype(BF16)
-        reach = product(grad_scores, normed) * temper
-        mixed_ref[v] = reach.astype(BF16)
-        reach_ref[...] += reach
-        left = jnp.concatenate([grad_scores.astype(F32), probs.astype(BF16).astype(F32)], 0)
-        right = jnp.concatenate([looked, back], 0)
-        grad = product(left.T.astype(BF16), right)
-        row = lax.broadcasted_iota(jnp.int32, (8, D), 0)
-        rows_ref[0] += jnp.where(row == v, grad[NPATCH : NPATCH + 1], 0.0)
-        token = lax.broadcasted_iota(jnp.int32, (TOKENS, D), 0)
-        grad = jnp.where(token < NPATCH, grad, 0.0)
-        rows_ref[1, 0:1] += jnp.sum(grad * unit, 0, keepdims=True)
-        rows_ref[2, 0:1] += jnp.sum(grad, 0, keepdims=True)
-        stream = norm_back(grad, norms[0:1], unit, scale)
-        place_ref[...] += stream
-        token_ref[v] = stream.astype(BF16)
-        return carry
-
-    lax.fori_loop(0, views, view, 0)
-    keyed = product(mixed_ref[...].reshape(views * HEADROWS, D), qkv_ref[:, D : 2 * D])
-    keyed = jnp.where(mask[None], keyed.reshape(views, HEADROWS, D), 0.0)
-    grad_query = jnp.sum(keyed, 1).astype(BF16)
-    class_row = rows_ref[0][:views] + product_t(grad_query, qkv_ref[:, :D])
-    class_stream = norm_back(class_row, norms[0:1], class_unit, class_scale) + grad_middle
-    extra_ref[...] = jnp.concatenate(
-        [
-            jnp.sum(class_stream, 0, keepdims=True),
-            rows_ref[1, 0:1] + jnp.sum(class_row * class_unit, 0, keepdims=True),
-            rows_ref[2, 0:1] + jnp.sum(class_row, 0, keepdims=True),
-            gain_two,
-            shift_two,
-            jnp.sum(grad_query.astype(F32), 0, keepdims=True),
-            jnp.zeros((2, D), F32),
-        ],
-        0,
-    )
-
-
-def backward(plan, gathered, grad_rows, kept):
+
+def rows_back(plan, gathered, grad_rows, kept):
     views = grad_rows.shape[0]
-    shapes = [
-        ((views, 5 * D + F + B + 2 * H), BF16),
-        ((views, TOKENS, D), BF16),
-        ((TOKENS, D), F32),
-        ((8, D), F32),
-        ((HEADROWS, D), F32),
-    ]
+    shapes = [((views, 5 * D + F + B + 2 * H), BF16), ((views, D), F32), ((8, D), F32)]
     most, longest = plan.largest()
     return pl.pallas_call(
-        functools.partial(backward_kernel, plan),
+        functools.partial(rows_back_kernel, plan),
         out_shape=[jax.ShapeDtypeStruct(shape, dtype) for shape, dtype in shapes],
         in_specs=[pl.BlockSpec(memory_space=pl.ANY)]
         + [pl.BlockSpec(memory_space=pltpu.VMEM)] * (1 + len(kept)),
         out_specs=[pl.BlockSpec(memory_space=pltpu.VMEM)] * len(shapes),
         scratch_shapes=[
             pltpu.VMEM((plan.count, plan.buffer // TILE, TILE, LANES), BF16),
-            pltpu.VMEM((1, views, longest), F32),
+            pltpu.VMEM((most, views, longest), F32),
             pltpu.VMEM((views, F), F32),
             pltpu.VMEM((views, F + 2 * LANES), F32),
-            pltpu.VMEM((views, HEADROWS, D), BF16),
-            pltpu.VMEM((views, HEADROWS, D), BF16),
-            pltpu.VMEM((3, 8, D), F32),
             pltpu.SemaphoreType.DMA((plan.count,)),
         ],
         compiler_params=pltpu.CompilerParams(vmem_limit_bytes=VMEM_LIMIT),
         cost_estimate=pl.CostEstimate(
-            flops=60 * 10**9, bytes_accessed=40 * 10**6, transcendentals=10**5
+            flops=30 * 10**9, bytes_accessed=30 * 10**6, transcendentals=10**5
         ),
     )(gathered, grad_rows, *kept)
 
 
-def grad_kernel(plan, most, spans, tab_ref, *refs):
-    refs, out_ref, line_ref = refs[:-2], refs[-2], refs[-1]
+def tokens_back_kernel(
+    odd_ref,
+    behind_ref,
+    stream_ref,
+    ends_ref,
+    unit_ref,
+    scale_ref,
+    probs_ref,
+    looked_ref,
+    class_ref,
+    qkv_ref,
+    pixels_ref,
+    kept_ref,
+    sent_ref,
+    patch_ref,
+    place_ref,
+    reach_ref,
+    back_ref,
+    mixed_ref,
+    rows_ref,
+):
+    v = pl.program_id(0)
+    views = stream_ref.shape[0]
+    temper = HDIM ** (-0.5)
+    norms = class_ref[4:8]
+    class_unit, class_normed, class_scale = (class_ref[row : row + 1] for row in (0, 1, 3))
+
+    @pl.when(v == 0)
+    def _():
+        place = 2 * D + F + B + 2 * H
+        grad_att = behind_ref[:, place : place + D].astype(F32)
+        spread = jnp.where(head_mask()[None], grad_att[:, None, :], 0.0).astype(BF16)
+        back = product_t(spread.reshape(views * HEADROWS, D), qkv_ref[:, 2 * D :])
+        back_ref[...] = back.astype(BF16).reshape(views, HEADROWS, D)
+        patch_ref[...] = jnp.zeros(patch_ref.shape, F32)
+        place_ref[...] = jnp.zeros(place_ref.shape, F32)
+        reach_ref[...] = jnp.zeros(reach_ref.shape, F32)
+        rows_ref[...] = jnp.zeros(rows_ref.shape, F32)
+
+    unit = unit_ref[0]
+    scale = scale_ref[0][:, :1]
+    normed = token_norms(unit, norms, class_normed)
+    back = back_ref[v]
+    probs = probs_ref[0]
+    grad_probs = product_t(back, normed)
+    delta = jnp.sum(probs * grad_probs, -1, keepdims=True)
+    grad_scores = (probs * (grad_probs - delta)).astype(BF16)
+    reach = product(grad_scores, normed) * temper
+    mixed_ref[v] = reach.astype(BF16)
+    reach_ref[...] += reach
+    left = jnp.concatenate([grad_scores.astype(F32), probs.astype(BF16).astype(F32)], 0)
+    looked = (looked_ref[...].astype(F32) * temper).astype(BF16)
+    grad = product(left.T.astype(BF16), jnp.concatenate([looked, back], 0))
+    row = lax.broadcasted_iota(jnp.int32, (8, D), 0)
+    rows_ref[0] += jnp.where(row == v, grad[NPATCH : NPATCH + 1], 0.0)
+    token = lax.broadcasted_iota(jnp.int32, (TOKENS, D), 0)
+    grad = jnp.where(token < NPATCH, grad, 0.0)
+    rows_ref[1, 0:1] += jnp.sum(grad * unit, 0, keepdims=True)
+    rows_ref[2, 0:1] += jnp.sum(grad, 0, keepdims=True)
+    stream = norm_back(grad, norms[0:1], unit, scale)
+    place_ref[...] += stream
+    patch_ref[...] += product(pixels_ref[0], stream.astype(BF16))
+
+    @pl.when(v == views - 1)
+    def _():
+        keyed = product(mixed_ref[...].reshape(views * HEADROWS, D), qkv_ref[:, D : 2 * D])
+        keyed = jnp.where(head_mask()[None], keyed.reshape(views, HEADROWS, D), 0.0)
+        grad_query = jnp.sum(keyed, 1).astype(BF16)
+        class_row = rows_ref[0][:views] + product_t(grad_query, qkv_ref[:, :D])
+        class_stream = norm_back(class_row, norms[0:1], class_unit, class_scale)
+        class_stream = class_stream + stream_ref[...]
+        ends = [
+            (0, jnp.sum(class_stream, 0, keepdims=True)),
+            (NTOK, rows_ref[1, 0:1] + jnp.sum(class_row * class_unit, 0, keepdims=True)),
+            (NTOK + 1, rows_ref[2, 0:1] + jnp.sum(class_row, 0, keepdims=True)),
+            (NTOK + 2, ends_ref[0:1]),
+            (NTOK + 3, ends_ref[1:2]),
+        ]
+        tail = pltpu.roll(place_ref[...], 1, 0)
+        for row, value in ends:
+            tail = jnp.where(token == row, value, tail)
+        upper = 2 * SET - 8
+        rest = jnp.zeros((2 * SET - (PD - upper) - TOKENS, D), F32)
+        query_row = lax.broadcasted_iota(jnp.int32, (SHARED - HEADROWS, D), 0) == 0
+        total = jnp.sum(grad_query.astype(F32), 0, keepdims=True)
+        shared = jnp.concatenate([reach_ref[...], jnp.where(query_row, total, 0.0)], 0)
+        kept_ref[2 * SET :] = shared
+        sent_ref[2 * SET :] = shared.astype(BF16)
+        last = jnp.concatenate([patch_ref[upper:], tail, rest], 0)
+
+        @pl.when(odd_ref[0] == 0)
+        def _():
+            kept_ref[: 2 * SET] = patch_ref[: 2 * SET]
+            sent_ref[: 2 * SET] = last.astype(BF16)
+
+        @pl.when(odd_ref[0] != 0)
+        def _():
+            kept_ref[: 2 * SET] = last
+            sent_ref[: 2 * SET] = patch_ref[: 2 * SET].astype(BF16)
+
+
+def tokens_back(odd, behind, grad_middle, ends, kept, pixels):
+    views = grad_middle.shape[0]
+
+    def whole(values):
+        return pl.BlockSpec(values.shape, lambda v: (0,) * values.ndim)
+
+    def by_view(values):
+        return pl.BlockSpec((1,) + values.shape[1:], lambda v: (v,) + (0,) * (values.ndim - 1))
+
+    unit, scale, probs, looked, classes, qkv_w = kept
+    shape = (2 * SET + SHARED, D)
+    return pl.pallas_call(
+        tokens_back_kernel,
+        grid=(views,),
+        out_shape=[jax.ShapeDtypeStruct(shape, F32), jax.ShapeDtypeStruct(shape, BF16)],
+        in_specs=[
+            pl.BlockSpec(memory_space=pltpu.SMEM),
+            whole(behind),
+            whole(grad_middle),
+            whole(ends),
+            by_view(unit),
+            by_view(scale),
+            by_view(probs),
+            whole(looked),
+            whole(classes),
+            whole(qkv_w),
+            by_view(pixels),
+        ],
+        out_specs=[pl.BlockSpec(shape, lambda v: (0, 0))] * 2,
+        scratch_shapes=[
+            pltpu.VMEM((PD, D), F32),
+            pltpu.VMEM((TOKENS, D), F32),
+            pltpu.VMEM((HEADROWS, D), F32),
+            pltpu.VMEM((views, HEADROWS, D), BF16),
+            pltpu.VMEM((views, HEADROWS, D), BF16),
+            pltpu.VMEM((3, 8, D), F32),
+        ],
+        compiler_params=pltpu.CompilerParams(vmem_limit_bytes=40 * 1024 * 1024),
+        cost_estimate=pl.CostEstimate(
+            flops=15 * 10**9, bytes_accessed=15 * 10**6, transcendentals=10**5
+        ),
+    )(odd, behind, grad_middle, ends, unit, scale, probs, looked, classes, qkv_w, pixels)
+
+
+SPANS = {
+    2: (0, 0),
+    3: (D, D),
+    4: (2 * D, D + F),
+    6: (2 * D + F, 2 * D + F + B + H),
+    7: (3 * D + F, 2 * D + F + B),
+    8: (3 * D + F + H, 2 * D + F),
+}
+ATT_COLUMN = 2 * D + F + B + 2 * H
+
+
+def early_kernel(plan, most, tab_ref, ahead_ref, behind_ref, line_ref, square_ref):
     line_ref[...] = jnp.zeros(line_ref.shape, F32)
+
+    def turned(lane):
+        start = pl.multiple_of(lane // LANES * LANES, LANES)
+        both = ahead_ref[:, pl.ds(start, 2 * LANES)].astype(F32)
+        both = pltpu.roll(both, lax.rem(2 * LANES - (lane - start), 2 * LANES), 1)
+        return both[:, :LANES].T.astype(BF16)
+
+    def store(goal, width, tile, block):
+        line_ref[pl.ds(goal + tile, block.shape[0], stride=width), :] = block
+
     for part in range(most):
         kind, base, chunks, row0 = (tab_ref[1 + 4 * part + i] for i in range(4))
-        for index, span in spans.items():
+        for index, (lane, column) in SPANS.items():
             cols = PIECES[index][2]
             width = cols // LANES
 
             @pl.when(kind == index)
-            def _():
-                def move(step, carry, span=span, cols=cols, width=width):
-                    row = pl.multiple_of(row0 + step * CHUNK, 8)
+            def _(lane=lane, column=column, cols=cols, width=width):
+                def move(step, carry):
                     goal = base + step * (CHUNK * width)
-                    if len(span) == 2:
-                        first = step * CHUNK if span[1] else row
-                        block = refs[span[0]][pl.ds(pl.multiple_of(first, 8), CHUNK), :]
-                    else:
-                        first, column = span[1:3]
-                        first = pl.multiple_of(first + row, 8)
-                        left = refs[0][pl.ds(first, CHUNK), :].astype(BF16)
-                        block = product(left, refs[1][:, column : column + cols])
+                    left = turned(lane + row0 + step * CHUNK)
+                    block = product(left, behind_ref[:, column : column + cols])
                     for tile in range(width):
-                        line_ref[pl.ds(goal + tile, CHUNK, stride=width), :] = block[
-                            :, tile * LANES : (tile + 1) * LANES
-                        ]
+                        store(goal, width, tile, block[:, tile * LANES : (tile + 1) * LANES])
                     return carry
 
                 lax.fori_loop(0, chunks, move, 0)
+
+        @pl.when(kind == 1)
+        def _():
+            def move(step, carry):
+                width = 3 * D // LANES
+                goal = base + step * (CHUNK * width)
+                side = lax.broadcasted_iota(jnp.int32, (CHUNK, LANES), 1)
+                for pair in range(HEADS // 2):
+                    column = ATT_COLUMN + pair * LANES
+                    right = behind_ref[:, column : column + LANES]
+                    lane = AHEAD + 2 * pair * D + row0 + step * CHUNK
+                    first, second = (product(turned(lane + D * head), right) for head in range(2))
+                    block = jnp.where(side < HDIM, first, second)
+                    store(goal, width, 2 * D // LANES + pair, block)
+                return carry
+
+            lax.fori_loop(0, chunks, move, 0)
+
+        @pl.when(kind == 5)
+        def _():
+            ends = jnp.sum(behind_ref[:, BEHIND - 2 * D :].astype(F32), 0, keepdims=True)
+            for tile in range(D // LANES):
+                rows = [
+                    ends[:, place + tile * LANES : place + (tile + 1) * LANES] for place in (0, D)
+                ]
+                rows.append(jnp.zeros((6, LANES), F32))
+                store(base, D // LANES, tile, jnp.concatenate(rows, 0))
+
+    shift = tab_ref[0]
+    shape = (STEPS, LANES)
+    place = lax.broadcasted_iota(jnp.int32, shape, 0) * LANES
+    place = place + lax.broadcasted_iota(jnp.int32, shape, 1) - shift
+
+    def clear(step, total):
+        start = pl.multiple_of(step * STEPS, 8)
+        entry = place + start * LANES
+        lines = pl.ds(pl.multiple_of(FRONT + start, 8), STEPS)
+        kept = jnp.where((entry >= 0) & (entry < plan.size), line_ref[lines, :], 0.0)
+        line_ref[lines, :] = kept
+        return total + kept * kept
+
+    total = lax.fori_loop(0, plan.lines // STEPS, clear, jnp.zeros(shape, F32))
+    square_ref[...] = jnp.sum(total.reshape(STEPS // 8, 8, LANES), 0)
+
+
+def early_gradient(plan, table, ahead, behind):
+    return pl.pallas_call(
+        functools.partial(early_kernel, plan, table.shape[0] // 4),
+        out_shape=[
+            jax.ShapeDtypeStruct((plan.grad_scratch, LANES), F32),
+            jax.ShapeDtypeStruct((8, LANES), F32),
+        ],
+        in_specs=[pl.BlockSpec(memory_space=pltpu.SMEM)]
+        + [pl.BlockSpec(memory_space=pltpu.VMEM)] * 2,
+        out_specs=[pl.BlockSpec(memory_space=pltpu.VMEM)] * 2,
+        compiler_params=pltpu.CompilerParams(vmem_limit_bytes=48 * 1024 * 1024),
+        cost_estimate=pl.CostEstimate(
+            flops=10 * 10**9, bytes_accessed=10 * 10**6, transcendentals=0
+        ),
+    )(table, ahead, behind)
+
+
+def late_kernel(plan, most, tab_ref, lines_ref, wide_ref, left_ref, right_ref, out_ref, line_ref):
+    line_ref[...] = lines_ref[...]
+
+    def add(goal, width, tile, block):
+        lines = pl.ds(goal + tile, CHUNK, stride=width)
+        line_ref[lines, :] = line_ref[lines, :] + block
+
+    for part in range(most):
+        kind, base, chunks, row0 = (tab_ref[1 + 4 * part + i] for i in range(4))
+
+        @pl.when(kind == 0)
+        def _():
+            def move(step, carry):
+                width = D // LANES
+                rows = pl.ds(pl.multiple_of(row0 + step * CHUNK, 8), CHUNK)
+                for tile in range(width):
+                    block = wide_ref[rows, tile * LANES : (tile + 1) * LANES]
+                    add(base + step * (CHUNK * width), width, tile, block)
+                return carry
+
+            lax.fori_loop(0, chunks, move, 0)
+
+        @pl.when(kind == 1)
+        def _():
+            def move(step, carry):
+                width = 3 * D // LANES
+                rows = pl.ds(pl.multiple_of(row0 + step * CHUNK, 8), CHUNK)
+                block = jnp.dot(
+                    left_ref[rows, :],
+                    right_ref[...],
+                    precision=PRECISE,
+                    preferred_element_type=F32,
+                )
+                for tile in range(2 * D // LANES):
+                    piece = block[:, tile * LANES : (tile + 1) * LANES]
+                    add(base + step * (CHUNK * width), width, tile, piece)
+                return carry
+
+            lax.fori_loop(0, chunks, move, 0)
 
     shift = tab_ref[0]
     turn = lax.rem(LANES - shift, LANES)
-    lane = lax.broadcasted_iota(jnp.int32, (CHUNK + 8, LANES), 1)
+    lane = lax.broadcasted_iota(jnp.int32, (STEPS + 8, LANES), 1)
 
     def align(step, carry):
-        start = pl.multiple_of(step * CHUNK, 8)
-        here = pltpu.roll(line_ref[pl.ds(pl.multiple_of(FRONT + start, 8), CHUNK + 8), :], turn, 1)
-        below = pltpu.roll(here, CHUNK + 7, 0)
+        start = pl.multiple_of(step * STEPS, 8)
+        lines = pl.ds(pl.multiple_of(FRONT + start, 8), STEPS + 8)
+        here = pltpu.roll(line_ref[lines, :], turn, 1)
+        below = pltpu.roll(here, STEPS + 7, 0)
         both = jnp.where(lane < LANES - shift, here, below)
-        out_ref[pl.ds(start, CHUNK), :] = both[:CHUNK]
+        out_ref[pl.ds(start, STEPS), :] = both[:STEPS]
         return carry
 
-    lax.fori_loop(0, plan.lines // CHUNK, align, 0)
-
-
-def flat_gradient(plan, table, spans, refs, device):
+    lax.fori_loop(0, plan.lines // STEPS, align, 0)
+
+
+def late_gradient(plan, table, lines, wide, left, right):
     return pl.pallas_call(
-        functools.partial(grad_kernel, plan, table.shape[1] // 4, spans),
+        functools.partial(late_kernel, plan, table.shape[0] // 4),
         out_shape=jax.ShapeDtypeStruct((plan.lines, LANES), F32),
         in_specs=[pl.BlockSpec(memory_space=pltpu.SMEM)]
-        + [pl.BlockSpec(memory_space=pltpu.VMEM)] * len(refs),
+        + [pl.BlockSpec(memory_space=pltpu.VMEM)] * 4,
         out_specs=pl.BlockSpec(memory_space=pltpu.VMEM),
         scratch_shapes=[pltpu.VMEM((plan.grad_scratch, LANES), F32)],
-        compiler_params=pltpu.CompilerParams(vmem_limit_bytes=48 * 1024 * 1024),
-    )(jnp.asarray(table)[device], *refs).reshape(-1)[: plan.size]
+        compiler_params=pltpu.CompilerParams(vmem_limit_bytes=32 * 1024 * 1024),
+    )(table, lines, wide, left, right).reshape(-1)[: plan.size]
 
 
 def adam_update(weight, grad, first, second, rate):
@@ -823,20 +1029,28 @@
         other = trade(values)
         return jnp.where(low, values, other), jnp.where(low, other, values)
 
+    pairs = [list(range(parity, reps, 2)) for parity in (0, 1)]
+    tables = jnp.stack([protos, teacher_protos]).astype(BF16)
+    tables = lax.all_to_all(
+        jnp.broadcast_to(tables[None], (reps // 2,) + tables.shape),
+        "rep",
+        0,
+        0,
+        axis_index_groups=pairs,
+    )
+
     table = jnp.asarray(plan.lay_table)[device]
     kept = lay_out(plan, table, jnp.where(low, params, teacher))
     given = trade(lay_out(plan, table, jnp.where(low, teacher, params)))
-    patches, partner, given = lax.optimization_barrier((patches, partner, given))
+    patches, partner, tables, given = lax.optimization_barrier((patches, partner, tables, given))
     shards = jnp.stack([jnp.where(low, kept, given), jnp.where(low, given, kept)])
     gathered = lax.all_gather(shards, BOTH, axis=0, axis_index_groups=halves)
     gathered = gathered.reshape(half, 2, -1, TILE, LANES)
     pixels = jnp.concatenate(in_order(patches), 0)
     pixels = jnp.pad(pixels, ((0, 0), (0, TOKENS - NPATCH), (0, 0)))
+    tables = jnp.stack(in_order(tables))
+    tables = tables.transpose(2, 1, 0, 3, 4).reshape(2, B, -1).astype(F32)
     places = in_order(partner.astype(F32))
-    tables = jnp.stack([protos, teacher_protos]).astype(BF16)
-    tables, gathered = lax.optimization_barrier((tables, gathered))
-    tables = lax.all_gather(tables, "rep", axis=1, tiled=True).astype(F32)
-
     def columns_of(values):
         scale = lax.rsqrt(jnp.sum(values * values, 0, keepdims=True) + 1e-06)
         return (values * scale).astype(BF16), scale
@@ -849,14 +1063,13 @@
     rows = kept[-1]
 
     def gather_rows(values):
-        values = trade_low(values)
         return lax.all_gather(values, BOTH, axis=0, axis_index_groups=halves).reshape(
             half * views, -1
         )
 
-    ahead = gather_rows(
-        jnp.concatenate([ahead, mixed[:, :HEADS].reshape(views, -1)], 1)
-    )
+    ahead = [ahead, mixed[:, :HEADS].reshape(views, -1)]
+    ahead.append(jnp.pad(classes[1:3], ((0, views - 2), (0, 0))).astype(BF16))
+    ahead = trade_low(jnp.concatenate(ahead, 1))
 
     here = jnp.arange(views)
     source = jnp.concatenate([places[0], places[1] + own_views]).astype(jnp.int32)
@@ -865,6 +1078,8 @@
     all_rows = lax.all_to_all(
         jnp.broadcast_to(rows[None], (count, views, B)), BOTH, 0, 0
     )
+    all_rows, ahead = lax.optimization_barrier((all_rows, ahead))
+    ahead = gather_rows(ahead)
     all_rows = all_rows.reshape(reps // 2, 2, groups * views, B)
     student_rows = all_rows[:, 0].reshape(-1, B)
     teacher_rows = all_rows[:, 1].reshape(-1, B)
@@ -919,95 +1134,94 @@
         - protos.astype(BF16).astype(F32) * column_scale**3 * inner
     )
 
-    saved = (unit, scale, probs, looked, classes, qkv_w) + tuple(kept[8:13])
-    behind, tokens, grad_place, extra, reach = backward(plan, gathered, grad_rows, saved)
-    cols_all = gather_rows(behind)
-    grad_patch = lax.dot_general(
-        pixels.reshape(-1, PD),
-        tokens.reshape(-1, D),
-        (((0,), (0,)), ((), ())),
-        preferred_element_type=F32,
-    )
-    partial = jnp.concatenate([grad_patch, extra[:1], grad_place[:NPATCH], extra[1:5]], 0)
-    shared = jnp.concatenate([extra[5:6], reach[:HEADS]], 0)
-    base = PD + NTOK + 4
-    depth = -(-base // half)
-    partial = jnp.pad(partial, ((0, half * depth - base), (0, 0))).reshape(half, depth, D)
-    slots = round_up(depth + shared.shape[0], 8)
-    partial = jnp.concatenate(
-        [
-            partial,
-            jnp.broadcast_to(shared[None], (half,) + shared.shape),
-            jnp.zeros((half, slots - depth - shared.shape[0], D), F32),
-        ],
-        1,
-    ).astype(BF16)
-    partial = lax.all_to_all(partial, BOTH, 0, 0, axis_index_groups=halves)
+    behind, grad_middle, ends = rows_back(
+        plan, gathered, grad_rows, (classes,) + tuple(kept[8:13])
+    )
+    odd, far = grp % 2 == 1, grp // 2 % 2 == 1
+    behind_rows = trade_low(behind)
+    kept_rows, sent_rows = tokens_back(
+        odd.astype(jnp.int32)[None],
+        behind,
+        grad_middle,
+        ends,
+        (unit, scale, probs, looked, classes, qkv_w),
+        pixels.transpose(0, 2, 1),
+    )
+    behind_rows, sent_rows = lax.optimization_barrier((behind_rows, sent_rows))
+    behind_rows = gather_rows(behind_rows)
+
+    def across(bit, values):
+        return lax.ppermute(values, "grp", [(g, g ^ bit) for g in range(groups)])
+
+    partial = kept_rows + across(1, sent_rows).astype(F32)
+    first, second = partial[:SET], partial[SET : 2 * SET]
+    shared = partial[2 * SET :]
+    other = jnp.concatenate([jnp.where(far, first, second), shared], 0).astype(BF16)
+    partial = jnp.concatenate([jnp.where(far, second, first), shared], 0)
+    partial = partial + across(2, other).astype(F32)
+    lines = reps // 2
+    depth = partial.shape[0] // lines
+    partial = lax.all_to_all(
+        partial.astype(BF16).reshape(lines, depth, D), "rep", 0, 0, axis_index_groups=pairs
+    )
     partial = jnp.sum(partial.astype(F32), 0)
-    shared = partial[depth : depth + shared.shape[0]]
-    shared = jnp.where(low, shared, trade(shared))
-    partial = partial[:depth]
-    slots = round_up(depth, 8)
-    summed = jnp.pad(partial, ((0, slots - depth), (0, 0))).astype(BF16)
     summed = lax.all_to_all(
-        jnp.broadcast_to(summed[None], (half, slots, D)), BOTH, 0, 0, axis_index_groups=halves
-    )
-    summed = summed[:, :depth].reshape(-1, D)[:base]
+        jnp.broadcast_to(partial.astype(BF16)[None], (lines, depth, D)),
+        "rep",
+        0,
+        0,
+        axis_index_groups=pairs,
+    ).reshape(-1, D)
+    shared, summed = trade_low(summed[SET:]).astype(F32), summed[:SET]
+    other = across(2, summed)
+    summed = jnp.concatenate([jnp.where(far, other, summed), jnp.where(far, summed, other)], 0)
+    if plan.all_sets:
+        other = across(1, summed)
+        summed = jnp.concatenate([jnp.where(odd, other, summed), jnp.where(odd, summed, other)], 0)
     if plan.odd_owner:
         summed = trade_low(summed)
-    summed = summed.astype(F32)
-
-    split = 3 * D + F + 2 * H
-    rows_all = jnp.pad(ahead[:, :split].astype(F32).T, ((0, CHUNK), (0, 0)))
-    mixed_rows = ahead[:, split:].reshape(half * views, HEADS, D)
-    ends = jnp.sum(cols_all[:, -2 * D :].astype(F32), 0).reshape(2, D)
-    ends = jnp.pad(ends, ((0, CHUNK - 2), (0, 0)))
-    spans = {
-        2: (0, 0, 0),
-        3: (0, D, D),
-        4: (0, 2 * D, D + F),
-        5: (2, False),
-        6: (0, 2 * D + F, 2 * D + F + B + H),
-        7: (0, 3 * D + F, 2 * D + F + B),
-        8: (0, 3 * D + F + H, 2 * D + F),
-    }
-    early = flat_gradient(plan, plan.grad_table, spans, (rows_all, cols_all, ends), device)
-    values_att = cols_all[:, 2 * D + F + B + 2 * H : 3 * D + F + B + 2 * H]
-    values_att = values_att.reshape(-1, HEADS, HDIM)
-    qkv_v = jnp.einsum(
-        "vhd,vhc->dhc", mixed_rows, values_att, preferred_element_type=F32
-    ).reshape(D, D)
-
-    classes = trade_low(classes)
-    class_normed, query = classes[1:2], classes[2:3]
+    wide_grad = jnp.pad(summed.astype(F32), ((0, CHUNK), (0, 0)))
+
+    early, squares = early_gradient(
+        plan, jnp.asarray(plan.grad_table)[device], ahead, behind_rows
+    )
+    class_rows = ahead[:2, AHEAD + HEADS * D :].astype(F32)
+    class_normed, query = class_rows[0:1], class_rows[1:2]
     by_head = jnp.where(head_mask()[:HEADS], query, 0.0)
-    sum_query, reach = shared[0], shared[1:]
-    outer = jnp.sum(class_normed * class_normed) * jnp.sum(sum_query * sum_query) + jnp.sum(
-        jnp.sum(reach * reach, 1) * jnp.sum(by_head * by_head, 1)
-    )
-    squares = jnp.sum(partial * partial) + (jnp.sum(qkv_v * qkv_v) + outer) / half
-    squares = jnp.where(low, squares, 0.0)
-    squares = squares + jnp.sum(early * early) + jnp.sum(grad_protos * grad_protos)
+    twice = odd & ~far & (jnp.arange(SET) < 8)
+    weights = jnp.concatenate(
+        [
+            jnp.where(twice, 0.0, 1.0),
+            jnp.sum(by_head * by_head, 1) / groups,
+            jnp.zeros((HEADROWS - HEADS,), F32),
+            jnp.sum(class_normed * class_normed)[None] / groups,
+            jnp.zeros((SHARED - HEADROWS - 1,), F32),
+        ]
+    )
+    weights = lax.dynamic_slice_in_dim(weights, rep // 2 * depth, depth)
+    pieces = jnp.sum(weights * jnp.sum(partial * partial, 1))
+    squares = jnp.sum(squares) + jnp.where(low, pieces, 0.0)
+    squares = squares + jnp.sum(grad_protos * grad_protos)
     squares = lax.all_to_all(
         jnp.broadcast_to(squares.reshape(1, 1, 1), (count, 1, LANES)), BOTH, 0, 0
     )
     grad_norm = jnp.sqrt(jnp.sum(squares[:, 0, 0]))
     factor = jnp.minimum(1.0, CLIP_NORM / (grad_norm + 1e-06))
 
-    qkv_grad = jnp.concatenate(
+    sum_query, reach = shared[HEADROWS : HEADROWS + 1], shared[:HEADS]
+    left = jnp.concatenate([class_normed, reach, jnp.zeros((LANES - 1 - HEADS, D), F32)], 0)
+    left = jnp.pad(left.T, ((0, CHUNK), (0, 0)))
+    right = jnp.concatenate(
         [
-            class_normed.T * sum_query[None],
-            lax.dot_general(reach, by_head, (((0,), (0,)), ((), ())), precision=PRECISE),
-            qkv_v,
+            jnp.pad(sum_query, ((0, 0), (0, D))),
+            jnp.pad(by_head, ((0, 0), (D, 0))),
+            jnp.zeros((LANES - 1 - HEADS, 2 * D), F32),
         ],
-        1,
-    )
-    qkv_grad = jnp.pad(qkv_grad, ((0, CHUNK), (0, 0)))
-    wide_grad = jnp.pad(summed, ((0, CHUNK), (0, 0)))
-    late = flat_gradient(
-        plan, plan.late_table, {0: (0, False), 1: (1, False)}, (wide_grad, qkv_grad), device
-    )
-    grad_flat = early + late
+        0,
+    )
+    grad_flat = late_gradient(
+        plan, jnp.asarray(plan.late_table)[device], early, wide_grad, left, right
+    )
     new_params, new_first, new_second = adam_update(
         params, grad_flat * factor, first_moment, second_moment, LEARNING_RATE
     )

time: 517 us -> 425 us (0.82)
  waiting for transfers between devices: 236 us -> 198 us
  Pallas kernels: 111 us -> 80.7 us
  starting transfers between devices: 49.8 us -> 35.2 us
  matrix products: 18.4 us -> 8.69 us
  local copies, waits for them, and re-layouts: 30 us -> 37.3 us
    all_gather x1, waiting for transfers between devices: 121 us -> 83.8 us  [per_device(): gathered = lax.all_gather(shards, BOTH, axis=0, axis_index_groups=halves)]
    pallas_call x3 -> x4, Pallas kernels: 72 us -> 41.5 us  [the longest x1 17.2 us: rows_back(): pl.pallas_call(functools.partial(rows_back_kernel, plan), out_shape=[jax....]
    all_to_all x2 -> x3, waiting for transfers between devices: 44.8 us -> 22.4 us  [the longest x1 18.1 us: per_device(): lax.all_to_all(partial.astype(BF16).reshape(lines, depth, D), 'rep', 0, 0...]
    ppermute x0 -> x3, waiting for transfers between devices: none -> 20.1 us  [across(): return lax.ppermute(values, 'grp', [(g, g ^ bit) for g in range(groups)])]
    all_to_all x1, starting transfers between devices: 23.6 us -> 5.17 us  [per_device(): lax.all_to_all(jnp.broadcast_to(squares.reshape(1, 1, 1), (count, 1, LANE...]
    ppermute x7, waiting for transfers between devices: 44.6 us -> 61.6 us  [trade(): return lax.ppermute(values, 'rep', swap)]
    dot_general x3 -> x0, matrix products: 10.5 us -> none  [the longest x1 4.09 us: per_device(): lax.dot_general(pixels.reshape(-1, PD), tokens.reshape(-1, D), (((0,), (0...]
    all_gather x1 -> x0, waiting for transfers between devices: 10.1 us -> none  [per_device(): tables = lax.all_gather(tables, 'rep', axis=1, tiled=True).astype(F32)]
  transfers between devices with their start and end apart: 16 -> 19, of which waited for: 12 -> 12; matrix products, arithmetic and copies ran while one was open for 13% -> 12% of each run, Pallas kernels for 18% -> 11%
where the time goes in v4:
time: 425 us; the launch traced here: 423 us
  waiting for transfers between devices  198 us (47%)
  Pallas kernels  80.7 us (19%)
  other arithmetic  43.5 us (10%)
  local copies, waits for them, and re-layouts  37.3 us (9%)
  starting transfers between devices  35.2 us (8%)
  between operations  18.9 us (4%)
  matrix products  8.69 us (2%)
    all_gather x1, waiting for transfers between devices, per_device(): gathered = lax.all_gather(shards, BOTH, axis=0, axis_index_groups=halves)  83.8 us
    ppermute x7, waiting for transfers between devices, trade(): return lax.ppermute(values, 'rep', swap)  61.6 us
    pallas_call x1, Pallas kernels, forward(): pl.pallas_call(functools.partial(forward_kernel, plan), out_shape=[jax.Sh...  28.6 us
    ppermute x3, waiting for transfers between devices, across(): return lax.ppermute(values, 'grp', [(g, g ^ bit) for g in range(groups)])  20.1 us
    all_to_all x1, waiting for transfers between devices, per_device(): lax.all_to_all(partial.astype(BF16).reshape(lines, depth, D), 'rep', 0, 0...  18.1 us
    pallas_call x1, Pallas kernels, rows_back(): pl.pallas_call(functools.partial(rows_back_kernel, plan), out_shape=[jax....  17.2 us
    unnamed x68, local copies, waits for them, and re-layouts  15.8 us
    pallas_call x1, Pallas kernels, tokens_back(): pl.pallas_call(tokens_back_kernel, grid=(views,), out_shape=[jax.ShapeDty...  13.5 us
  transfers between devices with their start and end apart: 19, of which 12 were waited for; matrix products, arithmetic and copies ran while one was open for 12% of the time, Pallas kernels for 11%

profile of v4, /device:TPU:0, one launch (start us, length us, event | category | flops | bytes accessed | tf_op | source)
XLA Modules:
  0.0 422.7 jit_solution(5418006144546936782)
XLA Ops:
  9.4 6.3 %all-to-all-start = ((bf16[4,2,32,2048]{3,2,1,0:T(8,128)(2,1)}), bf16[4,2,32,2048]{3,2,1,0:T(8,128)(2,1)S(1)}, u32[]{:S(2)}, u32[]{:S(2)}) async-start(bf16[4,2,32,2048]{3,2,1,0:T(8,128)(2,1)} %broadcast_in_dim.76), calls=%async_computation | async-start | bytes 2097152 | tf_op jit(solution)/shard_map/all_to_all | solution.py:1034
  15.7 3.4 broadcast_select_fusion.2
  20.0 5.4 %shard_map.221 = bf16[3648,128]{1,0:T(8,128)(2,1)S(1)} custom-call(s32[11]{0:T(128)S(1)} %fusion.46.tab_ref, f32[3464,128]{1,0:T(8,128)S(1)} %pad_bitcast_fusion.1.x_ref), custom_call_target="tpu_custom_call" | custom-call | tf_op jit(solution)/shard_map/pallas_call | solution.py:224
  25.3 1.4 collective-permute-start
  26.9 5.4 %shard_map.222 = bf16[3648,128]{1,0:T(8,128)(2,1)S(1)} custom-call(s32[11]{0:T(128)S(1)} %fusion.46.tab_ref, f32[3464,128]{1,0:T(8,128)S(1)} %pad_bitcast_fusion.x_ref), custom_call_target="tpu_custom_call" | custom-call | tf_op jit(solution)/shard_map/pallas_call | solution.py:224
  32.2 15.3 %collective-permute-done = bf16[3648,128]{1,0:T(8,128)(2,1)S(1)} collective-permute-done((bf16[3648,128]{1,0:T(8,128)(2,1)S(1)}, bf16[3648,128]{1,0:T(8,128)(2,1)S(1)}, u32[]{:S(2)}, u32[]{:S(2)}) %collective-permute-start) | collective-permute-done | bytes 933920 | tf_op jit(solution)/shard_map/ppermute | solution.py:1023
  50.1 1.4 collective-permute-start.4
  52.1 2.6 copy.81
  54.7 1.5 collective-permute-start.1
  56.2 43.7 %collective-permute-done.1 = f32[4]{0:T(128)S(1)} collective-permute-done((f32[4]{0:T(128)S(1)}, f32[4]{0:T(128)S(1)}, u32[]{:S(2)}, u32[]{:S(2)}) %collective-permute-start.1) | collective-permute-done | bytes 48 | tf_op jit(solution)/shard_map/ppermute | solution.py:1023
  100.0 1.5 select_bitcast_fusion.1
  105.9 3.6 copy.82
  109.5 1.6 broadcast_select_fusion.1
  111.2 2.2 fusion.55
  113.3 4.6 %copy.85.pixels_ref = bf16[8,208,768]{2,1,0:T(8,128)(2,1)} copy(bf16[8,208,768]{1,2,0:T(8,128)(2,1)} %get-tuple-element.90) | data formatting | bytes 5111808 | tf_op jit(solution)/shard_map/jit(_pad)/pad | solution.py:1050
  117.9 83.8 %all-gather.7.cloned.1.call-done = bf16[32,3648,128]{2,1,0:T(8,128)(2,1)} async-done(((bf16[2,3648,128]{2,1,0:T(8,128)(2,1)}), bf16[32,3648,128]{2,1,0:T(8,128)(2,1)}) %all-gather.7.cloned.1.call-update) | async-done | bytes 29884432 | tf_op jit(solution)/shard_map/all_gather | solution.py:1047
  201.7 28.6 %shard_map.223 = (f32[8,208,768]{2,1,0:T(8,128)}, f32[8,208,128]{2,1,0:T(8,128)}, f32[8,16,208]{2,1,0:T(8,128)}, bf16[8,16,768]{2,1,0:T(8,128)(2,1)}, bf16[16,76...) custom-call(bf16[16,2,228,16,128]{4,3,2,1,0:T(8,128)(2,1)} %bitcast., ...), custom_call_target="tpu_custom_call" | custom-call | flops 60000002048 | bytes 40000000 | tf_op jit(solution)/shard_map/pallas_call | solution.py:557
  232.0 1.6 fusion.33
  233.7 1.4 collective-permute-start.3
  235.1 2.8 fusion.6
  238.7 3.8 all-to-all-start.1
  244.3 6.5 %all-to-all-done.1 = bf16[32,8,256]{2,1,0:T(8,128)(2,1)} async-done(((bf16[32,8,256]{2,1,0:T(8,128)(2,1)}), bf16[32,8,256]{2,1,0:T(8,128)(2,1)}, u32[]{:S(2)}, u32[]{:S(2)}) %all-to-all-start.1) | async-done | bytes 131104 | tf_op jit(solution)/shard_map/all_to_all | solution.py:1078
  251.8 1.5 fusion.14
  253.3 1.6 exponential_reduce_fusion
  257.8 3.3 all-to-all-start.2
  261.4 3.9 all-to-all-done.2
  266.2 17.2 %shard_map.224 = (bf16[8,11264]{1,0:T(8,128)(2,1)}, f32[8,768]{1,0:T(8,128)}, f32[8,768]{1,0:T(8,128)}) custom-call(bf16[16,2,228,16,128]{4,3,2,1,0:T(8,128)(2,1)} %bitcast.117, f32[8,256]{1,0:T(8,128)} %fusion.39.grad_ref, f32[16,768]{1,0:T(8,128)} %get-tuple-element.46.class_ref, f32[8,3072]{1,0:T(8,128)} %get-tuple-element.50.hidden_ref, ...), custom_call_target="tpu_custom_call" | custom-call | flops 30000001024 | bytes 30000000 | tf_op jit(solution)/shard_map/pallas_call | solution.py:649
  285.1 2.0 copy-done.8
  289.7 13.5 %shard_map.225 = (f32[608,768]{1,0:T(8,128)S(1)}, bf16[608,768]{1,0:T(8,128)(2,1)S(1)}) custom-call(s32[1]{0:T(128)} %bitcast.30.odd_ref, bf16[8,11264]{1,0:T(8,128)(2,1)S(1)} %copy-done.4, f32[8,768]{1,0:T(8,128)S(1)} %copy-done.12, f32[8,768]{1,0:T(8,128)S(1)} %copy-done.13, f32[8,208,768]{2,1,0:T(8,128)} %get-tuple-element.58.unit_ref, ...), custom_call_target="tpu_custom_call" | custom-call | flops 15000000512 | bytes 15000000 | tf_op jit(solution)/shard_map/pallas_call | solution.py:781
  306.2 2.9 collective-permute-done.6
  309.1 1.7 convert_add_fusion
  311.2 15.1 %collective-permute-done.7 = bf16[320,768]{1,0:T(8,128)(2,1)S(1)} collective-permute-done((bf16[320,768]{1,0:T(8,128)(2,1)S(1)}, bf16[320,768]{1,0:T(8,128)(2,1)S(1)}, u32[]{:S(2)}, u32[]{:S(2)}) %collective-permute-start.7) | collective-permute-done | bytes 491552 | tf_op jit(solution)/shard_map/ppermute | solution.py:1154
  327.1 3.6 all-to-all-start.3
  333.8 18.1 %all-to-all-done.3 = bf16[4,80,768]{2,1,0:T(8,128)(2,1)S(1)} async-done(((bf16[4,80,768]{2,1,0:T(8,128)(2,1)}), bf16[4,80,768]{2,1,0:T(8,128)(2,1)S(1)}, u32[]{:S(2)}, u32[]{:S(2)}) %all-to-all-start.3) | async-done | bytes 491552 | tf_op jit(solution)/shard_map/all_to_all | solution.py:1164
  353.4 3.5 all-to-all-start.4
  358.2 4.3 %fusion.9 = (f32[2048]{0:T(1024)S(1)}, f32[256,2048]{1,0:T(8,128)}) fusion(f32[1,4,2,32,2048]{4,3,2,1,0:T(8,128)S(1)} %copy-done.15, bf16[128,256]{1,0:T(8,128)(2,1)S(1)} %bitcast.110, f32[128,2048]{1,0:T(8,128)} %copy-done.21, f32[128]{0:T(128)S(1)} %get-tuple-element.106, f32[128]{0:T(128)S(1)} %get-tuple-element.105, f32[128,2048]{1,0:T(8,128)} %get-tuple-element.118), kind=kOutput, calls=%fused_computation.19 | convolution fusion | flops 807401472 | bytes 6366208 | tf_op jit(solution)/shard_map/dot_general | solution.py:1127
  362.5 4.3 %all-to-all-done.4 = bf16[4,80,768]{2,1,0:T(8,128)(2,1)S(1)} async-done(((bf16[4,80,768]{2,1,0:T(8,128)(2,1)}), bf16[4,80,768]{2,1,0:T(8,128)(2,1)S(1)}, u32[]{:S(2)}, u32[]{:S(2)}) %all-to-all-start.4) | async-done | bytes 491552 | tf_op jit(solution)/shard_map/all_to_all | solution.py:1168
  367.1 1.6 multiply_reduce_fusion.1
  368.7 1.7 collective-permute-start.9
  371.0 1.8 collective-permute-done.9
  373.0 2.1 collective-permute-done.8
  379.7 1.8 copy-done.6
  381.5 5.4 %shard_map.226 = (f32[6736,128]{1,0:T(8,128)}, f32[8,128]{1,0:T(8,128)S(1)}) custom-call(s32[13]{0:T(128)S(1)} %fusion.45.tab_ref, bf16[128,19456]{1,0:T(8,128)(2,1)} %all-gather.9.cloned.1.call-done.ahead_ref, bf16[128,11264]{1,0:T(8,128)(2,1)S(1)} %copy-done.6), custom_call_target="tpu_custom_call" | custom-call | flops 10000000000 | bytes 10000000 | tf_op jit(solution)/shard_map/pallas_call | solution.py:900
  389.4 5.2 %all-to-all-start.5 = ((f32[32,1,128]{2,1,0:T(1,128)}), f32[32,1,128]{2,1,0:T(1,128)S(1)}, u32[]{:S(2)}, u32[]{:S(2)}) async-start(f32[32,1,128]{2,1,0:T(1,128)} %broadcast_in_dim.91), calls=%async_computation.5 | async-start | bytes 32768 | tf_op jit(solution)/shard_map/all_to_all | solution.py:1205
  395.9 2.0 copy-done.2
  397.9 5.3 %shard_map.227 = f32[3456,128]{1,0:T(8,128)S(1)} custom-call(s32[9]{0:T(128)S(1)} %fusion.44.tab_ref, f32[6736,128]{1,0:T(8,128)S(1)} %copy-done.2, f32[704,768]{1,0:T(8,128)S(1)} %fusion.13.wide_ref, f32[896,128]{1,0:T(8,128)S(1)} %pad.40.left_ref, f32[128,1536]{1,0:T(8,128)S(1)} %fusion.23.right_ref), custom_call_target="tpu_custom_call" | custom-call | tf_op jit(solution)/shard_map/pallas_call | solution.py:973
  405.9 2.1 multiply_add_fusion.2
  408.0 7.0 %multiply_add_fusion = (f32[441096]{0:T(1024)}, f32[441096]{0:T(1024)}, f32[441096]{0:T(1024)}, f32[441096]{0:T(1024)}) fusion(f32[441096]{0:T(1024)} %param.17, f32[441096]{0:T(1024)} %param.14, f32[]{:T(128)S(6)} %min.3, f32[442368]{0:T(1024)S(1)} %bitcast.102, f32[441096]{0:T(1024)} %param.15, f32[441096]{0:T(1024)} %param.16), kind=kLoop, calls=%fused_computation.28 | loop fusion | flops 8380824 | bytes 15879460 | tf_op jit(solution)/shard_map/add | solution.py:1231
  (167 shorter events, 42.9 us)
Async XLA Ops:
  9.4 38.1 %all-to-all-start = ((bf16[4,2,32,2048]{3,2,1,0:T(8,128)(2,1)}), bf16[4,2,32,2048]{3,2,1,0:T(8,128)(2,1)S(1)}, u32[]{:S(2)}, u32[]{:S(2)}) async-start(bf16[4,2,32,2048]{3,2,1,0:T(8,128)(2,1)} %broadcast_in_dim.76), calls=%async_computation | async-start | bytes 2097152 | tf_op jit(solution)/shard_map/all_to_all | solution.py:1034
  15.7 186.0 %all-gather.7.cloned.1.call-start = ((), (), s32[]{:S(2)}) async-start(), calls=%async_computation.6 | async-start | bytes 31752192 | tf_op jit(solution)/shard_map/all_gather | solution.py:1047
  19.9 6.8 %copy-start.17 = (f32[441096]{0:T(1024)S(1)}, f32[441096]{0:T(1024)}, u32[]{:S(2)}) copy-start(f32[441096]{0:T(1024)} %get-tuple-element.87) | copy-start | bytes 5293156
  25.3 22.2 %collective-permute-start = (bf16[3648,128]{1,0:T(8,128)(2,1)S(1)}, bf16[3648,128]{1,0:T(8,128)(2,1)S(1)}, u32[]{:S(2)}, u32[]{:S(2)}) collective-permute-start(bf16[3648,128]{1,0:T(8,128)(2,1)S(1)} %shard_map.221), channel_id=1, source_target_pairs={{0,4},{4,0},{8,12},{12,8},{16,20},{20,16},{24,28},{28,24},{1,5},{5... | collective-permute-start | bytes 2801672 | tf_op jit(solution)/shard_map/ppermute | solution.py:1023
  50.1 4.6 %copy-start.31 = (s32[4]{0:T(128)S(1)}, s32[4]{0:T(128)}, u32[]{:S(2)}) copy-start(s32[4]{0:T(128)} %param.24) | copy-start | bytes 52
  50.1 49.9 %collective-permute-start.4 = (bf16[4,2,32,2048]{3,2,0,1:T(8,128)(2,1)}, bf16[4,2,32,2048]{3,2,0,1:T(8,128)(2,1)}, u32[]{:S(2)}, u32[]{:S(2)}) collective-permute-start(bf16[4,2,32,2048]{3,2,0,1:T(8,128)(2,1)} %copy.87), channel_id=1, source_target_pairs={{0,4},{4,0},{8,12},{12,8},{16,20},{20,16},{24,28},{28,24},{1,5},{5... | collective-permute-start | bytes 3145736 | tf_op jit(solution)/shard_map/ppermute | solution.py:1023
  51.5 54.4 %collective-permute-start.2 = (bf16[4,196,768]{2,0,1:T(4,128)(2,1)}, bf16[4,196,768]{2,0,1:T(4,128)(2,1)}, u32[]{:S(2)}, u32[]{:S(2)}) collective-permute-start(bf16[4,196,768]{2,0,1:T(4,128)(2,1)} %param.23), channel_id=1, source_target_pairs={{0,4},{4,0},{8,12},{12,8},{16,20},{20,16},{24,28},{28,24},{1,5},{5... | collective-permute-start | bytes 3612680 | tf_op jit(solution)/shard_map/ppermute | solution.py:1023
  54.7 45.2 %collective-permute-start.1 = (f32[4]{0:T(128)S(1)}, f32[4]{0:T(128)S(1)}, u32[]{:S(2)}, u32[]{:S(2)}) collective-permute-start(f32[4]{0:T(128)S(1)} %convert_element_type.96), channel_id=1, source_target_pairs={{0,4},{4,0},{8,12},{12,8},{16,20},{20,16},{24,28},{28,24},{1,5},{5... | collective-permute-start | bytes 56 | tf_op jit(solution)/shard_map/ppermute | solution.py:1023
  102.3 1.3 copy-start.16
  102.3 2.5 copy-start.14
  232.0 5.8 %copy-start.32 = (bf16[8,256]{1,0:T(8,128)(2,1)S(1)}, bf16[8,256]{1,0:T(8,128)(2,1)}, u32[]{:S(2)}) copy-start(bf16[8,256]{1,0:T(8,128)(2,1)} %get-tuple-element.43) | copy-start | bytes 12292
  233.7 9.8 %copy-start.23 = (bf16[8,9472]{1,0:T(8,128)(2,1)S(1)}, bf16[8,9472]{1,0:T(8,128)(2,1)}, u32[]{:S(2)}) copy-start(bf16[8,9472]{1,0:T(8,128)(2,1)} %get-tuple-element.44) | copy-start | bytes 454660
  233.7 9.8 %collective-permute-start.3 = (bf16[8,19456]{1,0:T(8,128)(2,1)}, bf16[8,19456]{1,0:T(8,128)(2,1)}, u32[]{:S(2)}, u32[]{:S(2)}) collective-permute-start(bf16[8,19456]{1,0:T(8,128)(2,1)} %fusion.33), channel_id=1, source_target_pairs={{0,4},{4,0},{8,12},{12,8},{16,20},{20,16},{24,28},{28,24},{1,5},{5... | collective-permute-start | bytes 933896 | tf_op jit(solution)/shard_map/ppermute | solution.py:1023
  238.7 14.6 %copy-start.25 = (f32[2048]{0:T(1024)S(1)}, f32[2048]{0:T(1024)}, u32[]{:S(2)}) copy-start(f32[2048]{0:T(1024)} %param.22) | copy-start | bytes 24580
  238.7 12.1 %all-to-all-start.1 = ((bf16[32,8,256]{2,1,0:T(8,128)(2,1)}), bf16[32,8,256]{2,1,0:T(8,128)(2,1)}, u32[]{:S(2)}, u32[]{:S(2)}) async-start(bf16[32,8,256]{2,1,0:T(8,128)(2,1)} %broadcast_in_dim.77), calls=%async_computation.1 | async-start | bytes 262144 | tf_op jit(solution)/shard_map/all_to_all | solution.py:1078
  242.6 132.9 %all-gather.9.cloned.1.call-start = ((), (), s32[]{:S(2)}) async-start(), calls=%async_computation.7 | async-start | bytes 5292032 | tf_op jit(solution)/shard_map/all_gather | solution.py:1066
  250.8 2.5 copy-start.19
  253.3 2.6 copy-start.18
  254.9 1.0 copy-start.21
  257.8 7.5 %all-to-all-start.2 = ((f32[4,35,128]{2,1,0:T(8,128)}), f32[4,35,128]{2,1,0:T(8,128)S(1)}, u32[]{:S(2)}, u32[]{:S(2)}) async-start(f32[4,35,128]{2,1,0:T(8,128)} %reshape.180), calls=%async_computation.2 | async-start | bytes 163840 | tf_op jit(solution)/shard_map/all_to_all | solution.py:1114
  261.1 118.5 %all-gather.11.cloned.1.call-start = ((), (), s32[]{:S(2)}) async-start(), calls=%async_computation.8 | async-start | bytes 3063808 | tf_op jit(solution)/shard_map/all_gather | solution.py:1066
  266.2 18.0 %copy-start.5 = (f32[16,768]{1,0:T(8,128)S(1)}, f32[16,768]{1,0:T(8,128)}, u32[]{:S(2)}) copy-start(f32[16,768]{1,0:T(8,128)} %get-tuple-element.46.class_ref) | copy-start | bytes 147460
  266.2 18.0 %copy-start.10 = (f32[8,16,208]{2,1,0:T(8,128)S(1)}, f32[8,16,208]{2,1,0:T(8,128)}, u32[]{:S(2)}) copy-start(f32[8,16,208]{2,1,0:T(8,128)} %get-tuple-element.60.probs_ref) | copy-start | bytes 319492
  266.2 18.0 %copy-start.11 = (bf16[16,768]{1,0:T(8,128)(2,1)S(1)}, bf16[16,768]{1,0:T(8,128)(2,1)}, u32[]{:S(2)}) copy-start(bf16[16,768]{1,0:T(8,128)(2,1)} %get-tuple-element.61.looked_ref) | copy-start | bytes 73732
  283.4 22.0 %collective-permute-start.5 = (bf16[8,11264]{1,0:T(8,128)(2,1)}, bf16[8,11264]{1,0:T(8,128)(2,1)S(1)}, u32[]{:S(2)}, u32[]{:S(2)}) collective-permute-start(bf16[8,11264]{1,0:T(8,128)(2,1)} %get-tuple-element.55.behind_ref), channel_id=1, source_target_pairs={{0,4},{4,0},{8,12},{12,8},{16,20},{20,16},{24,28},{28,24},{1,5},{5... | collective-permute-start | bytes 540680 | tf_op jit(solution)/shard_map/ppermute | solution.py:1023
  285.1 2.0 copy-start.8
  287.1 1.2 copy-start.9
  303.2 1.3 copy-start.3
  306.2 3.0 collective-permute-start.6
  311.0 15.3 %collective-permute-start.7 = (bf16[320,768]{1,0:T(8,128)(2,1)S(1)}, bf16[320,768]{1,0:T(8,128)(2,1)S(1)}, u32[]{:S(2)}, u32[]{:S(2)}) collective-permute-start(bf16[320,768]{1,0:T(8,128)(2,1)S(1)} %pad_maximum_fusion.1), channel_id=1, source_target_pairs={{0,2},{1,3},{2,0},{3,1},{4,6},{5,7},{6,4},{7,5},{8,10},{9,11},{10,... | collective-permute-start | bytes 1474568 | tf_op jit(solution)/shard_map/ppermute | solution.py:1154
  327.1 31.0 %copy-start.15 = (f32[1,4,2,32,2048]{4,3,2,1,0:T(8,128)S(1)}, f32[1,4,2,32,2048]{4,3,2,1,0:T(8,128)}, u32[]{:S(2)}) copy-start(f32[1,4,2,32,2048]{4,3,2,1,0:T(8,128)} %copy-done.14) | copy-start | bytes 6291460
  327.1 24.7 %all-to-all-start.3 = ((bf16[4,80,768]{2,1,0:T(8,128)(2,1)}), bf16[4,80,768]{2,1,0:T(8,128)(2,1)S(1)}, u32[]{:S(2)}, u32[]{:S(2)}) async-start(bf16[4,80,768]{2,1,0:T(8,128)(2,1)} %bitcast.32), calls=%async_computation.3 | async-start | bytes 983040 | tf_op jit(solution)/shard_map/all_to_all | solution.py:1164
  353.4 13.4 %all-to-all-start.4 = ((bf16[4,80,768]{2,1,0:T(8,128)(2,1)}), bf16[4,80,768]{2,1,0:T(8,128)(2,1)S(1)}, u32[]{:S(2)}, u32[]{:S(2)}) async-start(bf16[4,80,768]{2,1,0:T(8,128)(2,1)} %broadcast_in_dim.83), calls=%async_computation.4 | async-start | bytes 983040 | tf_op jit(solution)/shard_map/all_to_all | solution.py:1168
  358.1 8.9 %copy-start.20 = (f32[32,2048]{1,0:T(8,128)S(1)}, f32[32,2048]{1,0:T(8,128)}, u32[]{:S(2)}) copy-start(f32[32,2048]{1,0:T(8,128)} %param.18) | copy-start | bytes 786436
  366.8 8.4 %collective-permute-start.8 = (bf16[288,768]{1,0:T(8,128)(2,1)S(1)}, bf16[288,768]{1,0:T(8,128)(2,1)S(1)}, u32[]{:S(2)}, u32[]{:S(2)}) collective-permute-start(bf16[288,768]{1,0:T(8,128)(2,1)S(1)} %slice.116), channel_id=1, source_target_pairs={{0,2},{1,3},{2,0},{3,1},{4,6},{5,7},{6,4},{7,5},{8,10},{9,11},{10,... | collective-permute-start | bytes 1327112 | tf_op jit(solution)/shard_map/ppermute | solution.py:1154
  368.7 4.1 collective-permute-start.9
  375.2 2.2 copy-start.26
  375.2 2.2 copy-start.30
  375.2 3.0 copy-start.27
  375.2 3.1 copy-start.28
  379.7 1.8 copy-start.6
  381.5 13.3 %copy-start.29 = (f32[128]{0:T(128)S(1)}, f32[128]{0:T(128)}, u32[]{:S(2)}) copy-start(f32[128]{0:T(128)} %pad.48.clone) | copy-start | bytes 1540
  389.4 15.1 %all-to-all-start.5 = ((f32[32,1,128]{2,1,0:T(1,128)}), f32[32,1,128]{2,1,0:T(1,128)S(1)}, u32[]{:S(2)}, u32[]{:S(2)}) async-start(f32[32,1,128]{2,1,0:T(1,128)} %broadcast_in_dim.91), calls=%async_computation.5 | async-start | bytes 32768 | tf_op jit(solution)/shard_map/all_to_all | solution.py:1205
  395.9 2.0 copy-start.2
  397.9 8.0 %copy-start.22 = (f32[32,2048]{1,0:T(8,128)S(1)}, f32[32,2048]{1,0:T(8,128)}, u32[]{:S(2)}) copy-start(f32[32,2048]{1,0:T(8,128)} %param.21) | copy-start | bytes 786436
  397.9 8.0 %copy-start.24 = (f32[32,2048]{1,0:T(8,128)S(1)}, f32[32,2048]{1,0:T(8,128)}, u32[]{:S(2)}) copy-start(f32[32,2048]{1,0:T(8,128)} %param.19) | copy-start | bytes 786436
  403.3 1.2 copy-start
  404.5 3.5 copy-start.1
  (4 other events, 3.3 us)
Sparse Core Ops, SparseCore 0:
  49.2 152.5 all-gather.6
  257.2 52.2 all-gather.8
  312.3 45.2 all-gather.10

commit v5 on v4

--- a/solution.py
+++ b/solution.py
@@ -64,12 +64,23 @@
 SET = 288
 SHARED = 32
 STEPS = 64
-AHEAD = 3 * D + F + 2 * H
-BEHIND = 5 * D + F + B + 2 * H
+AHEAD = 3 * D + F + H
 TILE = 16
 TOKENS = 208
 HEADROWS = 16
-VMEM_LIMIT = 60 * 1024 * 1024
+VMEM_LIMIT = 62 * 1024 * 1024
+
+
+SPANS = {
+    2: (0, 0),
+    3: (D, D),
+    4: (2 * D, D + F),
+    6: (2 * D + F, 2 * D + F + B + H),
+    7: (3 * D + F, 2 * D + F + B),
+}
+ATT_COLUMN = 2 * D + F + B + 2 * H
+SECOND = HEADS * D
+CLASS = SECOND + H
 
 
 def round_up(value, step):
@@ -128,8 +139,10 @@
         owners = [device for device in range(count) if device * self.size < edge]
         self.odd_owner = any(self.place(device)[1] for device in owners)
         self.all_sets = len(owners) > 2
-        self.grad_table = self.tabulate(lambda index: index)
-        self.late_table = self.tabulate(lambda index: index < 2, self.wide_row)
+        self.sent = [[] for _ in range(count)]
+        self.grad_table = self.tabulate(lambda index: index, self.sent_row)
+        self.late_table = self.tabulate(lambda index: index in (0, 1, 5), self.wide_row)
+        self.reach = max(place + size for sent in self.sent for _, size, place in sent)
         self.grad_scratch = FRONT + self.lines + CHUNK * max(WIDTHS) + 16
 
 
@@ -141,7 +154,7 @@
         rep, grp = divmod(device, self.groups)
         return rep // 2 * self.groups + grp, rep % 2
 
-    def tabulate(self, chosen, rows_of=lambda device, index, row0: row0):
+    def tabulate(self, chosen, rows_of):
         table = []
         for device in range(self.count):
             start = device * self.size
@@ -152,7 +165,7 @@
                 skew = row0 % 8
                 line -= skew * (PIECES[index][2] // LANES)
                 chunks = -(-(rows + skew) // CHUNK)
-                entry += [index, FRONT + line, chunks, rows_of(device, index, row0 - skew)]
+                entry += [index, FRONT + line, chunks, rows_of(device, index, row0 - skew, chunks)]
             table.append(entry)
         most = max(len(entry) for entry in table) // 4
         for device, entry in enumerate(table):
@@ -160,7 +173,15 @@
             entry.insert(0, device * self.size % LANES)
         return np.array(table, np.int32)
 
-    def wide_row(self, device, index, row0):
+    def sent_row(self, device, index, row0, chunks):
+        if index not in SPANS:
+            return row0
+        sent, size = self.sent[device], chunks * CHUNK
+        place = sum(before for _, before, _ in sent)
+        sent.append((SPANS[index][0] + row0, size, place))
+        return place
+
+    def wide_row(self, device, index, row0, chunks):
         if index:
             return row0
         late = row0 >= 2 * SET - 8
@@ -432,25 +453,31 @@
     plan,
     gathered_ref,
     pixels_ref,
-    unit_ref,
-    scale_ref,
+    turn_ref,
+    unit_out,
+    scale_out,
     probs_ref,
     mixed_ref,
     looked_ref,
     class_ref,
-    qkv_ref,
-    pack_ref,
+    qkv_out,
+    second_ref,
     hidden_ref,
     one_ref,
     two_ref,
     bottle_ref,
     middle_ref,
-    rows_ref,
+    send_ref,
     shards_ref,
     wide_ref,
     place_ref,
     left_ref,
     sums_ref,
+    pack_ref,
+    unit_ref,
+    scale_ref,
+    qkv_ref,
+    out_sems,
     sems,
 ):
     shards = Shards(plan, gathered_ref, shards_ref, sems, range(plan.count))
@@ -464,6 +491,8 @@
     class_unit, class_scale = normalised(class_place)
     class_normed = (class_unit * norms[0:1] + norms[1:2]).astype(BF16).astype(F32)
     shards.assemble(1, qkv_ref)
+    qkv_copy = pltpu.make_async_copy(qkv_ref, qkv_out, out_sems.at[4])
+    qkv_copy.start()
     mask = head_mask()
     query = jnp.broadcast_to(class_normed, (HEADROWS, D)).astype(BF16)
     query = product(query, qkv_ref[:, :D]).astype(BF16).astype(F32)
@@ -471,11 +500,26 @@
     looked = product_t(by_head, qkv_ref[:, D : 2 * D]).astype(BF16)
     looked_ref[...] = looked
 
+    def copies(v):
+        slot = lax.rem(v, 2)
+        return (
+            pltpu.make_async_copy(unit_ref.at[slot], unit_out.at[v], out_sems.at[slot]),
+            pltpu.make_async_copy(scale_ref.at[slot], scale_out.at[v], out_sems.at[2 + slot]),
+        )
+
     def view(v, carry):
         embedded = product(pixels_ref[v], wide_ref[:PD]) + place_ref[...]
         unit, scale = normalised(embedded)
-        unit_ref[v] = unit
-        scale_ref[v] = jnp.broadcast_to(scale, (TOKENS, LANES))
+
+        @pl.when(v >= 2)
+        def _():
+            for copy in copies(v - 2):
+                copy.wait()
+
+        unit_ref[lax.rem(v, 2)] = unit
+        scale_ref[lax.rem(v, 2)] = jnp.broadcast_to(scale, (TOKENS, LANES))
+        for copy in copies(v):
+            copy.start()
         normed = token_norms(unit, norms, class_normed)
         scores = product_t(looked, normed) * temper
         token = lax.broadcasted_iota(jnp.int32, scores.shape, 1)
@@ -492,16 +536,16 @@
     mixed = mixed_ref[...].reshape(views * HEADROWS, D)
     valued = product(mixed, qkv_ref[:, 2 * D :]).reshape(views, HEADROWS, D)
     attended = jnp.sum(jnp.where(mask[None], valued, 0.0), 1).astype(BF16)
-    pack_ref[:, :D] = attended
-    shards.times(2, 0, attended.astype(F32), left_ref, sums_ref)
+    pack_ref[:, :D] = attended.astype(F32)
+    shards.times(2, 0, pack_ref[:, :D], left_ref, sums_ref)
     middle = class_place + sums_ref[...]
     unit, scale = normalised(middle)
     middle_ref[0], middle_ref[1] = unit, jnp.broadcast_to(scale, (views, D))
     normed = (unit * norms[2:3] + norms[3:4]).astype(BF16)
-    pack_ref[:, D : 2 * D] = normed
-    shards.times(3, 0, normed.astype(F32), left_ref, hidden_ref)
+    pack_ref[:, D : 2 * D] = normed.astype(F32)
+    shards.times(3, 0, pack_ref[:, D : 2 * D], left_ref, hidden_ref)
     act = activate(hidden_ref[...]).astype(BF16)
-    pack_ref[:, 2 * D : 2 * D + F] = act
+    pack_ref[:, 2 * D : 2 * D + F] = act.astype(F32)
     shards.times(4, 0, act.astype(F32), left_ref, sums_ref)
     unit, scale = normalised(middle + sums_ref[...])
     middle_ref[2], middle_ref[3] = unit, jnp.broadcast_to(scale, (views, D))
@@ -510,17 +554,26 @@
     )
     cls = (unit * final[0:1] + final[1:2]).astype(BF16)
     place = 2 * D + F
-    pack_ref[:, place : place + D] = cls
+    pack_ref[:, place : place + D] = cls.astype(F32)
     shards.times(5, 0, cls.astype(F32), left_ref, one_ref)
     first = activate(one_ref[...]).astype(BF16)
-    pack_ref[:, place + D : place + D + H] = first
+    pack_ref[:, place + D : AHEAD] = first.astype(F32)
+    pack_ref[:, AHEAD:] = jnp.zeros((views, pack_ref.shape[1] - AHEAD), F32)
     shards.times(5, D, first.astype(F32), left_ref, two_ref)
     second = activate(two_ref[...]).astype(BF16)
-    pack_ref[:, place + D + H :] = second
+    second_ref[...] = second
     shards.times(6, 0, second.astype(F32), left_ref, bottle_ref)
     bottle = bottle_ref[...]
     scale = lax.rsqrt(jnp.sum(bottle * bottle, -1, keepdims=True) + 1e-06)
-    rows_ref[...] = (bottle * scale).astype(BF16)
+    rows = product(turn_ref[...], (bottle * scale).astype(BF16)).astype(BF16)
+    for device, sent in enumerate(plan.sent):
+        send_ref[device, :, :B] = rows
+        for lane, size, place in sent:
+            start = lane // LANES * LANES
+            piece = pack_ref[:, start : start + size + (LANES if lane > start else 0)]
+            if lane > start:
+                piece = pltpu.roll(piece, piece.shape[1] - (lane - start), 1)
+            send_ref[device, :, B + place : B + place + size] = piece[:, :size].astype(BF16)
     class_ref[...] = jnp.concatenate(
         [
             class_unit,
@@ -532,10 +585,14 @@
         ],
         0,
     )
+    for v in range(max(0, views - 2), views):
+        for copy in copies(v):
+            copy.wait()
+    qkv_copy.wait()
     shards.finish()
 
 
-def forward(plan, gathered, pixels):
+def forward(plan, gathered, pixels, turn):
     views = pixels.shape[0]
     shapes = [
         ((views, TOKENS, D), F32),
@@ -545,42 +602,169 @@
         ((HEADROWS, D), BF16),
         ((16, D), F32),
         ((D, 3 * D), BF16),
-        ((views, 3 * D + F + 2 * H), BF16),
+        ((views, H), BF16),
         ((views, F), F32),
         ((views, H), F32),
         ((views, H), F32),
         ((views, B), F32),
         ((4, views, D), F32),
-        ((views, B), BF16),
+        ((plan.count, views, B + plan.reach), BF16),
     ]
     most, longest = plan.largest()
     return pl.pallas_call(
         functools.partial(forward_kernel, plan),
         out_shape=[jax.ShapeDtypeStruct(shape, dtype) for shape, dtype in shapes],
-        in_specs=[
-            pl.BlockSpec(memory_space=pl.ANY),
-            pl.BlockSpec(memory_space=pltpu.VMEM),
+        in_specs=[pl.BlockSpec(memory_space=pl.ANY)]
+        + [pl.BlockSpec(memory_space=pltpu.VMEM)] * 2,
+        out_specs=[
+            pl.BlockSpec(memory_space=pl.ANY if index in (0, 1, 6) else pltpu.VMEM)
+            for index in range(len(shapes))
         ],
-        out_specs=[pl.BlockSpec(memory_space=pltpu.VMEM)] * len(shapes),
         scratch_shapes=[
             pltpu.VMEM((plan.count, plan.buffer // TILE, TILE, LANES), BF16),
             pltpu.VMEM((round_up(PD + NTOK + 4, TILE), D), BF16),
             pltpu.VMEM((TOKENS, D), F32),
             pltpu.VMEM((most, views, longest), F32),
             pltpu.VMEM((views, D), F32),
+            pltpu.VMEM((views, round_up(AHEAD + CHUNK, LANES) + LANES), F32),
+            pltpu.VMEM((2, TOKENS, D), F32),
+            pltpu.VMEM((2, TOKENS, LANES), F32),
+            pltpu.VMEM((D, 3 * D), BF16),
+            pltpu.SemaphoreType.DMA((5,)),
             pltpu.SemaphoreType.DMA((plan.count,)),
         ],
         compiler_params=pltpu.CompilerParams(vmem_limit_bytes=VMEM_LIMIT),
         cost_estimate=pl.CostEstimate(
             flops=60 * 10**9, bytes_accessed=40 * 10**6, transcendentals=10**5
         ),
-    )(gathered, pixels)
+    )(gathered, pixels, turn)
+
+
+def proto_kernel(
+    start_ref,
+    rows_ref,
+    columns_ref,
+    others_ref,
+    center_ref,
+    note_ref,
+    center_out_ref,
+    student_ref,
+    teacher_ref,
+    sums_ref,
+):
+    count, groups = rows_ref.shape[1], note_ref.shape[0]
+    views = (note_ref.shape[1] - 8 * -(-count // B)) // 3
+    logits = product(rows_ref[1], others_ref[...])
+    center = center_ref[...]
+    center_out_ref[...] = CENTER_MOMENTUM * center + (1.0 - CENTER_MOMENTUM) * jnp.mean(
+        logits, 0, keepdims=True
+    )
+    exp_teacher = jnp.exp((logits - center) / TEACHER_TEMP)
+    teacher_ref[...] = exp_teacher
+    scaled = product(rows_ref[0], columns_ref[...]) / STUDENT_TEMP
+    exp_student = jnp.exp(scaled)
+    student_ref[...] = exp_student
+    turned = []
+    for which, values in enumerate((exp_student, exp_teacher, exp_teacher * scaled)):
+        total = jnp.broadcast_to(jnp.sum(values, 1, keepdims=True), (count, LANES))
+        turned.append(total.T[0:1])
+        if which < 2:
+            sums_ref[:, which * LANES : (which + 1) * LANES] = total
+    turned = jnp.concatenate(turned + [jnp.zeros((5, count), F32)], 0)
+    for step in range(-(-count // B)):
+        part = turned[:, step * B : (step + 1) * B]
+        lines = slice(3 * views + 8 * step, 3 * views + 8 * (step + 1))
+        note_ref[:, lines, : part.shape[1]] = jnp.broadcast_to(part[None], (groups,) + part.shape)
+        if part.shape[1] < B:
+            note_ref[:, lines, part.shape[1] :] = jnp.zeros((groups, 8, B - part.shape[1]), F32)
+    start = pl.multiple_of(start_ref[0], 8)
+    columns = columns_ref[...].astype(F32)
+    for which, source in enumerate((student_ref, teacher_ref)):
+        pulls = lax.dot_general(
+            source[pl.ds(start, groups * views), :],
+            columns,
+            (((1,), (1,)), ((), ())),
+            precision=PRECISE,
+            preferred_element_type=F32,
+        )
+        note_ref[:, which * views : (which + 1) * views, :] = pulls.reshape(groups, views, B)
+    own = sums_ref[pl.ds(start, groups * views), :]
+    note_ref[:, 2 * views : 3 * views, :] = own.reshape(groups, views, B)
+
+
+def prototypes(start, rows, columns, others, center, groups, views):
+    count, width = rows.shape[1], columns.shape[1]
+    shapes = [(groups, 3 * views + 8 * -(-count // B), B), (1, width)]
+    return pl.pallas_call(
+        proto_kernel,
+        out_shape=[jax.ShapeDtypeStruct(shape, F32) for shape in shapes],
+        in_specs=[pl.BlockSpec(memory_space=pltpu.SMEM)]
+        + [pl.BlockSpec(memory_space=pltpu.VMEM)] * 4,
+        out_specs=[pl.BlockSpec(memory_space=pltpu.VMEM)] * len(shapes),
+        scratch_shapes=[pltpu.VMEM((count, width), F32)] * 2
+        + [pltpu.VMEM((count, 2 * LANES), F32)],
+        compiler_params=pltpu.CompilerParams(vmem_limit_bytes=32 * 1024 * 1024),
+        cost_estimate=pl.CostEstimate(
+            flops=3 * 10**9, bytes_accessed=6 * 10**6, transcendentals=10**6
+        ),
+    )(start, rows, columns, others, center)
+
+
+def proto_back_kernel(
+    start_ref,
+    rows_ref,
+    columns_ref,
+    others_ref,
+    center_ref,
+    totals_ref,
+    table_ref,
+    scale_ref,
+    grad_ref,
+    square_ref,
+    work_ref,
+):
+    count = rows_ref.shape[1]
+    totals = jnp.broadcast_to(totals_ref[0:2][:, None, :], (2, 8, count))
+    student, teacher = (totals[which].T[:, :1] for which in range(2))
+    logits = product(rows_ref[1], others_ref[...])
+    targets = jnp.exp((logits - center_ref[...]) / TEACHER_TEMP) / teacher
+    scaled = product(rows_ref[0], columns_ref[...]) / STUDENT_TEMP
+    grad = (jnp.exp(scaled) / student - targets) / STUDENT_TEMP
+    work_ref[...] = jnp.dot(
+        rows_ref[0].astype(F32).T, grad, precision=PRECISE, preferred_element_type=F32
+    )
+    scale = scale_ref[...]
+    inner = jnp.sum(work_ref[...] * table_ref[...], 0, keepdims=True)
+    start = pl.multiple_of(start_ref[0], 8)
+    lines = pl.ds(start, grad_ref.shape[0])
+    grad = work_ref[lines, :] * scale - table_ref[lines, :] * (scale * scale * scale * inner)
+    grad_ref[...] = grad
+    square = jnp.sum(grad * grad, 0, keepdims=True)
+    square_ref[...] = jnp.broadcast_to(square, square_ref.shape)
+
+
+def prototypes_back(start, depth, *values):
+    count, width = values[0].shape[1], values[1].shape[1]
+    shapes = [(depth, width), (8, width)]
+    return pl.pallas_call(
+        proto_back_kernel,
+        out_shape=[jax.ShapeDtypeStruct(shape, F32) for shape in shapes],
+        in_specs=[pl.BlockSpec(memory_space=pltpu.SMEM)]
+        + [pl.BlockSpec(memory_space=pltpu.VMEM)] * len(values),
+        out_specs=[pl.BlockSpec(memory_space=pltpu.VMEM)] * len(shapes),
+        scratch_shapes=[pltpu.VMEM((B, width), F32)],
+        compiler_params=pltpu.CompilerParams(vmem_limit_bytes=32 * 1024 * 1024),
+        cost_estimate=pl.CostEstimate(
+            flops=3 * 10**9, bytes_accessed=6 * 10**6, transcendentals=10**6
+        ),
+    )(start, *values)
 
 
 def rows_back_kernel(
     plan,
+    low_ref,
     gathered_ref,
-    grad_ref,
+    note_ref,
     class_ref,
     hidden_ref,
     one_ref,
@@ -600,7 +784,13 @@
     work = (values_ref, left_ref, wide_ref)
     norms, final = class_ref[4:8], class_ref[8:10]
 
-    grad_rows, bottle = grad_ref[...], bottle_ref[...]
+    views = bottle_ref.shape[0]
+    note = jnp.sum(note_ref[...], 0)
+    sums = note[2 * views : 3 * views]
+    student, teacher = sums[:, :1], sums[:, LANES : LANES + 1]
+    grad_rows = (note[:views] / student - note[views : 2 * views] / teacher) / STUDENT_TEMP
+    grad_rows = jnp.where(low_ref[0] == 0, 0.0, grad_rows).astype(BF16).astype(F32)
+    bottle = bottle_ref[...]
     scale = lax.rsqrt(jnp.sum(bottle * bottle, -1, keepdims=True) + 1e-06)
     grad_bottle = (
         grad_rows * scale - bottle * scale**3 * jnp.sum(grad_rows * bottle, -1, keepdims=True)
@@ -615,8 +805,8 @@
     pack_ref[:, place + B + H : place + B + 2 * H] = grad_one
     grad_cls = shards.back(5, 0, D, grad_one.astype(F32), *work)
     unit, scale = middle_ref[2], middle_ref[3]
-    pack_ref[:, place + B + 2 * H + D : place + B + 2 * H + 2 * D] = (grad_cls * unit).astype(BF16)
-    pack_ref[:, place + B + 2 * H + 2 * D :] = grad_cls.astype(BF16)
+    gain_last = jnp.sum(grad_cls * unit, 0, keepdims=True)
+    shift_last = jnp.sum(grad_cls, 0, keepdims=True)
     grad_stream = norm_back(grad_cls, final[0:1], unit, scale)
     grad_branch = grad_stream.astype(BF16)
     pack_ref[:, D + F : 2 * D + F] = grad_branch
@@ -629,7 +819,9 @@
         [
             jnp.sum(grad_normed * unit, 0, keepdims=True),
             jnp.sum(grad_normed, 0, keepdims=True),
-            jnp.zeros((6, D), F32),
+            gain_last,
+            shift_last,
+            jnp.zeros((4, D), F32),
         ],
         0,
     )
@@ -642,14 +834,14 @@
     shards.finish()
 
 
-def rows_back(plan, gathered, grad_rows, kept):
-    views = grad_rows.shape[0]
-    shapes = [((views, 5 * D + F + B + 2 * H), BF16), ((views, D), F32), ((8, D), F32)]
+def rows_back(plan, low, gathered, note, kept):
+    views = kept[-1].shape[1]
+    shapes = [((views, 3 * D + F + B + 2 * H), BF16), ((views, D), F32), ((8, D), F32)]
     most, longest = plan.largest()
     return pl.pallas_call(
         functools.partial(rows_back_kernel, plan),
         out_shape=[jax.ShapeDtypeStruct(shape, dtype) for shape, dtype in shapes],
-        in_specs=[pl.BlockSpec(memory_space=pl.ANY)]
+        in_specs=[pl.BlockSpec(memory_space=pltpu.SMEM), pl.BlockSpec(memory_space=pl.ANY)]
         + [pl.BlockSpec(memory_space=pltpu.VMEM)] * (1 + len(kept)),
         out_specs=[pl.BlockSpec(memory_space=pltpu.VMEM)] * len(shapes),
         scratch_shapes=[
@@ -659,11 +851,11 @@
             pltpu.VMEM((views, F + 2 * LANES), F32),
             pltpu.SemaphoreType.DMA((plan.count,)),
         ],
-        compiler_params=pltpu.CompilerParams(vmem_limit_bytes=VMEM_LIMIT),
+        compiler_params=pltpu.CompilerParams(vmem_limit_bytes=40 * 1024 * 1024),
         cost_estimate=pl.CostEstimate(
             flops=30 * 10**9, bytes_accessed=30 * 10**6, transcendentals=10**5
         ),
-    )(gathered, grad_rows, *kept)
+    )(low, gathered, note, *kept)
 
 
 def tokens_back_kernel(
@@ -678,6 +870,8 @@
     class_ref,
     qkv_ref,
     pixels_ref,
+    first_ref,
+    second_ref,
     kept_ref,
     sent_ref,
     patch_ref,
@@ -749,9 +943,10 @@
             tail = jnp.where(token == row, value, tail)
         upper = 2 * SET - 8
         rest = jnp.zeros((2 * SET - (PD - upper) - TOKENS, D), F32)
-        query_row = lax.broadcasted_iota(jnp.int32, (SHARED - HEADROWS, D), 0) == 0
+        query_row = lax.broadcasted_iota(jnp.int32, (8, D), 0) == 0
         total = jnp.sum(grad_query.astype(F32), 0, keepdims=True)
-        shared = jnp.concatenate([reach_ref[...], jnp.where(query_row, total, 0.0)], 0)
+        shared = [reach_ref[...], jnp.where(query_row, total, pltpu.roll(ends_ref[...], 7, 0))]
+        shared = jnp.concatenate(shared + [jnp.zeros((SHARED - HEADROWS - 8, D), F32)], 0)
         kept_ref[2 * SET :] = shared
         sent_ref[2 * SET :] = shared.astype(BF16)
         last = jnp.concatenate([patch_ref[upper:], tail, rest], 0)
@@ -767,7 +962,7 @@
             sent_ref[: 2 * SET] = patch_ref[: 2 * SET].astype(BF16)
 
 
-def tokens_back(odd, behind, grad_middle, ends, kept, pixels):
+def tokens_back(odd, behind, grad_middle, ends, kept, pixels, *before):
     views = grad_middle.shape[0]
 
     def whole(values):
@@ -794,7 +989,8 @@
             whole(classes),
             whole(qkv_w),
             by_view(pixels),
-        ],
+        ]
+        + [pl.BlockSpec(memory_space=pl.ANY)] * len(before),
         out_specs=[pl.BlockSpec(shape, lambda v: (0, 0))] * 2,
         scratch_shapes=[
             pltpu.VMEM((PD, D), F32),
@@ -804,30 +1000,38 @@
             pltpu.VMEM((views, HEADROWS, D), BF16),
             pltpu.VMEM((3, 8, D), F32),
         ],
-        compiler_params=pltpu.CompilerParams(vmem_limit_bytes=40 * 1024 * 1024),
+        compiler_params=pltpu.CompilerParams(vmem_limit_bytes=60 * 1024 * 1024),
         cost_estimate=pl.CostEstimate(
             flops=15 * 10**9, bytes_accessed=15 * 10**6, transcendentals=10**5
         ),
-    )(odd, behind, grad_middle, ends, unit, scale, probs, looked, classes, qkv_w, pixels)
-
-
-SPANS = {
-    2: (0, 0),
-    3: (D, D),
-    4: (2 * D, D + F),
-    6: (2 * D + F, 2 * D + F + B + H),
-    7: (3 * D + F, 2 * D + F + B),
-    8: (3 * D + F + H, 2 * D + F),
-}
-ATT_COLUMN = 2 * D + F + B + 2 * H
-
-
-def early_kernel(plan, most, tab_ref, ahead_ref, behind_ref, line_ref, square_ref):
+    )(odd, behind, grad_middle, ends, unit, scale, probs, looked, classes, qkv_w, pixels, *before)
+
+
+def early_kernel(
+    plan,
+    most,
+    tab_ref,
+    ahead_ref,
+    common_hbm,
+    behind_hbm,
+    line_ref,
+    square_ref,
+    common_ref,
+    behind_ref,
+    sem,
+):
     line_ref[...] = jnp.zeros(line_ref.shape, F32)
+
+    def fetch(source, target, column, size):
+        copy = pltpu.make_async_copy(
+            source.at[:, pl.ds(column, size)], target.at[:, pl.ds(0, size)], sem
+        )
+        copy.start()
+        copy.wait()
 
     def turned(lane):
         start = pl.multiple_of(lane // LANES * LANES, LANES)
-        both = ahead_ref[:, pl.ds(start, 2 * LANES)].astype(F32)
+        both = common_ref[:, pl.ds(start, 2 * LANES)].astype(F32)
         both = pltpu.roll(both, lax.rem(2 * LANES - (lane - start), 2 * LANES), 1)
         return both[:, :LANES].T.astype(BF16)
 
@@ -836,48 +1040,63 @@
 
     for part in range(most):
         kind, base, chunks, row0 = (tab_ref[1 + 4 * part + i] for i in range(4))
-        for index, (lane, column) in SPANS.items():
+        for index, (_, column) in SPANS.items():
             cols = PIECES[index][2]
             width = cols // LANES
 
             @pl.when(kind == index)
-            def _(lane=lane, column=column, cols=cols, width=width):
+            def _(column=column, cols=cols, width=width):
+                fetch(behind_hbm, behind_ref, column, cols)
+
                 def move(step, carry):
                     goal = base + step * (CHUNK * width)
-                    left = turned(lane + row0 + step * CHUNK)
-                    block = product(left, behind_ref[:, column : column + cols])
+                    lanes = pl.ds(pl.multiple_of(row0 + step * CHUNK, LANES), CHUNK)
+                    left = ahead_ref[:, lanes].astype(F32).T.astype(BF16)
+                    block = product(left, behind_ref[:, :cols])
                     for tile in range(width):
                         store(goal, width, tile, block[:, tile * LANES : (tile + 1) * LANES])
                     return carry
 
                 lax.fori_loop(0, chunks, move, 0)
 
+        @pl.when(kind == 8)
+        def _():
+            fetch(behind_hbm, behind_ref, 2 * D + F, B)
+            fetch(common_hbm, common_ref, SECOND, H + D)
+
+            def move(step, carry):
+                left = turned(row0 + step * CHUNK)
+                block = product(left, behind_ref[:, :B])
+                for tile in range(B // LANES):
+                    piece = block[:, tile * LANES : (tile + 1) * LANES]
+                    store(base + step * (CHUNK * B // LANES), B // LANES, tile, piece)
+                return carry
+
+            lax.fori_loop(0, chunks, move, 0)
+
+        @pl.when(kind == 5)
+        def _():
+            for tile in range(D // LANES):
+                store(base, D // LANES, tile, jnp.zeros((8, LANES), F32))
+
         @pl.when(kind == 1)
         def _():
+            fetch(behind_hbm, behind_ref, ATT_COLUMN, D)
+            fetch(common_hbm, common_ref, 0, common_ref.shape[1])
+
             def move(step, carry):
                 width = 3 * D // LANES
                 goal = base + step * (CHUNK * width)
                 side = lax.broadcasted_iota(jnp.int32, (CHUNK, LANES), 1)
                 for pair in range(HEADS // 2):
-                    column = ATT_COLUMN + pair * LANES
-                    right = behind_ref[:, column : column + LANES]
-                    lane = AHEAD + 2 * pair * D + row0 + step * CHUNK
+                    right = behind_ref[:, pair * LANES : (pair + 1) * LANES]
+                    lane = 2 * pair * D + row0 + step * CHUNK
                     first, second = (product(turned(lane + D * head), right) for head in range(2))
                     block = jnp.where(side < HDIM, first, second)
                     store(goal, width, 2 * D // LANES + pair, block)
                 return carry
 
             lax.fori_loop(0, chunks, move, 0)
-
-        @pl.when(kind == 5)
-        def _():
-            ends = jnp.sum(behind_ref[:, BEHIND - 2 * D :].astype(F32), 0, keepdims=True)
-            for tile in range(D // LANES):
-                rows = [
-                    ends[:, place + tile * LANES : place + (tile + 1) * LANES] for place in (0, D)
-                ]
-                rows.append(jnp.zeros((6, LANES), F32))
-                store(base, D // LANES, tile, jnp.concatenate(rows, 0))
 
     shift = tab_ref[0]
     shape = (STEPS, LANES)
@@ -896,25 +1115,49 @@
     square_ref[...] = jnp.sum(total.reshape(STEPS // 8, 8, LANES), 0)
 
 
-def early_gradient(plan, table, ahead, behind):
+def early_gradient(plan, table, ahead, common, behind):
     return pl.pallas_call(
         functools.partial(early_kernel, plan, table.shape[0] // 4),
         out_shape=[
             jax.ShapeDtypeStruct((plan.grad_scratch, LANES), F32),
             jax.ShapeDtypeStruct((8, LANES), F32),
         ],
-        in_specs=[pl.BlockSpec(memory_space=pltpu.SMEM)]
-        + [pl.BlockSpec(memory_space=pltpu.VMEM)] * 2,
+        in_specs=[
+            pl.BlockSpec(memory_space=pltpu.SMEM),
+            pl.BlockSpec(memory_space=pltpu.VMEM),
+            pl.BlockSpec(memory_space=pl.ANY),
+            pl.BlockSpec(memory_space=pl.ANY),
+        ],
         out_specs=[pl.BlockSpec(memory_space=pltpu.VMEM)] * 2,
-        compiler_params=pltpu.CompilerParams(vmem_limit_bytes=48 * 1024 * 1024),
+        scratch_shapes=[
+            pltpu.VMEM(common.shape, BF16),
+            pltpu.VMEM((behind.shape[0], F), BF16),
+            pltpu.SemaphoreType.DMA,
+        ],
+        compiler_params=pltpu.CompilerParams(vmem_limit_bytes=60 * 1024 * 1024),
         cost_estimate=pl.CostEstimate(
             flops=10 * 10**9, bytes_accessed=10 * 10**6, transcendentals=0
         ),
-    )(table, ahead, behind)
-
-
-def late_kernel(plan, most, tab_ref, lines_ref, wide_ref, left_ref, right_ref, out_ref, line_ref):
-    line_ref[...] = lines_ref[...]
+    )(table, ahead, common, behind)
+
+
+def late_kernel(
+    plan,
+    most,
+    tab_ref,
+    lines_ref,
+    wide_ref,
+    left_ref,
+    right_ref,
+    ends_ref,
+    out_ref,
+    line_ref,
+    sem,
+):
+    used = FRONT + plan.lines + 8
+    copy = pltpu.make_async_copy(lines_ref.at[pl.ds(0, used)], line_ref.at[pl.ds(0, used)], sem)
+    copy.start()
+    copy.wait()
 
     def add(goal, width, tile, block):
         lines = pl.ds(goal + tile, CHUNK, stride=width)
@@ -953,6 +1196,14 @@
 
             lax.fori_loop(0, chunks, move, 0)
 
+        @pl.when(kind == 5)
+        def _():
+            width = D // LANES
+            for tile in range(width):
+                lines = pl.ds(base + tile, 8, stride=width)
+                block = ends_ref[:, tile * LANES : (tile + 1) * LANES]
+                line_ref[lines, :] = line_ref[lines, :] + block
+
     shift = tab_ref[0]
     turn = lax.rem(LANES - shift, LANES)
     lane = lax.broadcasted_iota(jnp.int32, (STEPS + 8, LANES), 1)
@@ -969,16 +1220,19 @@
     lax.fori_loop(0, plan.lines // STEPS, align, 0)
 
 
-def late_gradient(plan, table, lines, wide, left, right):
+def late_gradient(plan, table, lines, *values):
     return pl.pallas_call(
         functools.partial(late_kernel, plan, table.shape[0] // 4),
         out_shape=jax.ShapeDtypeStruct((plan.lines, LANES), F32),
-        in_specs=[pl.BlockSpec(memory_space=pltpu.SMEM)]
-        + [pl.BlockSpec(memory_space=pltpu.VMEM)] * 4,
+        in_specs=[pl.BlockSpec(memory_space=pltpu.SMEM), pl.BlockSpec(memory_space=pl.ANY)]
+        + [pl.BlockSpec(memory_space=pltpu.VMEM)] * len(values),
         out_specs=pl.BlockSpec(memory_space=pltpu.VMEM),
-        scratch_shapes=[pltpu.VMEM((plan.grad_scratch, LANES), F32)],
-        compiler_params=pltpu.CompilerParams(vmem_limit_bytes=32 * 1024 * 1024),
-    )(table, lines, wide, left, right).reshape(-1)[: plan.size]
+        scratch_shapes=[
+            pltpu.VMEM((plan.grad_scratch, LANES), F32),
+            pltpu.SemaphoreType.DMA,
+        ],
+        compiler_params=pltpu.CompilerParams(vmem_limit_bytes=24 * 1024 * 1024),
+    )(table, lines, *values).reshape(-1)[: plan.size]
 
 
 def adam_update(weight, grad, first, second, rate):
@@ -1030,27 +1284,28 @@
         return jnp.where(low, values, other), jnp.where(low, other, values)
 
     pairs = [list(range(parity, reps, 2)) for parity in (0, 1)]
+    lines = reps // 2
     tables = jnp.stack([protos, teacher_protos]).astype(BF16)
-    tables = lax.all_to_all(
-        jnp.broadcast_to(tables[None], (reps // 2,) + tables.shape),
-        "rep",
-        0,
-        0,
-        axis_index_groups=pairs,
-    )
+    around = [tables]
+    for step in range(2, reps, 2):
+        around.append(lax.ppermute(tables, "rep", [(r, (r + step) % reps) for r in range(reps)]))
 
     table = jnp.asarray(plan.lay_table)[device]
+    given = trade(lay_out(plan, table, jnp.where(low, teacher, params)))
     kept = lay_out(plan, table, jnp.where(low, params, teacher))
-    given = trade(lay_out(plan, table, jnp.where(low, teacher, params)))
-    patches, partner, tables, given = lax.optimization_barrier((patches, partner, tables, given))
+    given, around = lax.optimization_barrier((given, around))
     shards = jnp.stack([jnp.where(low, kept, given), jnp.where(low, given, kept)])
     gathered = lax.all_gather(shards, BOTH, axis=0, axis_index_groups=halves)
     gathered = gathered.reshape(half, 2, -1, TILE, LANES)
+    patches, partner, given = lax.optimization_barrier((patches, partner, given))
     pixels = jnp.concatenate(in_order(patches), 0)
     pixels = jnp.pad(pixels, ((0, 0), (0, TOKENS - NPATCH), (0, 0)))
-    tables = jnp.stack(in_order(tables))
+    around = jnp.concatenate([jnp.stack(around[::-1])] * 2)
+    around = lax.dynamic_slice_in_dim(around, lines - 1 - rep // 2, lines, 0)
+    tables = jnp.stack(in_order(around))
     tables = tables.transpose(2, 1, 0, 3, 4).reshape(2, B, -1).astype(F32)
     places = in_order(partner.astype(F32))
+
     def columns_of(values):
         scale = lax.rsqrt(jnp.sum(values * values, 0, keepdims=True) + 1e-06)
         return (values * scale).astype(BF16), scale
@@ -1058,84 +1313,56 @@
     columns, column_scale = columns_of(tables[0])
     teacher_columns = columns_of(tables[1])[0]
 
-    kept = forward(plan, gathered, pixels)
-    unit, scale, probs, mixed, looked, classes, qkv_w, ahead = kept[:8]
-    rows = kept[-1]
+    here = jnp.arange(views)
+    source = jnp.concatenate([places[0], places[1] + own_views]).astype(jnp.int32)
+    source = jnp.where(low, here, source)
+    turn = (source[:, None] == here[None, :]).astype(BF16)
+
+    turn, columns, teacher_columns = lax.optimization_barrier((turn, columns, teacher_columns))
+    kept = forward(plan, gathered, pixels, turn)
+    unit, scale, probs, mixed, looked, classes, qkv_w, second = kept[:8]
+    received = lax.all_to_all(kept[-1], BOTH, 0, 0)
+    received = received.reshape(reps // 2, 2, groups * views, -1)
+    all_rows = received[..., :B]
+    ahead = received[:, 0, :, B:].reshape(half * views, -1)
 
     def gather_rows(values):
         return lax.all_gather(values, BOTH, axis=0, axis_index_groups=halves).reshape(
             half * views, -1
         )
 
-    ahead = [ahead, mixed[:, :HEADS].reshape(views, -1)]
-    ahead.append(jnp.pad(classes[1:3], ((0, views - 2), (0, 0))).astype(BF16))
-    ahead = trade_low(jnp.concatenate(ahead, 1))
-
-    here = jnp.arange(views)
-    source = jnp.concatenate([places[0], places[1] + own_views]).astype(jnp.int32)
-    source = jnp.where(low, here, source)
-    rows = product((source[:, None] == here[None, :]).astype(BF16), rows).astype(BF16)
-    all_rows = lax.all_to_all(
-        jnp.broadcast_to(rows[None], (count, views, B)), BOTH, 0, 0
-    )
-    all_rows, ahead = lax.optimization_barrier((all_rows, ahead))
-    ahead = gather_rows(ahead)
-    all_rows = all_rows.reshape(reps // 2, 2, groups * views, B)
-    student_rows = all_rows[:, 0].reshape(-1, B)
-    teacher_rows = all_rows[:, 1].reshape(-1, B)
-
-    teacher_logits = product(teacher_rows, teacher_columns)
-    new_center = CENTER_MOMENTUM * center + (1.0 - CENTER_MOMENTUM) * jnp.mean(teacher_logits, 0)
-    exp_teacher = jnp.exp((teacher_logits - center) / TEACHER_TEMP)
-    scaled = product(student_rows, columns) / STUDENT_TEMP
-    exp_student = jnp.exp(scaled)
-    sums = jnp.stack(
-        [jnp.sum(exp_student, 1), jnp.sum(exp_teacher, 1), jnp.sum(exp_teacher * scaled, 1)]
-    )
-    band = groups * views
-    start = rep // 2 * band
-    pulls = jnp.concatenate(
-        [
-            lax.dynamic_slice_in_dim(exp_student, start, band, 0),
-            lax.dynamic_slice_in_dim(exp_teacher, start, band, 0),
-        ],
-        0,
-    )
-    pulls = lax.dot_general(
-        pulls, columns.astype(F32), (((1,), (1,)), ((), ())), precision=PRECISE
-    ).reshape(2, groups, views * B)
-    note = jnp.concatenate(
-        [
-            pulls.transpose(1, 0, 2).reshape(groups, -1),
-            jnp.broadcast_to(sums.reshape(1, -1), (groups, sums.size)),
-        ],
-        1,
-    ).reshape(groups, -1, LANES)
-    note = jnp.sum(lax.all_to_all(note, "grp", 0, 0), 0).reshape(-1)
-    pulls = note[: 2 * views * B].reshape(2, views, B)
-    sum_student, sum_teacher, crossed = note[2 * views * B :].reshape(3, -1)
-    loss_value = jnp.sum(jnp.log(sum_student) - crossed / sum_teacher)
-    own = place * views
-    own_student = lax.dynamic_slice_in_dim(sum_student, own, views)[:, None]
-    own_teacher = lax.dynamic_slice_in_dim(sum_teacher, own, views)[:, None]
-    grad_rows = (pulls[0] / own_student - pulls[1] / own_teacher) / STUDENT_TEMP
-    grad_rows = jnp.where(low, grad_rows, 0.0).astype(BF16).astype(F32)
-
-    grad_logits = (
-        exp_student / sum_student[:, None] - exp_teacher / sum_teacher[:, None]
-    ) / STUDENT_TEMP
-    grad_columns = lax.dot_general(
-        student_rows.astype(F32), grad_logits, (((0,), (0,)), ((), ())), precision=PRECISE
-    )
-    inner = jnp.sum(grad_columns * tables[0], 0, keepdims=True)
+    common = [mixed[:, :HEADS].reshape(views, -1), second]
+    common.append(jnp.pad(classes[1:3], ((0, views - 2), (0, 0))).astype(BF16))
+    common = jnp.concatenate(common, 1)
+    other = trade(common)
+    all_rows, ahead, other = lax.optimization_barrier((all_rows, ahead, other))
+    common = jnp.where(low, common, other)
+
+    all_rows = all_rows.transpose(1, 0, 2, 3).reshape(2, -1, B)
+    start = (rep // 2 * groups * views).astype(jnp.int32)[None]
+    note, new_center = prototypes(
+        start, all_rows, columns, teacher_columns, center[None], groups, views
+    )
+    common = gather_rows(common)
+    new_center = new_center[0]
+    note = lax.all_to_all(note, "grp", 0, 0)
+    totals = jnp.sum(note[:, 3 * views :], 0)
+    totals = totals.reshape(-1, 8, B).transpose(1, 0, 2).reshape(8, -1)[:, : half * views]
+    loss_value = jnp.sum(jnp.log(totals[0]) - totals[2] / totals[1])
     depth = protos.shape[0]
-    grad_protos = (
-        lax.dynamic_slice_in_dim(grad_columns, rep * depth, depth, 0) * column_scale
-        - protos.astype(BF16).astype(F32) * column_scale**3 * inner
-    )
-
+    grad_protos, proto_squares = prototypes_back(
+        (rep * depth).astype(jnp.int32)[None],
+        depth,
+        all_rows,
+        columns,
+        teacher_columns,
+        center[None],
+        totals,
+        tables[0],
+        column_scale,
+    )
     behind, grad_middle, ends = rows_back(
-        plan, gathered, grad_rows, (classes,) + tuple(kept[8:13])
+        plan, low.astype(jnp.int32)[None], gathered, note, (classes,) + tuple(kept[8:13])
     )
     odd, far = grp % 2 == 1, grp // 2 % 2 == 1
     behind_rows = trade_low(behind)
@@ -1146,9 +1373,9 @@
         ends,
         (unit, scale, probs, looked, classes, qkv_w),
         pixels.transpose(0, 2, 1),
-    )
-    behind_rows, sent_rows = lax.optimization_barrier((behind_rows, sent_rows))
-    behind_rows = gather_rows(behind_rows)
+        behind_rows,
+        grad_protos,
+    )
 
     def across(bit, values):
         return lax.ppermute(values, "grp", [(g, g ^ bit) for g in range(groups)])
@@ -1159,33 +1386,17 @@
     other = jnp.concatenate([jnp.where(far, first, second), shared], 0).astype(BF16)
     partial = jnp.concatenate([jnp.where(far, second, first), shared], 0)
     partial = partial + across(2, other).astype(F32)
-    lines = reps // 2
+    behind_rows, partial = lax.optimization_barrier((behind_rows, partial))
+    behind_rows = gather_rows(behind_rows)
     depth = partial.shape[0] // lines
     partial = lax.all_to_all(
         partial.astype(BF16).reshape(lines, depth, D), "rep", 0, 0, axis_index_groups=pairs
     )
     partial = jnp.sum(partial.astype(F32), 0)
-    summed = lax.all_to_all(
-        jnp.broadcast_to(partial.astype(BF16)[None], (lines, depth, D)),
-        "rep",
-        0,
-        0,
-        axis_index_groups=pairs,
-    ).reshape(-1, D)
-    shared, summed = trade_low(summed[SET:]).astype(F32), summed[:SET]
-    other = across(2, summed)
-    summed = jnp.concatenate([jnp.where(far, other, summed), jnp.where(far, summed, other)], 0)
-    if plan.all_sets:
-        other = across(1, summed)
-        summed = jnp.concatenate([jnp.where(odd, other, summed), jnp.where(odd, summed, other)], 0)
-    if plan.odd_owner:
-        summed = trade_low(summed)
-    wide_grad = jnp.pad(summed.astype(F32), ((0, CHUNK), (0, 0)))
-
     early, squares = early_gradient(
-        plan, jnp.asarray(plan.grad_table)[device], ahead, behind_rows
-    )
-    class_rows = ahead[:2, AHEAD + HEADS * D :].astype(F32)
+        plan, jnp.asarray(plan.grad_table)[device], ahead, common, behind_rows
+    )
+    class_rows = common[:2, CLASS:].astype(F32)
     class_normed, query = class_rows[0:1], class_rows[1:2]
     by_head = jnp.where(head_mask()[:HEADS], query, 0.0)
     twice = odd & ~far & (jnp.arange(SET) < 8)
@@ -1195,20 +1406,38 @@
             jnp.sum(by_head * by_head, 1) / groups,
             jnp.zeros((HEADROWS - HEADS,), F32),
             jnp.sum(class_normed * class_normed)[None] / groups,
-            jnp.zeros((SHARED - HEADROWS - 1,), F32),
+            jnp.full((2,), 1.0 / groups, F32),
+            jnp.zeros((SHARED - HEADROWS - 3,), F32),
         ]
     )
     weights = lax.dynamic_slice_in_dim(weights, rep // 2 * depth, depth)
     pieces = jnp.sum(weights * jnp.sum(partial * partial, 1))
     squares = jnp.sum(squares) + jnp.where(low, pieces, 0.0)
-    squares = squares + jnp.sum(grad_protos * grad_protos)
+    squares = squares + jnp.sum(proto_squares[0])
+    summed = lax.all_to_all(
+        jnp.broadcast_to(partial.astype(BF16)[None], (lines, depth, D)),
+        "rep",
+        0,
+        0,
+        axis_index_groups=pairs,
+    ).reshape(-1, D)
+    shared, summed = trade_low(summed[SET:]).astype(F32), summed[:SET]
+    other, squares = lax.optimization_barrier((across(2, summed), squares))
     squares = lax.all_to_all(
         jnp.broadcast_to(squares.reshape(1, 1, 1), (count, 1, LANES)), BOTH, 0, 0
     )
     grad_norm = jnp.sqrt(jnp.sum(squares[:, 0, 0]))
     factor = jnp.minimum(1.0, CLIP_NORM / (grad_norm + 1e-06))
+    summed = jnp.concatenate([jnp.where(far, other, summed), jnp.where(far, summed, other)], 0)
+    if plan.all_sets:
+        other = across(1, summed)
+        summed = jnp.concatenate([jnp.where(odd, other, summed), jnp.where(odd, summed, other)], 0)
+    if plan.odd_owner:
+        summed = trade_low(summed)
+    wide_grad = jnp.pad(summed.astype(F32), ((0, CHUNK), (0, 0)))
 
     sum_query, reach = shared[HEADROWS : HEADROWS + 1], shared[:HEADS]
+    ends = jnp.pad(shared[HEADROWS + 1 : HEADROWS + 3], ((0, 6), (0, 0)))
     left = jnp.concatenate([class_normed, reach, jnp.zeros((LANES - 1 - HEADS, D), F32)], 0)
     left = jnp.pad(left.T, ((0, CHUNK), (0, 0)))
     right = jnp.concatenate(
@@ -1220,7 +1449,7 @@
         0,
     )
     grad_flat = late_gradient(
-        plan, jnp.asarray(plan.late_table)[device], early, wide_grad, left, right
+        plan, jnp.asarray(plan.late_table)[device], early, wide_grad, left, right, ends
     )
     new_params, new_first, new_second = adam_update(
         params, grad_flat * factor, first_moment, second_moment, LEARNING_RATE

time: 425 us -> 409 us (0.962)
  blocking collectives: 0 us -> 20.9 us
  local copies, waits for them, and re-layouts: 37.3 us -> 24.7 us
  other arithmetic: 43.5 us -> 31.5 us
  matrix products: 8.69 us -> 0 us
  waiting for transfers between devices: 198 us -> 191 us
  Pallas kernels: 80.7 us -> 85.9 us
    all_to_all x0 -> x1, blocking collectives: none -> 20.9 us  [per_device(): lax.all_to_all(partial.astype(BF16).reshape(lines, depth, D), 'rep', 0, 0...]
    all_to_all x1, waiting for transfers between devices: 4.29 us -> 19.4 us  [per_device(): lax.all_to_all(jnp.broadcast_to(partial.astype(BF16)[None], (lines, depth...]
    all_to_all x4 -> x2, waiting for transfers between devices: 28.5 us -> 13.7 us  [the longest x1 10 us: per_device(): received = lax.all_to_all(kept[-1], BOTH, 0, 0)]
    ppermute x7, waiting for transfers between devices: 61.6 us -> 48.1 us  [trade(): return lax.ppermute(values, 'rep', swap)]
    unnamed x68 -> x51, local copies, waits for them, and re-layouts: 15.8 us -> 4.44 us
    ppermute x0 -> x3, waiting for transfers between devices: none -> 10 us  [per_device(): lax.ppermute(tables, 'rep', [(r, (r + step) % reps) for r in range(reps)])]
    all_to_all x4 -> x2, starting transfers between devices: 17.1 us -> 8.1 us  [the longest x1 4.77 us: per_device(): received = lax.all_to_all(kept[-1], BOTH, 0, 0)]
    dot_general x5 -> x0, matrix products: 8.69 us -> none  [the longest x1 4.3 us: per_device(): lax.dot_general(student_rows.astype(F32), grad_logits, (((0,), (0,)), (()...]
  transfers between devices with their start and end apart: 19 -> 20, of which waited for: 12 -> 10; matrix products, arithmetic and copies ran while one was open for 12% -> 9% of each run, Pallas kernels for 11% -> 12%
where the time goes in v5:
time: 409 us; the launch traced here: 407 us
  waiting for transfers between devices  191 us (47%)
  Pallas kernels  85.9 us (21%)
  starting transfers between devices  34.5 us (8%)
  other arithmetic  31.5 us (8%)
  local copies, waits for them, and re-layouts  24.7 us (6%)
  blocking collectives  20.9 us (5%)
  between operations  19.1 us (5%)
    all_gather x1, waiting for transfers between devices, per_device(): gathered = lax.all_gather(shards, BOTH, axis=0, axis_index_groups=halves)  84.2 us
    ppermute x7, waiting for transfers between devices, trade(): return lax.ppermute(values, 'rep', swap)  48.1 us
    pallas_call x1, Pallas kernels, forward(): pl.pallas_call(functools.partial(forward_kernel, plan), out_shape=[jax.Sh...  26.4 us
    all_to_all x1, blocking collectives, per_device(): lax.all_to_all(partial.astype(BF16).reshape(lines, depth, D), 'rep', 0, 0...  20.9 us
    all_to_all x1, waiting for transfers between devices, per_device(): lax.all_to_all(jnp.broadcast_to(partial.astype(BF16)[None], (lines, depth...  19.4 us
    pallas_call x1, Pallas kernels, tokens_back(): pl.pallas_call(tokens_back_kernel, grid=(views,), out_shape=[jax.ShapeDty...  17 us
    pallas_call x1, Pallas kernels, rows_back(): pl.pallas_call(functools.partial(rows_back_kernel, plan), out_shape=[jax....  15.6 us
    ppermute x3, waiting for transfers between devices, across(): return lax.ppermute(values, 'grp', [(g, g ^ bit) for g in range(groups)])  15.3 us
  transfers between devices with their start and end apart: 20, of which 10 were waited for; matrix products, arithmetic and copies ran while one was open for 9% of the time, Pallas kernels for 12%

profile of v5, /device:TPU:0, one launch (start us, length us, event | category | flops | bytes accessed | tf_op | source)
XLA Modules:
  0.0 407.3 jit_solution(3442842964946147495)
XLA Ops:
  7.2 2.2 broadcast_select_fusion.3
  10.4 5.4 %shard_map.222 = bf16[3648,128]{1,0:T(8,128)(2,1)S(1)} custom-call(s32[11]{0:T(128)S(1)} %fusion.25.tab_ref, f32[3464,128]{1,0:T(8,128)S(1)} %pad_bitcast_fusion.x_ref), custom_call_target="tpu_custom_call" | custom-call | tf_op jit(solution)/shard_map/pallas_call | solution.py:245
  15.7 2.9 collective-permute-start
  18.7 1.7 collective-permute-start.1
  20.4 2.8 collective-permute-start.2
  23.3 1.3 collective-permute-start.3
  24.8 5.4 %shard_map.221 = bf16[3648,128]{1,0:T(8,128)(2,1)S(1)} custom-call(s32[11]{0:T(128)S(1)} %fusion.25.tab_ref, f32[3464,128]{1,0:T(8,128)S(1)} %pad_bitcast_fusion.1.x_ref), custom_call_target="tpu_custom_call" | custom-call | tf_op jit(solution)/shard_map/pallas_call | solution.py:245
  30.1 10.0 %collective-permute-done.2 = bf16[2,32,2048]{2,1,0:T(8,128)(2,1)S(1)} collective-permute-done((bf16[2,32,2048]{2,1,0:T(8,128)(2,1)S(1)}, bf16[2,32,2048]{2,1,0:T(8,128)(2,1)S(1)}, u32[]{:S(2)}, u32[]{:S(2)}) %collective-permute-start.2) | collective-permute-done | bytes 262176 | tf_op jit(solution)/shard_map/ppermute | solution.py:1291
  40.4 1.4 pad_maximum_fusion
  42.0 1.0 constant_dynamic-slice_fusion
  43.1 1.0 collective-permute-start.6
  44.1 3.6 copy.90
  47.6 1.0 collective-permute-start.4
  48.7 1.0 collective-permute-start.5
  49.7 44.5 %collective-permute-done.5 = f32[4]{0:T(128)S(1)} collective-permute-done((f32[4]{0:T(128)S(1)}, f32[4]{0:T(128)S(1)}, u32[]{:S(2)}, u32[]{:S(2)}) %collective-permute-start.5) | collective-permute-done | bytes 48 | tf_op jit(solution)/shard_map/ppermute | solution.py:1277
  97.6 1.2 fusion.6.others_ref
  98.8 3.7 copy.91
  102.5 2.1 broadcast_select_fusion.1
  104.6 3.1 fusion.28
  107.7 4.7 %copy.96.pixels_ref = bf16[8,208,768]{2,1,0:T(8,128)(2,1)} copy(bf16[8,208,768]{1,2,0:T(8,128)(2,1)} %get-tuple-element.110) | data formatting | bytes 5111808 | tf_op jit(solution)/shard_map/jit(_pad)/pad | solution.py:1302
  112.4 84.2 %all-gather.7.cloned.1.call-done = bf16[32,3648,128]{2,1,0:T(8,128)(2,1)} async-done(((bf16[2,3648,128]{2,1,0:T(8,128)(2,1)}), bf16[32,3648,128]{2,1,0:T(8,128)(2,1)}) %all-gather.7.cloned.1.call-update) | async-done | bytes 29884432 | tf_op jit(solution)/shard_map/all_gather | solution.py:1298
  196.6 26.4 %shard_map.223 = (f32[8,208,768]{2,1,0:T(8,128)}, f32[8,208,128]{2,1,0:T(8,128)}, f32[8,16,208]{2,1,0:T(8,128)}, bf16[8,16,768]{2,1,0:T(8,128)(2,1)}, bf16[16,76...) custom-call(bf16[16,2,228,16,128]{4,3,2,1,0:T(8,128)(2,1)} %bitcast., ...), custom_call_target="tpu_custom_call" | custom-call | flops 60000002048 | bytes 40000000 | tf_op jit(solution)/shard_map/pallas_call | solution.py:614
  223.0 4.8 %all-to-all-start = ((bf16[32,8,896]{2,1,0:T(8,128)(2,1)}), bf16[32,8,896]{2,1,0:T(8,128)(2,1)S(1)}, u32[]{:S(2)}, u32[]{:S(2)}) async-start(bf16[32,8,896]{2,1,0:T(8,128)(2,1)} %get-tuple-element.61), calls=%async_computation | async-start | bytes 917504 | tf_op jit(solution)/shard_map/all_to_all | solution.py:1324
  230.3 1.7 collective-permute-start.7
  232.0 10.0 %all-to-all-done = bf16[32,8,896]{2,1,0:T(8,128)(2,1)S(1)} async-done(((bf16[32,8,896]{2,1,0:T(8,128)(2,1)}), bf16[32,8,896]{2,1,0:T(8,128)(2,1)S(1)}, u32[]{:S(2)}, u32[]{:S(2)}) %all-to-all-start) | async-done | bytes 458784 | tf_op jit(solution)/shard_map/all_to_all | solution.py:1324
  242.8 4.7 %shard_map.224 = (f32[4,32,256]{2,1,0:T(8,128)}, f32[1,2048]{1,0:T(1,128)}) custom-call(s32[1]{0:T(128)} %bitcast.22.start_ref, bf16[2,128,256]{2,1,0:T(8,128)(2,1)S(1)} %bitcast.74, bf16[256,2048]{1,0:T(8,128)(2,1)S(1)} %multiply_convert_fusion.columns_ref, bf16[256,2048]{1,0:T(8,128)(2,1)S(1)} %copy-done.3, f32[1,2048]{1,0:T(1,128)S(1)} %bitcast.77), custom_call_target="tpu_custom_call" | custom-call | flops 3000000000 | bytes 6000000 | tf_op jit(solution)/shard_map/pallas_call | solution.py:698
  247.5 3.3 all-to-all-start.1
  251.7 3.7 all-to-all-done.1.note_ref
  255.5 15.6 %shard_map.225 = (bf16[8,9728]{1,0:T(8,128)(2,1)S(1)}, f32[8,768]{1,0:T(8,128)S(1)}, f32[8,768]{1,0:T(8,128)S(1)}) custom-call(s32[1]{0:T(128)} %bitcast.21.low_ref, bf16[16,2,228,16,128]{4,3,2,1,0:T(8,128)(2,1)} %bitcast.90, f32[4,32,256]{2,1,0:T(8,128)S(1)} %all-to-all-done.1.note_ref, f32[16,768]{1,0:T(8,128)S(1)} %copy-done.7, f32[8,3072]{1,0:T(8,128)S(1)} %copy-done.9, ...), custom_call_target="tpu_custom_call" | custom-call | flops 30000001024 | bytes 30000000 | tf_op jit(solution)/shard_map/pallas_call | solution.py:841
  271.1 1.2 collective-permute-start.8
  272.3 2.5 shard_map.226
  275.5 1.0 collective-permute-done.8
  277.2 17.0 %shard_map.227 = (f32[608,768]{1,0:T(8,128)}, bf16[608,768]{1,0:T(8,128)(2,1)}) custom-call(s32[1]{0:T(128)} %bitcast.26.odd_ref, bf16[8,9728]{1,0:T(8,128)(2,1)} %copy-done.6, f32[8,768]{1,0:T(8,128)} %copy-done.11, f32[8,768]{1,0:T(8,128)} %copy-done.12, f32[8,208,768]{2,1,0:T(8,128)} %get-tuple-element.79.unit_ref, ...), custom_call_target="tpu_custom_call" | custom-call | flops 15000000512 | bytes 15000000 | tf_op jit(solution)/shard_map/pallas_call | solution.py:976
  294.3 2.7 collective-permute-done.9
  296.9 1.7 convert_add_fusion
  299.5 12.6 %collective-permute-done.10 = bf16[320,768]{1,0:T(8,128)(2,1)S(1)} collective-permute-done((bf16[320,768]{1,0:T(8,128)(2,1)S(1)}, bf16[320,768]{1,0:T(8,128)(2,1)S(1)}, u32[]{:S(2)}, u32[]{:S(2)}) %collective-permute-start.10) | collective-permute-done | bytes 491552 | tf_op jit(solution)/shard_map/ppermute | solution.py:1381
  312.2 20.9 %all_to_all.25 = bf16[4,80,768]{2,1,0:T(8,128)(2,1)S(1)} all-to-all(bf16[4,80,768]{2,1,0:T(8,128)(2,1)S(1)} %bitcast.83), channel_id=1, replica_groups={{0,8,16,24},{4,12,20,28},{1,9,17,25},{5,13,21,29},{2,10,18,26},{6,14,22..., dimensions={0} | all-to-all | bytes 983040 | tf_op jit(solution)/shard_map/all_to_all | solution.py:1392
  334.1 3.7 all-to-all-start.3
  337.9 1.2 fusion.24.tab_ref
  340.5 19.4 %all-to-all-done.3 = bf16[4,80,768]{2,1,0:T(8,128)(2,1)S(1)} async-done(((bf16[4,80,768]{2,1,0:T(8,128)(2,1)}), bf16[4,80,768]{2,1,0:T(8,128)(2,1)S(1)}, u32[]{:S(2)}, u32[]{:S(2)}) %all-to-all-start.3) | async-done | bytes 491552 | tf_op jit(solution)/shard_map/all_to_all | solution.py:1417
  361.3 2.6 collective-permute-done.12
  368.3 3.7 shard_map.228
  372.0 1.3 reduce_sum.112
  375.2 6.4 %all-to-all-start.4 = ((f32[32,1,128]{2,1,0:T(1,128)}), f32[32,1,128]{2,1,0:T(1,128)S(1)}, u32[]{:S(2)}, u32[]{:S(2)}) async-start(f32[32,1,128]{2,1,0:T(1,128)} %broadcast_in_dim.79), calls=%async_computation.4 | async-start | bytes 32768 | tf_op jit(solution)/shard_map/all_to_all | solution.py:1426
  381.9 1.7 copy-done.2
  383.7 5.3 %shard_map.229 = f32[3456,128]{1,0:T(8,128)S(1)} custom-call(s32[9]{0:T(128)S(1)} %fusion.23.tab_ref, f32[6736,128]{1,0:T(8,128)S(1)} %copy-done.2, f32[704,768]{1,0:T(8,128)S(1)} %fusion.9.wide_ref, f32[896,128]{1,0:T(8,128)S(1)} %pad.43.left_ref, f32[128,1536]{1,0:T(8,128)S(1)} %fusion.10.right_ref, f32[8,768]{1,0:T(8,128)S(1)} %pad.46.ends_ref), custom_call_target="tpu_custom_call" | custom-call | tf_op jit(solution)/shard_map/pallas_call | solution.py:1224
  390.4 2.4 multiply_add_fusion.2
  392.8 6.8 %multiply_add_fusion = (f32[441096]{0:T(1024)}, f32[441096]{0:T(1024)}, f32[441096]{0:T(1024)}, f32[441096]{0:T(1024)}) fusion(f32[441096]{0:T(1024)S(1)} %copy-done.16, f32[441096]{0:T(1024)} %param.14, f32[]{:T(128)S(6)} %min.3, f32[442368]{0:T(1024)S(1)} %bitcast.73, f32[441096]{0:T(1024)} %param.15, f32[441096]{0:T(1024)} %param.16), kind=kLoop, calls=%fused_computation.21 | loop fusion | flops 8380824 | bytes 15879460 | tf_op jit(solution)/shard_map/add | solution.py:1460
  (142 shorter events, 19.7 us)
Async XLA Ops:
  7.2 189.4 %all-gather.7.cloned.1.call-start = ((), (), s32[]{:S(2)}) async-start(), calls=%async_computation.5 | async-start | bytes 31752192 | tf_op jit(solution)/shard_map/all_gather | solution.py:1298
  9.6 9.0 %copy-start.17 = (f32[32,2048]{1,0:T(8,128)S(1)}, f32[32,2048]{1,0:T(8,128)}, u32[]{:S(2)}) copy-start(f32[32,2048]{1,0:T(8,128)} %param.21) | copy-start | bytes 786436
  9.6 9.0 %copy-start.18 = (f32[32,2048]{1,0:T(8,128)S(1)}, f32[32,2048]{1,0:T(8,128)}, u32[]{:S(2)}) copy-start(f32[32,2048]{1,0:T(8,128)} %param.18) | copy-start | bytes 786436
  15.7 24.4 %collective-permute-start = (bf16[3648,128]{1,0:T(8,128)(2,1)S(1)}, bf16[3648,128]{1,0:T(8,128)(2,1)S(1)}, u32[]{:S(2)}, u32[]{:S(2)}) collective-permute-start(bf16[3648,128]{1,0:T(8,128)(2,1)S(1)} %shard_map.222), channel_id=1, source_target_pairs={{0,4},{4,0},{8,12},{12,8},{16,20},{20,16},{24,28},{28,24},{1,5},{5... | collective-permute-start | bytes 2801672 | tf_op jit(solution)/shard_map/ppermute | solution.py:1277
  18.7 11.4 %collective-permute-start.1 = (bf16[2,32,2048]{2,1,0:T(8,128)(2,1)S(1)}, bf16[2,32,2048]{2,1,0:T(8,128)(2,1)S(1)}, u32[]{:S(2)}, u32[]{:S(2)}) collective-permute-start(bf16[2,32,2048]{2,1,0:T(8,128)(2,1)S(1)} %pad_maximum_fusion.2), channel_id=1, source_target_pairs={{0,8},{4,12},{8,16},{12,20},{16,24},{20,28},{24,0},{28,4},{1,9},{5... | collective-permute-start | bytes 786440 | tf_op jit(solution)/shard_map/ppermute | solution.py:1291
  20.4 19.7 %collective-permute-start.2 = (bf16[2,32,2048]{2,1,0:T(8,128)(2,1)S(1)}, bf16[2,32,2048]{2,1,0:T(8,128)(2,1)S(1)}, u32[]{:S(2)}, u32[]{:S(2)}) collective-permute-start(bf16[2,32,2048]{2,1,0:T(8,128)(2,1)S(1)} %pad_maximum_fusion.2), channel_id=1, source_target_pairs={{0,16},{4,20},{8,24},{12,28},{16,0},{20,4},{24,8},{28,12},{1,17},{... | collective-permute-start | bytes 786440 | tf_op jit(solution)/shard_map/ppermute | solution.py:1291
  23.3 16.8 %collective-permute-start.3 = (bf16[2,32,2048]{2,1,0:T(8,128)(2,1)S(1)}, bf16[2,32,2048]{2,1,0:T(8,128)(2,1)S(1)}, u32[]{:S(2)}, u32[]{:S(2)}) collective-permute-start(bf16[2,32,2048]{2,1,0:T(8,128)(2,1)S(1)} %pad_maximum_fusion.2), channel_id=1, source_target_pairs={{0,24},{4,28},{8,0},{12,4},{16,8},{20,12},{24,16},{28,20},{1,25},{... | collective-permute-start | bytes 786440 | tf_op jit(solution)/shard_map/ppermute | solution.py:1291
  43.1 5.6 %copy-start.20 = (s32[4]{0:T(128)S(1)}, s32[4]{0:T(128)}, u32[]{:S(2)}) copy-start(s32[4]{0:T(128)} %param.24) | copy-start | bytes 52
  43.1 51.9 %collective-permute-start.6 = (bf16[4,2,32,2048]{3,2,1,0:T(8,128)(2,1)}, bf16[4,2,32,2048]{3,2,1,0:T(8,128)(2,1)S(1)}, u32[]{:S(2)}, u32[]{:S(2)}) collective-permute-start(bf16[4,2,32,2048]{3,2,1,0:T(8,128)(2,1)} %constant_dynamic-slice_fusion), channel_id=1, source_target_pairs={{0,4},{4,0},{8,12},{12,8},{16,20},{20,16},{24,28},{28,24},{1,5},{5... | collective-permute-start | bytes 3145736 | tf_op jit(solution)/shard_map/ppermute | solution.py:1277
  47.6 51.2 %collective-permute-start.4 = (bf16[4,196,768]{2,0,1:T(4,128)(2,1)}, bf16[4,196,768]{2,0,1:T(4,128)(2,1)}, u32[]{:S(2)}, u32[]{:S(2)}) collective-permute-start(bf16[4,196,768]{2,0,1:T(4,128)(2,1)} %param.23), channel_id=1, source_target_pairs={{0,4},{4,0},{8,12},{12,8},{16,20},{20,16},{24,28},{28,24},{1,5},{5... | collective-permute-start | bytes 3612680 | tf_op jit(solution)/shard_map/ppermute | solution.py:1277
  48.7 45.5 %collective-permute-start.5 = (f32[4]{0:T(128)S(1)}, f32[4]{0:T(128)S(1)}, u32[]{:S(2)}, u32[]{:S(2)}) collective-permute-start(f32[4]{0:T(128)S(1)} %convert_element_type.73), channel_id=1, source_target_pairs={{0,4},{4,0},{8,12},{12,8},{16,20},{20,16},{24,28},{28,24},{1,5},{5... | collective-permute-start | bytes 56 | tf_op jit(solution)/shard_map/ppermute | solution.py:1277
  96.1 1.4 copy-start
  223.0 19.7 %copy-start.3 = (bf16[256,2048]{1,0:T(8,128)(2,1)S(1)}, bf16[256,2048]{1,0:T(8,128)(2,1)}, u32[]{:S(2)}) copy-start(bf16[256,2048]{1,0:T(8,128)(2,1)} %fusion.6.others_ref) | copy-start | bytes 3145732
  223.0 19.7 %copy-start.8 = (f32[2048]{0:T(1024)S(1)}, f32[2048]{0:T(1024)}, u32[]{:S(2)}) copy-start(f32[2048]{0:T(1024)} %param.22) | copy-start | bytes 24580
  223.0 19.0 %all-to-all-start = ((bf16[32,8,896]{2,1,0:T(8,128)(2,1)}), bf16[32,8,896]{2,1,0:T(8,128)(2,1)S(1)}, u32[]{:S(2)}, u32[]{:S(2)}) async-start(bf16[32,8,896]{2,1,0:T(8,128)(2,1)} %get-tuple-element.61), calls=%async_computation | async-start | bytes 917504 | tf_op jit(solution)/shard_map/all_to_all | solution.py:1324
  230.3 12.4 %collective-permute-start.7 = (bf16[8,12032]{1,0:T(8,128)(2,1)S(1)}, bf16[8,12032]{1,0:T(8,128)(2,1)}, u32[]{:S(2)}, u32[]{:S(2)}) collective-permute-start(bf16[8,12032]{1,0:T(8,128)(2,1)S(1)} %fusion.14), channel_id=1, source_target_pairs={{0,4},{4,0},{8,12},{12,8},{16,20},{20,16},{24,28},{28,24},{1,5},{5... | collective-permute-start | bytes 577544 | tf_op jit(solution)/shard_map/ppermute | solution.py:1277
  242.7 8.2 %copy-start.19 = (bf16[8,2048]{1,0:T(8,128)(2,1)S(1)}, bf16[8,2048]{1,0:T(8,128)(2,1)}, u32[]{:S(2)}) copy-start(bf16[8,2048]{1,0:T(8,128)(2,1)} %get-tuple-element.63) | copy-start | bytes 98308
  242.7 12.7 %copy-start.7 = (f32[16,768]{1,0:T(8,128)S(1)}, f32[16,768]{1,0:T(8,128)}, u32[]{:S(2)}) copy-start(f32[16,768]{1,0:T(8,128)} %get-tuple-element.64.class_ref) | copy-start | bytes 147460
  242.7 12.7 %copy-start.9 = (f32[8,3072]{1,0:T(8,128)S(1)}, f32[8,3072]{1,0:T(8,128)}, u32[]{:S(2)}) copy-start(f32[8,3072]{1,0:T(8,128)} %get-tuple-element.71.hidden_ref) | copy-start | bytes 294916
  242.7 12.7 %copy-start.10 = (f32[4,8,768]{2,1,0:T(8,128)S(1)}, f32[4,8,768]{2,1,0:T(8,128)}, u32[]{:S(2)}) copy-start(f32[4,8,768]{2,1,0:T(8,128)} %get-tuple-element.75.middle_ref) | copy-start | bytes 294916
  242.7 12.7 %copy-start.13 = (f32[8,2048]{1,0:T(8,128)S(1)}, f32[8,2048]{1,0:T(8,128)}, u32[]{:S(2)}) copy-start(f32[8,2048]{1,0:T(8,128)} %get-tuple-element.72.one_ref) | copy-start | bytes 196612
  242.7 12.7 %copy-start.14 = (f32[8,2048]{1,0:T(8,128)S(1)}, f32[8,2048]{1,0:T(8,128)}, u32[]{:S(2)}) copy-start(f32[8,2048]{1,0:T(8,128)} %get-tuple-element.73.two_ref) | copy-start | bytes 196612
  242.8 12.7 %copy-start.15 = (f32[8,256]{1,0:T(8,128)S(1)}, f32[8,256]{1,0:T(8,128)}, u32[]{:S(2)}) copy-start(f32[8,256]{1,0:T(8,128)} %get-tuple-element.74.bottle_ref) | copy-start | bytes 24580
  247.5 7.9 %all-to-all-start.1 = ((f32[4,32,256]{2,1,0:T(8,128)}), f32[4,32,256]{2,1,0:T(8,128)S(1)}, u32[]{:S(2)}, u32[]{:S(2)}) async-start(f32[4,32,256]{2,1,0:T(8,128)} %get-tuple-element.70), calls=%async_computation.1 | async-start | bytes 262144 | tf_op jit(solution)/shard_map/all_to_all | solution.py:1348
  250.8 113.4 %all-gather.9.cloned.1.call-start = ((), (), s32[]{:S(2)}) async-start(), calls=%async_computation.6 | async-start | bytes 3272704 | tf_op jit(solution)/shard_map/all_gather | solution.py:1330
  251.7 116.7 %all-gather.11.cloned.1.call-start = ((), (), s32[]{:S(2)}) async-start(), calls=%async_computation.7 | async-start | bytes 2646016 | tf_op jit(solution)/shard_map/all_gather | solution.py:1330
  255.5 16.8 %copy-start.1 = (f32[1,4,2,32,2048]{4,3,2,1,0:T(8,128)S(1)}, f32[1,4,2,32,2048]{4,3,2,1,0:T(8,128)}, u32[]{:S(2)}) copy-start(f32[1,4,2,32,2048]{4,3,2,1,0:T(8,128)} %copy-done) | copy-start | bytes 6291460
  271.0 3.7 copy-start.11
  271.1 3.7 copy-start.12
  271.1 5.5 %copy-start.6 = (bf16[8,9728]{1,0:T(8,128)(2,1)}, bf16[8,9728]{1,0:T(8,128)(2,1)S(1)}, u32[]{:S(2)}) copy-start(bf16[8,9728]{1,0:T(8,128)(2,1)S(1)} %get-tuple-element.76.behind_ref) | copy-start | bytes 466948
  271.1 5.5 %collective-permute-start.8 = (bf16[8,9728]{1,0:T(8,128)(2,1)S(1)}, bf16[8,9728]{1,0:T(8,128)(2,1)S(1)}, u32[]{:S(2)}, u32[]{:S(2)}) collective-permute-start(bf16[8,9728]{1,0:T(8,128)(2,1)S(1)} %get-tuple-element.76.behind_ref), channel_id=1, source_target_pairs={{0,4},{4,0},{8,12},{12,8},{16,20},{20,16},{24,28},{28,24},{1,5},{5... | collective-permute-start | bytes 466952 | tf_op jit(solution)/shard_map/ppermute | solution.py:1277
  274.8 0.7 copy-start.4
  294.2 2.7 collective-permute-start.9
  298.8 13.3 %collective-permute-start.10 = (bf16[320,768]{1,0:T(8,128)(2,1)S(1)}, bf16[320,768]{1,0:T(8,128)(2,1)S(1)}, u32[]{:S(2)}, u32[]{:S(2)}) collective-permute-start(bf16[320,768]{1,0:T(8,128)(2,1)S(1)} %pad_maximum_fusion.1), channel_id=1, source_target_pairs={{0,2},{1,3},{2,0},{3,1},{4,6},{5,7},{6,4},{7,5},{8,10},{9,11},{10,... | collective-permute-start | bytes 1474568 | tf_op jit(solution)/shard_map/ppermute | solution.py:1381
  334.1 25.7 %all-to-all-start.3 = ((bf16[4,80,768]{2,1,0:T(8,128)(2,1)}), bf16[4,80,768]{2,1,0:T(8,128)(2,1)S(1)}, u32[]{:S(2)}, u32[]{:S(2)}) async-start(bf16[4,80,768]{2,1,0:T(8,128)(2,1)} %broadcast_in_dim.71), calls=%async_computation.3 | async-start | bytes 983040 | tf_op jit(solution)/shard_map/all_to_all | solution.py:1417
  359.8 4.1 %collective-permute-start.12 = (bf16[32,768]{1,0:T(8,128)(2,1)S(1)}, bf16[32,768]{1,0:T(8,128)(2,1)S(1)}, u32[]{:S(2)}, u32[]{:S(2)}) collective-permute-start(bf16[32,768]{1,0:T(8,128)(2,1)S(1)} %slice.125), channel_id=1, source_target_pairs={{0,4},{4,0},{8,12},{12,8},{16,20},{20,16},{24,28},{28,24},{1,5},{5... | collective-permute-start | bytes 147464 | tf_op jit(solution)/shard_map/ppermute | solution.py:1277
  360.7 13.9 %collective-permute-start.11 = (bf16[288,768]{1,0:T(8,128)(2,1)S(1)}, bf16[288,768]{1,0:T(8,128)(2,1)S(1)}, u32[]{:S(2)}, u32[]{:S(2)}) collective-permute-start(bf16[288,768]{1,0:T(8,128)(2,1)S(1)} %slice.121), channel_id=1, source_target_pairs={{0,2},{1,3},{2,0},{3,1},{4,6},{5,7},{6,4},{7,5},{8,10},{9,11},{10,... | collective-permute-start | bytes 1327112 | tf_op jit(solution)/shard_map/ppermute | solution.py:1381
  375.2 13.8 %all-to-all-start.4 = ((f32[32,1,128]{2,1,0:T(1,128)}), f32[32,1,128]{2,1,0:T(1,128)S(1)}, u32[]{:S(2)}, u32[]{:S(2)}) async-start(f32[32,1,128]{2,1,0:T(1,128)} %broadcast_in_dim.79), calls=%async_computation.4 | async-start | bytes 32768 | tf_op jit(solution)/shard_map/all_to_all | solution.py:1426
  381.7 2.0 copy-start.2
  383.7 6.7 %copy-start.5 = (f32[32,2048]{1,0:T(8,128)S(1)}, f32[32,2048]{1,0:T(8,128)}, u32[]{:S(2)}) copy-start(f32[32,2048]{1,0:T(8,128)} %copy-done.4) | copy-start | bytes 786436
  390.4 2.5 copy-start.16
Sparse Core Ops, SparseCore 0:
  41.9 154.6 all-gather.6
  254.4 44.3 all-gather.8
  312.4 48.9 all-gather.10

commit v6 on v5

--- a/solution.py
+++ b/solution.py
@@ -139,6 +139,18 @@
         owners = [device for device in range(count) if device * self.size < edge]
         self.odd_owner = any(self.place(device)[1] for device in owners)
         self.all_sets = len(owners) > 2
+        edge = sum(rows * cols for _, rows, cols in SEGMENTS[:2])
+        self.near = all(
+            device < 2 * groups for device in range(count) if device * self.size < edge
+        )
+        offset, rows, cols = PIECES[5]
+        self.final_reps = sorted(
+            {
+                device // groups
+                for device in range(count)
+                if device * self.size < offset + rows * cols and (device + 1) * self.size > offset
+            }
+        )
         self.sent = [[] for _ in range(count)]
         self.grad_table = self.tabulate(lambda index: index, self.sent_row)
         self.late_table = self.tabulate(lambda index: index in (0, 1, 5), self.wide_row)
@@ -361,7 +373,7 @@
             out_ref[:, pl.ds(pl.multiple_of(pair * 2 * LANES, LANES), 2 * LANES)] = total
             return carry
 
-        lax.fori_loop(0, SEGMENTS[index][2] // LANES // 2, column, 0)
+        lax.fori_loop(0, SEGMENTS[index][2] // LANES // 2, column, 0, unroll=2)
 
 
     def back(self, index, first, count, values, grad_ref, left_ref, wide_ref):
@@ -384,7 +396,7 @@
                 left_ref[number, :, :size] += product_t(left, self.columns(index, block, pair))
             return carry
 
-        lax.fori_loop(0, cols // LANES // 2, column, 0)
+        lax.fori_loop(0, cols // LANES // 2, column, 0, unroll=2)
         for number, (_, _, tile0, tiles) in enumerate(blocks):
             start = 8 * tile0 // LANES * LANES
             turn = 8 * tile0 - start
@@ -532,7 +544,7 @@
         mixed_ref[v] = product(probs.astype(BF16), normed).astype(BF16)
         return carry
 
-    lax.fori_loop(0, views, view, 0)
+    lax.fori_loop(0, views, view, 0, unroll=2)
     mixed = mixed_ref[...].reshape(views * HEADROWS, D)
     valued = product(mixed, qkv_ref[:, 2 * D :]).reshape(views, HEADROWS, D)
     attended = jnp.sum(jnp.where(mask[None], valued, 0.0), 1).astype(BF16)
@@ -780,7 +792,8 @@
     wide_ref,
     sems,
 ):
-    shards = Shards(plan, gathered_ref, shards_ref, sems, reversed(range(plan.count)))
+    used = {block[0] for blocks in plan.blocks[2:] for block in blocks}
+    shards = Shards(plan, gathered_ref, shards_ref, sems, sorted(used, reverse=True))
     work = (values_ref, left_ref, wide_ref)
     norms, final = class_ref[4:8], class_ref[8:10]
 
@@ -1014,6 +1027,7 @@
     ahead_ref,
     common_hbm,
     behind_hbm,
+    rest_ref,
     line_ref,
     square_ref,
     common_ref,
@@ -1112,21 +1126,23 @@
         return total + kept * kept
 
     total = lax.fori_loop(0, plan.lines // STEPS, clear, jnp.zeros(shape, F32))
-    square_ref[...] = jnp.sum(total.reshape(STEPS // 8, 8, LANES), 0)
-
-
-def early_gradient(plan, table, ahead, common, behind):
+    total = jnp.sum(total, keepdims=True) + rest_ref[...]
+    square_ref[...] = jnp.broadcast_to(total[None], square_ref.shape)
+
+
+def early_gradient(plan, table, ahead, common, behind, rest):
     return pl.pallas_call(
         functools.partial(early_kernel, plan, table.shape[0] // 4),
         out_shape=[
             jax.ShapeDtypeStruct((plan.grad_scratch, LANES), F32),
-            jax.ShapeDtypeStruct((8, LANES), F32),
+            jax.ShapeDtypeStruct((plan.count, 1, LANES), F32),
         ],
         in_specs=[
             pl.BlockSpec(memory_space=pltpu.SMEM),
             pl.BlockSpec(memory_space=pltpu.VMEM),
             pl.BlockSpec(memory_space=pl.ANY),
             pl.BlockSpec(memory_space=pl.ANY),
+            pl.BlockSpec(memory_space=pltpu.VMEM),
         ],
         out_specs=[pl.BlockSpec(memory_space=pltpu.VMEM)] * 2,
         scratch_shapes=[
@@ -1138,7 +1154,7 @@
         cost_estimate=pl.CostEstimate(
             flops=10 * 10**9, bytes_accessed=10 * 10**6, transcendentals=0
         ),
-    )(table, ahead, common, behind)
+    )(table, ahead, common, behind, rest)
 
 
 def late_kernel(
@@ -1388,14 +1404,20 @@
     partial = partial + across(2, other).astype(F32)
     behind_rows, partial = lax.optimization_barrier((behind_rows, partial))
     behind_rows = gather_rows(behind_rows)
-    depth = partial.shape[0] // lines
-    partial = lax.all_to_all(
-        partial.astype(BF16).reshape(lines, depth, D), "rep", 0, 0, axis_index_groups=pairs
-    )
-    partial = jnp.sum(partial.astype(F32), 0)
-    early, squares = early_gradient(
-        plan, jnp.asarray(plan.grad_table)[device], ahead, common, behind_rows
-    )
+    if plan.near:
+        step = 1
+        while step < lines:
+            hops = [(r, r - 2 * step) for r in range(reps) if r // 2 % (2 * step) == step]
+            partial = partial + lax.ppermute(partial.astype(BF16), "rep", hops).astype(F32)
+            step *= 2
+        depth, first_rows, holds = partial.shape[0], 0, rep == 0
+    else:
+        depth = partial.shape[0] // lines
+        partial = lax.all_to_all(
+            partial.astype(BF16).reshape(lines, depth, D), "rep", 0, 0, axis_index_groups=pairs
+        )
+        partial = jnp.sum(partial.astype(F32), 0)
+        first_rows, holds = rep // 2 * depth, low
     class_rows = common[:2, CLASS:].astype(F32)
     class_normed, query = class_rows[0:1], class_rows[1:2]
     by_head = jnp.where(head_mask()[:HEADS], query, 0.0)
@@ -1410,22 +1432,20 @@
             jnp.zeros((SHARED - HEADROWS - 3,), F32),
         ]
     )
-    weights = lax.dynamic_slice_in_dim(weights, rep // 2 * depth, depth)
+    weights = lax.dynamic_slice_in_dim(weights, first_rows, depth)
     pieces = jnp.sum(weights * jnp.sum(partial * partial, 1))
-    squares = jnp.sum(squares) + jnp.where(low, pieces, 0.0)
-    squares = squares + jnp.sum(proto_squares[0])
-    summed = lax.all_to_all(
-        jnp.broadcast_to(partial.astype(BF16)[None], (lines, depth, D)),
-        "rep",
-        0,
-        0,
-        axis_index_groups=pairs,
-    ).reshape(-1, D)
-    shared, summed = trade_low(summed[SET:]).astype(F32), summed[:SET]
+    rest = jnp.where(holds, pieces, 0.0) + jnp.sum(proto_squares[0])
+    early, squares = early_gradient(
+        plan, jnp.asarray(plan.grad_table)[device], ahead, common, behind_rows, rest.reshape(1, 1)
+    )
+    summed = partial.astype(BF16)
+    if not plan.near:
+        summed = lax.all_to_all(
+            jnp.broadcast_to(summed[None], (lines, depth, D)), "rep", 0, 0, axis_index_groups=pairs
+        ).reshape(-1, D)
+    shared, summed = summed[SET:], summed[:SET]
     other, squares = lax.optimization_barrier((across(2, summed), squares))
-    squares = lax.all_to_all(
-        jnp.broadcast_to(squares.reshape(1, 1, 1), (count, 1, LANES)), BOTH, 0, 0
-    )
+    squares = lax.all_to_all(squares, BOTH, 0, 0)
     grad_norm = jnp.sqrt(jnp.sum(squares[:, 0, 0]))
     factor = jnp.minimum(1.0, CLIP_NORM / (grad_norm + 1e-06))
     summed = jnp.concatenate([jnp.where(far, other, summed), jnp.where(far, summed, other)], 0)
@@ -1436,8 +1456,17 @@
         summed = trade_low(summed)
     wide_grad = jnp.pad(summed.astype(F32), ((0, CHUNK), (0, 0)))
 
+    ends = shared[HEADROWS + 1 : HEADROWS + 3]
+    shared = trade_low(shared).astype(F32)
+    if plan.near:
+        for owner in plan.final_reps:
+            moved = lax.ppermute(ends, "rep", [(0, owner)]) if owner else ends
+            ends = jnp.where(rep == owner, moved, ends)
+        ends = ends.astype(F32)
+    else:
+        ends = shared[HEADROWS + 1 : HEADROWS + 3]
+    ends = jnp.pad(ends, ((0, 6), (0, 0)))
     sum_query, reach = shared[HEADROWS : HEADROWS + 1], shared[:HEADS]
-    ends = jnp.pad(shared[HEADROWS + 1 : HEADROWS + 3], ((0, 6), (0, 0)))
     left = jnp.concatenate([class_normed, reach, jnp.zeros((LANES - 1 - HEADS, D), F32)], 0)
     left = jnp.pad(left.T, ((0, CHUNK), (0, 0)))
     right = jnp.concatenate(

time: 409 us -> 394 us (0.963)
  blocking collectives: 20.9 us -> 0 us
  waiting for transfers between devices: 191 us -> 204 us
  Pallas kernels: 85.9 us -> 80.3 us
    ppermute x0 -> x3, waiting for transfers between devices: none -> 32.9 us  [the longest x2 32.9 us: per_device(): lax.ppermute(partial.astype(BF16), 'rep', hops).astype(F32)]
    all_to_all x1 -> x0, blocking collectives: 20.9 us -> none  [per_device(): lax.all_to_all(partial.astype(BF16).reshape(lines, depth, D), 'rep', 0, 0...]
    all_to_all x2 -> x1, waiting for transfers between devices: 19.4 us -> 0.01 us  [per_device(): squares = lax.all_to_all(squares, BOTH, 0, 0)]
    ppermute x0 -> x3, starting transfers between devices: none -> 4.19 us  [the longest x2 2.8 us: per_device(): lax.ppermute(partial.astype(BF16), 'rep', hops).astype(F32)]
    all_to_all x2 -> x1, starting transfers between devices: 10.1 us -> 6.13 us  [per_device(): squares = lax.all_to_all(squares, BOTH, 0, 0)]
  transfers between devices with their start and end apart: 20 -> 22, of which waited for: 10 -> 11; matrix products, arithmetic and copies ran while one was open for 9% -> 9% of each run, Pallas kernels for 12% -> 12%
where the time goes in v6:
time: 394 us; the launch traced here: 392 us
  waiting for transfers between devices  204 us (52%)
  Pallas kernels  80.3 us (20%)
  starting transfers between devices  35.5 us (9%)
  other arithmetic  30.5 us (8%)
  local copies, waits for them, and re-layouts  23.3 us (6%)
  between operations  18.4 us (5%)
    all_gather x1, waiting for transfers between devices, per_device(): gathered = lax.all_gather(shards, BOTH, axis=0, axis_index_groups=halves)  84.1 us
    ppermute x7, waiting for transfers between devices, trade(): return lax.ppermute(values, 'rep', swap)  48.8 us
    ppermute x2, waiting for transfers between devices, per_device(): lax.ppermute(partial.astype(BF16), 'rep', hops).astype(F32)  32.9 us
    pallas_call x1, Pallas kernels, forward(): pl.pallas_call(functools.partial(forward_kernel, plan), out_shape=[jax.Sh...  23.5 us
    pallas_call x1, Pallas kernels, tokens_back(): pl.pallas_call(tokens_back_kernel, grid=(views,), out_shape=[jax.ShapeDty...  16.7 us
    ppermute x3, waiting for transfers between devices, across(): return lax.ppermute(values, 'grp', [(g, g ^ bit) for g in range(groups)])  14.8 us
    pallas_call x1, Pallas kernels, rows_back(): pl.pallas_call(functools.partial(rows_back_kernel, plan), out_shape=[jax....  13.2 us
    pallas_call x2, Pallas kernels, lay_out(): pl.pallas_call(functools.partial(lay_kernel, plan), out_shape=jax.ShapeDt...  10.7 us
  transfers between devices with their start and end apart: 22, of which 11 were waited for; matrix products, arithmetic and copies ran while one was open for 9% of the time, Pallas kernels for 12%

profile of v6, /device:TPU:0, one launch (start us, length us, event | category | flops | bytes accessed | tf_op | source)
XLA Modules:
  0.0 392.4 jit_solution(7201291759964095829)
XLA Ops:
  7.2 2.2 broadcast_select_fusion.3
  10.4 5.4 %shard_map.222 = bf16[3648,128]{1,0:T(8,128)(2,1)S(1)} custom-call(s32[11]{0:T(128)S(1)} %fusion.27.tab_ref, f32[3464,128]{1,0:T(8,128)S(1)} %pad_bitcast_fusion.x_ref), custom_call_target="tpu_custom_call" | custom-call | tf_op jit(solution)/shard_map/pallas_call | solution.py:257
  15.7 2.9 collective-permute-start
  18.7 1.7 collective-permute-start.1
  20.4 2.8 collective-permute-start.2
  23.3 1.3 collective-permute-start.3
  24.8 5.4 %shard_map.221 = bf16[3648,128]{1,0:T(8,128)(2,1)S(1)} custom-call(s32[11]{0:T(128)S(1)} %fusion.27.tab_ref, f32[3464,128]{1,0:T(8,128)S(1)} %pad_bitcast_fusion.1.x_ref), custom_call_target="tpu_custom_call" | custom-call | tf_op jit(solution)/shard_map/pallas_call | solution.py:257
  30.1 10.0 %collective-permute-done.2 = bf16[2,32,2048]{2,1,0:T(8,128)(2,1)S(1)} collective-permute-done((bf16[2,32,2048]{2,1,0:T(8,128)(2,1)S(1)}, bf16[2,32,2048]{2,1,0:T(8,128)(2,1)S(1)}, u32[]{:S(2)}, u32[]{:S(2)}) %collective-permute-start.2) | collective-permute-done | bytes 262176 | tf_op jit(solution)/shard_map/ppermute | solution.py:1307
  40.4 1.4 pad_maximum_fusion
  42.0 1.0 constant_dynamic-slice_fusion
  44.1 3.6 copy.64
  47.6 1.0 collective-permute-start.4
  49.7 44.5 %collective-permute-done.5 = f32[4]{0:T(128)S(1)} collective-permute-done((f32[4]{0:T(128)S(1)}, f32[4]{0:T(128)S(1)}, u32[]{:S(2)}, u32[]{:S(2)}) %collective-permute-start.5) | collective-permute-done | bytes 48 | tf_op jit(solution)/shard_map/ppermute | solution.py:1293
  97.7 1.2 fusion.6.others_ref
  98.8 3.6 copy.65
  102.5 2.1 broadcast_select_fusion.1
  104.6 3.2 fusion.30
  107.8 4.7 %copy.70.pixels_ref = bf16[8,208,768]{2,1,0:T(8,128)(2,1)} copy(bf16[8,208,768]{1,2,0:T(8,128)(2,1)} %get-tuple-element.110) | data formatting | bytes 5111808 | tf_op jit(solution)/shard_map/jit(_pad)/pad | solution.py:1318
  112.5 84.1 %all-gather.7.cloned.1.call-done = bf16[32,3648,128]{2,1,0:T(8,128)(2,1)} async-done(((bf16[2,3648,128]{2,1,0:T(8,128)(2,1)}), bf16[32,3648,128]{2,1,0:T(8,128)(2,1)}) %all-gather.7.cloned.1.call-update) | async-done | bytes 29884432 | tf_op jit(solution)/shard_map/all_gather | solution.py:1314
  196.6 23.5 %shard_map.223 = (f32[8,208,768]{2,1,0:T(8,128)}, f32[8,208,128]{2,1,0:T(8,128)}, f32[8,16,208]{2,1,0:T(8,128)}, bf16[8,16,768]{2,1,0:T(8,128)(2,1)}, bf16[16,76...) custom-call(bf16[16,2,228,16,128]{4,3,2,1,0:T(8,128)(2,1)} %bitcast., ...), custom_call_target="tpu_custom_call" | custom-call | flops 60000002048 | bytes 40000000 | tf_op jit(solution)/shard_map/pallas_call | solution.py:626
  220.1 4.8 %all-to-all-start = ((bf16[32,8,896]{2,1,0:T(8,128)(2,1)}), bf16[32,8,896]{2,1,0:T(8,128)(2,1)S(1)}, u32[]{:S(2)}, u32[]{:S(2)}) async-start(bf16[32,8,896]{2,1,0:T(8,128)(2,1)} %get-tuple-element.61), calls=%async_computation | async-start | bytes 917504 | tf_op jit(solution)/shard_map/all_to_all | solution.py:1340
  227.4 1.7 collective-permute-start.7
  229.1 10.0 %all-to-all-done = bf16[32,8,896]{2,1,0:T(8,128)(2,1)S(1)} async-done(((bf16[32,8,896]{2,1,0:T(8,128)(2,1)}), bf16[32,8,896]{2,1,0:T(8,128)(2,1)S(1)}, u32[]{:S(2)}, u32[]{:S(2)}) %all-to-all-start) | async-done | bytes 458784 | tf_op jit(solution)/shard_map/all_to_all | solution.py:1340
  239.9 4.7 %shard_map.224 = (f32[4,32,256]{2,1,0:T(8,128)}, f32[1,2048]{1,0:T(1,128)}) custom-call(s32[1]{0:T(128)} %bitcast.22.start_ref, bf16[2,128,256]{2,1,0:T(8,128)(2,1)S(1)} %bitcast.73, bf16[256,2048]{1,0:T(8,128)(2,1)S(1)} %multiply_convert_fusion.columns_ref, bf16[256,2048]{1,0:T(8,128)(2,1)S(1)} %copy-done.3, f32[1,2048]{1,0:T(1,128)S(1)} %bitcast.76), custom_call_target="tpu_custom_call" | custom-call | flops 3000000000 | bytes 6000000 | tf_op jit(solution)/shard_map/pallas_call | solution.py:710
  244.6 3.3 all-to-all-start.1
  248.8 3.7 all-to-all-done.1.note_ref
  252.6 13.2 %shard_map.225 = (bf16[8,9728]{1,0:T(8,128)(2,1)S(1)}, f32[8,768]{1,0:T(8,128)S(1)}, f32[8,768]{1,0:T(8,128)S(1)}) custom-call(s32[1]{0:T(128)} %bitcast.21.low_ref, bf16[16,2,228,16,128]{4,3,2,1,0:T(8,128)(2,1)} %bitcast.84, f32[4,32,256]{2,1,0:T(8,128)S(1)} %all-to-all-done.1.note_ref, f32[16,768]{1,0:T(8,128)S(1)} %copy-done.7, f32[8,3072]{1,0:T(8,128)S(1)} %copy-done.9, ...), custom_call_target="tpu_custom_call" | custom-call | flops 30000001024 | bytes 30000000 | tf_op jit(solution)/shard_map/pallas_call | solution.py:854
  265.8 1.2 collective-permute-start.8
  267.0 2.5 shard_map.226
  270.2 1.0 collective-permute-done.8
  271.9 16.7 %shard_map.227 = (f32[608,768]{1,0:T(8,128)}, bf16[608,768]{1,0:T(8,128)(2,1)}) custom-call(s32[1]{0:T(128)} %bitcast.26.odd_ref, bf16[8,9728]{1,0:T(8,128)(2,1)} %copy-done.6, f32[8,768]{1,0:T(8,128)} %copy-done.11, f32[8,768]{1,0:T(8,128)} %copy-done.12, f32[8,208,768]{2,1,0:T(8,128)} %get-tuple-element.79.unit_ref, ...), custom_call_target="tpu_custom_call" | custom-call | flops 15000000512 | bytes 15000000 | tf_op jit(solution)/shard_map/pallas_call | solution.py:989
  288.7 2.7 collective-permute-done.9
  291.3 1.7 convert_add_fusion
  293.2 1.1 collective-permute-start.10
  294.4 12.2 %collective-permute-done.10 = bf16[320,768]{1,0:T(8,128)(2,1)S(1)} collective-permute-done((bf16[320,768]{1,0:T(8,128)(2,1)S(1)}, bf16[320,768]{1,0:T(8,128)(2,1)S(1)}, u32[]{:S(2)}, u32[]{:S(2)}) %collective-permute-start.10) | collective-permute-done | bytes 491552 | tf_op jit(solution)/shard_map/ppermute | solution.py:1397
  306.7 1.3 collective-permute-start.11
  308.0 1.2 fusion.26.tab_ref
  309.2 16.7 %collective-permute-done.11 = bf16[320,768]{1,0:T(8,128)(2,1)S(1)} collective-permute-done((bf16[320,768]{1,0:T(8,128)(2,1)S(1)}, bf16[320,768]{1,0:T(8,128)(2,1)S(1)}, u32[]{:S(2)}, u32[]{:S(2)}) %collective-permute-start.11) | collective-permute-done | bytes 491552 | tf_op jit(solution)/shard_map/ppermute | solution.py:1411
  326.0 1.5 collective-permute-start.12
  329.0 16.2 %collective-permute-done.12 = bf16[320,768]{1,0:T(8,128)(2,1)S(1)} collective-permute-done((bf16[320,768]{1,0:T(8,128)(2,1)S(1)}, bf16[320,768]{1,0:T(8,128)(2,1)S(1)}, u32[]{:S(2)}, u32[]{:S(2)}) %collective-permute-start.12) | collective-permute-done | bytes 491552 | tf_op jit(solution)/shard_map/ppermute | solution.py:1411
  345.5 1.4 collective-permute-start.15
  348.7 3.2 collective-permute-done.14
  356.9 3.7 shard_map.228
  360.6 6.1 %all-to-all-start.2 = ((f32[32,1,128]{2,1,0:T(1,128)}), f32[32,1,128]{2,1,0:T(1,128)S(1)}, u32[]{:S(2)}, u32[]{:S(2)}) async-start(f32[32,1,128]{2,1,0:T(1,128)} %get-tuple-element.93), calls=%async_computation.2 | async-start | bytes 32768 | tf_op jit(solution)/shard_map/all_to_all | solution.py:1448
  367.0 1.7 copy-done.2
  368.8 5.3 %shard_map.229 = f32[3456,128]{1,0:T(8,128)S(1)} custom-call(s32[9]{0:T(128)S(1)} %fusion.25.tab_ref, f32[6736,128]{1,0:T(8,128)S(1)} %copy-done.2, f32[704,768]{1,0:T(8,128)S(1)} %fusion.9.wide_ref, f32[896,128]{1,0:T(8,128)S(1)} %pad.45.left_ref, f32[128,1536]{1,0:T(8,128)S(1)} %fusion.10.right_ref, f32[8,768]{1,0:T(8,128)S(1)} %pad_convert_fusion.ends_ref), custom_call_target="tpu_custom_call" | custom-call | tf_op jit(solution)/shard_map/pallas_call | solution.py:1240
  375.5 2.4 multiply_add_fusion.2
  377.9 6.8 %multiply_add_fusion = (f32[441096]{0:T(1024)}, f32[441096]{0:T(1024)}, f32[441096]{0:T(1024)}, f32[441096]{0:T(1024)}) fusion(f32[441096]{0:T(1024)S(1)} %copy-done.16, f32[441096]{0:T(1024)} %param.14, f32[]{:T(128)S(6)} %min.3, f32[442368]{0:T(1024)S(1)} %bitcast.72, f32[441096]{0:T(1024)} %param.15, f32[441096]{0:T(1024)} %param.16), kind=kLoop, calls=%fused_computation.21 | loop fusion | flops 8380824 | bytes 15879460 | tf_op jit(solution)/shard_map/add | solution.py:1489
  (144 shorter events, 20.2 us)
Async XLA Ops:
  7.2 189.4 %all-gather.7.cloned.1.call-start = ((), (), s32[]{:S(2)}) async-start(), calls=%async_computation.3 | async-start | bytes 31752192 | tf_op jit(solution)/shard_map/all_gather | solution.py:1314
  9.6 9.0 %copy-start.17 = (f32[32,2048]{1,0:T(8,128)S(1)}, f32[32,2048]{1,0:T(8,128)}, u32[]{:S(2)}) copy-start(f32[32,2048]{1,0:T(8,128)} %param.21) | copy-start | bytes 786436
  9.6 9.0 %copy-start.18 = (f32[32,2048]{1,0:T(8,128)S(1)}, f32[32,2048]{1,0:T(8,128)}, u32[]{:S(2)}) copy-start(f32[32,2048]{1,0:T(8,128)} %param.18) | copy-start | bytes 786436
  15.7 24.4 %collective-permute-start = (bf16[3648,128]{1,0:T(8,128)(2,1)S(1)}, bf16[3648,128]{1,0:T(8,128)(2,1)S(1)}, u32[]{:S(2)}, u32[]{:S(2)}) collective-permute-start(bf16[3648,128]{1,0:T(8,128)(2,1)S(1)} %shard_map.222), channel_id=1, source_target_pairs={{0,4},{4,0},{8,12},{12,8},{16,20},{20,16},{24,28},{28,24},{1,5},{5... | collective-permute-start | bytes 2801672 | tf_op jit(solution)/shard_map/ppermute | solution.py:1293
  18.7 11.4 %collective-permute-start.1 = (bf16[2,32,2048]{2,1,0:T(8,128)(2,1)S(1)}, bf16[2,32,2048]{2,1,0:T(8,128)(2,1)S(1)}, u32[]{:S(2)}, u32[]{:S(2)}) collective-permute-start(bf16[2,32,2048]{2,1,0:T(8,128)(2,1)S(1)} %pad_maximum_fusion.2), channel_id=1, source_target_pairs={{0,8},{4,12},{8,16},{12,20},{16,24},{20,28},{24,0},{28,4},{1,9},{5... | collective-permute-start | bytes 786440 | tf_op jit(solution)/shard_map/ppermute | solution.py:1307
  20.4 19.7 %collective-permute-start.2 = (bf16[2,32,2048]{2,1,0:T(8,128)(2,1)S(1)}, bf16[2,32,2048]{2,1,0:T(8,128)(2,1)S(1)}, u32[]{:S(2)}, u32[]{:S(2)}) collective-permute-start(bf16[2,32,2048]{2,1,0:T(8,128)(2,1)S(1)} %pad_maximum_fusion.2), channel_id=1, source_target_pairs={{0,16},{4,20},{8,24},{12,28},{16,0},{20,4},{24,8},{28,12},{1,17},{... | collective-permute-start | bytes 786440 | tf_op jit(solution)/shard_map/ppermute | solution.py:1307
  23.3 16.8 %collective-permute-start.3 = (bf16[2,32,2048]{2,1,0:T(8,128)(2,1)S(1)}, bf16[2,32,2048]{2,1,0:T(8,128)(2,1)S(1)}, u32[]{:S(2)}, u32[]{:S(2)}) collective-permute-start(bf16[2,32,2048]{2,1,0:T(8,128)(2,1)S(1)} %pad_maximum_fusion.2), channel_id=1, source_target_pairs={{0,24},{4,28},{8,0},{12,4},{16,8},{20,12},{24,16},{28,20},{1,25},{... | collective-permute-start | bytes 786440 | tf_op jit(solution)/shard_map/ppermute | solution.py:1307
  43.1 5.6 %copy-start.20 = (s32[4]{0:T(128)S(1)}, s32[4]{0:T(128)}, u32[]{:S(2)}) copy-start(s32[4]{0:T(128)} %param.24) | copy-start | bytes 52
  43.1 51.9 %collective-permute-start.6 = (bf16[4,2,32,2048]{3,2,1,0:T(8,128)(2,1)}, bf16[4,2,32,2048]{3,2,1,0:T(8,128)(2,1)S(1)}, u32[]{:S(2)}, u32[]{:S(2)}) collective-permute-start(bf16[4,2,32,2048]{3,2,1,0:T(8,128)(2,1)} %constant_dynamic-slice_fusion), channel_id=1, source_target_pairs={{0,4},{4,0},{8,12},{12,8},{16,20},{20,16},{24,28},{28,24},{1,5},{5... | collective-permute-start | bytes 3145736 | tf_op jit(solution)/shard_map/ppermute | solution.py:1293
  47.6 51.2 %collective-permute-start.4 = (bf16[4,196,768]{2,0,1:T(4,128)(2,1)}, bf16[4,196,768]{2,0,1:T(4,128)(2,1)}, u32[]{:S(2)}, u32[]{:S(2)}) collective-permute-start(bf16[4,196,768]{2,0,1:T(4,128)(2,1)} %param.23), channel_id=1, source_target_pairs={{0,4},{4,0},{8,12},{12,8},{16,20},{20,16},{24,28},{28,24},{1,5},{5... | collective-permute-start | bytes 3612680 | tf_op jit(solution)/shard_map/ppermute | solution.py:1293
  48.7 45.5 %collective-permute-start.5 = (f32[4]{0:T(128)S(1)}, f32[4]{0:T(128)S(1)}, u32[]{:S(2)}, u32[]{:S(2)}) collective-permute-start(f32[4]{0:T(128)S(1)} %convert_element_type.76), channel_id=1, source_target_pairs={{0,4},{4,0},{8,12},{12,8},{16,20},{20,16},{24,28},{28,24},{1,5},{5... | collective-permute-start | bytes 56 | tf_op jit(solution)/shard_map/ppermute | solution.py:1293
  96.1 1.4 copy-start
  220.1 19.7 %copy-start.3 = (bf16[256,2048]{1,0:T(8,128)(2,1)S(1)}, bf16[256,2048]{1,0:T(8,128)(2,1)}, u32[]{:S(2)}) copy-start(bf16[256,2048]{1,0:T(8,128)(2,1)} %fusion.6.others_ref) | copy-start | bytes 3145732
  220.1 19.7 %copy-start.8 = (f32[2048]{0:T(1024)S(1)}, f32[2048]{0:T(1024)}, u32[]{:S(2)}) copy-start(f32[2048]{0:T(1024)} %param.22) | copy-start | bytes 24580
  220.1 19.0 %all-to-all-start = ((bf16[32,8,896]{2,1,0:T(8,128)(2,1)}), bf16[32,8,896]{2,1,0:T(8,128)(2,1)S(1)}, u32[]{:S(2)}, u32[]{:S(2)}) async-start(bf16[32,8,896]{2,1,0:T(8,128)(2,1)} %get-tuple-element.61), calls=%async_computation | async-start | bytes 917504 | tf_op jit(solution)/shard_map/all_to_all | solution.py:1340
  227.4 12.4 %collective-permute-start.7 = (bf16[8,12032]{1,0:T(8,128)(2,1)S(1)}, bf16[8,12032]{1,0:T(8,128)(2,1)}, u32[]{:S(2)}, u32[]{:S(2)}) collective-permute-start(bf16[8,12032]{1,0:T(8,128)(2,1)S(1)} %fusion.16), channel_id=1, source_target_pairs={{0,4},{4,0},{8,12},{12,8},{16,20},{20,16},{24,28},{28,24},{1,5},{5... | collective-permute-start | bytes 577544 | tf_op jit(solution)/shard_map/ppermute | solution.py:1293
  239.8 8.2 %copy-start.19 = (bf16[8,2048]{1,0:T(8,128)(2,1)S(1)}, bf16[8,2048]{1,0:T(8,128)(2,1)}, u32[]{:S(2)}) copy-start(bf16[8,2048]{1,0:T(8,128)(2,1)} %get-tuple-element.63) | copy-start | bytes 98308
  239.8 12.7 %copy-start.7 = (f32[16,768]{1,0:T(8,128)S(1)}, f32[16,768]{1,0:T(8,128)}, u32[]{:S(2)}) copy-start(f32[16,768]{1,0:T(8,128)} %get-tuple-element.64.class_ref) | copy-start | bytes 147460
  239.8 12.7 %copy-start.9 = (f32[8,3072]{1,0:T(8,128)S(1)}, f32[8,3072]{1,0:T(8,128)}, u32[]{:S(2)}) copy-start(f32[8,3072]{1,0:T(8,128)} %get-tuple-element.71.hidden_ref) | copy-start | bytes 294916
  239.8 12.7 %copy-start.10 = (f32[4,8,768]{2,1,0:T(8,128)S(1)}, f32[4,8,768]{2,1,0:T(8,128)}, u32[]{:S(2)}) copy-start(f32[4,8,768]{2,1,0:T(8,128)} %get-tuple-element.75.middle_ref) | copy-start | bytes 294916
  239.8 12.7 %copy-start.13 = (f32[8,2048]{1,0:T(8,128)S(1)}, f32[8,2048]{1,0:T(8,128)}, u32[]{:S(2)}) copy-start(f32[8,2048]{1,0:T(8,128)} %get-tuple-element.72.one_ref) | copy-start | bytes 196612
  239.8 12.7 %copy-start.14 = (f32[8,2048]{1,0:T(8,128)S(1)}, f32[8,2048]{1,0:T(8,128)}, u32[]{:S(2)}) copy-start(f32[8,2048]{1,0:T(8,128)} %get-tuple-element.73.two_ref) | copy-start | bytes 196612
  239.9 12.7 %copy-start.15 = (f32[8,256]{1,0:T(8,128)S(1)}, f32[8,256]{1,0:T(8,128)}, u32[]{:S(2)}) copy-start(f32[8,256]{1,0:T(8,128)} %get-tuple-element.74.bottle_ref) | copy-start | bytes 24580
  244.6 7.9 %all-to-all-start.1 = ((f32[4,32,256]{2,1,0:T(8,128)}), f32[4,32,256]{2,1,0:T(8,128)S(1)}, u32[]{:S(2)}, u32[]{:S(2)}) async-start(f32[4,32,256]{2,1,0:T(8,128)} %get-tuple-element.70), calls=%async_computation.1 | async-start | bytes 262144 | tf_op jit(solution)/shard_map/all_to_all | solution.py:1364
  247.9 104.3 %all-gather.9.cloned.1.call-start = ((), (), s32[]{:S(2)}) async-start(), calls=%async_computation.4 | async-start | bytes 3272704 | tf_op jit(solution)/shard_map/all_gather | solution.py:1346
  248.8 108.1 %all-gather.11.cloned.1.call-start = ((), (), s32[]{:S(2)}) async-start(), calls=%async_computation.5 | async-start | bytes 2646016 | tf_op jit(solution)/shard_map/all_gather | solution.py:1346
  252.6 14.4 %copy-start.1 = (f32[1,4,2,32,2048]{4,3,2,1,0:T(8,128)S(1)}, f32[1,4,2,32,2048]{4,3,2,1,0:T(8,128)}, u32[]{:S(2)}) copy-start(f32[1,4,2,32,2048]{4,3,2,1,0:T(8,128)} %copy-done) | copy-start | bytes 6291460
  265.8 3.7 copy-start.11
  265.8 3.7 copy-start.12
  265.8 5.5 %copy-start.6 = (bf16[8,9728]{1,0:T(8,128)(2,1)}, bf16[8,9728]{1,0:T(8,128)(2,1)S(1)}, u32[]{:S(2)}) copy-start(bf16[8,9728]{1,0:T(8,128)(2,1)S(1)} %get-tuple-element.76.behind_ref) | copy-start | bytes 466948
  265.8 5.5 %collective-permute-start.8 = (bf16[8,9728]{1,0:T(8,128)(2,1)S(1)}, bf16[8,9728]{1,0:T(8,128)(2,1)S(1)}, u32[]{:S(2)}, u32[]{:S(2)}) collective-permute-start(bf16[8,9728]{1,0:T(8,128)(2,1)S(1)} %get-tuple-element.76.behind_ref), channel_id=1, source_target_pairs={{0,4},{4,0},{8,12},{12,8},{16,20},{20,16},{24,28},{28,24},{1,5},{5... | collective-permute-start | bytes 466952 | tf_op jit(solution)/shard_map/ppermute | solution.py:1293
  269.5 0.7 copy-start.4
  288.6 2.7 collective-permute-start.9
  293.2 13.3 %collective-permute-start.10 = (bf16[320,768]{1,0:T(8,128)(2,1)S(1)}, bf16[320,768]{1,0:T(8,128)(2,1)S(1)}, u32[]{:S(2)}, u32[]{:S(2)}) collective-permute-start(bf16[320,768]{1,0:T(8,128)(2,1)S(1)} %pad_maximum_fusion.1), channel_id=1, source_target_pairs={{0,2},{1,3},{2,0},{3,1},{4,6},{5,7},{6,4},{7,5},{8,10},{9,11},{10,... | collective-permute-start | bytes 1474568 | tf_op jit(solution)/shard_map/ppermute | solution.py:1397
  306.7 19.2 %collective-permute-start.11 = (bf16[320,768]{1,0:T(8,128)(2,1)S(1)}, bf16[320,768]{1,0:T(8,128)(2,1)S(1)}, u32[]{:S(2)}, u32[]{:S(2)}) collective-permute-start(bf16[320,768]{1,0:T(8,128)(2,1)S(1)} %convert_element_type.86), channel_id=1, source_target_pairs={{8,0},{12,4},{24,16},{28,20},{9,1},{13,5},{25,17},{29,21},{10,2},{... | collective-permute-start | bytes 1474568 | tf_op jit(solution)/shard_map/ppermute | solution.py:1411
  326.0 19.1 %collective-permute-start.12 = (bf16[320,768]{1,0:T(8,128)(2,1)S(1)}, bf16[320,768]{1,0:T(8,128)(2,1)S(1)}, u32[]{:S(2)}, u32[]{:S(2)}) collective-permute-start(bf16[320,768]{1,0:T(8,128)(2,1)S(1)} %fusion.12), channel_id=1, source_target_pairs={{16,0},{20,4},{17,1},{21,5},{18,2},{22,6},{19,3},{23,7}} | collective-permute-start | bytes 1474568 | tf_op jit(solution)/shard_map/ppermute | solution.py:1411
  345.5 3.2 collective-permute-start.15
  347.5 13.1 %collective-permute-start.13 = (bf16[288,768]{1,0:T(8,128)(2,1)S(1)}, bf16[288,768]{1,0:T(8,128)(2,1)S(1)}, u32[]{:S(2)}, u32[]{:S(2)}) collective-permute-start(bf16[288,768]{1,0:T(8,128)(2,1)S(1)} %slice.125), channel_id=1, source_target_pairs={{0,2},{1,3},{2,0},{3,1},{4,6},{5,7},{6,4},{7,5},{8,10},{9,11},{10,... | collective-permute-start | bytes 1327112 | tf_op jit(solution)/shard_map/ppermute | solution.py:1397
  347.9 4.1 %collective-permute-start.14 = (bf16[32,768]{1,0:T(8,128)(2,1)S(1)}, bf16[32,768]{1,0:T(8,128)(2,1)S(1)}, u32[]{:S(2)}, u32[]{:S(2)}) collective-permute-start(bf16[32,768]{1,0:T(8,128)(2,1)S(1)} %slice.126), channel_id=1, source_target_pairs={{0,4},{4,0},{8,12},{12,8},{16,20},{20,16},{24,28},{28,24},{1,5},{5... | collective-permute-start | bytes 147464 | tf_op jit(solution)/shard_map/ppermute | solution.py:1293
  360.6 13.5 %all-to-all-start.2 = ((f32[32,1,128]{2,1,0:T(1,128)}), f32[32,1,128]{2,1,0:T(1,128)S(1)}, u32[]{:S(2)}, u32[]{:S(2)}) async-start(f32[32,1,128]{2,1,0:T(1,128)} %get-tuple-element.93), calls=%async_computation.2 | async-start | bytes 32768 | tf_op jit(solution)/shard_map/all_to_all | solution.py:1448
  366.8 2.0 copy-start.2
  368.8 6.7 %copy-start.5 = (f32[32,2048]{1,0:T(8,128)S(1)}, f32[32,2048]{1,0:T(8,128)}, u32[]{:S(2)}) copy-start(f32[32,2048]{1,0:T(8,128)} %copy-done.4) | copy-start | bytes 786436
  375.5 2.5 copy-start.16
Sparse Core Ops, SparseCore 0:
  41.9 154.6 all-gather.6
  251.5 44.0 all-gather.8
  306.7 43.6 all-gather.10

commit v7 on v6

--- a/solution.py
+++ b/solution.py
@@ -87,6 +87,10 @@
     return -(-value // step) * step
 
 
+def steps_at_once(count):
+    return max(size for size in range(1, 8) if count % size == 0)
+
+
 def shard_parts(start, stop, table):
     parts = []
     line0 = start // LANES
@@ -109,6 +113,7 @@
         self.count, self.groups = count, groups
         self.size = PFLAT // count
         self.lines = round_up(-(-self.size // LANES) + 1, STEPS)
+        self.steps = self.lines // STEPS
         self.scratch = FRONT + self.lines + 8 * max(WIDTHS) + 16
         table = []
         self.blocks = [[] for _ in SEGMENTS]
@@ -183,6 +188,7 @@
         for device, entry in enumerate(table):
             entry += [-1, 0, 0, 0] * (most - len(entry) // 4)
             entry.insert(0, device * self.size % LANES)
+            entry += [device < self.groups, device % 4 == 1]
         return np.array(table, np.int32)
 
     def sent_row(self, device, index, row0, chunks):
@@ -219,7 +225,7 @@
         line_ref[pl.ds(pl.multiple_of(FRONT + base, 8), STEPS), :] = both[8:]
         return carry
 
-    lax.fori_loop(0, plan.lines // STEPS, align, 0)
+    lax.fori_loop(0, plan.steps, align, 0, unroll=steps_at_once(plan.steps))
     for part in range(2):
         kind, base, pairs, odd, target = (tab_ref[1 + 5 * part + i] for i in range(5))
         for index, width in enumerate(WIDTHS):
@@ -751,13 +757,12 @@
     lines = pl.ds(start, grad_ref.shape[0])
     grad = work_ref[lines, :] * scale - table_ref[lines, :] * (scale * scale * scale * inner)
     grad_ref[...] = grad
-    square = jnp.sum(grad * grad, 0, keepdims=True)
-    square_ref[...] = jnp.broadcast_to(square, square_ref.shape)
+    square_ref[...] = jnp.broadcast_to(jnp.sum(grad * grad, keepdims=True), square_ref.shape)
 
 
 def prototypes_back(start, depth, *values):
     count, width = values[0].shape[1], values[1].shape[1]
-    shapes = [(depth, width), (8, width)]
+    shapes = [(depth, width), (8, LANES)]
     return pl.pallas_call(
         proto_back_kernel,
         out_shape=[jax.ShapeDtypeStruct(shape, F32) for shape in shapes],
@@ -1028,12 +1033,13 @@
     common_hbm,
     behind_hbm,
     rest_ref,
-    line_ref,
-    square_ref,
-    common_ref,
-    behind_ref,
-    sem,
+    *refs,
 ):
+    line_ref, square_ref, common_ref, behind_ref, class_ref, sem, class_sem = refs[-7:]
+    class_copy = pltpu.make_async_copy(
+        common_hbm.at[pl.ds(0, TILE), pl.ds(CLASS, D)], class_ref, class_sem
+    )
+    class_copy.start()
     line_ref[...] = jnp.zeros(line_ref.shape, F32)
 
     def fetch(source, target, column, size):
@@ -1125,14 +1131,31 @@
         line_ref[lines, :] = kept
         return total + kept * kept
 
-    total = lax.fori_loop(0, plan.lines // STEPS, clear, jnp.zeros(shape, F32))
-    total = jnp.sum(total, keepdims=True) + rest_ref[...]
+    total = lax.fori_loop(
+        0, plan.steps, clear, jnp.zeros(shape, F32), unroll=steps_at_once(plan.steps)
+    )
+    total = jnp.sum(total, keepdims=True) + rest_ref[0:1, 0:1]
+    class_copy.wait()
+    if len(refs) > 7:
+        holds, twice = (tab_ref[1 + 4 * most + which] for which in range(2))
+        rows = jnp.sum(refs[0][...] * refs[0][...], 1, keepdims=True)
+        place = lax.broadcasted_iota(jnp.int32, (SET, 1), 0)
+        pieces = jnp.sum(jnp.where((place < 8) & (twice != 0), 0.0, rows[:SET]), keepdims=True)
+        classes = class_ref[...].astype(F32)
+        by_head = jnp.where(head_mask(), classes[1:2], 0.0)
+        by_head = jnp.sum(by_head * by_head, 1, keepdims=True)
+        normed = jnp.sum(classes[0:1] * classes[0:1], 1, keepdims=True)
+        outer = jnp.sum(rows[SET : SET + HEADROWS] * by_head, keepdims=True)
+        outer = outer + rows[SET + HEADROWS : SET + HEADROWS + 1] * normed
+        outer = outer + rows[SET + HEADROWS + 1 : SET + HEADROWS + 2]
+        outer = outer + rows[SET + HEADROWS + 2 : SET + HEADROWS + 3]
+        total = total + jnp.where(holds != 0, pieces + outer / plan.groups, 0.0)
     square_ref[...] = jnp.broadcast_to(total[None], square_ref.shape)
 
 
-def early_gradient(plan, table, ahead, common, behind, rest):
+def early_gradient(plan, table, ahead, common, behind, *values):
     return pl.pallas_call(
-        functools.partial(early_kernel, plan, table.shape[0] // 4),
+        functools.partial(early_kernel, plan, (table.shape[0] - 3) // 4),
         out_shape=[
             jax.ShapeDtypeStruct((plan.grad_scratch, LANES), F32),
             jax.ShapeDtypeStruct((plan.count, 1, LANES), F32),
@@ -1142,19 +1165,21 @@
             pl.BlockSpec(memory_space=pltpu.VMEM),
             pl.BlockSpec(memory_space=pl.ANY),
             pl.BlockSpec(memory_space=pl.ANY),
-            pl.BlockSpec(memory_space=pltpu.VMEM),
-        ],
+        ]
+        + [pl.BlockSpec(memory_space=pltpu.VMEM)] * len(values),
         out_specs=[pl.BlockSpec(memory_space=pltpu.VMEM)] * 2,
         scratch_shapes=[
             pltpu.VMEM(common.shape, BF16),
             pltpu.VMEM((behind.shape[0], F), BF16),
+            pltpu.VMEM((TILE, D), BF16),
+            pltpu.SemaphoreType.DMA,
             pltpu.SemaphoreType.DMA,
         ],
         compiler_params=pltpu.CompilerParams(vmem_limit_bytes=60 * 1024 * 1024),
         cost_estimate=pl.CostEstimate(
             flops=10 * 10**9, bytes_accessed=10 * 10**6, transcendentals=0
         ),
-    )(table, ahead, common, behind, rest)
+    )(table, ahead, common, behind, *values)
 
 
 def late_kernel(
@@ -1233,12 +1258,12 @@
         out_ref[pl.ds(start, STEPS), :] = both[:STEPS]
         return carry
 
-    lax.fori_loop(0, plan.lines // STEPS, align, 0)
+    lax.fori_loop(0, plan.steps, align, 0, unroll=steps_at_once(plan.steps))
 
 
 def late_gradient(plan, table, lines, *values):
     return pl.pallas_call(
-        functools.partial(late_kernel, plan, table.shape[0] // 4),
+        functools.partial(late_kernel, plan, (table.shape[0] - 3) // 4),
         out_shape=jax.ShapeDtypeStruct((plan.lines, LANES), F32),
         in_specs=[pl.BlockSpec(memory_space=pltpu.SMEM), pl.BlockSpec(memory_space=pl.ANY)]
         + [pl.BlockSpec(memory_space=pltpu.VMEM)] * len(values),
@@ -1410,33 +1435,33 @@
             hops = [(r, r - 2 * step) for r in range(reps) if r // 2 % (2 * step) == step]
             partial = partial + lax.ppermute(partial.astype(BF16), "rep", hops).astype(F32)
             step *= 2
-        depth, first_rows, holds = partial.shape[0], 0, rep == 0
     else:
         depth = partial.shape[0] // lines
         partial = lax.all_to_all(
             partial.astype(BF16).reshape(lines, depth, D), "rep", 0, 0, axis_index_groups=pairs
         )
         partial = jnp.sum(partial.astype(F32), 0)
-        first_rows, holds = rep // 2 * depth, low
     class_rows = common[:2, CLASS:].astype(F32)
     class_normed, query = class_rows[0:1], class_rows[1:2]
     by_head = jnp.where(head_mask()[:HEADS], query, 0.0)
-    twice = odd & ~far & (jnp.arange(SET) < 8)
-    weights = jnp.concatenate(
-        [
-            jnp.where(twice, 0.0, 1.0),
-            jnp.sum(by_head * by_head, 1) / groups,
-            jnp.zeros((HEADROWS - HEADS,), F32),
-            jnp.sum(class_normed * class_normed)[None] / groups,
-            jnp.full((2,), 1.0 / groups, F32),
-            jnp.zeros((SHARED - HEADROWS - 3,), F32),
-        ]
-    )
-    weights = lax.dynamic_slice_in_dim(weights, first_rows, depth)
-    pieces = jnp.sum(weights * jnp.sum(partial * partial, 1))
-    rest = jnp.where(holds, pieces, 0.0) + jnp.sum(proto_squares[0])
+    values = (proto_squares, partial)
+    if not plan.near:
+        twice = odd & ~far & (jnp.arange(SET) < 8)
+        weights = jnp.concatenate(
+            [
+                jnp.where(twice, 0.0, 1.0),
+                jnp.sum(by_head * by_head, 1) / groups,
+                jnp.zeros((HEADROWS - HEADS,), F32),
+                jnp.sum(class_normed * class_normed)[None] / groups,
+                jnp.full((2,), 1.0 / groups, F32),
+                jnp.zeros((SHARED - HEADROWS - 3,), F32),
+            ]
+        )
+        weights = lax.dynamic_slice_in_dim(weights, rep // 2 * depth, depth)
+        pieces = jnp.sum(weights * jnp.sum(partial * partial, 1))
+        values = (proto_squares + jnp.where(low, pieces, 0.0),)
     early, squares = early_gradient(
-        plan, jnp.asarray(plan.grad_table)[device], ahead, common, behind_rows, rest.reshape(1, 1)
+        plan, jnp.asarray(plan.grad_table)[device], ahead, common, behind_rows, *values
     )
     summed = partial.astype(BF16)
     if not plan.near:

time: 394 us -> 387 us (0.982)
  Pallas kernels: 80.3 us -> 71.3 us
  waiting for transfers between devices: 204 us -> 211 us
    pallas_call x2, Pallas kernels: 10.7 us -> 4.35 us  [lay_out(): pl.pallas_call(functools.partial(lay_kernel, plan), out_shape=jax.ShapeDt...]
  transfers between devices with their start and end apart: 22 -> 22, of which waited for: 11 -> 13; matrix products, arithmetic and copies ran while one was open for 9% -> 9% of each run, Pallas kernels for 12% -> 11%
where the time goes in v7:
time: 387 us; the launch traced here: 386 us
  waiting for transfers between devices  211 us (55%)
  Pallas kernels  71.3 us (18%)
  starting transfers between devices  35 us (9%)
  other arithmetic  29.2 us (8%)
  local copies, waits for them, and re-layouts  23.2 us (6%)
  between operations  16.4 us (4%)
    all_gather x1, waiting for transfers between devices, per_device(): gathered = lax.all_gather(shards, BOTH, axis=0, axis_index_groups=halves)  84.1 us
    ppermute x7, waiting for transfers between devices, trade(): return lax.ppermute(values, 'rep', swap)  49.1 us
    ppermute x2, waiting for transfers between devices, per_device(): lax.ppermute(partial.astype(BF16), 'rep', hops).astype(F32)  32.9 us
    pallas_call x1, Pallas kernels, forward(): pl.pallas_call(functools.partial(forward_kernel, plan), out_shape=[jax.Sh...  23.5 us
    pallas_call x1, Pallas kernels, tokens_back(): pl.pallas_call(tokens_back_kernel, grid=(views,), out_shape=[jax.ShapeDty...  16.7 us
    ppermute x3, waiting for transfers between devices, across(): return lax.ppermute(values, 'grp', [(g, g ^ bit) for g in range(groups)])  14.8 us
    ppermute x3, waiting for transfers between devices, per_device(): lax.ppermute(tables, 'rep', [(r, (r + step) % reps) for r in range(reps)])  13.2 us
    pallas_call x1, Pallas kernels, rows_back(): pl.pallas_call(functools.partial(rows_back_kernel, plan), out_shape=[jax....  13.2 us
  transfers between devices with their start and end apart: 22, of which 13 were waited for; matrix products, arithmetic and copies ran while one was open for 9% of the time, Pallas kernels for 11%

profile of v7, /device:TPU:0, one launch (start us, length us, event | category | flops | bytes accessed | tf_op | source)
XLA Modules:
  0.0 386.0 jit_solution(9508041113732137589)
XLA Ops:
  7.2 2.2 broadcast_select_fusion.3
  10.4 2.2 shard_map.222
  12.6 2.9 collective-permute-start
  15.5 1.7 collective-permute-start.1
  17.3 2.8 collective-permute-start.2
  20.1 1.3 collective-permute-start.3
  21.6 2.2 shard_map.221
  23.8 3.1 collective-permute-done.1
  26.9 10.1 %collective-permute-done.2 = bf16[2,32,2048]{2,1,0:T(8,128)(2,1)S(1)} collective-permute-done((bf16[2,32,2048]{2,1,0:T(8,128)(2,1)S(1)}, bf16[2,32,2048]{2,1,0:T(8,128)(2,1)S(1)}, u32[]{:S(2)}, u32[]{:S(2)}) %collective-permute-start.2) | collective-permute-done | bytes 262176 | tf_op jit(solution)/shard_map/ppermute | solution.py:1332
  37.2 1.4 pad_maximum_fusion
  41.0 3.6 copy.63
  46.6 44.5 %collective-permute-done.5 = f32[4]{0:T(128)S(1)} collective-permute-done((f32[4]{0:T(128)S(1)}, f32[4]{0:T(128)S(1)}, u32[]{:S(2)}, u32[]{:S(2)}) %collective-permute-start.5) | collective-permute-done | bytes 48 | tf_op jit(solution)/shard_map/ppermute | solution.py:1318
  94.5 1.2 fusion.6.others_ref
  95.7 3.6 copy.64
  99.3 2.1 broadcast_select_fusion.1
  101.4 3.2 fusion.27
  104.6 4.7 %copy.69.pixels_ref = bf16[8,208,768]{2,1,0:T(8,128)(2,1)} copy(bf16[8,208,768]{1,2,0:T(8,128)(2,1)} %get-tuple-element.110) | data formatting | bytes 5111808 | tf_op jit(solution)/shard_map/jit(_pad)/pad | solution.py:1343
  109.3 84.1 %all-gather.7.cloned.1.call-done = bf16[32,3648,128]{2,1,0:T(8,128)(2,1)} async-done(((bf16[2,3648,128]{2,1,0:T(8,128)(2,1)}), bf16[32,3648,128]{2,1,0:T(8,128)(2,1)}) %all-gather.7.cloned.1.call-update) | async-done | bytes 29884432 | tf_op jit(solution)/shard_map/all_gather | solution.py:1339
  193.4 23.5 %shard_map.223 = (f32[8,208,768]{2,1,0:T(8,128)}, f32[8,208,128]{2,1,0:T(8,128)}, f32[8,16,208]{2,1,0:T(8,128)}, bf16[8,16,768]{2,1,0:T(8,128)(2,1)}, bf16[16,76...) custom-call(bf16[16,2,228,16,128]{4,3,2,1,0:T(8,128)(2,1)} %bitcast., ...), custom_call_target="tpu_custom_call" | custom-call | flops 60000002048 | bytes 40000000 | tf_op jit(solution)/shard_map/pallas_call | solution.py:632
  217.0 4.8 %all-to-all-start = ((bf16[32,8,896]{2,1,0:T(8,128)(2,1)}), bf16[32,8,896]{2,1,0:T(8,128)(2,1)S(1)}, u32[]{:S(2)}, u32[]{:S(2)}) async-start(bf16[32,8,896]{2,1,0:T(8,128)(2,1)} %get-tuple-element.61), calls=%async_computation | async-start | bytes 917504 | tf_op jit(solution)/shard_map/all_to_all | solution.py:1365
  224.3 1.7 collective-permute-start.7
  225.9 10.0 %all-to-all-done = bf16[32,8,896]{2,1,0:T(8,128)(2,1)S(1)} async-done(((bf16[32,8,896]{2,1,0:T(8,128)(2,1)}), bf16[32,8,896]{2,1,0:T(8,128)(2,1)S(1)}, u32[]{:S(2)}, u32[]{:S(2)}) %all-to-all-start) | async-done | bytes 458784 | tf_op jit(solution)/shard_map/all_to_all | solution.py:1365
  236.7 4.7 %shard_map.224 = (f32[4,32,256]{2,1,0:T(8,128)}, f32[1,2048]{1,0:T(1,128)}) custom-call(s32[1]{0:T(128)} %bitcast.22.start_ref, bf16[2,128,256]{2,1,0:T(8,128)(2,1)S(1)} %bitcast.71, bf16[256,2048]{1,0:T(8,128)(2,1)S(1)} %multiply_convert_fusion.columns_ref, bf16[256,2048]{1,0:T(8,128)(2,1)S(1)} %copy-done.3, f32[1,2048]{1,0:T(1,128)S(1)} %bitcast.74), custom_call_target="tpu_custom_call" | custom-call | flops 3000000000 | bytes 6000000 | tf_op jit(solution)/shard_map/pallas_call | solution.py:716
  241.5 3.3 all-to-all-start.1
  245.7 3.7 all-to-all-done.1.note_ref
  249.5 13.2 %shard_map.225 = (bf16[8,9728]{1,0:T(8,128)(2,1)S(1)}, f32[8,768]{1,0:T(8,128)S(1)}, f32[8,768]{1,0:T(8,128)S(1)}) custom-call(s32[1]{0:T(128)} %bitcast.21.low_ref, bf16[16,2,228,16,128]{4,3,2,1,0:T(8,128)(2,1)} %bitcast.82, f32[4,32,256]{2,1,0:T(8,128)S(1)} %all-to-all-done.1.note_ref, f32[16,768]{1,0:T(8,128)S(1)} %copy-done.7, f32[8,3072]{1,0:T(8,128)S(1)} %copy-done.10, ...), custom_call_target="tpu_custom_call" | custom-call | flops 30000001024 | bytes 30000000 | tf_op jit(solution)/shard_map/pallas_call | solution.py:859
  262.7 1.2 collective-permute-start.8
  263.9 2.7 shard_map.226
  268.8 16.7 %shard_map.227 = (f32[608,768]{1,0:T(8,128)}, bf16[608,768]{1,0:T(8,128)(2,1)}) custom-call(s32[1]{0:T(128)} %bitcast.26.odd_ref, bf16[8,9728]{1,0:T(8,128)(2,1)} %copy-done.6, f32[8,768]{1,0:T(8,128)} %copy-done.12, f32[8,768]{1,0:T(8,128)} %copy-done.13, f32[8,208,768]{2,1,0:T(8,128)} %get-tuple-element.79.unit_ref, ...), custom_call_target="tpu_custom_call" | custom-call | flops 15000000512 | bytes 15000000 | tf_op jit(solution)/shard_map/pallas_call | solution.py:994
  285.6 2.7 collective-permute-done.9
  288.3 1.7 convert_add_fusion
  290.1 1.1 collective-permute-start.10
  291.3 12.2 %collective-permute-done.10 = bf16[320,768]{1,0:T(8,128)(2,1)S(1)} collective-permute-done((bf16[320,768]{1,0:T(8,128)(2,1)S(1)}, bf16[320,768]{1,0:T(8,128)(2,1)S(1)}, u32[]{:S(2)}, u32[]{:S(2)}) %collective-permute-start.10) | collective-permute-done | bytes 491552 | tf_op jit(solution)/shard_map/ppermute | solution.py:1422
  303.6 1.3 collective-permute-start.11
  304.9 17.8 %collective-permute-done.11 = bf16[320,768]{1,0:T(8,128)(2,1)S(1)} collective-permute-done((bf16[320,768]{1,0:T(8,128)(2,1)S(1)}, bf16[320,768]{1,0:T(8,128)(2,1)S(1)}, u32[]{:S(2)}, u32[]{:S(2)}) %collective-permute-start.11) | collective-permute-done | bytes 491552 | tf_op jit(solution)/shard_map/ppermute | solution.py:1436
  322.9 1.5 collective-permute-start.12
  324.5 1.2 fusion.23.tab_ref
  326.4 15.0 %collective-permute-done.12 = bf16[320,768]{1,0:T(8,128)(2,1)S(1)} collective-permute-done((bf16[320,768]{1,0:T(8,128)(2,1)S(1)}, bf16[320,768]{1,0:T(8,128)(2,1)S(1)}, u32[]{:S(2)}, u32[]{:S(2)}) %collective-permute-start.12) | collective-permute-done | bytes 491552 | tf_op jit(solution)/shard_map/ppermute | solution.py:1436
  341.5 1.2 fusion.30
  342.6 1.4 collective-permute-start.15
  345.5 3.8 collective-permute-done.14
  350.9 4.0 %shard_map.228 = (f32[6736,128]{1,0:T(8,128)}, f32[32,1,128]{2,1,0:T(1,128)}) custom-call(s32[15]{0:T(128)} %fusion.23.tab_ref, bf16[128,640]{1,0:T(8,128)(2,1)} %bitcast.80, bf16[128,12032]{1,0:T(8,128)(2,1)} %all-gather.9.cloned.1.call-done.common_hbm, bf16[128,9728]{1,0:T(8,128)(2,1)} %all-gather.11.cloned.1.call-done.behind_hbm, f32[8,128]{1,0:T(8,128)} %copy-done.9, ...), custom_call_target="tpu_custom_call" | custom-call | flops 10000000000 | bytes 10000000 | tf_op jit(solution)/shard_map/pallas_call | solution.py:1157
  354.9 5.9 %all-to-all-start.2 = ((f32[32,1,128]{2,1,0:T(1,128)}), f32[32,1,128]{2,1,0:T(1,128)S(1)}, u32[]{:S(2)}, u32[]{:S(2)}) async-start(f32[32,1,128]{2,1,0:T(1,128)} %get-tuple-element.93), calls=%async_computation.2 | async-start | bytes 32768 | tf_op jit(solution)/shard_map/all_to_all | solution.py:1473
  361.1 1.7 copy-done.2
  362.8 2.1 shard_map.229
  365.0 2.9 all-to-all-done.2
  369.3 2.4 multiply_add_fusion.2
  371.7 6.6 %multiply_add_fusion = (f32[441096]{0:T(1024)}, f32[441096]{0:T(1024)}, f32[441096]{0:T(1024)}, f32[441096]{0:T(1024)}) fusion(f32[441096]{0:T(1024)S(1)} %copy-done.17, f32[441096]{0:T(1024)} %param.14, f32[]{:T(128)S(6)} %min_shard_map.3, f32[442368]{0:T(1024)S(1)} %bitcast.70, f32[441096]{0:T(1024)} %param.15, f32[441096]{0:T(1024)} %param.16), kind=kLoop, calls=%fused_computation.21 | loop fusion | flops 8380824 | bytes 15879460 | tf_op jit(solution)/shard_map/add | solution.py:1514
  (138 shorter events, 20.5 us)
Async XLA Ops:
  7.2 186.3 %all-gather.7.cloned.1.call-start = ((), (), s32[]{:S(2)}) async-start(), calls=%async_computation.3 | async-start | bytes 31752192 | tf_op jit(solution)/shard_map/all_gather | solution.py:1339
  9.6 5.9 %copy-start.18 = (f32[32,2048]{1,0:T(8,128)S(1)}, f32[32,2048]{1,0:T(8,128)}, u32[]{:S(2)}) copy-start(f32[32,2048]{1,0:T(8,128)} %param.21) | copy-start | bytes 786436
  9.6 5.9 %copy-start.19 = (f32[32,2048]{1,0:T(8,128)S(1)}, f32[32,2048]{1,0:T(8,128)}, u32[]{:S(2)}) copy-start(f32[32,2048]{1,0:T(8,128)} %param.18) | copy-start | bytes 786436
  12.6 24.4 %collective-permute-start = (bf16[3648,128]{1,0:T(8,128)(2,1)S(1)}, bf16[3648,128]{1,0:T(8,128)(2,1)S(1)}, u32[]{:S(2)}, u32[]{:S(2)}) collective-permute-start(bf16[3648,128]{1,0:T(8,128)(2,1)S(1)} %shard_map.222), channel_id=1, source_target_pairs={{0,4},{4,0},{8,12},{12,8},{16,20},{20,16},{24,28},{28,24},{1,5},{5... | collective-permute-start | bytes 2801672 | tf_op jit(solution)/shard_map/ppermute | solution.py:1318
  15.5 11.3 %collective-permute-start.1 = (bf16[2,32,2048]{2,1,0:T(8,128)(2,1)S(1)}, bf16[2,32,2048]{2,1,0:T(8,128)(2,1)S(1)}, u32[]{:S(2)}, u32[]{:S(2)}) collective-permute-start(bf16[2,32,2048]{2,1,0:T(8,128)(2,1)S(1)} %pad_maximum_fusion.2), channel_id=1, source_target_pairs={{0,8},{4,12},{8,16},{12,20},{16,24},{20,28},{24,0},{28,4},{1,9},{5... | collective-permute-start | bytes 786440 | tf_op jit(solution)/shard_map/ppermute | solution.py:1332
  17.3 19.7 %collective-permute-start.2 = (bf16[2,32,2048]{2,1,0:T(8,128)(2,1)S(1)}, bf16[2,32,2048]{2,1,0:T(8,128)(2,1)S(1)}, u32[]{:S(2)}, u32[]{:S(2)}) collective-permute-start(bf16[2,32,2048]{2,1,0:T(8,128)(2,1)S(1)} %pad_maximum_fusion.2), channel_id=1, source_target_pairs={{0,16},{4,20},{8,24},{12,28},{16,0},{20,4},{24,8},{28,12},{1,17},{... | collective-permute-start | bytes 786440 | tf_op jit(solution)/shard_map/ppermute | solution.py:1332
  20.1 16.8 %collective-permute-start.3 = (bf16[2,32,2048]{2,1,0:T(8,128)(2,1)S(1)}, bf16[2,32,2048]{2,1,0:T(8,128)(2,1)S(1)}, u32[]{:S(2)}, u32[]{:S(2)}) collective-permute-start(bf16[2,32,2048]{2,1,0:T(8,128)(2,1)S(1)} %pad_maximum_fusion.2), channel_id=1, source_target_pairs={{0,24},{4,28},{8,0},{12,4},{16,8},{20,12},{24,16},{28,20},{1,25},{... | collective-permute-start | bytes 786440 | tf_op jit(solution)/shard_map/ppermute | solution.py:1332
  39.9 5.6 %copy-start.21 = (s32[4]{0:T(128)S(1)}, s32[4]{0:T(128)}, u32[]{:S(2)}) copy-start(s32[4]{0:T(128)} %param.24) | copy-start | bytes 52
  39.9 51.9 %collective-permute-start.6 = (bf16[4,2,32,2048]{3,2,1,0:T(8,128)(2,1)}, bf16[4,2,32,2048]{3,2,1,0:T(8,128)(2,1)S(1)}, u32[]{:S(2)}, u32[]{:S(2)}) collective-permute-start(bf16[4,2,32,2048]{3,2,1,0:T(8,128)(2,1)} %constant_dynamic-slice_fusion), channel_id=1, source_target_pairs={{0,4},{4,0},{8,12},{12,8},{16,20},{20,16},{24,28},{28,24},{1,5},{5... | collective-permute-start | bytes 3145736 | tf_op jit(solution)/shard_map/ppermute | solution.py:1318
  44.5 51.2 %collective-permute-start.4 = (bf16[4,196,768]{2,0,1:T(4,128)(2,1)}, bf16[4,196,768]{2,0,1:T(4,128)(2,1)}, u32[]{:S(2)}, u32[]{:S(2)}) collective-permute-start(bf16[4,196,768]{2,0,1:T(4,128)(2,1)} %param.23), channel_id=1, source_target_pairs={{0,4},{4,0},{8,12},{12,8},{16,20},{20,16},{24,28},{28,24},{1,5},{5... | collective-permute-start | bytes 3612680 | tf_op jit(solution)/shard_map/ppermute | solution.py:1318
  45.5 45.5 %collective-permute-start.5 = (f32[4]{0:T(128)S(1)}, f32[4]{0:T(128)S(1)}, u32[]{:S(2)}, u32[]{:S(2)}) collective-permute-start(f32[4]{0:T(128)S(1)} %convert_element_type.76), channel_id=1, source_target_pairs={{0,4},{4,0},{8,12},{12,8},{16,20},{20,16},{24,28},{28,24},{1,5},{5... | collective-permute-start | bytes 56 | tf_op jit(solution)/shard_map/ppermute | solution.py:1318
  92.9 1.4 copy-start
  216.9 19.7 %copy-start.3 = (bf16[256,2048]{1,0:T(8,128)(2,1)S(1)}, bf16[256,2048]{1,0:T(8,128)(2,1)}, u32[]{:S(2)}) copy-start(bf16[256,2048]{1,0:T(8,128)(2,1)} %fusion.6.others_ref) | copy-start | bytes 3145732
  217.0 19.7 %copy-start.8 = (f32[2048]{0:T(1024)S(1)}, f32[2048]{0:T(1024)}, u32[]{:S(2)}) copy-start(f32[2048]{0:T(1024)} %param.22) | copy-start | bytes 24580
  217.0 19.0 %all-to-all-start = ((bf16[32,8,896]{2,1,0:T(8,128)(2,1)}), bf16[32,8,896]{2,1,0:T(8,128)(2,1)S(1)}, u32[]{:S(2)}, u32[]{:S(2)}) async-start(bf16[32,8,896]{2,1,0:T(8,128)(2,1)} %get-tuple-element.61), calls=%async_computation | async-start | bytes 917504 | tf_op jit(solution)/shard_map/all_to_all | solution.py:1365
  224.3 12.4 %collective-permute-start.7 = (bf16[8,12032]{1,0:T(8,128)(2,1)S(1)}, bf16[8,12032]{1,0:T(8,128)(2,1)S(1)}, u32[]{:S(2)}, u32[]{:S(2)}) collective-permute-start(bf16[8,12032]{1,0:T(8,128)(2,1)S(1)} %fusion.15), channel_id=1, source_target_pairs={{0,4},{4,0},{8,12},{12,8},{16,20},{20,16},{24,28},{28,24},{1,5},{5... | collective-permute-start | bytes 577544 | tf_op jit(solution)/shard_map/ppermute | solution.py:1318
  236.7 8.2 %copy-start.20 = (bf16[8,2048]{1,0:T(8,128)(2,1)S(1)}, bf16[8,2048]{1,0:T(8,128)(2,1)}, u32[]{:S(2)}) copy-start(bf16[8,2048]{1,0:T(8,128)(2,1)} %get-tuple-element.63) | copy-start | bytes 98308
  236.7 12.7 %copy-start.7 = (f32[16,768]{1,0:T(8,128)S(1)}, f32[16,768]{1,0:T(8,128)}, u32[]{:S(2)}) copy-start(f32[16,768]{1,0:T(8,128)} %get-tuple-element.64.class_ref) | copy-start | bytes 147460
  236.7 12.7 %copy-start.10 = (f32[8,3072]{1,0:T(8,128)S(1)}, f32[8,3072]{1,0:T(8,128)}, u32[]{:S(2)}) copy-start(f32[8,3072]{1,0:T(8,128)} %get-tuple-element.71.hidden_ref) | copy-start | bytes 294916
  236.7 12.7 %copy-start.11 = (f32[4,8,768]{2,1,0:T(8,128)S(1)}, f32[4,8,768]{2,1,0:T(8,128)}, u32[]{:S(2)}) copy-start(f32[4,8,768]{2,1,0:T(8,128)} %get-tuple-element.75.middle_ref) | copy-start | bytes 294916
  236.7 12.7 %copy-start.14 = (f32[8,2048]{1,0:T(8,128)S(1)}, f32[8,2048]{1,0:T(8,128)}, u32[]{:S(2)}) copy-start(f32[8,2048]{1,0:T(8,128)} %get-tuple-element.72.one_ref) | copy-start | bytes 196612
  236.7 12.7 %copy-start.15 = (f32[8,2048]{1,0:T(8,128)S(1)}, f32[8,2048]{1,0:T(8,128)}, u32[]{:S(2)}) copy-start(f32[8,2048]{1,0:T(8,128)} %get-tuple-element.73.two_ref) | copy-start | bytes 196612
  236.7 12.7 %copy-start.16 = (f32[8,256]{1,0:T(8,128)S(1)}, f32[8,256]{1,0:T(8,128)}, u32[]{:S(2)}) copy-start(f32[8,256]{1,0:T(8,128)} %get-tuple-element.74.bottle_ref) | copy-start | bytes 24580
  241.5 7.9 %all-to-all-start.1 = ((f32[4,32,256]{2,1,0:T(8,128)}), f32[4,32,256]{2,1,0:T(8,128)S(1)}, u32[]{:S(2)}, u32[]{:S(2)}) async-start(f32[4,32,256]{2,1,0:T(8,128)} %get-tuple-element.70), calls=%async_computation.1 | async-start | bytes 262144 | tf_op jit(solution)/shard_map/all_to_all | solution.py:1389
  244.8 104.8 %all-gather.9.cloned.1.call-start = ((), (), s32[]{:S(2)}) async-start(), calls=%async_computation.4 | async-start | bytes 3272704 | tf_op jit(solution)/shard_map/all_gather | solution.py:1371
  245.6 105.3 %all-gather.11.cloned.1.call-start = ((), (), s32[]{:S(2)}) async-start(), calls=%async_computation.5 | async-start | bytes 2646016 | tf_op jit(solution)/shard_map/all_gather | solution.py:1371
  249.4 14.4 %copy-start.1 = (f32[1,4,2,32,2048]{4,3,2,1,0:T(8,128)S(1)}, f32[1,4,2,32,2048]{4,3,2,1,0:T(8,128)}, u32[]{:S(2)}) copy-start(f32[1,4,2,32,2048]{4,3,2,1,0:T(8,128)} %copy-done) | copy-start | bytes 6291460
  262.6 4.0 %copy-start.12 = (f32[8,768]{1,0:T(8,128)}, f32[8,768]{1,0:T(8,128)S(1)}, u32[]{:S(2)}) copy-start(f32[8,768]{1,0:T(8,128)S(1)} %get-tuple-element.77.stream_ref) | copy-start | bytes 73732
  262.6 4.0 %copy-start.13 = (f32[8,768]{1,0:T(8,128)}, f32[8,768]{1,0:T(8,128)S(1)}, u32[]{:S(2)}) copy-start(f32[8,768]{1,0:T(8,128)S(1)} %get-tuple-element.78.ends_ref) | copy-start | bytes 73732
  262.7 5.5 %copy-start.6 = (bf16[8,9728]{1,0:T(8,128)(2,1)}, bf16[8,9728]{1,0:T(8,128)(2,1)S(1)}, u32[]{:S(2)}) copy-start(bf16[8,9728]{1,0:T(8,128)(2,1)S(1)} %get-tuple-element.76.behind_ref) | copy-start | bytes 466948
  262.7 5.5 %collective-permute-start.8 = (bf16[8,9728]{1,0:T(8,128)(2,1)S(1)}, bf16[8,9728]{1,0:T(8,128)(2,1)S(1)}, u32[]{:S(2)}, u32[]{:S(2)}) collective-permute-start(bf16[8,9728]{1,0:T(8,128)(2,1)S(1)} %get-tuple-element.76.behind_ref), channel_id=1, source_target_pairs={{0,4},{4,0},{8,12},{12,8},{16,20},{20,16},{24,28},{28,24},{1,5},{5... | collective-permute-start | bytes 466952 | tf_op jit(solution)/shard_map/ppermute | solution.py:1318
  266.6 0.7 copy-start.4
  267.3 18.2 %copy-start.9 = (f32[8,128]{1,0:T(8,128)}, f32[8,128]{1,0:T(8,128)S(1)}, u32[]{:S(2)}) copy-start(f32[8,128]{1,0:T(8,128)S(1)} %get-tuple-element.88.rest_ref) | copy-start | bytes 12292
  285.5 2.8 collective-permute-start.9
  290.1 13.3 %collective-permute-start.10 = (bf16[320,768]{1,0:T(8,128)(2,1)S(1)}, bf16[320,768]{1,0:T(8,128)(2,1)S(1)}, u32[]{:S(2)}, u32[]{:S(2)}) collective-permute-start(bf16[320,768]{1,0:T(8,128)(2,1)S(1)} %pad_maximum_fusion.1), channel_id=1, source_target_pairs={{0,2},{1,3},{2,0},{3,1},{4,6},{5,7},{6,4},{7,5},{8,10},{9,11},{10,... | collective-permute-start | bytes 1474568 | tf_op jit(solution)/shard_map/ppermute | solution.py:1422
  303.6 19.1 %collective-permute-start.11 = (bf16[320,768]{1,0:T(8,128)(2,1)S(1)}, bf16[320,768]{1,0:T(8,128)(2,1)S(1)}, u32[]{:S(2)}, u32[]{:S(2)}) collective-permute-start(bf16[320,768]{1,0:T(8,128)(2,1)S(1)} %convert_element_type.85), channel_id=1, source_target_pairs={{8,0},{12,4},{24,16},{28,20},{9,1},{13,5},{25,17},{29,21},{10,2},{... | collective-permute-start | bytes 1474568 | tf_op jit(solution)/shard_map/ppermute | solution.py:1436
  322.9 18.6 %collective-permute-start.12 = (bf16[320,768]{1,0:T(8,128)(2,1)S(1)}, bf16[320,768]{1,0:T(8,128)(2,1)S(1)}, u32[]{:S(2)}, u32[]{:S(2)}) collective-permute-start(bf16[320,768]{1,0:T(8,128)(2,1)S(1)} %fusion.12), channel_id=1, source_target_pairs={{16,0},{20,4},{17,1},{21,5},{18,2},{22,6},{19,3},{23,7}} | collective-permute-start | bytes 1474568 | tf_op jit(solution)/shard_map/ppermute | solution.py:1436
  342.6 2.9 collective-permute-start.15
  344.7 10.2 %collective-permute-start.13 = (bf16[288,768]{1,0:T(8,128)(2,1)S(1)}, bf16[288,768]{1,0:T(8,128)(2,1)S(1)}, u32[]{:S(2)}, u32[]{:S(2)}) collective-permute-start(bf16[288,768]{1,0:T(8,128)(2,1)S(1)} %slice.118), channel_id=1, source_target_pairs={{0,2},{1,3},{2,0},{3,1},{4,6},{5,7},{6,4},{7,5},{8,10},{9,11},{10,... | collective-permute-start | bytes 1327112 | tf_op jit(solution)/shard_map/ppermute | solution.py:1422
  345.2 4.1 %collective-permute-start.14 = (bf16[32,768]{1,0:T(8,128)(2,1)S(1)}, bf16[32,768]{1,0:T(8,128)(2,1)S(1)}, u32[]{:S(2)}, u32[]{:S(2)}) collective-permute-start(bf16[32,768]{1,0:T(8,128)(2,1)S(1)} %slice.121), channel_id=1, source_target_pairs={{0,4},{4,0},{8,12},{12,8},{16,20},{20,16},{24,28},{28,24},{1,5},{5... | collective-permute-start | bytes 147464 | tf_op jit(solution)/shard_map/ppermute | solution.py:1318
  354.9 13.0 %all-to-all-start.2 = ((f32[32,1,128]{2,1,0:T(1,128)}), f32[32,1,128]{2,1,0:T(1,128)S(1)}, u32[]{:S(2)}, u32[]{:S(2)}) async-start(f32[32,1,128]{2,1,0:T(1,128)} %get-tuple-element.93), calls=%async_computation.2 | async-start | bytes 32768 | tf_op jit(solution)/shard_map/all_to_all | solution.py:1473
  360.8 2.0 copy-start.2
  362.8 6.5 %copy-start.5 = (f32[32,2048]{1,0:T(8,128)S(1)}, f32[32,2048]{1,0:T(8,128)}, u32[]{:S(2)}) copy-start(f32[32,2048]{1,0:T(8,128)} %copy-done.4) | copy-start | bytes 786436
  369.3 2.5 copy-start.17
Sparse Core Ops, SparseCore 0:
  38.8 154.6 all-gather.6
  248.4 44.0 all-gather.8
  303.7 43.4 all-gather.10

commit v8 on v7

--- a/solution.py
+++ b/solution.py
@@ -81,6 +81,7 @@
 ATT_COLUMN = 2 * D + F + B + 2 * H
 SECOND = HEADS * D
 CLASS = SECOND + H
+ROWS = CLASS + D
 
 
 def round_up(value, step):
@@ -156,10 +157,20 @@
                 if device * self.size < offset + rows * cols and (device + 1) * self.size > offset
             }
         )
-        self.sent = [[] for _ in range(count)]
-        self.grad_table = self.tabulate(lambda index: index, self.sent_row)
+        self.grad_table = self.tabulate(lambda index: index, lambda device, index, row0, chunks: row0)
+        self.most_chunks = {
+            index: max(
+                [1]
+                + [
+                    entry[3 + place]
+                    for entry in self.grad_table
+                    for place in range(0, len(entry) - 3, 4)
+                    if entry[1 + place] == index
+                ]
+            )
+            for index in SPANS
+        }
         self.late_table = self.tabulate(lambda index: index in (0, 1, 5), self.wide_row)
-        self.reach = max(place + size for sent in self.sent for _, size, place in sent)
         self.grad_scratch = FRONT + self.lines + CHUNK * max(WIDTHS) + 16
 
 
@@ -191,14 +202,6 @@
             entry += [device < self.groups, device % 4 == 1]
         return np.array(table, np.int32)
 
-    def sent_row(self, device, index, row0, chunks):
-        if index not in SPANS:
-            return row0
-        sent, size = self.sent[device], chunks * CHUNK
-        place = sum(before for _, before, _ in sent)
-        sent.append((SPANS[index][0] + row0, size, place))
-        return place
-
     def wide_row(self, device, index, row0, chunks):
         if index:
             return row0
@@ -479,13 +482,13 @@
     looked_ref,
     class_ref,
     qkv_out,
-    second_ref,
     hidden_ref,
     one_ref,
     two_ref,
     bottle_ref,
     middle_ref,
-    send_ref,
+    rows_ref,
+    pack_out,
     shards_ref,
     wide_ref,
     place_ref,
@@ -576,22 +579,23 @@
     shards.times(5, 0, cls.astype(F32), left_ref, one_ref)
     first = activate(one_ref[...]).astype(BF16)
     pack_ref[:, place + D : AHEAD] = first.astype(F32)
-    pack_ref[:, AHEAD:] = jnp.zeros((views, pack_ref.shape[1] - AHEAD), F32)
     shards.times(5, D, first.astype(F32), left_ref, two_ref)
     second = activate(two_ref[...]).astype(BF16)
-    second_ref[...] = second
     shards.times(6, 0, second.astype(F32), left_ref, bottle_ref)
     bottle = bottle_ref[...]
     scale = lax.rsqrt(jnp.sum(bottle * bottle, -1, keepdims=True) + 1e-06)
     rows = product(turn_ref[...], (bottle * scale).astype(BF16)).astype(BF16)
-    for device, sent in enumerate(plan.sent):
-        send_ref[device, :, :B] = rows
-        for lane, size, place in sent:
-            start = lane // LANES * LANES
-            piece = pack_ref[:, start : start + size + (LANES if lane > start else 0)]
-            if lane > start:
-                piece = pltpu.roll(piece, piece.shape[1] - (lane - start), 1)
-            send_ref[device, :, B + place : B + place + size] = piece[:, :size].astype(BF16)
+    rows_ref[...] = jnp.broadcast_to(rows[None], rows_ref.shape)
+    mixed = mixed_ref[...].astype(F32)
+    for head in range(HEADS):
+        pack_out[:, head * D : (head + 1) * D] = mixed[:, head, :].astype(BF16)
+    pack_out[:, SECOND:CLASS] = second
+    row = lax.broadcasted_iota(jnp.int32, (views, D), 0)
+    pack_out[:, CLASS:ROWS] = jnp.where(
+        row == 0, class_normed, jnp.where(row == 1, query[0:1], 0.0)
+    ).astype(BF16)
+    pack_out[:, ROWS : ROWS + AHEAD] = pack_ref[...].astype(BF16)
+    pack_out[:, ROWS + AHEAD :] = jnp.zeros((views, pack_out.shape[1] - ROWS - AHEAD), BF16)
     class_ref[...] = jnp.concatenate(
         [
             class_unit,
@@ -620,13 +624,13 @@
         ((HEADROWS, D), BF16),
         ((16, D), F32),
         ((D, 3 * D), BF16),
-        ((views, H), BF16),
         ((views, F), F32),
         ((views, H), F32),
         ((views, H), F32),
         ((views, B), F32),
         ((4, views, D), F32),
-        ((plan.count, views, B + plan.reach), BF16),
+        ((plan.count, views, B), BF16),
+        ((views, ROWS + AHEAD + (max(plan.most_chunks.values()) + 1) * CHUNK), BF16),
     ]
     most, longest = plan.largest()
     return pl.pallas_call(
@@ -644,7 +648,7 @@
             pltpu.VMEM((TOKENS, D), F32),
             pltpu.VMEM((most, views, longest), F32),
             pltpu.VMEM((views, D), F32),
-            pltpu.VMEM((views, round_up(AHEAD + CHUNK, LANES) + LANES), F32),
+            pltpu.VMEM((views, AHEAD), F32),
             pltpu.VMEM((2, TOKENS, D), F32),
             pltpu.VMEM((2, TOKENS, LANES), F32),
             pltpu.VMEM((D, 3 * D), BF16),
@@ -1029,7 +1033,6 @@
     plan,
     most,
     tab_ref,
-    ahead_ref,
     common_hbm,
     behind_hbm,
     rest_ref,
@@ -1060,19 +1063,20 @@
 
     for part in range(most):
         kind, base, chunks, row0 = (tab_ref[1 + 4 * part + i] for i in range(4))
-        for index, (_, column) in SPANS.items():
+        for index, (lane, column) in SPANS.items():
             cols = PIECES[index][2]
             width = cols // LANES
+            size = (plan.most_chunks[index] + 1) * CHUNK
 
             @pl.when(kind == index)
-            def _(column=column, cols=cols, width=width):
+            def _(lane=lane, column=column, cols=cols, width=width, size=size):
+                skew = lax.rem(row0, LANES)
+                fetch(common_hbm, common_ref, pl.multiple_of(ROWS + lane + row0 - skew, LANES), size)
                 fetch(behind_hbm, behind_ref, column, cols)
 
                 def move(step, carry):
                     goal = base + step * (CHUNK * width)
-                    lanes = pl.ds(pl.multiple_of(row0 + step * CHUNK, LANES), CHUNK)
-                    left = ahead_ref[:, lanes].astype(F32).T.astype(BF16)
-                    block = product(left, behind_ref[:, :cols])
+                    block = product(turned(skew + step * CHUNK), behind_ref[:, :cols])
                     for tile in range(width):
                         store(goal, width, tile, block[:, tile * LANES : (tile + 1) * LANES])
                     return carry
@@ -1102,7 +1106,7 @@
         @pl.when(kind == 1)
         def _():
             fetch(behind_hbm, behind_ref, ATT_COLUMN, D)
-            fetch(common_hbm, common_ref, 0, common_ref.shape[1])
+            fetch(common_hbm, common_ref, 0, ROWS)
 
             def move(step, carry):
                 width = 3 * D // LANES
@@ -1153,7 +1157,7 @@
     square_ref[...] = jnp.broadcast_to(total[None], square_ref.shape)
 
 
-def early_gradient(plan, table, ahead, common, behind, *values):
+def early_gradient(plan, table, common, behind, *values):
     return pl.pallas_call(
         functools.partial(early_kernel, plan, (table.shape[0] - 3) // 4),
         out_shape=[
@@ -1162,14 +1166,13 @@
         ],
         in_specs=[
             pl.BlockSpec(memory_space=pltpu.SMEM),
-            pl.BlockSpec(memory_space=pltpu.VMEM),
             pl.BlockSpec(memory_space=pl.ANY),
             pl.BlockSpec(memory_space=pl.ANY),
         ]
         + [pl.BlockSpec(memory_space=pltpu.VMEM)] * len(values),
         out_specs=[pl.BlockSpec(memory_space=pltpu.VMEM)] * 2,
         scratch_shapes=[
-            pltpu.VMEM(common.shape, BF16),
+            pltpu.VMEM((common.shape[0], ROWS), BF16),
             pltpu.VMEM((behind.shape[0], F), BF16),
             pltpu.VMEM((TILE, D), BF16),
             pltpu.SemaphoreType.DMA,
@@ -1179,7 +1182,7 @@
         cost_estimate=pl.CostEstimate(
             flops=10 * 10**9, bytes_accessed=10 * 10**6, transcendentals=0
         ),
-    )(table, ahead, common, behind, *values)
+    )(table, common, behind, *values)
 
 
 def late_kernel(
@@ -1361,25 +1364,19 @@
 
     turn, columns, teacher_columns = lax.optimization_barrier((turn, columns, teacher_columns))
     kept = forward(plan, gathered, pixels, turn)
-    unit, scale, probs, mixed, looked, classes, qkv_w, second = kept[:8]
-    received = lax.all_to_all(kept[-1], BOTH, 0, 0)
-    received = received.reshape(reps // 2, 2, groups * views, -1)
-    all_rows = received[..., :B]
-    ahead = received[:, 0, :, B:].reshape(half * views, -1)
+    unit, scale, probs, _, looked, classes, qkv_w = kept[:7]
+    all_rows, common = lax.all_to_all(kept[12], BOTH, 0, 0), kept[13]
 
     def gather_rows(values):
         return lax.all_gather(values, BOTH, axis=0, axis_index_groups=halves).reshape(
             half * views, -1
         )
 
-    common = [mixed[:, :HEADS].reshape(views, -1), second]
-    common.append(jnp.pad(classes[1:3], ((0, views - 2), (0, 0))).astype(BF16))
-    common = jnp.concatenate(common, 1)
     other = trade(common)
-    all_rows, ahead, other = lax.optimization_barrier((all_rows, ahead, other))
+    all_rows, other = lax.optimization_barrier((all_rows, other))
     common = jnp.where(low, common, other)
 
-    all_rows = all_rows.transpose(1, 0, 2, 3).reshape(2, -1, B)
+    all_rows = all_rows.reshape(reps // 2, 2, -1, B).transpose(1, 0, 2, 3).reshape(2, -1, B)
     start = (rep // 2 * groups * views).astype(jnp.int32)[None]
     note, new_center = prototypes(
         start, all_rows, columns, teacher_columns, center[None], groups, views
@@ -1403,7 +1400,7 @@
         column_scale,
     )
     behind, grad_middle, ends = rows_back(
-        plan, low.astype(jnp.int32)[None], gathered, note, (classes,) + tuple(kept[8:13])
+        plan, low.astype(jnp.int32)[None], gathered, note, (classes,) + tuple(kept[7:12])
     )
     odd, far = grp % 2 == 1, grp // 2 % 2 == 1
     behind_rows = trade_low(behind)
@@ -1427,7 +1424,7 @@
     other = jnp.concatenate([jnp.where(far, first, second), shared], 0).astype(BF16)
     partial = jnp.concatenate([jnp.where(far, second, first), shared], 0)
     partial = partial + across(2, other).astype(F32)
-    behind_rows, partial = lax.optimization_barrier((behind_rows, partial))
+    behind_rows, common, partial = lax.optimization_barrier((behind_rows, common, partial))
     behind_rows = gather_rows(behind_rows)
     if plan.near:
         step = 1
@@ -1441,7 +1438,7 @@
             partial.astype(BF16).reshape(lines, depth, D), "rep", 0, 0, axis_index_groups=pairs
         )
         partial = jnp.sum(partial.astype(F32), 0)
-    class_rows = common[:2, CLASS:].astype(F32)
+    class_rows = common[:2, CLASS:ROWS].astype(F32)
     class_normed, query = class_rows[0:1], class_rows[1:2]
     by_head = jnp.where(head_mask()[:HEADS], query, 0.0)
     values = (proto_squares, partial)
@@ -1461,7 +1458,7 @@
         pieces = jnp.sum(weights * jnp.sum(partial * partial, 1))
         values = (proto_squares + jnp.where(low, pieces, 0.0),)
     early, squares = early_gradient(
-        plan, jnp.asarray(plan.grad_table)[device], ahead, common, behind_rows, *values
+        plan, jnp.asarray(plan.grad_table)[device], common, behind_rows, *values
     )
     summed = partial.astype(BF16)
     if not plan.near:

time: 387 us -> 383 us (0.990)
  blocking collectives: 0 us -> 11.9 us
  waiting for transfers between devices: 211 us -> 201 us
  starting transfers between devices: 35 us -> 30.2 us
    all_to_all x0 -> x1, blocking collectives: none -> 11.9 us  [per_device(): all_rows, common = (lax.all_to_all(kept[12], BOTH, 0, 0), kept[13])]
    all_to_all x1 -> x0, waiting for transfers between devices: 10 us -> none  [per_device(): received = lax.all_to_all(kept[-1], BOTH, 0, 0)]
    all_to_all x1 -> x0, starting transfers between devices: 4.77 us -> none  [per_device(): received = lax.all_to_all(kept[-1], BOTH, 0, 0)]
  transfers between devices with their start and end apart: 22 -> 21, of which waited for: 13 -> 13; matrix products, arithmetic and copies ran while one was open for 9% -> 8% of each run, Pallas kernels for 11% -> 12%
where the time goes in v8:
time: 383 us; the launch traced here: 382 us
  waiting for transfers between devices  201 us (52%)
  Pallas kernels  71.3 us (19%)
  starting transfers between devices  30.2 us (8%)
  other arithmetic  29.3 us (8%)
  local copies, waits for them, and re-layouts  22.6 us (6%)
  between operations  16.4 us (4%)
  blocking collectives  11.9 us (3%)
    all_gather x1, waiting for transfers between devices, per_device(): gathered = lax.all_gather(shards, BOTH, axis=0, axis_index_groups=halves)  84.1 us
    ppermute x7, waiting for transfers between devices, trade(): return lax.ppermute(values, 'rep', swap)  49.2 us
    ppermute x2, waiting for transfers between devices, per_device(): lax.ppermute(partial.astype(BF16), 'rep', hops).astype(F32)  30.9 us
    pallas_call x1, Pallas kernels, forward(): pl.pallas_call(functools.partial(forward_kernel, plan), out_shape=[jax.Sh...  23.7 us
    pallas_call x1, Pallas kernels, tokens_back(): pl.pallas_call(tokens_back_kernel, grid=(views,), out_shape=[jax.ShapeDty...  16.7 us
    ppermute x3, waiting for transfers between devices, across(): return lax.ppermute(values, 'grp', [(g, g ^ bit) for g in range(groups)])  15.4 us
    pallas_call x1, Pallas kernels, rows_back(): pl.pallas_call(functools.partial(rows_back_kernel, plan), out_shape=[jax....  13.2 us
    ppermute x3, waiting for transfers between devices, per_device(): lax.ppermute(tables, 'rep', [(r, (r + step) % reps) for r in range(reps)])  13.2 us
  transfers between devices with their start and end apart: 21, of which 13 were waited for; matrix products, arithmetic and copies ran while one was open for 8% of the time, Pallas kernels for 12%

profile of v8, /device:TPU:0, one launch (start us, length us, event | category | flops | bytes accessed | tf_op | source)
XLA Modules:
  0.0 382.4 jit_solution(3546363949333400917)
XLA Ops:
  7.2 2.2 broadcast_select_fusion.3
  10.4 2.2 shard_map.222
  12.6 2.9 collective-permute-start
  15.6 1.7 collective-permute-start.1
  17.3 2.8 collective-permute-start.2
  20.1 1.3 collective-permute-start.3
  21.6 2.2 shard_map.221
  23.8 3.1 collective-permute-done.1
  26.9 10.1 %collective-permute-done.2 = bf16[2,32,2048]{2,1,0:T(8,128)(2,1)S(1)} collective-permute-done((bf16[2,32,2048]{2,1,0:T(8,128)(2,1)S(1)}, bf16[2,32,2048]{2,1,0:T(8,128)(2,1)S(1)}, u32[]{:S(2)}, u32[]{:S(2)}) %collective-permute-start.2) | collective-permute-done | bytes 262176 | tf_op jit(solution)/shard_map/ppermute | solution.py:1335
  37.2 1.4 pad_maximum_fusion
  42.0 3.6 copy.47
  46.6 44.5 %collective-permute-done.5 = f32[4]{0:T(128)S(1)} collective-permute-done((f32[4]{0:T(128)S(1)}, f32[4]{0:T(128)S(1)}, u32[]{:S(2)}, u32[]{:S(2)}) %collective-permute-start.5) | collective-permute-done | bytes 48 | tf_op jit(solution)/shard_map/ppermute | solution.py:1321
  94.5 1.2 multiply_convert_fusion.columns_ref
  95.7 3.6 copy.48
  99.3 2.1 broadcast_select_fusion.1
  101.4 3.2 fusion.25
  104.6 4.7 %copy.53.pixels_ref = bf16[8,208,768]{2,1,0:T(8,128)(2,1)} copy(bf16[8,208,768]{1,2,0:T(8,128)(2,1)} %get-tuple-element.108) | data formatting | bytes 5111808 | tf_op jit(solution)/shard_map/jit(_pad)/pad | solution.py:1346
  109.3 84.1 %all-gather.7.cloned.1.call-done = bf16[32,3648,128]{2,1,0:T(8,128)(2,1)} async-done(((bf16[2,3648,128]{2,1,0:T(8,128)(2,1)}), bf16[32,3648,128]{2,1,0:T(8,128)(2,1)}) %all-gather.7.cloned.1.call-update) | async-done | bytes 29884432 | tf_op jit(solution)/shard_map/all_gather | solution.py:1342
  193.4 23.7 %shard_map.223 = (f32[8,208,768]{2,1,0:T(8,128)}, f32[8,208,128]{2,1,0:T(8,128)}, f32[8,16,208]{2,1,0:T(8,128)}, bf16[8,16,768]{2,1,0:T(8,128)(2,1)}, bf16[16,76...) custom-call(bf16[16,2,228,16,128]{4,3,2,1,0:T(8,128)(2,1)} %bitcast., ...), custom_call_target="tpu_custom_call" | custom-call | flops 60000002048 | bytes 40000000 | tf_op jit(solution)/shard_map/pallas_call | solution.py:636
  217.1 1.5 collective-permute-start.7
  218.6 11.9 %all_to_all.15 = bf16[32,8,256]{2,1,0:T(8,128)(2,1)S(1)} all-to-all(bf16[32,8,256]{2,1,0:T(8,128)(2,1)} %get-tuple-element.60), channel_id=1, replica_groups=mesh['rep'=8,'grp'=4] {'rep','grp'}, dimensions={0} | all-to-all | bytes 262144 | tf_op jit(solution)/shard_map/all_to_all | solution.py:1368
  230.5 1.7 broadcast_select_fusion.6
  232.3 1.2 copy-done.3
  233.6 4.7 %shard_map.224 = (f32[4,32,256]{2,1,0:T(8,128)}, f32[1,2048]{1,0:T(1,128)}) custom-call(s32[1]{0:T(128)} %bitcast.11.start_ref, bf16[2,128,256]{2,1,0:T(8,128)(2,1)S(1)} %bitcast.65, bf16[256,2048]{1,0:T(8,128)(2,1)S(1)} %copy-done.3, bf16[256,2048]{1,0:T(8,128)(2,1)S(1)} %fusion.6.others_ref, f32[1,2048]{1,0:T(1,128)S(1)} %bitcast.68), custom_call_target="tpu_custom_call" | custom-call | flops 3000000000 | bytes 6000000 | tf_op jit(solution)/shard_map/pallas_call | solution.py:720
  238.3 3.3 all-to-all-start.1
  241.7 4.5 %all-to-all-done.1.note_ref = f32[4,32,256]{2,1,0:T(8,128)S(1)} async-done(((f32[4,32,256]{2,1,0:T(8,128)}), f32[4,32,256]{2,1,0:T(8,128)S(1)}, u32[]{:S(2)}, u32[]{:S(2)}) %all-to-all-start.1) | async-done | bytes 131104 | tf_op jit(solution)/shard_map/all_to_all | solution.py:1386
  246.3 13.2 %shard_map.225 = (bf16[8,9728]{1,0:T(8,128)(2,1)S(1)}, f32[8,768]{1,0:T(8,128)S(1)}, f32[8,768]{1,0:T(8,128)S(1)}) custom-call(s32[1]{0:T(128)} %bitcast.2.low_ref, bf16[16,2,228,16,128]{4,3,2,1,0:T(8,128)(2,1)} %bitcast.72, f32[4,32,256]{2,1,0:T(8,128)S(1)} %all-to-all-done.1.note_ref, f32[16,768]{1,0:T(8,128)S(1)} %copy-done.10, f32[8,3072]{1,0:T(8,128)S(1)} %copy-done.11, ...), custom_call_target="tpu_custom_call" | custom-call | flops 30000001024 | bytes 30000000 | tf_op jit(solution)/shard_map/pallas_call | solution.py:863
  260.0 2.6 shard_map.226
  263.9 1.5 collective-permute-done.8
  266.1 16.7 %shard_map.227 = (f32[608,768]{1,0:T(8,128)}, bf16[608,768]{1,0:T(8,128)(2,1)}) custom-call(s32[1]{0:T(128)} %bitcast.25.odd_ref, bf16[8,9728]{1,0:T(8,128)(2,1)} %copy-done.7, f32[8,768]{1,0:T(8,128)} %copy-done.13, f32[8,768]{1,0:T(8,128)} %copy-done.14, f32[8,208,768]{2,1,0:T(8,128)} %get-tuple-element.76.unit_ref, ...), custom_call_target="tpu_custom_call" | custom-call | flops 15000000512 | bytes 15000000 | tf_op jit(solution)/shard_map/pallas_call | solution.py:998
  282.8 2.7 collective-permute-done.9
  285.5 1.7 convert_add_fusion
  287.9 12.7 %collective-permute-done.10 = bf16[320,768]{1,0:T(8,128)(2,1)S(1)} collective-permute-done((bf16[320,768]{1,0:T(8,128)(2,1)S(1)}, bf16[320,768]{1,0:T(8,128)(2,1)S(1)}, u32[]{:S(2)}, u32[]{:S(2)}) %collective-permute-start.10) | collective-permute-done | bytes 491552 | tf_op jit(solution)/shard_map/ppermute | solution.py:1419
  300.8 1.3 collective-permute-start.11
  302.2 1.2 fusion.21.tab_ref
  304.2 14.8 %collective-permute-done.11 = bf16[320,768]{1,0:T(8,128)(2,1)S(1)} collective-permute-done((bf16[320,768]{1,0:T(8,128)(2,1)S(1)}, bf16[320,768]{1,0:T(8,128)(2,1)S(1)}, u32[]{:S(2)}, u32[]{:S(2)}) %collective-permute-start.11) | collective-permute-done | bytes 491552 | tf_op jit(solution)/shard_map/ppermute | solution.py:1433
  319.1 1.3 collective-permute-start.12
  321.8 16.0 %collective-permute-done.12 = bf16[320,768]{1,0:T(8,128)(2,1)S(1)} collective-permute-done((bf16[320,768]{1,0:T(8,128)(2,1)S(1)}, bf16[320,768]{1,0:T(8,128)(2,1)S(1)}, u32[]{:S(2)}, u32[]{:S(2)}) %collective-permute-start.12) | collective-permute-done | bytes 491552 | tf_op jit(solution)/shard_map/ppermute | solution.py:1433
  337.8 1.2 fusion.28
  339.0 1.5 collective-permute-start.15
  341.8 3.2 collective-permute-done.14
  345.6 3.9 %shard_map.228 = (f32[6736,128]{1,0:T(8,128)}, f32[32,1,128]{2,1,0:T(1,128)}) custom-call(s32[15]{0:T(128)} %fusion.21.tab_ref, bf16[128,20224]{1,0:T(8,128)(2,1)} %all-gather.9.cloned.1.call-done.common_hbm, bf16[128,9728]{1,0:T(8,128)(2,1)} %all-gather.11.cloned.1.call-done.behind_hbm, f32[8,128]{1,0:T(8,128)} %copy-done.9, ...), custom_call_target="tpu_custom_call" | custom-call | flops 10000000000 | bytes 10000000 | tf_op jit(solution)/shard_map/pallas_call | solution.py:1161
  349.5 7.7 %all-to-all-start.2 = ((f32[32,1,128]{2,1,0:T(1,128)}), f32[32,1,128]{2,1,0:T(1,128)S(1)}, u32[]{:S(2)}, u32[]{:S(2)}) async-start(f32[32,1,128]{2,1,0:T(1,128)} %get-tuple-element.91), calls=%async_computation.2 | async-start | bytes 32768 | tf_op jit(solution)/shard_map/all_to_all | solution.py:1470
  357.5 1.7 copy-done.2
  359.2 2.1 shard_map.229
  361.3 2.9 all-to-all-done.2
  365.7 2.4 multiply_add_fusion.2
  368.1 6.6 %multiply_add_fusion = (f32[441096]{0:T(1024)}, f32[441096]{0:T(1024)}, f32[441096]{0:T(1024)}, f32[441096]{0:T(1024)}) fusion(f32[441096]{0:T(1024)S(1)} %copy-done.18, f32[441096]{0:T(1024)} %param.14, f32[]{:T(128)S(6)} %min_shard_map.3, f32[442368]{0:T(1024)S(1)} %bitcast.64, f32[441096]{0:T(1024)} %param.15, f32[441096]{0:T(1024)} %param.16), kind=kLoop, calls=%fused_computation.21 | loop fusion | flops 8380824 | bytes 15879460 | tf_op jit(solution)/shard_map/add | solution.py:1511
  (131 shorter events, 17.4 us)
Async XLA Ops:
  7.2 186.2 %all-gather.7.cloned.1.call-start = ((), (), s32[]{:S(2)}) async-start(), calls=%async_computation.3 | async-start | bytes 31752192 | tf_op jit(solution)/shard_map/all_gather | solution.py:1342
  9.6 5.9 %copy-start.19 = (f32[32,2048]{1,0:T(8,128)S(1)}, f32[32,2048]{1,0:T(8,128)}, u32[]{:S(2)}) copy-start(f32[32,2048]{1,0:T(8,128)} %param.21) | copy-start | bytes 786436
  9.6 5.9 %copy-start.20 = (f32[32,2048]{1,0:T(8,128)S(1)}, f32[32,2048]{1,0:T(8,128)}, u32[]{:S(2)}) copy-start(f32[32,2048]{1,0:T(8,128)} %param.18) | copy-start | bytes 786436
  12.6 24.4 %collective-permute-start = (bf16[3648,128]{1,0:T(8,128)(2,1)S(1)}, bf16[3648,128]{1,0:T(8,128)(2,1)S(1)}, u32[]{:S(2)}, u32[]{:S(2)}) collective-permute-start(bf16[3648,128]{1,0:T(8,128)(2,1)S(1)} %shard_map.222), channel_id=1, source_target_pairs={{0,4},{4,0},{8,12},{12,8},{16,20},{20,16},{24,28},{28,24},{1,5},{5... | collective-permute-start | bytes 2801672 | tf_op jit(solution)/shard_map/ppermute | solution.py:1321
  15.6 11.3 %collective-permute-start.1 = (bf16[2,32,2048]{2,1,0:T(8,128)(2,1)S(1)}, bf16[2,32,2048]{2,1,0:T(8,128)(2,1)S(1)}, u32[]{:S(2)}, u32[]{:S(2)}) collective-permute-start(bf16[2,32,2048]{2,1,0:T(8,128)(2,1)S(1)} %pad_maximum_fusion.2), channel_id=1, source_target_pairs={{0,8},{4,12},{8,16},{12,20},{16,24},{20,28},{24,0},{28,4},{1,9},{5... | collective-permute-start | bytes 786440 | tf_op jit(solution)/shard_map/ppermute | solution.py:1335
  17.3 19.7 %collective-permute-start.2 = (bf16[2,32,2048]{2,1,0:T(8,128)(2,1)S(1)}, bf16[2,32,2048]{2,1,0:T(8,128)(2,1)S(1)}, u32[]{:S(2)}, u32[]{:S(2)}) collective-permute-start(bf16[2,32,2048]{2,1,0:T(8,128)(2,1)S(1)} %pad_maximum_fusion.2), channel_id=1, source_target_pairs={{0,16},{4,20},{8,24},{12,28},{16,0},{20,4},{24,8},{28,12},{1,17},{... | collective-permute-start | bytes 786440 | tf_op jit(solution)/shard_map/ppermute | solution.py:1335
  20.1 16.8 %collective-permute-start.3 = (bf16[2,32,2048]{2,1,0:T(8,128)(2,1)S(1)}, bf16[2,32,2048]{2,1,0:T(8,128)(2,1)S(1)}, u32[]{:S(2)}, u32[]{:S(2)}) collective-permute-start(bf16[2,32,2048]{2,1,0:T(8,128)(2,1)S(1)} %pad_maximum_fusion.2), channel_id=1, source_target_pairs={{0,24},{4,28},{8,0},{12,4},{16,8},{20,12},{24,16},{28,20},{1,25},{... | collective-permute-start | bytes 786440 | tf_op jit(solution)/shard_map/ppermute | solution.py:1335
  38.6 262.1 %all-gather.9.cloned.1.call-start = ((), (), s32[]{:S(2)}) async-start(), calls=%async_computation.4 | async-start | bytes 5500928 | tf_op jit(solution)/shard_map/all_gather | solution.py:1371
  40.0 5.6 %copy-start.21 = (s32[4]{0:T(128)S(1)}, s32[4]{0:T(128)}, u32[]{:S(2)}) copy-start(s32[4]{0:T(128)} %param.24) | copy-start | bytes 52
  40.0 51.9 %collective-permute-start.6 = (bf16[4,2,32,2048]{3,2,1,0:T(8,128)(2,1)}, bf16[4,2,32,2048]{3,2,1,0:T(8,128)(2,1)S(1)}, u32[]{:S(2)}, u32[]{:S(2)}) collective-permute-start(bf16[4,2,32,2048]{3,2,1,0:T(8,128)(2,1)} %constant_dynamic-slice_fusion), channel_id=1, source_target_pairs={{0,4},{4,0},{8,12},{12,8},{16,20},{20,16},{24,28},{28,24},{1,5},{5... | collective-permute-start | bytes 3145736 | tf_op jit(solution)/shard_map/ppermute | solution.py:1321
  40.9 54.7 %collective-permute-start.4 = (bf16[4,196,768]{2,0,1:T(4,128)(2,1)}, bf16[4,196,768]{2,0,1:T(4,128)(2,1)}, u32[]{:S(2)}, u32[]{:S(2)}) collective-permute-start(bf16[4,196,768]{2,0,1:T(4,128)(2,1)} %param.23), channel_id=1, source_target_pairs={{0,4},{4,0},{8,12},{12,8},{16,20},{20,16},{24,28},{28,24},{1,5},{5... | collective-permute-start | bytes 3612680 | tf_op jit(solution)/shard_map/ppermute | solution.py:1321
  45.6 45.5 %collective-permute-start.5 = (f32[4]{0:T(128)S(1)}, f32[4]{0:T(128)S(1)}, u32[]{:S(2)}, u32[]{:S(2)}) collective-permute-start(f32[4]{0:T(128)S(1)} %convert_element_type.74), channel_id=1, source_target_pairs={{0,4},{4,0},{8,12},{12,8},{16,20},{20,16},{24,28},{28,24},{1,5},{5... | collective-permute-start | bytes 56 | tf_op jit(solution)/shard_map/ppermute | solution.py:1321
  93.2 1.3 copy-start
  193.4 38.9 %copy-start.8 = (f32[2048]{0:T(1024)S(1)}, f32[2048]{0:T(1024)}, u32[]{:S(2)}) copy-start(f32[2048]{0:T(1024)} %param.22) | copy-start | bytes 24580
  217.1 13.5 %collective-permute-start.7 = (bf16[8,20224]{1,0:T(8,128)(2,1)}, bf16[8,20224]{1,0:T(8,128)(2,1)S(1)}, u32[]{:S(2)}, u32[]{:S(2)}) collective-permute-start(bf16[8,20224]{1,0:T(8,128)(2,1)} %get-tuple-element.61), channel_id=1, source_target_pairs={{0,4},{4,0},{8,12},{12,8},{16,20},{20,16},{24,28},{28,24},{1,5},{5... | collective-permute-start | bytes 970760 | tf_op jit(solution)/shard_map/ppermute | solution.py:1321
  232.3 1.2 copy-start.3
  233.5 12.7 %copy-start.10 = (f32[16,768]{1,0:T(8,128)S(1)}, f32[16,768]{1,0:T(8,128)}, u32[]{:S(2)}) copy-start(f32[16,768]{1,0:T(8,128)} %get-tuple-element.66.class_ref) | copy-start | bytes 147460
  233.5 12.7 %copy-start.11 = (f32[8,3072]{1,0:T(8,128)S(1)}, f32[8,3072]{1,0:T(8,128)}, u32[]{:S(2)}) copy-start(f32[8,3072]{1,0:T(8,128)} %get-tuple-element.67.hidden_ref) | copy-start | bytes 294916
  233.5 12.7 %copy-start.12 = (f32[4,8,768]{2,1,0:T(8,128)S(1)}, f32[4,8,768]{2,1,0:T(8,128)}, u32[]{:S(2)}) copy-start(f32[4,8,768]{2,1,0:T(8,128)} %get-tuple-element.71.middle_ref) | copy-start | bytes 294916
  233.5 12.7 %copy-start.15 = (f32[8,2048]{1,0:T(8,128)S(1)}, f32[8,2048]{1,0:T(8,128)}, u32[]{:S(2)}) copy-start(f32[8,2048]{1,0:T(8,128)} %get-tuple-element.68.one_ref) | copy-start | bytes 196612
  233.5 12.7 %copy-start.16 = (f32[8,2048]{1,0:T(8,128)S(1)}, f32[8,2048]{1,0:T(8,128)}, u32[]{:S(2)}) copy-start(f32[8,2048]{1,0:T(8,128)} %get-tuple-element.69.two_ref) | copy-start | bytes 196612
  233.5 12.7 %copy-start.17 = (f32[8,256]{1,0:T(8,128)S(1)}, f32[8,256]{1,0:T(8,128)}, u32[]{:S(2)}) copy-start(f32[8,256]{1,0:T(8,128)} %get-tuple-element.70.bottle_ref) | copy-start | bytes 24580
  238.3 7.9 %all-to-all-start.1 = ((f32[4,32,256]{2,1,0:T(8,128)}), f32[4,32,256]{2,1,0:T(8,128)S(1)}, u32[]{:S(2)}, u32[]{:S(2)}) async-start(f32[4,32,256]{2,1,0:T(8,128)} %get-tuple-element.65), calls=%async_computation.1 | async-start | bytes 262144 | tf_op jit(solution)/shard_map/all_to_all | solution.py:1386
  241.6 104.0 %all-gather.11.cloned.1.call-start = ((), (), s32[]{:S(2)}) async-start(), calls=%async_computation.5 | async-start | bytes 2646016 | tf_op jit(solution)/shard_map/all_gather | solution.py:1371
  246.3 13.7 %copy-start.1 = (f32[1,4,2,32,2048]{4,3,2,1,0:T(8,128)S(1)}, f32[1,4,2,32,2048]{4,3,2,1,0:T(8,128)}, u32[]{:S(2)}) copy-start(f32[1,4,2,32,2048]{4,3,2,1,0:T(8,128)} %copy-done) | copy-start | bytes 6291460
  246.3 13.7 %copy-start.4 = (bf16[256,2048]{1,0:T(8,128)(2,1)S(1)}, bf16[256,2048]{1,0:T(8,128)(2,1)}, u32[]{:S(2)}) copy-start(bf16[256,2048]{1,0:T(8,128)(2,1)} %multiply_convert_fusion.columns_ref) | copy-start | bytes 3145732
  259.5 3.1 copy-start.13
  259.5 3.1 copy-start.14
  259.5 5.9 %copy-start.7 = (bf16[8,9728]{1,0:T(8,128)(2,1)}, bf16[8,9728]{1,0:T(8,128)(2,1)S(1)}, u32[]{:S(2)}) copy-start(bf16[8,9728]{1,0:T(8,128)(2,1)S(1)} %get-tuple-element.72.behind_ref) | copy-start | bytes 466948
  259.5 5.9 %collective-permute-start.8 = (bf16[8,9728]{1,0:T(8,128)(2,1)S(1)}, bf16[8,9728]{1,0:T(8,128)(2,1)S(1)}, u32[]{:S(2)}, u32[]{:S(2)}) collective-permute-start(bf16[8,9728]{1,0:T(8,128)(2,1)S(1)} %get-tuple-element.72.behind_ref), channel_id=1, source_target_pairs={{0,4},{4,0},{8,12},{12,8},{16,20},{20,16},{24,28},{28,24},{1,5},{5... | collective-permute-start | bytes 466952 | tf_op jit(solution)/shard_map/ppermute | solution.py:1321
  262.6 0.7 copy-start.5
  263.3 0.6 copy-start.9
  282.8 2.7 collective-permute-start.9
  287.3 13.3 %collective-permute-start.10 = (bf16[320,768]{1,0:T(8,128)(2,1)S(1)}, bf16[320,768]{1,0:T(8,128)(2,1)S(1)}, u32[]{:S(2)}, u32[]{:S(2)}) collective-permute-start(bf16[320,768]{1,0:T(8,128)(2,1)S(1)} %pad_maximum_fusion.1), channel_id=1, source_target_pairs={{0,2},{1,3},{2,0},{3,1},{4,6},{5,7},{6,4},{7,5},{8,10},{9,11},{10,... | collective-permute-start | bytes 1474568 | tf_op jit(solution)/shard_map/ppermute | solution.py:1419
  300.8 18.1 %collective-permute-start.11 = (bf16[320,768]{1,0:T(8,128)(2,1)S(1)}, bf16[320,768]{1,0:T(8,128)(2,1)S(1)}, u32[]{:S(2)}, u32[]{:S(2)}) collective-permute-start(bf16[320,768]{1,0:T(8,128)(2,1)S(1)} %convert_element_type.83), channel_id=1, source_target_pairs={{8,0},{12,4},{24,16},{28,20},{9,1},{13,5},{25,17},{29,21},{10,2},{... | collective-permute-start | bytes 1474568 | tf_op jit(solution)/shard_map/ppermute | solution.py:1433
  319.1 18.7 %collective-permute-start.12 = (bf16[320,768]{1,0:T(8,128)(2,1)S(1)}, bf16[320,768]{1,0:T(8,128)(2,1)S(1)}, u32[]{:S(2)}, u32[]{:S(2)}) collective-permute-start(bf16[320,768]{1,0:T(8,128)(2,1)S(1)} %fusion.12), channel_id=1, source_target_pairs={{16,0},{20,4},{17,1},{21,5},{18,2},{22,6},{19,3},{23,7}} | collective-permute-start | bytes 1474568 | tf_op jit(solution)/shard_map/ppermute | solution.py:1433
  339.0 2.8 collective-permute-start.15
  340.7 8.8 %collective-permute-start.13 = (bf16[288,768]{1,0:T(8,128)(2,1)S(1)}, bf16[288,768]{1,0:T(8,128)(2,1)S(1)}, u32[]{:S(2)}, u32[]{:S(2)}) collective-permute-start(bf16[288,768]{1,0:T(8,128)(2,1)S(1)} %slice.98), channel_id=1, source_target_pairs={{0,2},{1,3},{2,0},{3,1},{4,6},{5,7},{6,4},{7,5},{8,10},{9,11},{10,... | collective-permute-start | bytes 1327112 | tf_op jit(solution)/shard_map/ppermute | solution.py:1419
  340.9 4.1 %collective-permute-start.14 = (bf16[32,768]{1,0:T(8,128)(2,1)S(1)}, bf16[32,768]{1,0:T(8,128)(2,1)S(1)}, u32[]{:S(2)}, u32[]{:S(2)}) collective-permute-start(bf16[32,768]{1,0:T(8,128)(2,1)S(1)} %slice.100), channel_id=1, source_target_pairs={{0,4},{4,0},{8,12},{12,8},{16,20},{20,16},{24,28},{28,24},{1,5},{5... | collective-permute-start | bytes 147464 | tf_op jit(solution)/shard_map/ppermute | solution.py:1321
  349.5 14.7 %all-to-all-start.2 = ((f32[32,1,128]{2,1,0:T(1,128)}), f32[32,1,128]{2,1,0:T(1,128)S(1)}, u32[]{:S(2)}, u32[]{:S(2)}) async-start(f32[32,1,128]{2,1,0:T(1,128)} %get-tuple-element.91), calls=%async_computation.2 | async-start | bytes 32768 | tf_op jit(solution)/shard_map/all_to_all | solution.py:1470
  357.2 2.0 copy-start.2
  359.2 6.5 %copy-start.6 = (f32[32,2048]{1,0:T(8,128)S(1)}, f32[32,2048]{1,0:T(8,128)}, u32[]{:S(2)}) copy-start(f32[32,2048]{1,0:T(8,128)} %copy-done.5) | copy-start | bytes 786436
  365.7 2.5 copy-start.18
Sparse Core Ops, SparseCore 0:
  38.7 154.6 all-gather.6
  232.4 54.0 all-gather.8
  300.9 44.0 all-gather.10

commit v9 on v8

--- a/solution.py
+++ b/solution.py
@@ -168,10 +168,15 @@
                     if entry[1 + place] == index
                 ]
             )
-            for index in SPANS
+            for index in (1,) + tuple(SPANS)
         }
+        self.fetched = max(
+            [HEADS * (self.most_chunks[1] + 1) * CHUNK, H + D]
+            + [(chunks + 1) * CHUNK for chunks in self.most_chunks.values()]
+        )
         self.late_table = self.tabulate(lambda index: index in (0, 1, 5), self.wide_row)
         self.grad_scratch = FRONT + self.lines + CHUNK * max(WIDTHS) + 16
+        self.used = FRONT + self.lines + 8
 
 
     def largest(self):
@@ -382,7 +387,7 @@
             out_ref[:, pl.ds(pl.multiple_of(pair * 2 * LANES, LANES), 2 * LANES)] = total
             return carry
 
-        lax.fori_loop(0, SEGMENTS[index][2] // LANES // 2, column, 0, unroll=2)
+        lax.fori_loop(0, SEGMENTS[index][2] // LANES // 2, column, 0, unroll=4)
 
 
     def back(self, index, first, count, values, grad_ref, left_ref, wide_ref):
@@ -405,7 +410,7 @@
                 left_ref[number, :, :size] += product_t(left, self.columns(index, block, pair))
             return carry
 
-        lax.fori_loop(0, cols // LANES // 2, column, 0, unroll=2)
+        lax.fori_loop(0, cols // LANES // 2, column, 0, unroll=4)
         for number, (_, _, tile0, tiles) in enumerate(blocks):
             start = 8 * tile0 // LANES * LANES
             turn = 8 * tile0 - start
@@ -700,16 +705,18 @@
         if part.shape[1] < B:
             note_ref[:, lines, part.shape[1] :] = jnp.zeros((groups, 8, B - part.shape[1]), F32)
     start = pl.multiple_of(start_ref[0], 8)
-    columns = columns_ref[...].astype(F32)
-    for which, source in enumerate((student_ref, teacher_ref)):
-        pulls = lax.dot_general(
-            source[pl.ds(start, groups * views), :],
-            columns,
-            (((1,), (1,)), ((), ())),
-            precision=PRECISE,
-            preferred_element_type=F32,
-        )
-        note_ref[:, which * views : (which + 1) * views, :] = pulls.reshape(groups, views, B)
+    band, parts = groups * views, []
+    for source in (student_ref, teacher_ref):
+        rest = source[pl.ds(start, band), :]
+        for _ in range(3):
+            parts.append(rest.astype(BF16))
+            rest = rest - parts[-1].astype(F32)
+    pulls = product_t(jnp.concatenate(parts, 0), columns_ref[...])
+    for which in range(2):
+        first = 3 * which * band
+        total = pulls[first : first + band] + pulls[first + band : first + 2 * band]
+        total = total + pulls[first + 2 * band : first + 3 * band]
+        note_ref[:, which * views : (which + 1) * views, :] = total.reshape(groups, views, B)
     own = sums_ref[pl.ds(start, groups * views), :]
     note_ref[:, 2 * views : 3 * views, :] = own.reshape(groups, views, B)
 
@@ -1038,7 +1045,8 @@
     rest_ref,
     *refs,
 ):
-    line_ref, square_ref, common_ref, behind_ref, class_ref, sem, class_sem = refs[-7:]
+    line_out, square_ref, common_ref, behind_ref, class_ref, line_ref, sem, class_sem = refs[-8:]
+    slab = (plan.most_chunks[1] + 1) * CHUNK
     class_copy = pltpu.make_async_copy(
         common_hbm.at[pl.ds(0, TILE), pl.ds(CLASS, D)], class_ref, class_sem
     )
@@ -1046,11 +1054,12 @@
     line_ref[...] = jnp.zeros(line_ref.shape, F32)
 
     def fetch(source, target, column, size):
+        which = 0 if target is common_ref else 1
         copy = pltpu.make_async_copy(
-            source.at[:, pl.ds(column, size)], target.at[:, pl.ds(0, size)], sem
+            source.at[:, pl.ds(column, size)], target.at[:, pl.ds(0, size)], sem.at[which]
         )
         copy.start()
-        copy.wait()
+        return copy
 
     def turned(lane):
         start = pl.multiple_of(lane // LANES * LANES, LANES)
@@ -1071,8 +1080,13 @@
             @pl.when(kind == index)
             def _(lane=lane, column=column, cols=cols, width=width, size=size):
                 skew = lax.rem(row0, LANES)
-                fetch(common_hbm, common_ref, pl.multiple_of(ROWS + lane + row0 - skew, LANES), size)
-                fetch(behind_hbm, behind_ref, column, cols)
+                place = pl.multiple_of(ROWS + lane + row0 - skew, LANES)
+                copies = [
+                    fetch(common_hbm, common_ref, place, size),
+                    fetch(behind_hbm, behind_ref, column, cols),
+                ]
+                for copy in copies:
+                    copy.wait()
 
                 def move(step, carry):
                     goal = base + step * (CHUNK * width)
@@ -1085,18 +1099,23 @@
 
         @pl.when(kind == 8)
         def _():
-            fetch(behind_hbm, behind_ref, 2 * D + F, B)
-            fetch(common_hbm, common_ref, SECOND, H + D)
+            copies = [
+                fetch(behind_hbm, behind_ref, 2 * D + F, B),
+                fetch(common_hbm, common_ref, SECOND, H + D),
+            ]
+            for copy in copies:
+                copy.wait()
 
             def move(step, carry):
-                left = turned(row0 + step * CHUNK)
-                block = product(left, behind_ref[:, :B])
-                for tile in range(B // LANES):
-                    piece = block[:, tile * LANES : (tile + 1) * LANES]
-                    store(base + step * (CHUNK * B // LANES), B // LANES, tile, piece)
+                for own in range(2):
+                    place = 2 * step + own
+                    block = product(turned(row0 + place * CHUNK), behind_ref[:, :B])
+                    for tile in range(B // LANES):
+                        piece = block[:, tile * LANES : (tile + 1) * LANES]
+                        store(base + place * (CHUNK * B // LANES), B // LANES, tile, piece)
                 return carry
 
-            lax.fori_loop(0, chunks, move, 0)
+            lax.fori_loop(0, (chunks + 1) // 2, move, 0)
 
         @pl.when(kind == 5)
         def _():
@@ -1105,8 +1124,20 @@
 
         @pl.when(kind == 1)
         def _():
-            fetch(behind_hbm, behind_ref, ATT_COLUMN, D)
-            fetch(common_hbm, common_ref, 0, ROWS)
+            skew = lax.rem(row0, LANES)
+            first = pl.multiple_of(row0 - skew, LANES)
+            copies = [fetch(behind_hbm, behind_ref, ATT_COLUMN, D)]
+            for head in range(HEADS):
+                copies.append(
+                    pltpu.make_async_copy(
+                        common_hbm.at[:, pl.ds(pl.multiple_of(head * D + first, LANES), slab)],
+                        common_ref.at[:, pl.ds(head * slab, slab)],
+                        sem.at[2 + head],
+                    )
+                )
+                copies[-1].start()
+            for copy in copies:
+                copy.wait()
 
             def move(step, carry):
                 width = 3 * D // LANES
@@ -1114,9 +1145,9 @@
                 side = lax.broadcasted_iota(jnp.int32, (CHUNK, LANES), 1)
                 for pair in range(HEADS // 2):
                     right = behind_ref[:, pair * LANES : (pair + 1) * LANES]
-                    lane = 2 * pair * D + row0 + step * CHUNK
-                    first, second = (product(turned(lane + D * head), right) for head in range(2))
-                    block = jnp.where(side < HDIM, first, second)
+                    lane = 2 * pair * slab + skew + step * CHUNK
+                    left, other = (product(turned(lane + slab * head), right) for head in range(2))
+                    block = jnp.where(side < HDIM, left, other)
                     store(goal, width, 2 * D // LANES + pair, block)
                 return carry
 
@@ -1138,9 +1169,11 @@
     total = lax.fori_loop(
         0, plan.steps, clear, jnp.zeros(shape, F32), unroll=steps_at_once(plan.steps)
     )
+    line_copy = pltpu.make_async_copy(line_ref.at[pl.ds(0, plan.used)], line_out, sem.at[0])
+    line_copy.start()
     total = jnp.sum(total, keepdims=True) + rest_ref[0:1, 0:1]
     class_copy.wait()
-    if len(refs) > 7:
+    if len(refs) > 8:
         holds, twice = (tab_ref[1 + 4 * most + which] for which in range(2))
         rows = jnp.sum(refs[0][...] * refs[0][...], 1, keepdims=True)
         place = lax.broadcasted_iota(jnp.int32, (SET, 1), 0)
@@ -1155,13 +1188,14 @@
         outer = outer + rows[SET + HEADROWS + 2 : SET + HEADROWS + 3]
         total = total + jnp.where(holds != 0, pieces + outer / plan.groups, 0.0)
     square_ref[...] = jnp.broadcast_to(total[None], square_ref.shape)
+    line_copy.wait()
 
 
 def early_gradient(plan, table, common, behind, *values):
     return pl.pallas_call(
         functools.partial(early_kernel, plan, (table.shape[0] - 3) // 4),
         out_shape=[
-            jax.ShapeDtypeStruct((plan.grad_scratch, LANES), F32),
+            jax.ShapeDtypeStruct((plan.used, LANES), F32),
             jax.ShapeDtypeStruct((plan.count, 1, LANES), F32),
         ],
         in_specs=[
@@ -1170,12 +1204,16 @@
             pl.BlockSpec(memory_space=pl.ANY),
         ]
         + [pl.BlockSpec(memory_space=pltpu.VMEM)] * len(values),
-        out_specs=[pl.BlockSpec(memory_space=pltpu.VMEM)] * 2,
+        out_specs=[
+            pl.BlockSpec(memory_space=pl.ANY),
+            pl.BlockSpec(memory_space=pltpu.VMEM),
+        ],
         scratch_shapes=[
-            pltpu.VMEM((common.shape[0], ROWS), BF16),
+            pltpu.VMEM((common.shape[0], plan.fetched), BF16),
             pltpu.VMEM((behind.shape[0], F), BF16),
             pltpu.VMEM((TILE, D), BF16),
-            pltpu.SemaphoreType.DMA,
+            pltpu.VMEM((plan.grad_scratch, LANES), F32),
+            pltpu.SemaphoreType.DMA((2 + HEADS,)),
             pltpu.SemaphoreType.DMA,
         ],
         compiler_params=pltpu.CompilerParams(vmem_limit_bytes=60 * 1024 * 1024),
@@ -1198,8 +1236,7 @@
     line_ref,
     sem,
 ):
-    used = FRONT + plan.lines + 8
-    copy = pltpu.make_async_copy(lines_ref.at[pl.ds(0, used)], line_ref.at[pl.ds(0, used)], sem)
+    copy = pltpu.make_async_copy(lines_ref, line_ref.at[pl.ds(0, plan.used)], sem)
     copy.start()
     copy.wait()
 
@@ -1373,15 +1410,14 @@
         )
 
     other = trade(common)
-    all_rows, other = lax.optimization_barrier((all_rows, other))
-    common = jnp.where(low, common, other)
 
     all_rows = all_rows.reshape(reps // 2, 2, -1, B).transpose(1, 0, 2, 3).reshape(2, -1, B)
     start = (rep // 2 * groups * views).astype(jnp.int32)[None]
     note, new_center = prototypes(
         start, all_rows, columns, teacher_columns, center[None], groups, views
     )
-    common = gather_rows(common)
+    note, other = lax.optimization_barrier((note, other))
+    common = gather_rows(jnp.where(low, common, other))
     new_center = new_center[0]
     note = lax.all_to_all(note, "grp", 0, 0)
     totals = jnp.sum(note[:, 3 * views :], 0)

time: 383 us -> 378 us (0.987)
  blocking collectives: 11.9 us -> 0 us
  starting transfers between devices: 30.2 us -> 36.5 us
  waiting for transfers between devices: 201 us -> 205 us
    all_to_all x1 -> x0, blocking collectives: 11.9 us -> none  [per_device(): all_rows, common = (lax.all_to_all(kept[12], BOTH, 0, 0), kept[13])]
    all_to_all x0 -> x1, waiting for transfers between devices: none -> 6.45 us  [per_device(): all_rows, common = (lax.all_to_all(kept[12], BOTH, 0, 0), kept[13])]
    all_to_all x0 -> x1, starting transfers between devices: none -> 4.58 us  [per_device(): all_rows, common = (lax.all_to_all(kept[12], BOTH, 0, 0), kept[13])]
  transfers between devices with their start and end apart: 21 -> 22, of which waited for: 13 -> 13; matrix products, arithmetic and copies ran while one was open for 8% -> 8% of each run, Pallas kernels for 12% -> 11%
where the time goes in v9:
time: 378 us; the launch traced here: 377 us
  waiting for transfers between devices  205 us (54%)
  Pallas kernels  68.8 us (18%)
  starting transfers between devices  36.5 us (10%)
  other arithmetic  28.4 us (8%)
  local copies, waits for them, and re-layouts  22.2 us (6%)
  between operations  16.4 us (4%)
    all_gather x1, waiting for transfers between devices, per_device(): gathered = lax.all_gather(shards, BOTH, axis=0, axis_index_groups=halves)  84.1 us
    ppermute x7, waiting for transfers between devices, trade(): return lax.ppermute(values, 'rep', swap)  47.8 us
    ppermute x2, waiting for transfers between devices, per_device(): lax.ppermute(partial.astype(BF16), 'rep', hops).astype(F32)  30.6 us
    pallas_call x1, Pallas kernels, forward(): pl.pallas_call(functools.partial(forward_kernel, plan), out_shape=[jax.Sh...  23.3 us
    pallas_call x1, Pallas kernels, tokens_back(): pl.pallas_call(tokens_back_kernel, grid=(views,), out_shape=[jax.ShapeDty...  17.3 us
    ppermute x3, waiting for transfers between devices, across(): return lax.ppermute(values, 'grp', [(g, g ^ bit) for g in range(groups)])  15 us
    ppermute x3, waiting for transfers between devices, per_device(): lax.ppermute(tables, 'rep', [(r, (r + step) % reps) for r in range(reps)])  13.2 us
    pallas_call x1, Pallas kernels, rows_back(): pl.pallas_call(functools.partial(rows_back_kernel, plan), out_shape=[jax....  13 us
  transfers between devices with their start and end apart: 22, of which 13 were waited for; matrix products, arithmetic and copies ran while one was open for 8% of the time, Pallas kernels for 11%

profile of v9, /device:TPU:0, one launch (start us, length us, event | category | flops | bytes accessed | tf_op | source)
XLA Modules:
  0.0 377.3 jit_solution(984236029632380820)
XLA Ops:
  7.2 2.2 broadcast_select_fusion.3
  10.4 2.2 shard_map.222
  12.6 2.9 collective-permute-start
  15.6 1.7 collective-permute-start.1
  17.3 2.8 collective-permute-start.2
  20.1 1.3 collective-permute-start.3
  21.6 2.2 shard_map.221
  23.8 3.1 collective-permute-done.1
  26.9 10.1 %collective-permute-done.2 = bf16[2,32,2048]{2,1,0:T(8,128)(2,1)S(1)} collective-permute-done((bf16[2,32,2048]{2,1,0:T(8,128)(2,1)S(1)}, bf16[2,32,2048]{2,1,0:T(8,128)(2,1)S(1)}, u32[]{:S(2)}, u32[]{:S(2)}) %collective-permute-start.2) | collective-permute-done | bytes 262176 | tf_op jit(solution)/shard_map/ppermute | solution.py:1372
  37.2 1.4 pad_maximum_fusion
  41.9 3.6 copy.47
  46.5 44.5 %collective-permute-done.5 = f32[4]{0:T(128)S(1)} collective-permute-done((f32[4]{0:T(128)S(1)}, f32[4]{0:T(128)S(1)}, u32[]{:S(2)}, u32[]{:S(2)}) %collective-permute-start.5) | collective-permute-done | bytes 48 | tf_op jit(solution)/shard_map/ppermute | solution.py:1358
  94.5 1.2 multiply_convert_fusion.columns_ref
  95.6 3.6 copy.48
  99.3 2.1 broadcast_select_fusion.1
  101.4 3.2 fusion.25
  104.6 4.7 %copy.53.pixels_ref = bf16[8,208,768]{2,1,0:T(8,128)(2,1)} copy(bf16[8,208,768]{1,2,0:T(8,128)(2,1)} %get-tuple-element.108) | data formatting | bytes 5111808 | tf_op jit(solution)/shard_map/jit(_pad)/pad | solution.py:1383
  109.3 84.1 %all-gather.7.cloned.1.call-done = bf16[32,3648,128]{2,1,0:T(8,128)(2,1)} async-done(((bf16[2,3648,128]{2,1,0:T(8,128)(2,1)}), bf16[32,3648,128]{2,1,0:T(8,128)(2,1)}) %all-gather.7.cloned.1.call-update) | async-done | bytes 29884432 | tf_op jit(solution)/shard_map/all_gather | solution.py:1379
  193.4 23.3 %shard_map.223 = (f32[8,208,768]{2,1,0:T(8,128)}, f32[8,208,128]{2,1,0:T(8,128)}, f32[8,16,208]{2,1,0:T(8,128)}, bf16[8,16,768]{2,1,0:T(8,128)(2,1)}, bf16[16,76...) custom-call(bf16[16,2,228,16,128]{4,3,2,1,0:T(8,128)(2,1)} %bitcast., ...), custom_call_target="tpu_custom_call" | custom-call | flops 60000002048 | bytes 40000000 | tf_op jit(solution)/shard_map/pallas_call | solution.py:641
  216.7 4.6 %all-to-all-start = ((bf16[32,8,256]{2,1,0:T(8,128)(2,1)}), bf16[32,8,256]{2,1,0:T(8,128)(2,1)S(1)}, u32[]{:S(2)}, u32[]{:S(2)}) async-start(bf16[32,8,256]{2,1,0:T(8,128)(2,1)} %get-tuple-element.60), calls=%async_computation | async-start | bytes 262144 | tf_op jit(solution)/shard_map/all_to_all | solution.py:1405
  221.4 1.8 collective-permute-start.7
  223.2 6.4 %all-to-all-done = bf16[32,8,256]{2,1,0:T(8,128)(2,1)S(1)} async-done(((bf16[32,8,256]{2,1,0:T(8,128)(2,1)}), bf16[32,8,256]{2,1,0:T(8,128)(2,1)S(1)}, u32[]{:S(2)}, u32[]{:S(2)}) %all-to-all-start) | async-done | bytes 131104 | tf_op jit(solution)/shard_map/all_to_all | solution.py:1405
  229.7 1.2 copy-done.3
  230.9 1.8 shard_map.224
  233.5 3.3 all-to-all-start.1
  237.1 4.4 %all-to-all-done.1.note_ref = f32[4,32,256]{2,1,0:T(8,128)S(1)} async-done(((f32[4,32,256]{2,1,0:T(8,128)}), f32[4,32,256]{2,1,0:T(8,128)S(1)}, u32[]{:S(2)}, u32[]{:S(2)}) %all-to-all-start.1) | async-done | bytes 131104 | tf_op jit(solution)/shard_map/all_to_all | solution.py:1422
  241.6 13.0 %shard_map.225 = (bf16[8,9728]{1,0:T(8,128)(2,1)S(1)}, f32[8,768]{1,0:T(8,128)S(1)}, f32[8,768]{1,0:T(8,128)S(1)}) custom-call(s32[1]{0:T(128)} %bitcast.2.low_ref, bf16[16,2,228,16,128]{4,3,2,1,0:T(8,128)(2,1)} %bitcast.72, f32[4,32,256]{2,1,0:T(8,128)S(1)} %all-to-all-done.1.note_ref, f32[16,768]{1,0:T(8,128)S(1)} %copy-done.10, f32[8,3072]{1,0:T(8,128)S(1)} %copy-done.11, ...), custom_call_target="tpu_custom_call" | custom-call | flops 30000001024 | bytes 30000000 | tf_op jit(solution)/shard_map/pallas_call | solution.py:870
  254.6 1.5 collective-permute-start.8
  256.1 2.6 shard_map.226
  260.9 17.3 %shard_map.227 = (f32[608,768]{1,0:T(8,128)}, bf16[608,768]{1,0:T(8,128)(2,1)}) custom-call(s32[1]{0:T(128)} %bitcast.25.odd_ref, bf16[8,9728]{1,0:T(8,128)(2,1)} %copy-done.7, f32[8,768]{1,0:T(8,128)} %copy-done.13, f32[8,768]{1,0:T(8,128)} %copy-done.14, f32[8,208,768]{2,1,0:T(8,128)} %get-tuple-element.76.unit_ref, ...), custom_call_target="tpu_custom_call" | custom-call | flops 15000000512 | bytes 15000000 | tf_op jit(solution)/shard_map/pallas_call | solution.py:1005
  278.2 2.7 collective-permute-done.9
  280.9 1.7 convert_add_fusion
  283.8 12.3 %collective-permute-done.10 = bf16[320,768]{1,0:T(8,128)(2,1)S(1)} collective-permute-done((bf16[320,768]{1,0:T(8,128)(2,1)S(1)}, bf16[320,768]{1,0:T(8,128)(2,1)S(1)}, u32[]{:S(2)}, u32[]{:S(2)}) %collective-permute-start.10) | collective-permute-done | bytes 491552 | tf_op jit(solution)/shard_map/ppermute | solution.py:1455
  296.4 1.3 collective-permute-start.11
  297.8 1.2 fusion.21.tab_ref
  299.7 14.0 %collective-permute-done.11 = bf16[320,768]{1,0:T(8,128)(2,1)S(1)} collective-permute-done((bf16[320,768]{1,0:T(8,128)(2,1)S(1)}, bf16[320,768]{1,0:T(8,128)(2,1)S(1)}, u32[]{:S(2)}, u32[]{:S(2)}) %collective-permute-start.11) | collective-permute-done | bytes 491552 | tf_op jit(solution)/shard_map/ppermute | solution.py:1469
  313.8 1.3 collective-permute-start.12
  316.4 16.6 %collective-permute-done.12 = bf16[320,768]{1,0:T(8,128)(2,1)S(1)} collective-permute-done((bf16[320,768]{1,0:T(8,128)(2,1)S(1)}, bf16[320,768]{1,0:T(8,128)(2,1)S(1)}, u32[]{:S(2)}, u32[]{:S(2)}) %collective-permute-start.12) | collective-permute-done | bytes 491552 | tf_op jit(solution)/shard_map/ppermute | solution.py:1469
  334.2 1.4 collective-permute-start.15
  335.8 1.2 collective-permute-start.13
  338.0 3.2 collective-permute-done.14
  341.7 4.3 %shard_map.228 = (f32[3656,128]{1,0:T(8,128)}, f32[32,1,128]{2,1,0:T(1,128)}) custom-call(s32[15]{0:T(128)} %fusion.21.tab_ref, bf16[128,20224]{1,0:T(8,128)(2,1)} %all-gather.9.cloned.1.call-done.common_hbm, bf16[128,9728]{1,0:T(8,128)(2,1)} %all-gather.11.cloned.1.call-done.behind_hbm, f32[8,128]{1,0:T(8,128)} %copy-done.9, ...), custom_call_target="tpu_custom_call" | custom-call | flops 10000000000 | bytes 10000000 | tf_op jit(solution)/shard_map/pallas_call | solution.py:1195
  346.0 6.1 %all-to-all-start.2 = ((f32[32,1,128]{2,1,0:T(1,128)}), f32[32,1,128]{2,1,0:T(1,128)S(1)}, u32[]{:S(2)}, u32[]{:S(2)}) async-start(f32[32,1,128]{2,1,0:T(1,128)} %get-tuple-element.91), calls=%async_computation.2 | async-start | bytes 32768 | tf_op jit(solution)/shard_map/all_to_all | solution.py:1506
  352.3 1.3 copy-done.2
  353.7 2.1 shard_map.229
  355.8 3.3 all-to-all-done.2
  360.6 2.4 multiply_add_fusion.2
  363.0 6.6 %multiply_add_fusion = (f32[441096]{0:T(1024)}, f32[441096]{0:T(1024)}, f32[441096]{0:T(1024)}, f32[441096]{0:T(1024)}) fusion(f32[441096]{0:T(1024)S(1)} %copy-done.18, f32[441096]{0:T(1024)} %param.14, f32[]{:T(128)S(6)} %min_shard_map.3, f32[442368]{0:T(1024)S(1)} %bitcast.64, f32[441096]{0:T(1024)} %param.15, f32[441096]{0:T(1024)} %param.16), kind=kLoop, calls=%fused_computation.21 | loop fusion | flops 8380824 | bytes 15879460 | tf_op jit(solution)/shard_map/add | solution.py:1547
  (134 shorter events, 19.6 us)
Async XLA Ops:
  7.2 186.2 %all-gather.7.cloned.1.call-start = ((), (), s32[]{:S(2)}) async-start(), calls=%async_computation.3 | async-start | bytes 31752192 | tf_op jit(solution)/shard_map/all_gather | solution.py:1379
  9.6 5.9 %copy-start.19 = (f32[32,2048]{1,0:T(8,128)S(1)}, f32[32,2048]{1,0:T(8,128)}, u32[]{:S(2)}) copy-start(f32[32,2048]{1,0:T(8,128)} %param.21) | copy-start | bytes 786436
  9.6 5.9 %copy-start.20 = (f32[32,2048]{1,0:T(8,128)S(1)}, f32[32,2048]{1,0:T(8,128)}, u32[]{:S(2)}) copy-start(f32[32,2048]{1,0:T(8,128)} %param.18) | copy-start | bytes 786436
  12.6 24.4 %collective-permute-start = (bf16[3648,128]{1,0:T(8,128)(2,1)S(1)}, bf16[3648,128]{1,0:T(8,128)(2,1)S(1)}, u32[]{:S(2)}, u32[]{:S(2)}) collective-permute-start(bf16[3648,128]{1,0:T(8,128)(2,1)S(1)} %shard_map.222), channel_id=1, source_target_pairs={{0,4},{4,0},{8,12},{12,8},{16,20},{20,16},{24,28},{28,24},{1,5},{5... | collective-permute-start | bytes 2801672 | tf_op jit(solution)/shard_map/ppermute | solution.py:1358
  15.6 11.3 %collective-permute-start.1 = (bf16[2,32,2048]{2,1,0:T(8,128)(2,1)S(1)}, bf16[2,32,2048]{2,1,0:T(8,128)(2,1)S(1)}, u32[]{:S(2)}, u32[]{:S(2)}) collective-permute-start(bf16[2,32,2048]{2,1,0:T(8,128)(2,1)S(1)} %pad_maximum_fusion.2), channel_id=1, source_target_pairs={{0,8},{4,12},{8,16},{12,20},{16,24},{20,28},{24,0},{28,4},{1,9},{5... | collective-permute-start | bytes 786440 | tf_op jit(solution)/shard_map/ppermute | solution.py:1372
  17.3 19.7 %collective-permute-start.2 = (bf16[2,32,2048]{2,1,0:T(8,128)(2,1)S(1)}, bf16[2,32,2048]{2,1,0:T(8,128)(2,1)S(1)}, u32[]{:S(2)}, u32[]{:S(2)}) collective-permute-start(bf16[2,32,2048]{2,1,0:T(8,128)(2,1)S(1)} %pad_maximum_fusion.2), channel_id=1, source_target_pairs={{0,16},{4,20},{8,24},{12,28},{16,0},{20,4},{24,8},{28,12},{1,17},{... | collective-permute-start | bytes 786440 | tf_op jit(solution)/shard_map/ppermute | solution.py:1372
  20.1 16.8 %collective-permute-start.3 = (bf16[2,32,2048]{2,1,0:T(8,128)(2,1)S(1)}, bf16[2,32,2048]{2,1,0:T(8,128)(2,1)S(1)}, u32[]{:S(2)}, u32[]{:S(2)}) collective-permute-start(bf16[2,32,2048]{2,1,0:T(8,128)(2,1)S(1)} %pad_maximum_fusion.2), channel_id=1, source_target_pairs={{0,24},{4,28},{8,0},{12,4},{16,8},{20,12},{24,16},{28,20},{1,25},{... | collective-permute-start | bytes 786440 | tf_op jit(solution)/shard_map/ppermute | solution.py:1372
  39.9 5.6 %copy-start.22 = (s32[4]{0:T(128)S(1)}, s32[4]{0:T(128)}, u32[]{:S(2)}) copy-start(s32[4]{0:T(128)} %param.24) | copy-start | bytes 52
  39.9 51.9 %collective-permute-start.6 = (bf16[4,2,32,2048]{3,2,1,0:T(8,128)(2,1)}, bf16[4,2,32,2048]{3,2,1,0:T(8,128)(2,1)S(1)}, u32[]{:S(2)}, u32[]{:S(2)}) collective-permute-start(bf16[4,2,32,2048]{3,2,1,0:T(8,128)(2,1)} %constant_dynamic-slice_fusion), channel_id=1, source_target_pairs={{0,4},{4,0},{8,12},{12,8},{16,20},{20,16},{24,28},{28,24},{1,5},{5... | collective-permute-start | bytes 3145736 | tf_op jit(solution)/shard_map/ppermute | solution.py:1358
  40.9 54.7 %collective-permute-start.4 = (bf16[4,196,768]{2,0,1:T(4,128)(2,1)}, bf16[4,196,768]{2,0,1:T(4,128)(2,1)}, u32[]{:S(2)}, u32[]{:S(2)}) collective-permute-start(bf16[4,196,768]{2,0,1:T(4,128)(2,1)} %param.23), channel_id=1, source_target_pairs={{0,4},{4,0},{8,12},{12,8},{16,20},{20,16},{24,28},{28,24},{1,5},{5... | collective-permute-start | bytes 3612680 | tf_op jit(solution)/shard_map/ppermute | solution.py:1358
  45.5 45.5 %collective-permute-start.5 = (f32[4]{0:T(128)S(1)}, f32[4]{0:T(128)S(1)}, u32[]{:S(2)}, u32[]{:S(2)}) collective-permute-start(f32[4]{0:T(128)S(1)} %convert_element_type.74), channel_id=1, source_target_pairs={{0,4},{4,0},{8,12},{12,8},{16,20},{20,16},{24,28},{28,24},{1,5},{5... | collective-permute-start | bytes 56 | tf_op jit(solution)/shard_map/ppermute | solution.py:1358
  93.1 1.4 copy-start
  193.4 36.3 %copy-start.8 = (f32[2048]{0:T(1024)S(1)}, f32[2048]{0:T(1024)}, u32[]{:S(2)}) copy-start(f32[2048]{0:T(1024)} %param.22) | copy-start | bytes 24580
  216.7 12.9 %all-to-all-start = ((bf16[32,8,256]{2,1,0:T(8,128)(2,1)}), bf16[32,8,256]{2,1,0:T(8,128)(2,1)S(1)}, u32[]{:S(2)}, u32[]{:S(2)}) async-start(bf16[32,8,256]{2,1,0:T(8,128)(2,1)} %get-tuple-element.60), calls=%async_computation | async-start | bytes 262144 | tf_op jit(solution)/shard_map/all_to_all | solution.py:1405
  221.3 75.0 %all-gather.9.cloned.1.call-start = ((), (), s32[]{:S(2)}) async-start(), calls=%async_computation.4 | async-start | bytes 5500928 | tf_op jit(solution)/shard_map/all_gather | solution.py:1408
  221.4 11.4 %collective-permute-start.7 = (bf16[8,20224]{1,0:T(8,128)(2,1)}, bf16[8,20224]{1,0:T(8,128)(2,1)S(1)}, u32[]{:S(2)}, u32[]{:S(2)}) collective-permute-start(bf16[8,20224]{1,0:T(8,128)(2,1)} %get-tuple-element.64), channel_id=1, source_target_pairs={{0,4},{4,0},{8,12},{12,8},{16,20},{20,16},{24,28},{28,24},{1,5},{5... | collective-permute-start | bytes 970760 | tf_op jit(solution)/shard_map/ppermute | solution.py:1358
  229.7 1.2 copy-start.3
  230.9 1.9 copy-start.21
  230.9 10.6 %copy-start.10 = (f32[16,768]{1,0:T(8,128)S(1)}, f32[16,768]{1,0:T(8,128)}, u32[]{:S(2)}) copy-start(f32[16,768]{1,0:T(8,128)} %get-tuple-element.66.class_ref) | copy-start | bytes 147460
  230.9 10.6 %copy-start.11 = (f32[8,3072]{1,0:T(8,128)S(1)}, f32[8,3072]{1,0:T(8,128)}, u32[]{:S(2)}) copy-start(f32[8,3072]{1,0:T(8,128)} %get-tuple-element.67.hidden_ref) | copy-start | bytes 294916
  230.9 10.6 %copy-start.12 = (f32[4,8,768]{2,1,0:T(8,128)S(1)}, f32[4,8,768]{2,1,0:T(8,128)}, u32[]{:S(2)}) copy-start(f32[4,8,768]{2,1,0:T(8,128)} %get-tuple-element.71.middle_ref) | copy-start | bytes 294916
  230.9 10.6 %copy-start.15 = (f32[8,2048]{1,0:T(8,128)S(1)}, f32[8,2048]{1,0:T(8,128)}, u32[]{:S(2)}) copy-start(f32[8,2048]{1,0:T(8,128)} %get-tuple-element.68.one_ref) | copy-start | bytes 196612
  230.9 10.6 %copy-start.16 = (f32[8,2048]{1,0:T(8,128)S(1)}, f32[8,2048]{1,0:T(8,128)}, u32[]{:S(2)}) copy-start(f32[8,2048]{1,0:T(8,128)} %get-tuple-element.69.two_ref) | copy-start | bytes 196612
  230.9 10.6 %copy-start.17 = (f32[8,256]{1,0:T(8,128)S(1)}, f32[8,256]{1,0:T(8,128)}, u32[]{:S(2)}) copy-start(f32[8,256]{1,0:T(8,128)} %get-tuple-element.70.bottle_ref) | copy-start | bytes 24580
  233.5 7.9 %all-to-all-start.1 = ((f32[4,32,256]{2,1,0:T(8,128)}), f32[4,32,256]{2,1,0:T(8,128)S(1)}, u32[]{:S(2)}, u32[]{:S(2)}) async-start(f32[4,32,256]{2,1,0:T(8,128)} %get-tuple-element.65), calls=%async_computation.1 | async-start | bytes 262144 | tf_op jit(solution)/shard_map/all_to_all | solution.py:1422
  236.9 104.8 %all-gather.11.cloned.1.call-start = ((), (), s32[]{:S(2)}) async-start(), calls=%async_computation.5 | async-start | bytes 2646016 | tf_op jit(solution)/shard_map/all_gather | solution.py:1408
  241.5 14.6 %copy-start.1 = (f32[1,4,2,32,2048]{4,3,2,1,0:T(8,128)S(1)}, f32[1,4,2,32,2048]{4,3,2,1,0:T(8,128)}, u32[]{:S(2)}) copy-start(f32[1,4,2,32,2048]{4,3,2,1,0:T(8,128)} %copy-done) | copy-start | bytes 6291460
  241.6 14.6 %copy-start.4 = (bf16[256,2048]{1,0:T(8,128)(2,1)S(1)}, bf16[256,2048]{1,0:T(8,128)(2,1)}, u32[]{:S(2)}) copy-start(bf16[256,2048]{1,0:T(8,128)(2,1)} %multiply_convert_fusion.columns_ref) | copy-start | bytes 3145732
  254.6 4.1 %copy-start.13 = (f32[8,768]{1,0:T(8,128)}, f32[8,768]{1,0:T(8,128)S(1)}, u32[]{:S(2)}) copy-start(f32[8,768]{1,0:T(8,128)S(1)} %get-tuple-element.74.stream_ref) | copy-start | bytes 73732
  254.6 4.1 %copy-start.14 = (f32[8,768]{1,0:T(8,128)}, f32[8,768]{1,0:T(8,128)S(1)}, u32[]{:S(2)}) copy-start(f32[8,768]{1,0:T(8,128)S(1)} %get-tuple-element.75.ends_ref) | copy-start | bytes 73732
  254.6 5.6 %copy-start.7 = (bf16[8,9728]{1,0:T(8,128)(2,1)}, bf16[8,9728]{1,0:T(8,128)(2,1)S(1)}, u32[]{:S(2)}) copy-start(bf16[8,9728]{1,0:T(8,128)(2,1)S(1)} %get-tuple-element.72.behind_ref) | copy-start | bytes 466948
  254.6 5.6 %collective-permute-start.8 = (bf16[8,9728]{1,0:T(8,128)(2,1)S(1)}, bf16[8,9728]{1,0:T(8,128)(2,1)S(1)}, u32[]{:S(2)}, u32[]{:S(2)}) collective-permute-start(bf16[8,9728]{1,0:T(8,128)(2,1)S(1)} %get-tuple-element.72.behind_ref), channel_id=1, source_target_pairs={{0,4},{4,0},{8,12},{12,8},{16,20},{20,16},{24,28},{28,24},{1,5},{5... | collective-permute-start | bytes 466952 | tf_op jit(solution)/shard_map/ppermute | solution.py:1358
  258.7 0.7 copy-start.5
  259.5 0.6 copy-start.9
  278.2 2.7 collective-permute-start.9
  282.7 13.4 %collective-permute-start.10 = (bf16[320,768]{1,0:T(8,128)(2,1)S(1)}, bf16[320,768]{1,0:T(8,128)(2,1)S(1)}, u32[]{:S(2)}, u32[]{:S(2)}) collective-permute-start(bf16[320,768]{1,0:T(8,128)(2,1)S(1)} %pad_maximum_fusion.1), channel_id=1, source_target_pairs={{0,2},{1,3},{2,0},{3,1},{4,6},{5,7},{6,4},{7,5},{8,10},{9,11},{10,... | collective-permute-start | bytes 1474568 | tf_op jit(solution)/shard_map/ppermute | solution.py:1455
  296.4 17.3 %collective-permute-start.11 = (bf16[320,768]{1,0:T(8,128)(2,1)S(1)}, bf16[320,768]{1,0:T(8,128)(2,1)S(1)}, u32[]{:S(2)}, u32[]{:S(2)}) collective-permute-start(bf16[320,768]{1,0:T(8,128)(2,1)S(1)} %convert_element_type.83), channel_id=1, source_target_pairs={{8,0},{12,4},{24,16},{28,20},{9,1},{13,5},{25,17},{29,21},{10,2},{... | collective-permute-start | bytes 1474568 | tf_op jit(solution)/shard_map/ppermute | solution.py:1469
  313.8 19.2 %collective-permute-start.12 = (bf16[320,768]{1,0:T(8,128)(2,1)S(1)}, bf16[320,768]{1,0:T(8,128)(2,1)S(1)}, u32[]{:S(2)}, u32[]{:S(2)}) collective-permute-start(bf16[320,768]{1,0:T(8,128)(2,1)S(1)} %fusion.12), channel_id=1, source_target_pairs={{16,0},{20,4},{17,1},{21,5},{18,2},{22,6},{19,3},{23,7}} | collective-permute-start | bytes 1474568 | tf_op jit(solution)/shard_map/ppermute | solution.py:1469
  334.2 3.7 collective-permute-start.15
  335.8 10.2 %collective-permute-start.13 = (bf16[288,768]{1,0:T(8,128)(2,1)S(1)}, bf16[288,768]{1,0:T(8,128)(2,1)S(1)}, u32[]{:S(2)}, u32[]{:S(2)}) collective-permute-start(bf16[288,768]{1,0:T(8,128)(2,1)S(1)} %slice.98), channel_id=1, source_target_pairs={{0,2},{1,3},{2,0},{3,1},{4,6},{5,7},{6,4},{7,5},{8,10},{9,11},{10,... | collective-permute-start | bytes 1327112 | tf_op jit(solution)/shard_map/ppermute | solution.py:1455
  337.1 4.1 %collective-permute-start.14 = (bf16[32,768]{1,0:T(8,128)(2,1)S(1)}, bf16[32,768]{1,0:T(8,128)(2,1)S(1)}, u32[]{:S(2)}, u32[]{:S(2)}) collective-permute-start(bf16[32,768]{1,0:T(8,128)(2,1)S(1)} %slice.100), channel_id=1, source_target_pairs={{0,4},{4,0},{8,12},{12,8},{16,20},{20,16},{24,28},{28,24},{1,5},{5... | collective-permute-start | bytes 147464 | tf_op jit(solution)/shard_map/ppermute | solution.py:1358
  346.0 13.1 %all-to-all-start.2 = ((f32[32,1,128]{2,1,0:T(1,128)}), f32[32,1,128]{2,1,0:T(1,128)S(1)}, u32[]{:S(2)}, u32[]{:S(2)}) async-start(f32[32,1,128]{2,1,0:T(1,128)} %get-tuple-element.91), calls=%async_computation.2 | async-start | bytes 32768 | tf_op jit(solution)/shard_map/all_to_all | solution.py:1506
  352.2 1.5 copy-start.2
  353.7 6.9 %copy-start.6 = (f32[32,2048]{1,0:T(8,128)S(1)}, f32[32,2048]{1,0:T(8,128)}, u32[]{:S(2)}) copy-start(f32[32,2048]{1,0:T(8,128)} %copy-done.5) | copy-start | bytes 786436
  360.6 2.5 copy-start.18
Sparse Core Ops, SparseCore 0:
  38.7 154.6 all-gather.6
  233.7 55.7 all-gather.8
  296.4 45.1 all-gather.10

commit v10 on v9

--- a/solution.py
+++ b/solution.py
@@ -558,7 +558,7 @@
         mixed_ref[v] = product(probs.astype(BF16), normed).astype(BF16)
         return carry
 
-    lax.fori_loop(0, views, view, 0, unroll=2)
+    lax.fori_loop(0, views, view, 0, unroll=4)
     mixed = mixed_ref[...].reshape(views * HEADROWS, D)
     valued = product(mixed, qkv_ref[:, 2 * D :]).reshape(views, HEADROWS, D)
     attended = jnp.sum(jnp.where(mask[None], valued, 0.0), 1).astype(BF16)
@@ -1051,7 +1051,7 @@
         common_hbm.at[pl.ds(0, TILE), pl.ds(CLASS, D)], class_ref, class_sem
     )
     class_copy.start()
-    line_ref[...] = jnp.zeros(line_ref.shape, F32)
+    line_ref[pl.ds(0, plan.used), :] = jnp.zeros((plan.used, LANES), F32)
 
     def fetch(source, target, column, size):
         which = 0 if target is common_ref else 1
@@ -1154,20 +1154,29 @@
             lax.fori_loop(0, chunks, move, 0)
 
     shift = tab_ref[0]
-    shape = (STEPS, LANES)
-    place = lax.broadcasted_iota(jnp.int32, shape, 0) * LANES
-    place = place + lax.broadcasted_iota(jnp.int32, shape, 1) - shift
-
-    def clear(step, total):
-        start = pl.multiple_of(step * STEPS, 8)
-        entry = place + start * LANES
-        lines = pl.ds(pl.multiple_of(FRONT + start, 8), STEPS)
-        kept = jnp.where((entry >= 0) & (entry < plan.size), line_ref[lines, :], 0.0)
-        line_ref[lines, :] = kept
-        return total + kept * kept
+    place = lax.broadcasted_iota(jnp.int32, (8, LANES), 0) * LANES
+    place = place + lax.broadcasted_iota(jnp.int32, (8, LANES), 1)
+    head = line_ref[FRONT : FRONT + 8, :]
+    line_ref[FRONT : FRONT + 8, :] = jnp.where(place >= shift, head, 0.0)
+    end = shift + plan.size
+    block = pl.multiple_of(end // (8 * LANES) * 8, 8)
+    lines = pl.ds(pl.multiple_of(FRONT + block, 8), 8)
+    line_ref[lines, :] = jnp.where(place + block * LANES < end, line_ref[lines, :], 0.0)
+
+    def clear(step, carry):
+        start = pl.multiple_of(FRONT + block + 8 * step, 8)
+        line_ref[pl.ds(start, 8), :] = jnp.zeros((8, LANES), F32)
+        return carry
+
+    lax.fori_loop(1, (plan.lines + 8 - block) // 8, clear, 0)
+
+    def square(step, total):
+        start = pl.multiple_of(FRONT + step * STEPS, 8)
+        part = line_ref[pl.ds(start, STEPS), :]
+        return total + part * part
 
     total = lax.fori_loop(
-        0, plan.steps, clear, jnp.zeros(shape, F32), unroll=steps_at_once(plan.steps)
+        0, plan.steps, square, jnp.zeros((STEPS, LANES), F32), unroll=steps_at_once(plan.steps)
     )
     line_copy = pltpu.make_async_copy(line_ref.at[pl.ds(0, plan.used)], line_out, sem.at[0])
     line_copy.start()
@@ -1366,14 +1375,16 @@
 
     pairs = [list(range(parity, reps, 2)) for parity in (0, 1)]
     lines = reps // 2
-    tables = jnp.stack([protos, teacher_protos]).astype(BF16)
+    table = jnp.asarray(plan.lay_table)[device]
+    given = lay_out(plan, table, jnp.where(low, teacher, params))
+    later, given = lax.optimization_barrier(((params, teacher, protos, teacher_protos), given))
+    given = trade(given)
+    tables = jnp.stack(later[2:]).astype(BF16)
     around = [tables]
     for step in range(2, reps, 2):
         around.append(lax.ppermute(tables, "rep", [(r, (r + step) % reps) for r in range(reps)]))
 
-    table = jnp.asarray(plan.lay_table)[device]
-    given = trade(lay_out(plan, table, jnp.where(low, teacher, params)))
-    kept = lay_out(plan, table, jnp.where(low, params, teacher))
+    kept = lay_out(plan, table, jnp.where(low, later[0], later[1]))
     given, around = lax.optimization_barrier((given, around))
     shards = jnp.stack([jnp.where(low, kept, given), jnp.where(low, given, kept)])
     gathered = lax.all_gather(shards, BOTH, axis=0, axis_index_groups=halves)

time: 378 us -> 376 us (level)
  transfers between devices with their start and end apart: 22 -> 22, of which waited for: 13 -> 14; matrix products, arithmetic and copies ran while one was open for 8% -> 8% of each run, Pallas kernels for 11% -> 11%
where the time goes in v10:
time: 376 us; the launch traced here: 375 us
  waiting for transfers between devices  204 us (54%)
  Pallas kernels  68.1 us (18%)
  starting transfers between devices  36.9 us (10%)
  other arithmetic  27.8 us (7%)
  local copies, waits for them, and re-layouts  22 us (6%)
  between operations  16.4 us (4%)
    all_gather x1, waiting for transfers between devices, per_device(): gathered = lax.all_gather(shards, BOTH, axis=0, axis_index_groups=halves)  81.5 us
    ppermute x7, waiting for transfers between devices, trade(): return lax.ppermute(values, 'rep', swap)  51 us
    ppermute x2, waiting for transfers between devices, per_device(): lax.ppermute(partial.astype(BF16), 'rep', hops).astype(F32)  30.6 us
    pallas_call x1, Pallas kernels, forward(): pl.pallas_call(functools.partial(forward_kernel, plan), out_shape=[jax.Sh...  23 us
    pallas_call x1, Pallas kernels, tokens_back(): pl.pallas_call(tokens_back_kernel, grid=(views,), out_shape=[jax.ShapeDty...  17.3 us
    ppermute x3, waiting for transfers between devices, across(): return lax.ppermute(values, 'grp', [(g, g ^ bit) for g in range(groups)])  15 us
    pallas_call x1, Pallas kernels, rows_back(): pl.pallas_call(functools.partial(rows_back_kernel, plan), out_shape=[jax....  13 us
    ppermute x3, waiting for transfers between devices, per_device(): lax.ppermute(tables, 'rep', [(r, (r + step) % reps) for r in range(reps)])  11.7 us
  transfers between devices with their start and end apart: 22, of which 14 were waited for; matrix products, arithmetic and copies ran while one was open for 8% of the time, Pallas kernels for 11%

profile of v10, /device:TPU:0, one launch (start us, length us, event | category | flops | bytes accessed | tf_op | source)
XLA Modules:
  0.0 375.5 jit_solution(10580111336204633054)
XLA Ops:
  7.2 1.7 broadcast_select_fusion.3
  9.8 2.2 shard_map.221
  12.1 3.0 collective-permute-start.1
  15.1 2.9 collective-permute-start.2
  19.1 1.7 collective-permute-start
  21.2 2.2 shard_map.222
  23.4 1.3 collective-permute-done.1
  24.7 10.4 %collective-permute-done.2 = bf16[2,32,2048]{2,1,0:T(8,128)(2,1)S(1)} collective-permute-done((bf16[2,32,2048]{2,1,0:T(8,128)(2,1)S(1)}, bf16[2,32,2048]{2,1,0:T(8,128)(2,1)S(1)}, u32[]{:S(2)}, u32[]{:S(2)}) %collective-permute-start.2) | collective-permute-done | bytes 262176 | tf_op jit(solution)/shard_map/ppermute | solution.py:1385
  35.1 5.7 %collective-permute-done = bf16[3648,128]{1,0:T(8,128)(2,1)S(1)} collective-permute-done((bf16[3648,128]{1,0:T(8,128)(2,1)S(1)}, bf16[3648,128]{1,0:T(8,128)(2,1)S(1)}, u32[]{:S(2)}, u32[]{:S(2)}) %collective-permute-start) | collective-permute-done | bytes 933920 | tf_op jit(solution)/shard_map/ppermute | solution.py:1367
  40.9 1.4 pad_maximum_fusion
  43.6 1.7 collective-permute-start.6
  45.6 3.6 copy.47
  49.3 1.6 collective-permute-start.5
  50.9 42.0 %collective-permute-done.5 = f32[4]{0:T(128)S(1)} collective-permute-done((f32[4]{0:T(128)S(1)}, f32[4]{0:T(128)S(1)}, u32[]{:S(2)}, u32[]{:S(2)}) %collective-permute-start.5) | collective-permute-done | bytes 48 | tf_op jit(solution)/shard_map/ppermute | solution.py:1367
  97.6 3.6 copy.48
  101.2 2.2 broadcast_select_fusion.1
  103.3 3.1 fusion.25
  106.4 4.5 %copy.53.pixels_ref = bf16[8,208,768]{2,1,0:T(8,128)(2,1)} copy(bf16[8,208,768]{1,2,0:T(8,128)(2,1)} %get-tuple-element.116) | data formatting | bytes 5111808 | tf_op jit(solution)/shard_map/jit(_pad)/pad | solution.py:1394
  110.9 81.5 %all-gather.7.cloned.1.call-done = bf16[32,3648,128]{2,1,0:T(8,128)(2,1)} async-done(((bf16[2,3648,128]{2,1,0:T(8,128)(2,1)}), bf16[32,3648,128]{2,1,0:T(8,128)(2,1)}) %all-gather.7.cloned.1.call-update) | async-done | bytes 29884432 | tf_op jit(solution)/shard_map/all_gather | solution.py:1390
  192.4 23.0 %shard_map.223 = (f32[8,208,768]{2,1,0:T(8,128)}, f32[8,208,128]{2,1,0:T(8,128)}, f32[8,16,208]{2,1,0:T(8,128)}, bf16[8,16,768]{2,1,0:T(8,128)(2,1)}, bf16[16,76...) custom-call(bf16[16,2,228,16,128]{4,3,2,1,0:T(8,128)(2,1)} %bitcast., ...), custom_call_target="tpu_custom_call" | custom-call | flops 60000002048 | bytes 40000000 | tf_op jit(solution)/shard_map/pallas_call | solution.py:641
  215.4 4.6 %all-to-all-start = ((bf16[32,8,256]{2,1,0:T(8,128)(2,1)}), bf16[32,8,256]{2,1,0:T(8,128)(2,1)S(1)}, u32[]{:S(2)}, u32[]{:S(2)}) async-start(bf16[32,8,256]{2,1,0:T(8,128)(2,1)} %get-tuple-element.70), calls=%async_computation | async-start | bytes 262144 | tf_op jit(solution)/shard_map/all_to_all | solution.py:1416
  220.0 1.8 collective-permute-start.7
  221.9 6.4 %all-to-all-done = bf16[32,8,256]{2,1,0:T(8,128)(2,1)S(1)} async-done(((bf16[32,8,256]{2,1,0:T(8,128)(2,1)}), bf16[32,8,256]{2,1,0:T(8,128)(2,1)S(1)}, u32[]{:S(2)}, u32[]{:S(2)}) %all-to-all-start) | async-done | bytes 131104 | tf_op jit(solution)/shard_map/all_to_all | solution.py:1416
  228.4 1.2 copy-done.3
  229.6 1.8 shard_map.224
  232.2 3.3 all-to-all-start.1
  235.6 4.5 %all-to-all-done.1.note_ref = f32[4,32,256]{2,1,0:T(8,128)S(1)} async-done(((f32[4,32,256]{2,1,0:T(8,128)}), f32[4,32,256]{2,1,0:T(8,128)S(1)}, u32[]{:S(2)}, u32[]{:S(2)}) %all-to-all-start.1) | async-done | bytes 131104 | tf_op jit(solution)/shard_map/all_to_all | solution.py:1433
  240.2 13.0 %shard_map.225 = (bf16[8,9728]{1,0:T(8,128)(2,1)S(1)}, f32[8,768]{1,0:T(8,128)S(1)}, f32[8,768]{1,0:T(8,128)S(1)}) custom-call(s32[1]{0:T(128)} %bitcast.2.low_ref, bf16[16,2,228,16,128]{4,3,2,1,0:T(8,128)(2,1)} %bitcast.72, f32[4,32,256]{2,1,0:T(8,128)S(1)} %all-to-all-done.1.note_ref, f32[16,768]{1,0:T(8,128)S(1)} %copy-done.10, f32[8,3072]{1,0:T(8,128)S(1)} %copy-done.11, ...), custom_call_target="tpu_custom_call" | custom-call | flops 30000001024 | bytes 30000000 | tf_op jit(solution)/shard_map/pallas_call | solution.py:870
  253.3 1.5 collective-permute-start.8
  254.8 2.6 shard_map.226
  259.5 17.3 %shard_map.227 = (f32[608,768]{1,0:T(8,128)}, bf16[608,768]{1,0:T(8,128)(2,1)}) custom-call(s32[1]{0:T(128)} %bitcast.25.odd_ref, bf16[8,9728]{1,0:T(8,128)(2,1)} %copy-done.7, f32[8,768]{1,0:T(8,128)} %copy-done.13, f32[8,768]{1,0:T(8,128)} %copy-done.14, f32[8,208,768]{2,1,0:T(8,128)} %get-tuple-element.86.unit_ref, ...), custom_call_target="tpu_custom_call" | custom-call | flops 15000000512 | bytes 15000000 | tf_op jit(solution)/shard_map/pallas_call | solution.py:1005
  276.9 2.7 collective-permute-done.9
  279.6 1.7 convert_add_fusion
  282.5 12.3 %collective-permute-done.10 = bf16[320,768]{1,0:T(8,128)(2,1)S(1)} collective-permute-done((bf16[320,768]{1,0:T(8,128)(2,1)S(1)}, bf16[320,768]{1,0:T(8,128)(2,1)S(1)}, u32[]{:S(2)}, u32[]{:S(2)}) %collective-permute-start.10) | collective-permute-done | bytes 491552 | tf_op jit(solution)/shard_map/ppermute | solution.py:1466
  295.0 1.3 collective-permute-start.11
  296.4 1.2 fusion.21.tab_ref
  298.3 14.0 %collective-permute-done.11 = bf16[320,768]{1,0:T(8,128)(2,1)S(1)} collective-permute-done((bf16[320,768]{1,0:T(8,128)(2,1)S(1)}, bf16[320,768]{1,0:T(8,128)(2,1)S(1)}, u32[]{:S(2)}, u32[]{:S(2)}) %collective-permute-start.11) | collective-permute-done | bytes 491552 | tf_op jit(solution)/shard_map/ppermute | solution.py:1480
  312.5 1.3 collective-permute-start.12
  315.1 16.6 %collective-permute-done.12 = bf16[320,768]{1,0:T(8,128)(2,1)S(1)} collective-permute-done((bf16[320,768]{1,0:T(8,128)(2,1)S(1)}, bf16[320,768]{1,0:T(8,128)(2,1)S(1)}, u32[]{:S(2)}, u32[]{:S(2)}) %collective-permute-start.12) | collective-permute-done | bytes 491552 | tf_op jit(solution)/shard_map/ppermute | solution.py:1480
  332.8 1.4 collective-permute-start.15
  336.6 3.1 collective-permute-done.14
  340.3 3.9 %shard_map.228 = (f32[3656,128]{1,0:T(8,128)}, f32[32,1,128]{2,1,0:T(1,128)}) custom-call(s32[15]{0:T(128)} %fusion.21.tab_ref, bf16[128,20224]{1,0:T(8,128)(2,1)} %all-gather.9.cloned.1.call-done.common_hbm, bf16[128,9728]{1,0:T(8,128)(2,1)} %all-gather.11.cloned.1.call-done.behind_hbm, f32[8,128]{1,0:T(8,128)} %copy-done.9, ...), custom_call_target="tpu_custom_call" | custom-call | flops 10000000000 | bytes 10000000 | tf_op jit(solution)/shard_map/pallas_call | solution.py:1204
  344.2 6.1 %all-to-all-start.2 = ((f32[32,1,128]{2,1,0:T(1,128)}), f32[32,1,128]{2,1,0:T(1,128)S(1)}, u32[]{:S(2)}, u32[]{:S(2)}) async-start(f32[32,1,128]{2,1,0:T(1,128)} %get-tuple-element.101), calls=%async_computation.2 | async-start | bytes 32768 | tf_op jit(solution)/shard_map/all_to_all | solution.py:1517
  350.6 1.3 copy-done.2
  351.9 2.1 shard_map.229
  354.1 3.3 all-to-all-done.2
  358.8 2.4 multiply_add_fusion.2
  361.2 6.6 %multiply_add_fusion = (f32[441096]{0:T(1024)}, f32[441096]{0:T(1024)}, f32[441096]{0:T(1024)}, f32[441096]{0:T(1024)}) fusion(f32[441096]{0:T(1024)S(1)} %copy-done.19, f32[441096]{0:T(1024)} %param.14, f32[]{:T(128)S(6)} %min_shard_map.3, f32[442368]{0:T(1024)S(1)} %bitcast.64, f32[441096]{0:T(1024)} %param.15, f32[441096]{0:T(1024)} %param.16), kind=kLoop, calls=%fused_computation.21 | loop fusion | flops 8380824 | bytes 15879460 | tf_op jit(solution)/shard_map/add | solution.py:1558
  (139 shorter events, 20.3 us)
Async XLA Ops:
  7.2 185.2 %all-gather.7.cloned.1.call-start = ((), (), s32[]{:S(2)}) async-start(), calls=%async_computation.3 | async-start | bytes 31752192 | tf_op jit(solution)/shard_map/all_gather | solution.py:1390
  8.9 3.1 copy-start.22
  9.0 3.0 copy-start.21
  9.8 11.0 %copy-start.18 = (f32[441096]{0:T(1024)S(1)}, f32[441096]{0:T(1024)}, u32[]{:S(2)}) copy-start(f32[441096]{0:T(1024)} %param.17) | copy-start | bytes 5293156
  9.8 11.0 %copy-start.20 = (f32[441096]{0:T(1024)S(1)}, f32[441096]{0:T(1024)}, u32[]{:S(2)}) copy-start(f32[441096]{0:T(1024)} %param.14) | copy-start | bytes 5293156
  12.1 12.6 %collective-permute-start.1 = (bf16[2,32,2048]{2,1,0:T(8,128)(2,1)S(1)}, bf16[2,32,2048]{2,1,0:T(8,128)(2,1)S(1)}, u32[]{:S(2)}, u32[]{:S(2)}) collective-permute-start(bf16[2,32,2048]{2,1,0:T(8,128)(2,1)S(1)} %pad_maximum_fusion.2), channel_id=1, source_target_pairs={{0,8},{4,12},{8,16},{12,20},{16,24},{20,28},{24,0},{28,4},{1,9},{5... | collective-permute-start | bytes 786440 | tf_op jit(solution)/shard_map/ppermute | solution.py:1385
  15.1 20.0 %collective-permute-start.2 = (bf16[2,32,2048]{2,1,0:T(8,128)(2,1)S(1)}, bf16[2,32,2048]{2,1,0:T(8,128)(2,1)S(1)}, u32[]{:S(2)}, u32[]{:S(2)}) collective-permute-start(bf16[2,32,2048]{2,1,0:T(8,128)(2,1)S(1)} %pad_maximum_fusion.2), channel_id=1, source_target_pairs={{0,16},{4,20},{8,24},{12,28},{16,0},{20,4},{24,8},{28,12},{1,17},{... | collective-permute-start | bytes 786440 | tf_op jit(solution)/shard_map/ppermute | solution.py:1385
  18.0 17.1 %collective-permute-start.3 = (bf16[2,32,2048]{2,1,0:T(8,128)(2,1)S(1)}, bf16[2,32,2048]{2,1,0:T(8,128)(2,1)S(1)}, u32[]{:S(2)}, u32[]{:S(2)}) collective-permute-start(bf16[2,32,2048]{2,1,0:T(8,128)(2,1)S(1)} %pad_maximum_fusion.2), channel_id=1, source_target_pairs={{0,24},{4,28},{8,0},{12,4},{16,8},{20,12},{24,16},{28,20},{1,25},{... | collective-permute-start | bytes 786440 | tf_op jit(solution)/shard_map/ppermute | solution.py:1385
  19.1 21.7 %collective-permute-start = (bf16[3648,128]{1,0:T(8,128)(2,1)S(1)}, bf16[3648,128]{1,0:T(8,128)(2,1)S(1)}, u32[]{:S(2)}, u32[]{:S(2)}) collective-permute-start(bf16[3648,128]{1,0:T(8,128)(2,1)S(1)} %shard_map.221), channel_id=1, source_target_pairs={{0,4},{4,0},{8,12},{12,8},{16,20},{20,16},{24,28},{28,24},{1,5},{5... | collective-permute-start | bytes 2801672 | tf_op jit(solution)/shard_map/ppermute | solution.py:1367
  43.6 5.7 %copy-start.24 = (s32[4]{0:T(128)S(1)}, s32[4]{0:T(128)}, u32[]{:S(2)}) copy-start(s32[4]{0:T(128)} %param.24) | copy-start | bytes 52
  43.6 50.1 %collective-permute-start.6 = (bf16[4,2,32,2048]{3,2,1,0:T(8,128)(2,1)}, bf16[4,2,32,2048]{3,2,1,0:T(8,128)(2,1)S(1)}, u32[]{:S(2)}, u32[]{:S(2)}) collective-permute-start(bf16[4,2,32,2048]{3,2,1,0:T(8,128)(2,1)} %constant_dynamic-slice_fusion), channel_id=1, source_target_pairs={{0,4},{4,0},{8,12},{12,8},{16,20},{20,16},{24,28},{28,24},{1,5},{5... | collective-permute-start | bytes 3145736 | tf_op jit(solution)/shard_map/ppermute | solution.py:1367
  45.3 52.3 %collective-permute-start.4 = (bf16[4,196,768]{2,0,1:T(4,128)(2,1)}, bf16[4,196,768]{2,0,1:T(4,128)(2,1)}, u32[]{:S(2)}, u32[]{:S(2)}) collective-permute-start(bf16[4,196,768]{2,0,1:T(4,128)(2,1)} %param.23), channel_id=1, source_target_pairs={{0,4},{4,0},{8,12},{12,8},{16,20},{20,16},{24,28},{28,24},{1,5},{5... | collective-permute-start | bytes 3612680 | tf_op jit(solution)/shard_map/ppermute | solution.py:1367
  49.3 43.7 %collective-permute-start.5 = (f32[4]{0:T(128)S(1)}, f32[4]{0:T(128)S(1)}, u32[]{:S(2)}, u32[]{:S(2)}) collective-permute-start(f32[4]{0:T(128)S(1)} %convert_element_type.74), channel_id=1, source_target_pairs={{0,4},{4,0},{8,12},{12,8},{16,20},{20,16},{24,28},{28,24},{1,5},{5... | collective-permute-start | bytes 56 | tf_op jit(solution)/shard_map/ppermute | solution.py:1367
  95.1 1.4 copy-start
  192.4 36.0 %copy-start.8 = (f32[2048]{0:T(1024)S(1)}, f32[2048]{0:T(1024)}, u32[]{:S(2)}) copy-start(f32[2048]{0:T(1024)} %param.22) | copy-start | bytes 24580
  215.4 12.9 %all-to-all-start = ((bf16[32,8,256]{2,1,0:T(8,128)(2,1)}), bf16[32,8,256]{2,1,0:T(8,128)(2,1)S(1)}, u32[]{:S(2)}, u32[]{:S(2)}) async-start(bf16[32,8,256]{2,1,0:T(8,128)(2,1)} %get-tuple-element.70), calls=%async_computation | async-start | bytes 262144 | tf_op jit(solution)/shard_map/all_to_all | solution.py:1416
  220.0 75.0 %all-gather.9.cloned.1.call-start = ((), (), s32[]{:S(2)}) async-start(), calls=%async_computation.4 | async-start | bytes 5500928 | tf_op jit(solution)/shard_map/all_gather | solution.py:1419
  220.0 11.4 %collective-permute-start.7 = (bf16[8,20224]{1,0:T(8,128)(2,1)}, bf16[8,20224]{1,0:T(8,128)(2,1)S(1)}, u32[]{:S(2)}, u32[]{:S(2)}) collective-permute-start(bf16[8,20224]{1,0:T(8,128)(2,1)} %get-tuple-element.74), channel_id=1, source_target_pairs={{0,4},{4,0},{8,12},{12,8},{16,20},{20,16},{24,28},{28,24},{1,5},{5... | collective-permute-start | bytes 970760 | tf_op jit(solution)/shard_map/ppermute | solution.py:1367
  228.3 1.2 copy-start.3
  229.6 1.9 copy-start.23
  229.6 10.6 %copy-start.10 = (f32[16,768]{1,0:T(8,128)S(1)}, f32[16,768]{1,0:T(8,128)}, u32[]{:S(2)}) copy-start(f32[16,768]{1,0:T(8,128)} %get-tuple-element.76.class_ref) | copy-start | bytes 147460
  229.6 10.6 %copy-start.11 = (f32[8,3072]{1,0:T(8,128)S(1)}, f32[8,3072]{1,0:T(8,128)}, u32[]{:S(2)}) copy-start(f32[8,3072]{1,0:T(8,128)} %get-tuple-element.77.hidden_ref) | copy-start | bytes 294916
  229.6 10.6 %copy-start.12 = (f32[4,8,768]{2,1,0:T(8,128)S(1)}, f32[4,8,768]{2,1,0:T(8,128)}, u32[]{:S(2)}) copy-start(f32[4,8,768]{2,1,0:T(8,128)} %get-tuple-element.81.middle_ref) | copy-start | bytes 294916
  229.6 10.6 %copy-start.15 = (f32[8,2048]{1,0:T(8,128)S(1)}, f32[8,2048]{1,0:T(8,128)}, u32[]{:S(2)}) copy-start(f32[8,2048]{1,0:T(8,128)} %get-tuple-element.78.one_ref) | copy-start | bytes 196612
  229.6 10.6 %copy-start.16 = (f32[8,2048]{1,0:T(8,128)S(1)}, f32[8,2048]{1,0:T(8,128)}, u32[]{:S(2)}) copy-start(f32[8,2048]{1,0:T(8,128)} %get-tuple-element.79.two_ref) | copy-start | bytes 196612
  229.6 10.6 %copy-start.17 = (f32[8,256]{1,0:T(8,128)S(1)}, f32[8,256]{1,0:T(8,128)}, u32[]{:S(2)}) copy-start(f32[8,256]{1,0:T(8,128)} %get-tuple-element.80.bottle_ref) | copy-start | bytes 24580
  232.2 7.9 %all-to-all-start.1 = ((f32[4,32,256]{2,1,0:T(8,128)}), f32[4,32,256]{2,1,0:T(8,128)S(1)}, u32[]{:S(2)}, u32[]{:S(2)}) async-start(f32[4,32,256]{2,1,0:T(8,128)} %get-tuple-element.75), calls=%async_computation.1 | async-start | bytes 262144 | tf_op jit(solution)/shard_map/all_to_all | solution.py:1433
  235.6 104.8 %all-gather.11.cloned.1.call-start = ((), (), s32[]{:S(2)}) async-start(), calls=%async_computation.5 | async-start | bytes 2646016 | tf_op jit(solution)/shard_map/all_gather | solution.py:1419
  240.2 14.6 %copy-start.1 = (f32[1,4,2,32,2048]{4,3,2,1,0:T(8,128)S(1)}, f32[1,4,2,32,2048]{4,3,2,1,0:T(8,128)}, u32[]{:S(2)}) copy-start(f32[1,4,2,32,2048]{4,3,2,1,0:T(8,128)} %copy-done) | copy-start | bytes 6291460
  240.2 14.6 %copy-start.4 = (bf16[256,2048]{1,0:T(8,128)(2,1)S(1)}, bf16[256,2048]{1,0:T(8,128)(2,1)}, u32[]{:S(2)}) copy-start(bf16[256,2048]{1,0:T(8,128)(2,1)} %multiply_convert_fusion.columns_ref) | copy-start | bytes 3145732
  253.3 4.1 %copy-start.13 = (f32[8,768]{1,0:T(8,128)}, f32[8,768]{1,0:T(8,128)S(1)}, u32[]{:S(2)}) copy-start(f32[8,768]{1,0:T(8,128)S(1)} %get-tuple-element.84.stream_ref) | copy-start | bytes 73732
  253.3 4.1 %copy-start.14 = (f32[8,768]{1,0:T(8,128)}, f32[8,768]{1,0:T(8,128)S(1)}, u32[]{:S(2)}) copy-start(f32[8,768]{1,0:T(8,128)S(1)} %get-tuple-element.85.ends_ref) | copy-start | bytes 73732
  253.3 5.6 %copy-start.7 = (bf16[8,9728]{1,0:T(8,128)(2,1)}, bf16[8,9728]{1,0:T(8,128)(2,1)S(1)}, u32[]{:S(2)}) copy-start(bf16[8,9728]{1,0:T(8,128)(2,1)S(1)} %get-tuple-element.82.behind_ref) | copy-start | bytes 466948
  253.3 5.6 %collective-permute-start.8 = (bf16[8,9728]{1,0:T(8,128)(2,1)S(1)}, bf16[8,9728]{1,0:T(8,128)(2,1)S(1)}, u32[]{:S(2)}, u32[]{:S(2)}) collective-permute-start(bf16[8,9728]{1,0:T(8,128)(2,1)S(1)} %get-tuple-element.82.behind_ref), channel_id=1, source_target_pairs={{0,4},{4,0},{8,12},{12,8},{16,20},{20,16},{24,28},{28,24},{1,5},{5... | collective-permute-start | bytes 466952 | tf_op jit(solution)/shard_map/ppermute | solution.py:1367
  257.4 0.7 copy-start.5
  258.1 0.6 copy-start.9
  276.8 2.7 collective-permute-start.9
  281.4 13.5 %collective-permute-start.10 = (bf16[320,768]{1,0:T(8,128)(2,1)S(1)}, bf16[320,768]{1,0:T(8,128)(2,1)S(1)}, u32[]{:S(2)}, u32[]{:S(2)}) collective-permute-start(bf16[320,768]{1,0:T(8,128)(2,1)S(1)} %pad_maximum_fusion.1), channel_id=1, source_target_pairs={{0,2},{1,3},{2,0},{3,1},{4,6},{5,7},{6,4},{7,5},{8,10},{9,11},{10,... | collective-permute-start | bytes 1474568 | tf_op jit(solution)/shard_map/ppermute | solution.py:1466
  295.0 17.3 %collective-permute-start.11 = (bf16[320,768]{1,0:T(8,128)(2,1)S(1)}, bf16[320,768]{1,0:T(8,128)(2,1)S(1)}, u32[]{:S(2)}, u32[]{:S(2)}) collective-permute-start(bf16[320,768]{1,0:T(8,128)(2,1)S(1)} %convert_element_type.83), channel_id=1, source_target_pairs={{8,0},{12,4},{24,16},{28,20},{9,1},{13,5},{25,17},{29,21},{10,2},{... | collective-permute-start | bytes 1474568 | tf_op jit(solution)/shard_map/ppermute | solution.py:1480
  312.5 19.2 %collective-permute-start.12 = (bf16[320,768]{1,0:T(8,128)(2,1)S(1)}, bf16[320,768]{1,0:T(8,128)(2,1)S(1)}, u32[]{:S(2)}, u32[]{:S(2)}) collective-permute-start(bf16[320,768]{1,0:T(8,128)(2,1)S(1)} %fusion.12), channel_id=1, source_target_pairs={{16,0},{20,4},{17,1},{21,5},{18,2},{22,6},{19,3},{23,7}} | collective-permute-start | bytes 1474568 | tf_op jit(solution)/shard_map/ppermute | solution.py:1480
  332.8 3.7 collective-permute-start.15
  334.5 9.8 %collective-permute-start.13 = (bf16[288,768]{1,0:T(8,128)(2,1)S(1)}, bf16[288,768]{1,0:T(8,128)(2,1)S(1)}, u32[]{:S(2)}, u32[]{:S(2)}) collective-permute-start(bf16[288,768]{1,0:T(8,128)(2,1)S(1)} %slice.98), channel_id=1, source_target_pairs={{0,2},{1,3},{2,0},{3,1},{4,6},{5,7},{6,4},{7,5},{8,10},{9,11},{10,... | collective-permute-start | bytes 1327112 | tf_op jit(solution)/shard_map/ppermute | solution.py:1466
  335.7 4.1 %collective-permute-start.14 = (bf16[32,768]{1,0:T(8,128)(2,1)S(1)}, bf16[32,768]{1,0:T(8,128)(2,1)S(1)}, u32[]{:S(2)}, u32[]{:S(2)}) collective-permute-start(bf16[32,768]{1,0:T(8,128)(2,1)S(1)} %slice.100), channel_id=1, source_target_pairs={{0,4},{4,0},{8,12},{12,8},{16,20},{20,16},{24,28},{28,24},{1,5},{5... | collective-permute-start | bytes 147464 | tf_op jit(solution)/shard_map/ppermute | solution.py:1367
  344.2 13.2 %all-to-all-start.2 = ((f32[32,1,128]{2,1,0:T(1,128)}), f32[32,1,128]{2,1,0:T(1,128)S(1)}, u32[]{:S(2)}, u32[]{:S(2)}) async-start(f32[32,1,128]{2,1,0:T(1,128)} %get-tuple-element.101), calls=%async_computation.2 | async-start | bytes 32768 | tf_op jit(solution)/shard_map/all_to_all | solution.py:1517
  350.4 1.5 copy-start.2
  351.9 6.9 %copy-start.6 = (f32[32,2048]{1,0:T(8,128)S(1)}, f32[32,2048]{1,0:T(8,128)}, u32[]{:S(2)}) copy-start(f32[32,2048]{1,0:T(8,128)} %copy-done.5) | copy-start | bytes 786436
  358.8 2.5 copy-start.19
Sparse Core Ops, SparseCore 0:
  42.4 149.8 all-gather.6
  232.3 55.7 all-gather.8
  295.1 45.1 all-gather.10

commit v11 on v10

--- a/solution.py
+++ b/solution.py
@@ -759,9 +759,12 @@
     targets = jnp.exp((logits - center_ref[...]) / TEACHER_TEMP) / teacher
     scaled = product(rows_ref[0], columns_ref[...]) / STUDENT_TEMP
     grad = (jnp.exp(scaled) / student - targets) / STUDENT_TEMP
-    work_ref[...] = jnp.dot(
-        rows_ref[0].astype(F32).T, grad, precision=PRECISE, preferred_element_type=F32
-    )
+    parts, rest = [], grad
+    for _ in range(3):
+        parts.append(rest.astype(BF16))
+        rest = rest - parts[-1].astype(F32)
+    turned = rows_ref[0].astype(F32).T.astype(BF16)
+    work_ref[...] = product(jnp.concatenate([turned] * 3, 1), jnp.concatenate(parts, 0))
     scale = scale_ref[...]
     inner = jnp.sum(work_ref[...] * table_ref[...], 0, keepdims=True)
     start = pl.multiple_of(start_ref[0], 8)

time: 376 us -> 376 us (level)
  no operation moved by 1% of the time
where the time goes in v11:
time: 376 us; the launch traced here: 375 us
  waiting for transfers between devices  205 us (55%)
  Pallas kernels  67.2 us (18%)
  starting transfers between devices  36.9 us (10%)
  other arithmetic  27.8 us (7%)
  local copies, waits for them, and re-layouts  22 us (6%)
  between operations  16.4 us (4%)
    all_gather x1, waiting for transfers between devices, per_device(): gathered = lax.all_gather(shards, BOTH, axis=0, axis_index_groups=halves)  81.5 us
    ppermute x7, waiting for transfers between devices, trade(): return lax.ppermute(values, 'rep', swap)  51.9 us
    ppermute x2, waiting for transfers between devices, per_device(): lax.ppermute(partial.astype(BF16), 'rep', hops).astype(F32)  30.7 us
    pallas_call x1, Pallas kernels, forward(): pl.pallas_call(functools.partial(forward_kernel, plan), out_shape=[jax.Sh...  23 us
    pallas_call x1, Pallas kernels, tokens_back(): pl.pallas_call(tokens_back_kernel, grid=(views,), out_shape=[jax.ShapeDty...  17.3 us
    ppermute x3, waiting for transfers between devices, across(): return lax.ppermute(values, 'grp', [(g, g ^ bit) for g in range(groups)])  15 us
    pallas_call x1, Pallas kernels, rows_back(): pl.pallas_call(functools.partial(rows_back_kernel, plan), out_shape=[jax....  13 us
    ppermute x3, waiting for transfers between devices, per_device(): lax.ppermute(tables, 'rep', [(r, (r + step) % reps) for r in range(reps)])  11.7 us
  transfers between devices with their start and end apart: 22, of which 14 were waited for; matrix products, arithmetic and copies ran while one was open for 8% of the time, Pallas kernels for 11%

profile of v11, /device:TPU:0, one launch (start us, length us, event | category | flops | bytes accessed | tf_op | source)
XLA Modules:
  0.0 375.5 jit_solution(15026773788407560301)
XLA Ops:
  7.2 1.7 broadcast_select_fusion.3
  9.8 2.2 shard_map.221
  12.1 3.0 collective-permute-start.1
  15.1 2.9 collective-permute-start.2
  19.1 1.7 collective-permute-start
  21.2 2.2 shard_map.222
  23.4 1.3 collective-permute-done.1
  24.7 10.4 %collective-permute-done.2 = bf16[2,32,2048]{2,1,0:T(8,128)(2,1)S(1)} collective-permute-done((bf16[2,32,2048]{2,1,0:T(8,128)(2,1)S(1)}, bf16[2,32,2048]{2,1,0:T(8,128)(2,1)S(1)}, u32[]{:S(2)}, u32[]{:S(2)}) %collective-permute-start.2) | collective-permute-done | bytes 262176 | tf_op jit(solution)/shard_map/ppermute | solution.py:1388
  35.1 5.7 %collective-permute-done = bf16[3648,128]{1,0:T(8,128)(2,1)S(1)} collective-permute-done((bf16[3648,128]{1,0:T(8,128)(2,1)S(1)}, bf16[3648,128]{1,0:T(8,128)(2,1)S(1)}, u32[]{:S(2)}, u32[]{:S(2)}) %collective-permute-start) | collective-permute-done | bytes 933920 | tf_op jit(solution)/shard_map/ppermute | solution.py:1370
  40.9 1.4 pad_maximum_fusion
  43.6 1.7 collective-permute-start.6
  45.6 3.6 copy.47
  49.3 1.6 collective-permute-start.5
  50.9 42.0 %collective-permute-done.5 = f32[4]{0:T(128)S(1)} collective-permute-done((f32[4]{0:T(128)S(1)}, f32[4]{0:T(128)S(1)}, u32[]{:S(2)}, u32[]{:S(2)}) %collective-permute-start.5) | collective-permute-done | bytes 48 | tf_op jit(solution)/shard_map/ppermute | solution.py:1370
  97.6 3.6 copy.48
  101.2 2.2 broadcast_select_fusion.1
  103.3 3.1 fusion.25
  106.4 4.5 %copy.53.pixels_ref = bf16[8,208,768]{2,1,0:T(8,128)(2,1)} copy(bf16[8,208,768]{1,2,0:T(8,128)(2,1)} %get-tuple-element.116) | data formatting | bytes 5111808 | tf_op jit(solution)/shard_map/jit(_pad)/pad | solution.py:1397
  110.9 81.5 %all-gather.7.cloned.1.call-done = bf16[32,3648,128]{2,1,0:T(8,128)(2,1)} async-done(((bf16[2,3648,128]{2,1,0:T(8,128)(2,1)}), bf16[32,3648,128]{2,1,0:T(8,128)(2,1)}) %all-gather.7.cloned.1.call-update) | async-done | bytes 29884432 | tf_op jit(solution)/shard_map/all_gather | solution.py:1393
  192.4 23.0 %shard_map.223 = (f32[8,208,768]{2,1,0:T(8,128)}, f32[8,208,128]{2,1,0:T(8,128)}, f32[8,16,208]{2,1,0:T(8,128)}, bf16[8,16,768]{2,1,0:T(8,128)(2,1)}, bf16[16,76...) custom-call(bf16[16,2,228,16,128]{4,3,2,1,0:T(8,128)(2,1)} %bitcast., ...), custom_call_target="tpu_custom_call" | custom-call | flops 60000002048 | bytes 40000000 | tf_op jit(solution)/shard_map/pallas_call | solution.py:641
  215.4 4.6 %all-to-all-start = ((bf16[32,8,256]{2,1,0:T(8,128)(2,1)}), bf16[32,8,256]{2,1,0:T(8,128)(2,1)S(1)}, u32[]{:S(2)}, u32[]{:S(2)}) async-start(bf16[32,8,256]{2,1,0:T(8,128)(2,1)} %get-tuple-element.70), calls=%async_computation | async-start | bytes 262144 | tf_op jit(solution)/shard_map/all_to_all | solution.py:1419
  220.0 1.8 collective-permute-start.7
  221.9 6.4 %all-to-all-done = bf16[32,8,256]{2,1,0:T(8,128)(2,1)S(1)} async-done(((bf16[32,8,256]{2,1,0:T(8,128)(2,1)}), bf16[32,8,256]{2,1,0:T(8,128)(2,1)S(1)}, u32[]{:S(2)}, u32[]{:S(2)}) %all-to-all-start) | async-done | bytes 131104 | tf_op jit(solution)/shard_map/all_to_all | solution.py:1419
  228.4 1.2 copy-done.3
  229.6 1.8 shard_map.224
  232.2 3.3 all-to-all-start.1
  235.6 4.5 %all-to-all-done.1.note_ref = f32[4,32,256]{2,1,0:T(8,128)S(1)} async-done(((f32[4,32,256]{2,1,0:T(8,128)}), f32[4,32,256]{2,1,0:T(8,128)S(1)}, u32[]{:S(2)}, u32[]{:S(2)}) %all-to-all-start.1) | async-done | bytes 131104 | tf_op jit(solution)/shard_map/all_to_all | solution.py:1436
  240.2 13.0 %shard_map.225 = (bf16[8,9728]{1,0:T(8,128)(2,1)S(1)}, f32[8,768]{1,0:T(8,128)S(1)}, f32[8,768]{1,0:T(8,128)S(1)}) custom-call(s32[1]{0:T(128)} %bitcast.2.low_ref, bf16[16,2,228,16,128]{4,3,2,1,0:T(8,128)(2,1)} %bitcast.72, f32[4,32,256]{2,1,0:T(8,128)S(1)} %all-to-all-done.1.note_ref, f32[16,768]{1,0:T(8,128)S(1)} %copy-done.10, f32[8,3072]{1,0:T(8,128)S(1)} %copy-done.11, ...), custom_call_target="tpu_custom_call" | custom-call | flops 30000001024 | bytes 30000000 | tf_op jit(solution)/shard_map/pallas_call | solution.py:873
  253.3 1.5 collective-permute-start.8
  254.8 1.7 shard_map.226
  259.5 17.3 %shard_map.227 = (f32[608,768]{1,0:T(8,128)}, bf16[608,768]{1,0:T(8,128)(2,1)}) custom-call(s32[1]{0:T(128)} %bitcast.25.odd_ref, bf16[8,9728]{1,0:T(8,128)(2,1)} %copy-done.7, f32[8,768]{1,0:T(8,128)} %copy-done.13, f32[8,768]{1,0:T(8,128)} %copy-done.14, f32[8,208,768]{2,1,0:T(8,128)} %get-tuple-element.86.unit_ref, ...), custom_call_target="tpu_custom_call" | custom-call | flops 15000000512 | bytes 15000000 | tf_op jit(solution)/shard_map/pallas_call | solution.py:1008
  276.9 2.7 collective-permute-done.9
  279.6 1.7 convert_add_fusion
  282.5 12.3 %collective-permute-done.10 = bf16[320,768]{1,0:T(8,128)(2,1)S(1)} collective-permute-done((bf16[320,768]{1,0:T(8,128)(2,1)S(1)}, bf16[320,768]{1,0:T(8,128)(2,1)S(1)}, u32[]{:S(2)}, u32[]{:S(2)}) %collective-permute-start.10) | collective-permute-done | bytes 491552 | tf_op jit(solution)/shard_map/ppermute | solution.py:1469
  295.1 1.3 collective-permute-start.11
  296.4 1.2 fusion.21.tab_ref
  298.4 14.1 %collective-permute-done.11 = bf16[320,768]{1,0:T(8,128)(2,1)S(1)} collective-permute-done((bf16[320,768]{1,0:T(8,128)(2,1)S(1)}, bf16[320,768]{1,0:T(8,128)(2,1)S(1)}, u32[]{:S(2)}, u32[]{:S(2)}) %collective-permute-start.11) | collective-permute-done | bytes 491552 | tf_op jit(solution)/shard_map/ppermute | solution.py:1483
  312.6 1.3 collective-permute-start.12
  315.2 16.6 %collective-permute-done.12 = bf16[320,768]{1,0:T(8,128)(2,1)S(1)} collective-permute-done((bf16[320,768]{1,0:T(8,128)(2,1)S(1)}, bf16[320,768]{1,0:T(8,128)(2,1)S(1)}, u32[]{:S(2)}, u32[]{:S(2)}) %collective-permute-start.12) | collective-permute-done | bytes 491552 | tf_op jit(solution)/shard_map/ppermute | solution.py:1483
  332.9 1.3 collective-permute-start.15
  336.6 3.1 collective-permute-done.14
  340.3 3.9 %shard_map.228 = (f32[3656,128]{1,0:T(8,128)}, f32[32,1,128]{2,1,0:T(1,128)}) custom-call(s32[15]{0:T(128)} %fusion.21.tab_ref, bf16[128,20224]{1,0:T(8,128)(2,1)} %all-gather.9.cloned.1.call-done.common_hbm, bf16[128,9728]{1,0:T(8,128)(2,1)} %all-gather.11.cloned.1.call-done.behind_hbm, f32[8,128]{1,0:T(8,128)} %copy-done.9, ...), custom_call_target="tpu_custom_call" | custom-call | flops 10000000000 | bytes 10000000 | tf_op jit(solution)/shard_map/pallas_call | solution.py:1207
  344.2 6.1 %all-to-all-start.2 = ((f32[32,1,128]{2,1,0:T(1,128)}), f32[32,1,128]{2,1,0:T(1,128)S(1)}, u32[]{:S(2)}, u32[]{:S(2)}) async-start(f32[32,1,128]{2,1,0:T(1,128)} %get-tuple-element.101), calls=%async_computation.2 | async-start | bytes 32768 | tf_op jit(solution)/shard_map/all_to_all | solution.py:1520
  350.6 1.3 copy-done.2
  351.9 2.1 shard_map.229
  354.1 3.3 all-to-all-done.2
  358.8 2.4 multiply_add_fusion.2
  361.2 6.6 %multiply_add_fusion = (f32[441096]{0:T(1024)}, f32[441096]{0:T(1024)}, f32[441096]{0:T(1024)}, f32[441096]{0:T(1024)}) fusion(f32[441096]{0:T(1024)S(1)} %copy-done.19, f32[441096]{0:T(1024)} %param.14, f32[]{:T(128)S(6)} %min_shard_map.3, f32[442368]{0:T(1024)S(1)} %bitcast.64, f32[441096]{0:T(1024)} %param.15, f32[441096]{0:T(1024)} %param.16), kind=kLoop, calls=%fused_computation.21 | loop fusion | flops 8380824 | bytes 15879460 | tf_op jit(solution)/shard_map/add | solution.py:1561
  (139 shorter events, 21.2 us)
Async XLA Ops:
  7.2 185.2 %all-gather.7.cloned.1.call-start = ((), (), s32[]{:S(2)}) async-start(), calls=%async_computation.3 | async-start | bytes 31752192 | tf_op jit(solution)/shard_map/all_gather | solution.py:1393
  8.9 3.1 copy-start.22
  9.0 3.0 copy-start.21
  9.8 11.0 %copy-start.18 = (f32[441096]{0:T(1024)S(1)}, f32[441096]{0:T(1024)}, u32[]{:S(2)}) copy-start(f32[441096]{0:T(1024)} %param.17) | copy-start | bytes 5293156
  9.8 11.0 %copy-start.20 = (f32[441096]{0:T(1024)S(1)}, f32[441096]{0:T(1024)}, u32[]{:S(2)}) copy-start(f32[441096]{0:T(1024)} %param.14) | copy-start | bytes 5293156
  12.1 12.6 %collective-permute-start.1 = (bf16[2,32,2048]{2,1,0:T(8,128)(2,1)S(1)}, bf16[2,32,2048]{2,1,0:T(8,128)(2,1)S(1)}, u32[]{:S(2)}, u32[]{:S(2)}) collective-permute-start(bf16[2,32,2048]{2,1,0:T(8,128)(2,1)S(1)} %pad_maximum_fusion.2), channel_id=1, source_target_pairs={{0,8},{4,12},{8,16},{12,20},{16,24},{20,28},{24,0},{28,4},{1,9},{5... | collective-permute-start | bytes 786440 | tf_op jit(solution)/shard_map/ppermute | solution.py:1388
  15.1 20.0 %collective-permute-start.2 = (bf16[2,32,2048]{2,1,0:T(8,128)(2,1)S(1)}, bf16[2,32,2048]{2,1,0:T(8,128)(2,1)S(1)}, u32[]{:S(2)}, u32[]{:S(2)}) collective-permute-start(bf16[2,32,2048]{2,1,0:T(8,128)(2,1)S(1)} %pad_maximum_fusion.2), channel_id=1, source_target_pairs={{0,16},{4,20},{8,24},{12,28},{16,0},{20,4},{24,8},{28,12},{1,17},{... | collective-permute-start | bytes 786440 | tf_op jit(solution)/shard_map/ppermute | solution.py:1388
  18.0 17.1 %collective-permute-start.3 = (bf16[2,32,2048]{2,1,0:T(8,128)(2,1)S(1)}, bf16[2,32,2048]{2,1,0:T(8,128)(2,1)S(1)}, u32[]{:S(2)}, u32[]{:S(2)}) collective-permute-start(bf16[2,32,2048]{2,1,0:T(8,128)(2,1)S(1)} %pad_maximum_fusion.2), channel_id=1, source_target_pairs={{0,24},{4,28},{8,0},{12,4},{16,8},{20,12},{24,16},{28,20},{1,25},{... | collective-permute-start | bytes 786440 | tf_op jit(solution)/shard_map/ppermute | solution.py:1388
  19.1 21.7 %collective-permute-start = (bf16[3648,128]{1,0:T(8,128)(2,1)S(1)}, bf16[3648,128]{1,0:T(8,128)(2,1)S(1)}, u32[]{:S(2)}, u32[]{:S(2)}) collective-permute-start(bf16[3648,128]{1,0:T(8,128)(2,1)S(1)} %shard_map.221), channel_id=1, source_target_pairs={{0,4},{4,0},{8,12},{12,8},{16,20},{20,16},{24,28},{28,24},{1,5},{5... | collective-permute-start | bytes 2801672 | tf_op jit(solution)/shard_map/ppermute | solution.py:1370
  43.6 5.7 %copy-start.24 = (s32[4]{0:T(128)S(1)}, s32[4]{0:T(128)}, u32[]{:S(2)}) copy-start(s32[4]{0:T(128)} %param.24) | copy-start | bytes 52
  43.6 50.1 %collective-permute-start.6 = (bf16[4,2,32,2048]{3,2,1,0:T(8,128)(2,1)}, bf16[4,2,32,2048]{3,2,1,0:T(8,128)(2,1)S(1)}, u32[]{:S(2)}, u32[]{:S(2)}) collective-permute-start(bf16[4,2,32,2048]{3,2,1,0:T(8,128)(2,1)} %constant_dynamic-slice_fusion), channel_id=1, source_target_pairs={{0,4},{4,0},{8,12},{12,8},{16,20},{20,16},{24,28},{28,24},{1,5},{5... | collective-permute-start | bytes 3145736 | tf_op jit(solution)/shard_map/ppermute | solution.py:1370
  45.3 52.3 %collective-permute-start.4 = (bf16[4,196,768]{2,0,1:T(4,128)(2,1)}, bf16[4,196,768]{2,0,1:T(4,128)(2,1)}, u32[]{:S(2)}, u32[]{:S(2)}) collective-permute-start(bf16[4,196,768]{2,0,1:T(4,128)(2,1)} %param.23), channel_id=1, source_target_pairs={{0,4},{4,0},{8,12},{12,8},{16,20},{20,16},{24,28},{28,24},{1,5},{5... | collective-permute-start | bytes 3612680 | tf_op jit(solution)/shard_map/ppermute | solution.py:1370
  49.3 43.7 %collective-permute-start.5 = (f32[4]{0:T(128)S(1)}, f32[4]{0:T(128)S(1)}, u32[]{:S(2)}, u32[]{:S(2)}) collective-permute-start(f32[4]{0:T(128)S(1)} %convert_element_type.74), channel_id=1, source_target_pairs={{0,4},{4,0},{8,12},{12,8},{16,20},{20,16},{24,28},{28,24},{1,5},{5... | collective-permute-start | bytes 56 | tf_op jit(solution)/shard_map/ppermute | solution.py:1370
  95.1 1.4 copy-start
  192.4 36.0 %copy-start.8 = (f32[2048]{0:T(1024)S(1)}, f32[2048]{0:T(1024)}, u32[]{:S(2)}) copy-start(f32[2048]{0:T(1024)} %param.22) | copy-start | bytes 24580
  215.4 12.9 %all-to-all-start = ((bf16[32,8,256]{2,1,0:T(8,128)(2,1)}), bf16[32,8,256]{2,1,0:T(8,128)(2,1)S(1)}, u32[]{:S(2)}, u32[]{:S(2)}) async-start(bf16[32,8,256]{2,1,0:T(8,128)(2,1)} %get-tuple-element.70), calls=%async_computation | async-start | bytes 262144 | tf_op jit(solution)/shard_map/all_to_all | solution.py:1419
  220.0 75.0 %all-gather.9.cloned.1.call-start = ((), (), s32[]{:S(2)}) async-start(), calls=%async_computation.4 | async-start | bytes 5500928 | tf_op jit(solution)/shard_map/all_gather | solution.py:1422
  220.0 11.4 %collective-permute-start.7 = (bf16[8,20224]{1,0:T(8,128)(2,1)}, bf16[8,20224]{1,0:T(8,128)(2,1)S(1)}, u32[]{:S(2)}, u32[]{:S(2)}) collective-permute-start(bf16[8,20224]{1,0:T(8,128)(2,1)} %get-tuple-element.74), channel_id=1, source_target_pairs={{0,4},{4,0},{8,12},{12,8},{16,20},{20,16},{24,28},{28,24},{1,5},{5... | collective-permute-start | bytes 970760 | tf_op jit(solution)/shard_map/ppermute | solution.py:1370
  228.3 1.2 copy-start.3
  229.6 1.9 copy-start.23
  229.6 10.6 %copy-start.10 = (f32[16,768]{1,0:T(8,128)S(1)}, f32[16,768]{1,0:T(8,128)}, u32[]{:S(2)}) copy-start(f32[16,768]{1,0:T(8,128)} %get-tuple-element.76.class_ref) | copy-start | bytes 147460
  229.6 10.6 %copy-start.11 = (f32[8,3072]{1,0:T(8,128)S(1)}, f32[8,3072]{1,0:T(8,128)}, u32[]{:S(2)}) copy-start(f32[8,3072]{1,0:T(8,128)} %get-tuple-element.77.hidden_ref) | copy-start | bytes 294916
  229.6 10.6 %copy-start.12 = (f32[4,8,768]{2,1,0:T(8,128)S(1)}, f32[4,8,768]{2,1,0:T(8,128)}, u32[]{:S(2)}) copy-start(f32[4,8,768]{2,1,0:T(8,128)} %get-tuple-element.81.middle_ref) | copy-start | bytes 294916
  229.6 10.6 %copy-start.15 = (f32[8,2048]{1,0:T(8,128)S(1)}, f32[8,2048]{1,0:T(8,128)}, u32[]{:S(2)}) copy-start(f32[8,2048]{1,0:T(8,128)} %get-tuple-element.78.one_ref) | copy-start | bytes 196612
  229.6 10.6 %copy-start.16 = (f32[8,2048]{1,0:T(8,128)S(1)}, f32[8,2048]{1,0:T(8,128)}, u32[]{:S(2)}) copy-start(f32[8,2048]{1,0:T(8,128)} %get-tuple-element.79.two_ref) | copy-start | bytes 196612
  229.6 10.6 %copy-start.17 = (f32[8,256]{1,0:T(8,128)S(1)}, f32[8,256]{1,0:T(8,128)}, u32[]{:S(2)}) copy-start(f32[8,256]{1,0:T(8,128)} %get-tuple-element.80.bottle_ref) | copy-start | bytes 24580
  232.2 7.9 %all-to-all-start.1 = ((f32[4,32,256]{2,1,0:T(8,128)}), f32[4,32,256]{2,1,0:T(8,128)S(1)}, u32[]{:S(2)}, u32[]{:S(2)}) async-start(f32[4,32,256]{2,1,0:T(8,128)} %get-tuple-element.75), calls=%async_computation.1 | async-start | bytes 262144 | tf_op jit(solution)/shard_map/all_to_all | solution.py:1436
  235.6 104.8 %all-gather.11.cloned.1.call-start = ((), (), s32[]{:S(2)}) async-start(), calls=%async_computation.5 | async-start | bytes 2646016 | tf_op jit(solution)/shard_map/all_gather | solution.py:1422
  240.2 14.6 %copy-start.1 = (f32[1,4,2,32,2048]{4,3,2,1,0:T(8,128)S(1)}, f32[1,4,2,32,2048]{4,3,2,1,0:T(8,128)}, u32[]{:S(2)}) copy-start(f32[1,4,2,32,2048]{4,3,2,1,0:T(8,128)} %copy-done) | copy-start | bytes 6291460
  240.2 14.6 %copy-start.4 = (bf16[256,2048]{1,0:T(8,128)(2,1)S(1)}, bf16[256,2048]{1,0:T(8,128)(2,1)}, u32[]{:S(2)}) copy-start(bf16[256,2048]{1,0:T(8,128)(2,1)} %multiply_convert_fusion.columns_ref) | copy-start | bytes 3145732
  253.3 3.2 copy-start.13
  253.3 3.2 copy-start.14
  253.3 5.6 %copy-start.7 = (bf16[8,9728]{1,0:T(8,128)(2,1)}, bf16[8,9728]{1,0:T(8,128)(2,1)S(1)}, u32[]{:S(2)}) copy-start(bf16[8,9728]{1,0:T(8,128)(2,1)S(1)} %get-tuple-element.82.behind_ref) | copy-start | bytes 466948
  253.3 5.6 %collective-permute-start.8 = (bf16[8,9728]{1,0:T(8,128)(2,1)S(1)}, bf16[8,9728]{1,0:T(8,128)(2,1)S(1)}, u32[]{:S(2)}, u32[]{:S(2)}) collective-permute-start(bf16[8,9728]{1,0:T(8,128)(2,1)S(1)} %get-tuple-element.82.behind_ref), channel_id=1, source_target_pairs={{0,4},{4,0},{8,12},{12,8},{16,20},{20,16},{24,28},{28,24},{1,5},{5... | collective-permute-start | bytes 466952 | tf_op jit(solution)/shard_map/ppermute | solution.py:1370
  256.5 0.7 copy-start.5
  257.2 0.6 copy-start.9
  276.9 2.7 collective-permute-start.9
  281.4 13.5 %collective-permute-start.10 = (bf16[320,768]{1,0:T(8,128)(2,1)S(1)}, bf16[320,768]{1,0:T(8,128)(2,1)S(1)}, u32[]{:S(2)}, u32[]{:S(2)}) collective-permute-start(bf16[320,768]{1,0:T(8,128)(2,1)S(1)} %pad_maximum_fusion.1), channel_id=1, source_target_pairs={{0,2},{1,3},{2,0},{3,1},{4,6},{5,7},{6,4},{7,5},{8,10},{9,11},{10,... | collective-permute-start | bytes 1474568 | tf_op jit(solution)/shard_map/ppermute | solution.py:1469
  295.1 17.4 %collective-permute-start.11 = (bf16[320,768]{1,0:T(8,128)(2,1)S(1)}, bf16[320,768]{1,0:T(8,128)(2,1)S(1)}, u32[]{:S(2)}, u32[]{:S(2)}) collective-permute-start(bf16[320,768]{1,0:T(8,128)(2,1)S(1)} %convert_element_type.83), channel_id=1, source_target_pairs={{8,0},{12,4},{24,16},{28,20},{9,1},{13,5},{25,17},{29,21},{10,2},{... | collective-permute-start | bytes 1474568 | tf_op jit(solution)/shard_map/ppermute | solution.py:1483
  312.6 19.2 %collective-permute-start.12 = (bf16[320,768]{1,0:T(8,128)(2,1)S(1)}, bf16[320,768]{1,0:T(8,128)(2,1)S(1)}, u32[]{:S(2)}, u32[]{:S(2)}) collective-permute-start(bf16[320,768]{1,0:T(8,128)(2,1)S(1)} %fusion.12), channel_id=1, source_target_pairs={{16,0},{20,4},{17,1},{21,5},{18,2},{22,6},{19,3},{23,7}} | collective-permute-start | bytes 1474568 | tf_op jit(solution)/shard_map/ppermute | solution.py:1483
  332.9 3.7 collective-permute-start.15
  334.6 9.7 %collective-permute-start.13 = (bf16[288,768]{1,0:T(8,128)(2,1)S(1)}, bf16[288,768]{1,0:T(8,128)(2,1)S(1)}, u32[]{:S(2)}, u32[]{:S(2)}) collective-permute-start(bf16[288,768]{1,0:T(8,128)(2,1)S(1)} %slice.98), channel_id=1, source_target_pairs={{0,2},{1,3},{2,0},{3,1},{4,6},{5,7},{6,4},{7,5},{8,10},{9,11},{10,... | collective-permute-start | bytes 1327112 | tf_op jit(solution)/shard_map/ppermute | solution.py:1469
  335.6 4.1 %collective-permute-start.14 = (bf16[32,768]{1,0:T(8,128)(2,1)S(1)}, bf16[32,768]{1,0:T(8,128)(2,1)S(1)}, u32[]{:S(2)}, u32[]{:S(2)}) collective-permute-start(bf16[32,768]{1,0:T(8,128)(2,1)S(1)} %slice.100), channel_id=1, source_target_pairs={{0,4},{4,0},{8,12},{12,8},{16,20},{20,16},{24,28},{28,24},{1,5},{5... | collective-permute-start | bytes 147464 | tf_op jit(solution)/shard_map/ppermute | solution.py:1370
  344.2 13.2 %all-to-all-start.2 = ((f32[32,1,128]{2,1,0:T(1,128)}), f32[32,1,128]{2,1,0:T(1,128)S(1)}, u32[]{:S(2)}, u32[]{:S(2)}) async-start(f32[32,1,128]{2,1,0:T(1,128)} %get-tuple-element.101), calls=%async_computation.2 | async-start | bytes 32768 | tf_op jit(solution)/shard_map/all_to_all | solution.py:1520
  350.4 1.5 copy-start.2
  351.9 6.9 %copy-start.6 = (f32[32,2048]{1,0:T(8,128)S(1)}, f32[32,2048]{1,0:T(8,128)}, u32[]{:S(2)}) copy-start(f32[32,2048]{1,0:T(8,128)} %copy-done.5) | copy-start | bytes 786436
  358.8 2.5 copy-start.19
Sparse Core Ops, SparseCore 0:
  42.4 149.8 all-gather.6
  232.3 55.8 all-gather.8
  295.1 45.1 all-gather.10
